TPU v7x, 32 devices: a whole 2x2x4 slice. The times are simulated.
32 devices in a mesh: seq: 16 (over z, y, core), dp: 2 (over x).
Axes of the slice: x: 2, y: 2, z: 4, core: 2. Of those that a mesh axis runs over, the one named last changes fastest.
Arguments:
- bases: int32 [2, 2816], P('dp', 'seq'), may hold values from 0 to 3
- embed: bfloat16 [4, 768], replicated, may hold values from -6 to 6
- conv_weight: bfloat16 [3, 2304, 384], replicated, may hold values from -0.125 to 0.125
- point_weight: bfloat16 [3, 384, 768], replicated, may hold values from -0.3125 to 0.3125
- cotangent: bfloat16 [2, 2816, 768], P('dp', 'seq'), may hold values from -6 to 6
Outputs:
- features: float32 [2, 2816, 768], P('dp', 'seq')
- conv_grad: float32 [3, 2304, 384], P(None, 'seq')
- point_grad: float32 [3, 384, 768], P(None, None, 'seq')
- embed_grad: float32 [4, 768], P(None, 'seq')
All inputs are finite; a program needn't handle non-finite values.
Results may differ from a plain program's by a relative error of at most 0.012.
Values may be sent and summed in bfloat16 or wider, within the bound.
No kernel may reach another device: no remote copies, remote signals or barrier semaphores. Data moves between devices by JAX's collectives and lax.ppermute only.
A program may use at most 128 MiB of HBM per device.

v0:
```python
import math

import jax
import jax.numpy as jnp
from jax import lax
from jax.sharding import PartitionSpec as P


def padded(block, sides, width):
    for axis, dim in sides:
        count = lax.axis_size(axis)
        forward = [(i, i + 1) for i in range(count - 1)]
        backward = [(target, source) for source, target in forward]
        low = lax.ppermute(
            lax.slice_in_dim(block, block.shape[dim] - width, None, axis=dim), axis, forward
        )
        high = lax.ppermute(lax.slice_in_dim(block, 0, width, axis=dim), axis, backward)
        block = jnp.concatenate([low, block, high], axis=dim)
    return block


def passed_along(block, axis, distance):
    devices = range(lax.axis_size(axis))
    route = [(i - distance, i) for i in devices if i - distance in devices]
    return lax.ppermute(block, axis, route)


def gelu_pair(value_entry):
    coef = math.sqrt(2.0 / math.pi)
    inner = coef * (value_entry + 0.044715 * value_entry * value_entry * value_entry)
    tanh_val = jnp.tanh(inner)
    result = 0.5 * value_entry * (1.0 + tanh_val)
    slope = 0.5 * (1.0 + tanh_val) + 0.5 * value_entry * (1.0 - tanh_val * tanh_val) * coef * (
        1.0 + 3.0 * 0.044715 * value_entry * value_entry
    )
    return (result, slope)


def spread_kernel_taps(value_entry, dilation_step):
    row_block = value_entry.shape[0]
    if dilation_step < row_block:
        padded_rows = padded(value_entry, (("seq", 0),), dilation_step)
        lower_window = padded_rows[:row_block]
        upper_window = padded_rows[2 * dilation_step : 2 * dilation_step + row_block]
    else:
        hop_offsets = dilation_step // row_block
        lower_window = passed_along(value_entry, "seq", hop_offsets)
        upper_window = passed_along(value_entry, "seq", -hop_offsets)
    return jnp.concatenate([lower_window, value_entry, upper_window], axis=1)


def layer_entry(residual_state, weight_arrays, dilation_step):
    scale = lax.rsqrt(jnp.mean(residual_state * residual_state, axis=-1, keepdims=True) + 1e-06)
    normalized_rows = (residual_state * scale).astype(jnp.bfloat16)
    kernel_taps = spread_kernel_taps(normalized_rows, dilation_step)
    pre = jnp.dot(kernel_taps, weight_arrays, preferred_element_type=jnp.float32)
    act_f, slope = gelu_pair(pre)
    return (scale, kernel_taps, act_f.astype(jnp.bfloat16), slope)


def on_device(bases, embed, conv_weight, point_weight, cotangent):
    row_block = bases.shape[1]
    width = embed.shape[1]
    layers = conv_weight.shape[0]
    mid = conv_weight.shape[2]
    dilation_list = [row_block // 8, 2 * row_block, 8 * row_block]
    base_row = bases[0]
    onehot = base_row[:, None] == jnp.arange(4, dtype=jnp.int32)[None, :]
    residual_state = jnp.dot(onehot.astype(jnp.bfloat16), embed, preferred_element_type=jnp.float32)
    saved = []
    for layer in range(layers):
        scale, kernel_taps, act, slope = layer_entry(
            residual_state, conv_weight[layer], dilation_list[layer]
        )
        saved.append((residual_state, scale, kernel_taps, act, slope))
        residual_state = residual_state + jnp.dot(
            act, point_weight[layer], preferred_element_type=jnp.float32
        )
    features = residual_state[None]
    back = cotangent[0].astype(jnp.float32)
    conv_terms = [None] * layers
    point_terms = [None] * layers
    for layer in reversed(range(layers)):
        stream_in = saved[layer][0]
        scale, kernel_taps, act, slope = saved[layer][1:]
        back_rounded = back.astype(jnp.bfloat16)
        point_terms[layer] = lax.dot_general(
            act, back_rounded, (((0,), (0,)), ((), ())), preferred_element_type=jnp.float32
        )
        pre_grad = (
            lax.dot_general(
                back_rounded,
                point_weight[layer],
                (((1,), (1,)), ((), ())),
                preferred_element_type=jnp.float32,
            )
            * slope
        ).astype(jnp.bfloat16)
        conv_terms[layer] = lax.dot_general(
            kernel_taps, pre_grad, (((0,), (0,)), ((), ())), preferred_element_type=jnp.float32
        )
        grad_taps = spread_kernel_taps(pre_grad, dilation_list[layer]).reshape(row_block, 3, mid)
        blocks = conv_weight[layer].reshape(3, width, mid)[::-1]
        normed_grad = jnp.einsum(
            "pjm,jdm->pd", grad_taps, blocks, preferred_element_type=jnp.float32
        )
        inner = jnp.mean(normed_grad * stream_in, axis=-1, keepdims=True)
        back = back + scale * (normed_grad - stream_in * scale * scale * inner)
    embed_terms = lax.dot_general(
        onehot.astype(jnp.float32), back, (((0,), (0,)), ((), ())), precision=lax.Precision.HIGHEST
    )
    conv_all = jnp.stack(conv_terms)
    point_all = jnp.stack(point_terms)
    shares = (
        lax.psum_scatter(conv_all, "seq", scatter_dimension=1, tiled=True),
        lax.psum_scatter(point_all, "seq", scatter_dimension=2, tiled=True),
        lax.psum_scatter(embed_terms, "seq", scatter_dimension=1, tiled=True),
    )
    conv_grad, point_grad, embed_grad = lax.psum((shares[0], shares[1], shares[2]), "dp")
    return (features, conv_grad, point_grad, embed_grad)


def solution(mesh):
    in_specs = (P("dp", "seq"), P(), P(), P(), P("dp", "seq", None))
    out_specs = (P("dp", "seq", None), P(None, "seq", None), P(None, None, "seq"), P(None, "seq"))
    return jax.shard_map(
        on_device, mesh=mesh, in_specs=in_specs, out_specs=out_specs, check_vma=False
    )
```

profile of v0, /device:TPU:0, one launch (start us, length us, event | category | flops | bytes accessed | tf_op | source)
XLA Modules:
  0.0 440.4 jit_solution(17103908034882583499)
XLA Ops:
  7.2 0.6 copy-done
  7.9 1.1 multiply_reduce_fusion.5
  9.1 2.6 collective-permute-start
  11.7 1.6 collective-permute-start.1
  13.3 3.9 collective-permute-done.1
  17.2 0.6 copy-done.35
  17.9 2.1 fusion.4
  20.0 0.4 multiply_reduce_fusion.4
  20.6 1.3 collective-permute-start.3
  21.9 5.1 %collective-permute-start.2 = (bf16[176,768]{1,0:T(8,128)(2,1)S(1)}, bf16[176,768]{1,0:T(8,128)(2,1)S(1)}, u32[]{:S(2)}, u32[]{:S(2)}) collective-permute-start(bf16[176,768]{1,0:T(8,128)(2,1)S(1)} %multiply_convert_fusion.1), channel_id=1, source_target_pairs={{0,4},{2,6},{4,8},{6,10},{8,12},{10,14},{12,16},{14,18},{16,20},{1... | collective-permute-start | bytes 811016 | tf_op jit(solution)/shard_map/ppermute | solution.py:25
  27.0 3.5 collective-permute-done.3
  30.4 8.0 %collective-permute-done.2 = bf16[176,768]{1,0:T(8,128)(2,1)S(1)} collective-permute-done((bf16[176,768]{1,0:T(8,128)(2,1)S(1)}, bf16[176,768]{1,0:T(8,128)(2,1)S(1)}, u32[]{:S(2)}, u32[]{:S(2)}) %collective-permute-start.2) | collective-permute-done | bytes 270368 | tf_op jit(solution)/shard_map/ppermute | solution.py:25
  38.5 0.6 fusion.2
  39.1 0.1 copy-done.26
  39.2 0.4 multiply_reduce_fusion.3
  39.8 1.3 collective-permute-start.5
  41.1 5.5 %collective-permute-start.4 = (bf16[176,768]{1,0:T(8,128)(2,1)S(1)}, bf16[176,768]{1,0:T(8,128)(2,1)S(1)}, u32[]{:S(2)}, u32[]{:S(2)}) collective-permute-start(bf16[176,768]{1,0:T(8,128)(2,1)S(1)} %multiply_convert_fusion), channel_id=1, source_target_pairs={{0,16},{2,18},{4,20},{6,22},{8,24},{10,26},{12,28},{14,30},{1,17},... | collective-permute-start | bytes 811016 | tf_op jit(solution)/shard_map/ppermute | solution.py:25
  46.6 1.8 fusion.75
  48.3 8.7 %collective-permute-done.5 = bf16[176,768]{1,0:T(8,128)(2,1)S(1)} collective-permute-done((bf16[176,768]{1,0:T(8,128)(2,1)S(1)}, bf16[176,768]{1,0:T(8,128)(2,1)S(1)}, u32[]{:S(2)}, u32[]{:S(2)}) %collective-permute-start.5) | collective-permute-done | bytes 270368 | tf_op jit(solution)/shard_map/ppermute | solution.py:25
  57.1 0.6 fusion
  57.8 0.1 copy-done.30
  57.9 0.4 fusion.7
  58.3 1.3 collective-permute-start.7
  59.6 5.5 %collective-permute-start.6 = (bf16[176,384]{1,0:T(8,128)(2,1)S(1)}, bf16[176,384]{1,0:T(8,128)(2,1)S(1)}, u32[]{:S(2)}, u32[]{:S(2)}) collective-permute-start(bf16[176,384]{1,0:T(8,128)(2,1)S(1)} %fusion.7), channel_id=1, source_target_pairs={{0,16},{2,18},{4,20},{6,22},{8,24},{10,26},{12,28},{14,30},{1,17},... | collective-permute-start | bytes 405512 | tf_op jit(solution)/shard_map/ppermute | solution.py:25
  65.0 0.4 convolution_bitcast_fusion.3
  65.4 3.5 collective-permute-done.7
  69.0 0.8 multiply_reduce_fusion.2
  69.8 0.2 multiply_add_fusion.1
  70.0 0.4 fusion.8
  70.4 1.3 collective-permute-start.9
  71.7 4.8 %collective-permute-start.8 = (bf16[176,384]{1,0:T(8,128)(2,1)S(1)}, bf16[176,384]{1,0:T(8,128)(2,1)S(1)}, u32[]{:S(2)}, u32[]{:S(2)}) collective-permute-start(bf16[176,384]{1,0:T(8,128)(2,1)S(1)} %fusion.8), channel_id=1, source_target_pairs={{0,4},{2,6},{4,8},{6,10},{8,12},{10,14},{12,16},{14,18},{16,20},{1... | collective-permute-start | bytes 405512 | tf_op jit(solution)/shard_map/ppermute | solution.py:25
  76.6 0.4 convolution_bitcast_fusion.4
  77.0 0.6 collective-permute-done.9
  77.6 1.9 collective-permute-done.8
  79.5 0.8 multiply_reduce_fusion.1
  80.4 0.2 multiply_add_fusion
  80.6 0.8 copy-done.6
  81.4 0.4 convolution_bitcast_fusion.5
  81.8 0.2 pad_maximum_fusion.1
  82.0 3.9 copy.19
  86.0 0.8 copy-done.12
  86.9 0.1 copy-done.29
  87.1 0.8 convolution_bitcast_fusion
  88.0 0.8 convolution_bitcast_fusion.1
  88.8 0.2 copy-done.7
  89.1 1.5 fusion.9
  90.6 0.8 convolution_bitcast_fusion.2
  91.4 4.8 %pad_maximum_fusion = f32[3,2304,384]{2,1,0:T(8,128)} fusion(f32[1,2304,384]{2,1,0:T(8,128)S(1)} %convolution_bitcast_fusion, f32[1,2304,384]{2,1,0:T(8,128)S(1)} %convolution_bitcast_fusion.1, f32[1,2304,384]{2,1,0:T(8,128)S(1)} %convolution_bitcast_fusion.2), kind=kLoop, calls=%fused_computation | loop fusion | flops 5308416 | bytes 21233664 | tf_op jit(solution)/shard_map/stack | solution.py:112
  96.3 1.4 collective-permute-start.10
  97.8 1.3 collective-permute-start.11
  99.1 0.6 dynamic-slice
  100.3 3.3 collective-permute-done.11
  103.7 0.8 multiply_reduce_fusion
  104.5 1.7 convolution_bitcast_fusion.9
  106.3 100.9 %all-reduce.5.cloned.1.call-done = f32[3,384,768]{1,0,2:T(4,128)} async-done(((f32[3,384,768]{1,0,2:T(4,128)}), f32[3,384,768]{1,0,2:T(4,128)}) %all-reduce.5.cloned.1.call-update) | async-done | bytes 3538960
  207.2 1.7 constant_dynamic-slice_fusion
  208.9 122.3 %reduce-scatter.5.cloned.1.call-done = f32[3,144,384]{2,1,0:T(8,128)} async-done(((f32[3,2304,384]{2,1,0:T(8,128)}), f32[3,144,384]{2,1,0:T(8,128)}) %reduce-scatter.5.cloned.1.call-update) | async-done | bytes 663568 | tf_op jit(solution)/shard_map/reduce_scatter | solution.py:115
  331.2 2.2 fusion.6
  333.4 57.2 %reduce-scatter.7.cloned.1.call-done = f32[48,4]{1,0:T(8,128)} async-done(((f32[768,4]{1,0:T(8,128)}), f32[48,4]{1,0:T(8,128)}) %reduce-scatter.7.cloned.1.call-update) | async-done | bytes 784
  390.6 0.8 copy.23
  391.4 5.5 %psum.23 = f32[4,48]{1,0:T(4,128)} all-reduce(f32[4,48]{1,0:T(4,128)S(1)} %copy.23), channel_id=1, replica_groups=mesh['seq'=16,'dp'=2] {'dp'}, use_global_device_ids=true, to_apply=%region_11.0 | all-reduce | flops 192 | bytes 1536 | tf_op jit(solution)/shard_map/psum | solution.py:119
  396.9 33.4 %all-reduce.7.cloned.1.call-done = (f32[3,144,384]{2,1,0:T(8,128)}, f32[3,384,48]{1,0,2:T(4,128)}) async-done(((f32[3,144,384]{2,1,0:T(8,128)}, f32[3,384,48]{1,0,2:T(4,128)}), (f32[3,144,384]{2,1,0:T(8,128)}, f32[3,384,48]{1,0,2:T(4,128)})) %all-reduce.7.cloned.1.call-update) | async-done | bytes 884752 | tf_op jit(solution)/shard_map/psum | solution.py:119
  430.3 1.7 copy.21
  431.9 2.0 copy.48
  (99 shorter events, 1.2 us)
Async XLA Ops:
  7.2 0.7 copy-start
  7.2 200.0 %all-reduce.5.cloned.1.call-start = ((), (), s32[]{:S(2)}) async-start(), calls=%async_computation.4 | async-start | bytes 9437184
  8.9 11.0 %copy-start.1 = (f32[176,768]{1,0:T(8,128)}, f32[176,768]{1,0:T(8,128)S(1)}, u32[]{:S(2)}) copy-start(f32[176,768]{1,0:T(8,128)S(1)} %get-tuple-element.26) | copy-start | bytes 1622020
  8.9 29.5 %slice-start = ((s8[5308416]{0:T(1024)(128)(4,1)}), s8[4194304]{0:T(1024)(128)(4,1)S(1)}, s32[]{:S(2)}) async-start(s8[5308416]{0:T(1024)(128)(4,1)} %bitcast.90), calls=%async_computation.6 | async-start | bytes 8388608
  9.1 10.9 %copy-start.22 = (bf16[176,768]{1,0:T(8,128)(2,1)}, bf16[176,768]{1,0:T(8,128)(2,1)S(1)}, u32[]{:S(2)}) copy-start(bf16[176,768]{1,0:T(8,128)(2,1)S(1)} %multiply_convert_fusion.2) | copy-start | bytes 811012
  9.1 4.2 collective-permute-start
  11.7 8.3 %copy-start.8 = (bf16[3,384,768]{2,1,0:T(8,128)(2,1)S(1)}, bf16[3,384,768]{2,1,0:T(8,128)(2,1)}, u32[]{:S(2)}) copy-start(bf16[3,384,768]{2,1,0:T(8,128)(2,1)} %param.8) | copy-start | bytes 5308420
  11.7 26.8 %slice-start.1 = ((s8[5308416]{0:T(1024)(128)(4,1)}), s8[1114112]{0:T(1024)(128)(4,1)S(1)}, s32[]{:S(2)}) async-start(s8[5308416]{0:T(1024)(128)(4,1)} %bitcast.90), calls=%async_computation.7 | async-start | bytes 2228224
  11.7 5.5 %collective-permute-start.1 = (bf16[22,768]{1,0:T(8,128)(2,1)S(1)}, bf16[22,768]{1,0:T(8,128)(2,1)S(1)}, u32[]{:S(2)}, u32[]{:S(2)}) collective-permute-start(bf16[22,768]{1,0:T(8,128)(2,1)S(1)} %get-tuple-element.22), channel_id=1, source_target_pairs={{2,0},{4,2},{6,4},{8,6},{10,8},{12,10},{14,12},{16,14},{18,16},{20... | collective-permute-start | bytes 101384 | tf_op jit(solution)/shard_map/ppermute | solution.py:17
  13.3 3.9 copy-start.33
  17.2 0.6 copy-start.35
  20.0 60.6 %copy-start.14 = (f32[176,384]{1,0:T(8,128)}, f32[176,384]{1,0:T(8,128)S(1)}, u32[]{:S(2)}) copy-start(f32[176,384]{1,0:T(8,128)S(1)} %fusion.4) | copy-start | bytes 811012
  20.5 18.5 %copy-start.9 = (bf16[176,768]{1,0:T(8,128)(2,1)}, bf16[176,768]{1,0:T(8,128)(2,1)S(1)}, u32[]{:S(2)}) copy-start(bf16[176,768]{1,0:T(8,128)(2,1)S(1)} %multiply_convert_fusion.1) | copy-start | bytes 811012
  20.6 9.9 %collective-permute-start.3 = (bf16[176,768]{1,0:T(8,128)(2,1)S(1)}, bf16[176,768]{1,0:T(8,128)(2,1)S(1)}, u32[]{:S(2)}, u32[]{:S(2)}) collective-permute-start(bf16[176,768]{1,0:T(8,128)(2,1)S(1)} %multiply_convert_fusion.1), channel_id=1, source_target_pairs={{4,0},{6,2},{8,4},{10,6},{12,8},{14,10},{16,12},{18,14},{20,16},{2... | collective-permute-start | bytes 811016 | tf_op jit(solution)/shard_map/ppermute | solution.py:25
  21.9 16.6 %collective-permute-start.2 = (bf16[176,768]{1,0:T(8,128)(2,1)S(1)}, bf16[176,768]{1,0:T(8,128)(2,1)S(1)}, u32[]{:S(2)}, u32[]{:S(2)}) collective-permute-start(bf16[176,768]{1,0:T(8,128)(2,1)S(1)} %multiply_convert_fusion.1), channel_id=1, source_target_pairs={{0,4},{2,6},{4,8},{6,10},{8,12},{10,14},{12,16},{14,18},{16,20},{1... | collective-permute-start | bytes 811016 | tf_op jit(solution)/shard_map/ppermute | solution.py:25
  30.4 8.6 %copy-start.24 = (bf16[176,768]{1,0:T(8,128)(2,1)}, bf16[176,768]{1,0:T(8,128)(2,1)S(1)}, u32[]{:S(2)}) copy-start(bf16[176,768]{1,0:T(8,128)(2,1)S(1)} %collective-permute-done.3) | copy-start | bytes 811012
  38.5 0.7 copy-start.26
  39.6 30.2 %copy-start.3 = (f32[176,768]{1,0:T(8,128)}, f32[176,768]{1,0:T(8,128)S(1)}, u32[]{:S(2)}) copy-start(f32[176,768]{1,0:T(8,128)S(1)} %get-tuple-element.30) | copy-start | bytes 1622020
  39.8 17.3 %copy-start.11 = (bf16[176,768]{1,0:T(8,128)(2,1)}, bf16[176,768]{1,0:T(8,128)(2,1)S(1)}, u32[]{:S(2)}) copy-start(bf16[176,768]{1,0:T(8,128)(2,1)S(1)} %multiply_convert_fusion) | copy-start | bytes 811012
  39.8 17.3 %collective-permute-start.5 = (bf16[176,768]{1,0:T(8,128)(2,1)S(1)}, bf16[176,768]{1,0:T(8,128)(2,1)S(1)}, u32[]{:S(2)}, u32[]{:S(2)}) collective-permute-start(bf16[176,768]{1,0:T(8,128)(2,1)S(1)} %multiply_convert_fusion), channel_id=1, source_target_pairs={{16,0},{18,2},{20,4},{22,6},{24,8},{26,10},{28,12},{30,14},{17,1},... | collective-permute-start | bytes 811016 | tf_op jit(solution)/shard_map/ppermute | solution.py:25
  41.1 16.0 %collective-permute-start.4 = (bf16[176,768]{1,0:T(8,128)(2,1)S(1)}, bf16[176,768]{1,0:T(8,128)(2,1)S(1)}, u32[]{:S(2)}, u32[]{:S(2)}) collective-permute-start(bf16[176,768]{1,0:T(8,128)(2,1)S(1)} %multiply_convert_fusion), channel_id=1, source_target_pairs={{0,16},{2,18},{4,20},{6,22},{8,24},{10,26},{12,28},{14,30},{1,17},... | collective-permute-start | bytes 811016 | tf_op jit(solution)/shard_map/ppermute | solution.py:25
  48.3 9.6 %copy-start.13 = (bf16[1,176,768]{2,1,0:T(8,128)(2,1)S(1)}, bf16[1,176,768]{2,1,0:T(8,128)(2,1)}, u32[]{:S(2)}) copy-start(bf16[1,176,768]{2,1,0:T(8,128)(2,1)} %param.9) | copy-start | bytes 811012
  57.1 0.7 copy-start.28
  57.1 0.8 copy-start.30
  57.9 7.6 %copy-start.16 = (f32[176,384]{1,0:T(8,128)}, f32[176,384]{1,0:T(8,128)S(1)}, u32[]{:S(2)}) copy-start(f32[176,384]{1,0:T(8,128)S(1)} %fusion) | copy-start | bytes 811012
  58.3 11.5 %copy-start.18 = (bf16[176,384]{1,0:T(8,128)(2,1)}, bf16[176,384]{1,0:T(8,128)(2,1)S(1)}, u32[]{:S(2)}) copy-start(bf16[176,384]{1,0:T(8,128)(2,1)S(1)} %fusion.7) | copy-start | bytes 405508
  58.3 10.7 %collective-permute-start.7 = (bf16[176,384]{1,0:T(8,128)(2,1)S(1)}, bf16[176,384]{1,0:T(8,128)(2,1)S(1)}, u32[]{:S(2)}, u32[]{:S(2)}) collective-permute-start(bf16[176,384]{1,0:T(8,128)(2,1)S(1)} %fusion.7), channel_id=1, source_target_pairs={{16,0},{18,2},{20,4},{22,6},{24,8},{26,10},{28,12},{30,14},{17,1},... | collective-permute-start | bytes 405512 | tf_op jit(solution)/shard_map/ppermute | solution.py:25
  59.6 9.4 %collective-permute-start.6 = (bf16[176,384]{1,0:T(8,128)(2,1)S(1)}, bf16[176,384]{1,0:T(8,128)(2,1)S(1)}, u32[]{:S(2)}, u32[]{:S(2)}) collective-permute-start(bf16[176,384]{1,0:T(8,128)(2,1)S(1)} %fusion.7), channel_id=1, source_target_pairs={{0,16},{2,18},{4,20},{6,22},{8,24},{10,26},{12,28},{14,30},{1,17},... | collective-permute-start | bytes 405512 | tf_op jit(solution)/shard_map/ppermute | solution.py:25
  70.4 9.9 %copy-start.20 = (bf16[176,384]{1,0:T(8,128)(2,1)}, bf16[176,384]{1,0:T(8,128)(2,1)S(1)}, u32[]{:S(2)}) copy-start(bf16[176,384]{1,0:T(8,128)(2,1)S(1)} %fusion.8) | copy-start | bytes 405508
  70.4 7.2 %collective-permute-start.9 = (bf16[176,384]{1,0:T(8,128)(2,1)S(1)}, bf16[176,384]{1,0:T(8,128)(2,1)S(1)}, u32[]{:S(2)}, u32[]{:S(2)}) collective-permute-start(bf16[176,384]{1,0:T(8,128)(2,1)S(1)} %fusion.8), channel_id=1, source_target_pairs={{4,0},{6,2},{8,4},{10,6},{12,8},{14,10},{16,12},{18,14},{20,16},{2... | collective-permute-start | bytes 405512 | tf_op jit(solution)/shard_map/ppermute | solution.py:25
  71.7 7.8 %collective-permute-start.8 = (bf16[176,384]{1,0:T(8,128)(2,1)S(1)}, bf16[176,384]{1,0:T(8,128)(2,1)S(1)}, u32[]{:S(2)}, u32[]{:S(2)}) collective-permute-start(bf16[176,384]{1,0:T(8,128)(2,1)S(1)} %fusion.8), channel_id=1, source_target_pairs={{0,4},{2,6},{4,8},{6,10},{8,12},{10,14},{12,16},{14,18},{16,20},{1... | collective-permute-start | bytes 405512 | tf_op jit(solution)/shard_map/ppermute | solution.py:25
  80.6 0.8 copy-start.6
  85.9 1.0 copy-start.12
  85.9 1.0 copy-start.19
  85.9 1.1 copy-start.29
  85.9 1.2 copy-start.31
  86.0 2.0 copy-start.10
  86.0 2.0 copy-start.21
  86.0 2.0 copy-start.25
  86.0 2.0 copy-start.27
  86.0 245.2 %reduce-scatter.5.cloned.1.call-start = ((), (), s32[]{:S(2)}) async-start(), calls=%async_computation.2 | async-start | bytes 11280384 | tf_op jit(solution)/shard_map/reduce_scatter | solution.py:115
  88.0 1.1 copy-start.7
  88.0 1.1 copy-start.15
  89.1 1.5 copy-start.23
  89.1 1.5 copy-start.34
  89.1 1.5 copy-start.36
  96.2 2.8 copy-start.37
  96.2 7.5 %copy-start.2 = (f32[176,768]{1,0:T(8,128)S(1)}, f32[176,768]{1,0:T(8,128)}, u32[]{:S(2)}) copy-start(f32[176,768]{1,0:T(8,128)} %copy-done.1) | copy-start | bytes 1622020
  96.2 7.5 %copy-start.5 = (bf16[1,2304,384]{2,1,0:T(8,128)(2,1)S(1)}, bf16[1,2304,384]{2,1,0:T(8,128)(2,1)}, u32[]{:S(2)}) copy-start(bf16[1,2304,384]{2,1,0:T(8,128)(2,1)} %get-tuple-element.18) | copy-start | bytes 5308420
  96.3 294.3 %reduce-scatter.7.cloned.1.call-start = ((), (), s32[]{:S(2)}) async-start(), calls=%async_computation.3 | async-start | bytes 417792
  96.3 4.0 collective-permute-start.10
  97.8 5.8 %collective-permute-start.11 = (bf16[22,384]{1,0:T(8,128)(2,1)S(1)}, bf16[22,384]{1,0:T(8,128)(2,1)S(1)}, u32[]{:S(2)}, u32[]{:S(2)}) collective-permute-start(bf16[22,384]{1,0:T(8,128)(2,1)S(1)} %get-tuple-element.24), channel_id=1, source_target_pairs={{2,0},{4,2},{6,4},{8,6},{10,8},{12,10},{14,12},{16,14},{18,16},{20... | collective-permute-start | bytes 50696 | tf_op jit(solution)/shard_map/ppermute | solution.py:17
  103.7 0.8 copy-start.32
  104.5 226.7 %copy-start.4 = (f32[176,768]{1,0:T(8,128)S(1)}, f32[176,768]{1,0:T(8,128)}, u32[]{:S(2)}) copy-start(f32[176,768]{1,0:T(8,128)} %copy-done.3) | copy-start | bytes 1622020
  104.5 226.7 %copy-start.17 = (f32[176,384]{1,0:T(8,128)S(1)}, f32[176,384]{1,0:T(8,128)}, u32[]{:S(2)}) copy-start(f32[176,384]{1,0:T(8,128)} %copy-done.16) | copy-start | bytes 811012
  106.3 324.0 %all-reduce.7.cloned.1.call-start = ((), (), s32[]{:S(2)}) async-start(), calls=%async_computation.5 | async-start | bytes 1916928 | tf_op jit(solution)/shard_map/psum | solution.py:119
Sparse Core Ops, SparseCore 0:
  86.1 121.0 all-reduce.4
  211.3 119.8 reduce-scatter.4
  335.3 55.2 reduce-scatter.6
  392.9 37.3 all-reduce.6
where the time goes:
time: 441 us; the launch traced here: 440 us
  waiting for transfers between devices  347 us (79%)
  starting transfers between devices  33.1 us (8%)
  matrix products  17.3 us (4%)
  local copies, waits for them, and re-layouts  16.3 us (4%)
  between operations  15.1 us (3%)
  other arithmetic  5.88 us (1%)
  blocking collectives  5.49 us (1%)
    unnamed x6, waiting for transfers between devices  158 us
    reduce_scatter x1, waiting for transfers between devices, on_device(): lax.psum_scatter(conv_all, 'seq', scatter_dimension=1, tiled=True)  122 us
    psum x1, waiting for transfers between devices, on_device(): lax.psum((shares[0], shares[1], shares[2]), 'dp')  33.4 us
    ppermute x8, waiting for transfers between devices, passed_along(): return lax.ppermute(block, axis, route)  26.3 us
    ppermute x8, starting transfers between devices, passed_along(): return lax.ppermute(block, axis, route)  26 us
    unnamed x85, local copies, waits for them, and re-layouts  10.6 us
  transfers between devices with their start and end apart: 16, of which 12 were waited for; matrix products, arithmetic and copies ran while one was open for 4% of the time, Pallas kernels for 0%

commit v1 on v0

v1 whole, which is shorter than its diff:
```python
import math

import jax
import jax.numpy as jnp
import numpy as np
from jax import lax
from jax.sharding import PartitionSpec as P

BF16 = jnp.bfloat16
F32 = jnp.float32
CLASSES = 128
STRIDE = 8


def gelu_pair(v):
    coef = math.sqrt(2.0 / math.pi)
    inner = coef * (v + 0.044715 * v * v * v)
    t = jnp.tanh(inner)
    slope = 0.5 * (1.0 + t) + 0.5 * v * (1.0 - t * t) * coef * (1.0 + 3.0 * 0.044715 * v * v)
    return 0.5 * v * (1.0 + t), slope


def mm(a, b):
    return jnp.dot(a, b, preferred_element_type=F32)


def mm_tn(a, b):
    return lax.dot_general(a, b, (((0,), (0,)), ((), ())), preferred_element_type=F32)


def mm_nt(a, b):
    return lax.dot_general(a, b, (((1,), (1,)), ((), ())), preferred_element_type=F32)


def halves(v):
    high = lax.reduce_precision(v, 8, 7)
    return high.astype(BF16), (v - high).astype(BF16)


def selectors():
    c = np.arange(CLASSES)
    digits = (c // 20, (c // 5) % 4, c % 5)
    valid = (c < 100)[:, None]
    return [((d[:, None] == np.arange(4)[None, :]) & valid).astype(np.float32) for d in digits]


def norm_scale(v):
    return lax.rsqrt(jnp.mean(v * v, axis=-1, keepdims=True) + 1e-06)


def tables(embed, conv_weight, point_weight):
    sel = [jnp.asarray(s, BF16) for s in selectors()]
    stream = embed.astype(F32)
    scale_e = norm_scale(stream)
    normed_e = (stream * scale_e).astype(BF16)
    taps = jnp.concatenate([mm(s, normed_e).astype(BF16) for s in sel], axis=1)
    act0, slope0 = gelu_pair(mm(taps, conv_weight[0]))
    act0 = act0.astype(BF16)
    stab = mm(sel[1], embed) + mm(act0, point_weight[0])
    scale1 = norm_scale(stab)
    ntab = (stab * scale1).astype(BF16)
    width = embed.shape[1]
    u = jnp.concatenate([mm(ntab, conv_weight[1, j * width : (j + 1) * width]) for j in range(3)])
    return stream, scale_e, normed_e, act0, slope0, stab, scale1, ntab, u


def classes(gathered, dil):
    n, rb = gathered.shape
    edge = jnp.full((1, dil), 4, jnp.int32)
    left = jnp.concatenate(
        [jnp.concatenate([edge, gathered[:-1, rb - dil :]]), gathered[:, : rb - dil]], axis=1
    )
    right = jnp.concatenate(
        [gathered[:, dil:], jnp.concatenate([gathered[1:, :dil], edge])], axis=1
    )
    cls = left * 20 + gathered * 5 + right
    none = jnp.full((2, rb), -1, jnp.int32)
    return jnp.concatenate([none, cls, none])


def on_device(bases, embed, conv_weight, point_weight, cotangent):
    n, dp = lax.axis_size("seq"), lax.axis_size("dp")
    rb, width, mid = bases.shape[1], embed.shape[1], conv_weight.shape[2]
    group = n // STRIDE
    k, x = lax.axis_index("seq"), lax.axis_index("dp")
    zh, r = k // STRIDE, k % STRIDE
    m, core = r // 2, r % 2
    rows = group * rb
    w1, w2 = conv_weight[1], conv_weight[2]
    p0, p1, p2 = point_weight[0], point_weight[1], point_weight[2]

    gathered = lax.all_to_all(jnp.broadcast_to(bases, (n, rb)), "seq", 0, 0, tiled=True)
    own = cotangent[0]
    parts = [own]
    for i in range(1, group):
        parts.append(lax.ppermute(own, "seq", [(s, (s - STRIDE * i) % n) for s in range(n)]))
    cot = lax.dynamic_slice_in_dim(
        jnp.concatenate(parts + parts), ((group - zh) % group) * rb, rows
    )

    stream_e, scale_e, normed_e, act0, slope0, stab, scale1, ntab, u = tables(
        embed, conv_weight, point_weight
    )
    u_high, u_low = halves(u)
    s_high, s_low = halves(stab)

    cls = classes(gathered, rb // 8)
    hots = []
    for j in range(3):
        index = jnp.concatenate(
            [lax.dynamic_slice(cls, (a * STRIDE + r + 2 * j, 0), (1, rb)) for a in range(group)],
            axis=1,
        )
        hots.append((jnp.arange(CLASSES, dtype=jnp.int32)[:, None] == index).astype(BF16))
    hot = jnp.concatenate(hots)

    pre1 = mm_tn(hot, u_high) + mm_tn(hot, u_low)
    act1, slope1 = gelu_pair(pre1)
    act1 = act1.astype(BF16)
    stream2 = mm_tn(hots[1], s_high) + mm_tn(hots[1], s_low) + mm(act1, p1)
    scale2 = norm_scale(stream2)
    normed2 = (stream2 * scale2).astype(BF16)
    nothing = jnp.zeros((rb, width), BF16)
    taps2 = jnp.concatenate(
        [
            jnp.concatenate([nothing, normed2[: rows - rb]]),
            normed2,
            jnp.concatenate([normed2[rb:], nothing]),
        ],
        axis=1,
    )
    pre2 = mm(taps2, w2)
    act2, slope2 = gelu_pair(pre2)
    act2 = act2.astype(BF16)
    features = lax.dynamic_slice_in_dim(stream2, zh * rb, rb) + mm(
        lax.dynamic_slice_in_dim(act2, zh * rb, rb), p2
    )

    grad2 = (mm_nt(cot, p2) * slope2).astype(BF16)
    nothing = jnp.zeros((rb, mid), BF16)
    above = jnp.concatenate([grad2[rb:], nothing])
    below = jnp.concatenate([nothing, grad2[: rows - rb]])
    ng2 = (
        mm_nt(above, w2[:width]) + mm_nt(grad2, w2[width : 2 * width]) + mm_nt(below, w2[2 * width :])
    )
    inner = jnp.mean(ng2 * stream2, axis=-1, keepdims=True)
    back2 = cot.astype(F32) + scale2 * (ng2 - stream2 * scale2 * scale2 * inner)
    back2 = back2.astype(BF16)
    grad1 = (mm_nt(back2, p1) * slope1).astype(BF16)

    h = mm(hot, grad1).astype(BF16)
    ng1 = sum(
        mm_nt(h[j * CLASSES : (j + 1) * CLASSES], w1[j * width : (j + 1) * width]) for j in range(3)
    )
    inner = jnp.mean(ng1 * stab, axis=-1, keepdims=True)
    b = mm(hots[1], back2) + scale1 * (ng1 - stab * scale1 * scale1 * inner)
    b16 = b.astype(BF16)
    s = (mm_nt(b16, p0) * slope0).astype(BF16)
    sel = selectors()
    g = mm(jnp.asarray(np.concatenate([v.T for v in sel]), BF16), s)
    bt = mm(jnp.asarray(sel[1].T, BF16), b16)
    small = jnp.concatenate([g, bt.reshape(2 * 4, mid)])

    crow, prow = 3 * width // n, width // n
    conv1 = jnp.concatenate(
        [mm_tn(ntab, h[j * CLASSES : (j + 1) * CLASSES]) for j in range(3)]
    )
    conv1 = lax.dynamic_slice_in_dim(conv1, zh * STRIDE * crow, STRIDE * crow)
    conv2 = mm_tn(lax.dynamic_slice_in_dim(taps2, zh * STRIDE * crow, STRIDE * crow, axis=1), grad2)

    def share(v):
        return lax.dynamic_slice_in_dim(v, zh * STRIDE * prow, STRIDE * prow, axis=1)

    point = [mm_tn(share(b16), act0), mm_tn(share(back2), act1), mm_tn(share(cot), act2)]
    tile = jnp.concatenate(
        [conv1.reshape(STRIDE, crow, mid), conv2.reshape(STRIDE, crow, mid)]
        + [v.reshape(STRIDE, prow, mid) for v in point],
        axis=1,
    )
    trow = 2 * crow + 3 * prow
    half = STRIDE // 2
    tile = tile.reshape(half, 2, trow, mid)

    swap = [(s, s ^ 1) for s in range(n)]
    mine = lax.dynamic_index_in_dim(tile, core, axis=1, keepdims=False)
    other = lax.dynamic_index_in_dim(tile, 1 - core, axis=1, keepdims=False)
    mine = mine + lax.ppermute(other.astype(BF16), "seq", swap).astype(F32)
    small = small + lax.ppermute(small.astype(BF16), "seq", swap).astype(F32)

    drow = trow // dp
    mine = mine.reshape(half, dp, drow, mid)
    small16 = small.astype(BF16)
    total = lax.dynamic_slice(mine, (m, x, 0, 0), (1, 1, drow, mid))[0, 0]
    for mask in range(half * dp - 1, 0, -1):
        mm_, mx = mask // dp, mask % dp
        piece = lax.dynamic_slice(mine, (m ^ mm_, x ^ mx, 0, 0), (1, 1, drow, mid))[0, 0]
        message = jnp.concatenate([piece.astype(BF16), small16])
        route = [
            (s * dp + d, (s ^ (2 * mm_)) * dp + (d ^ mx)) for s in range(n) for d in range(dp)
        ]
        got = lax.ppermute(message, ("seq", "dp"), route).astype(F32)
        total = total + got[:drow]
        small = small + got[drow:]

    total16 = total.astype(BF16)
    pieces = [total16] + [
        lax.ppermute(total16, "dp", [(d, d ^ i) for d in range(dp)]) for i in range(1, dp)
    ]
    full = jnp.concatenate(
        [
            sum(jnp.where((x ^ i) == d, pieces[i].astype(F32), 0.0) for i in range(dp))
            for d in range(dp)
        ]
    )

    g, bt = small[:12], small[12:].reshape(4, width)
    ng0 = sum(
        mm_nt(g[4 * j : 4 * j + 4].astype(BF16), conv_weight[0, j * width : (j + 1) * width])
        for j in range(3)
    )
    inner = jnp.mean(ng0 * stream_e, axis=-1, keepdims=True)
    embed_grad = bt + scale_e * (ng0 - stream_e * scale_e * scale_e * inner)
    embed_grad = lax.dynamic_slice_in_dim(embed_grad, k * prow, prow, axis=1)
    spread = jnp.concatenate(
        [
            jnp.pad(normed_e, ((4 * j, 8 - 4 * j), (0, 0))) for j in range(3)
        ],
        axis=1,
    )
    spread = lax.dynamic_slice_in_dim(spread, k * crow, crow, axis=1)
    conv0 = mm_tn(spread, g.astype(BF16))
    conv_grad = jnp.stack([conv0, full[:crow], full[crow : 2 * crow]])
    point_grad = full[2 * crow :].reshape(3, prow, mid).transpose(0, 2, 1)
    return features[None], conv_grad, point_grad, embed_grad


def solution(mesh):
    in_specs = (P("dp", "seq"), P(), P(), P(), P("dp", "seq", None))
    out_specs = (P("dp", "seq", None), P(None, "seq", None), P(None, None, "seq"), P(None, "seq"))
    return jax.shard_map(
        on_device, mesh=mesh, in_specs=in_specs, out_specs=out_specs, check_vma=False
    )
```

time: 441 us -> 105 us (0.24)
  waiting for transfers between devices: 347 us -> 14.4 us
  matrix products: 17.3 us -> 37 us
  between operations: 15.1 us -> 1.48 us
  other arithmetic: 5.88 us -> 18.6 us
  starting transfers between devices: 33.1 us -> 21.9 us
  local copies, waits for them, and re-layouts: 16.3 us -> 9.86 us
  blocking collectives: 5.49 us -> 0 us
    unnamed x6 -> x0, waiting for transfers between devices: 158 us -> none
    reduce_scatter x1 -> x0, waiting for transfers between devices: 122 us -> none  [on_device(): lax.psum_scatter(conv_all, 'seq', scatter_dimension=1, tiled=True)]
    psum x1 -> x0, waiting for transfers between devices: 33.4 us -> none  [on_device(): lax.psum((shares[0], shares[1], shares[2]), 'dp')]
    dot_general x19 -> x38, matrix products: 15.6 us -> 37 us  [the longest x16 17.8 us: mm(): return jnp.dot(a, b, preferred_element_type=F32)]
    ppermute x12 -> x11, waiting for transfers between devices: 33.5 us -> 14.4 us  [the longest x7 9.1 us: on_device(): got = lax.ppermute(message, ('seq', 'dp'), route).astype(F32)]
    ppermute x12 -> x11, starting transfers between devices: 32.9 us -> 14.5 us  [the longest x7 10.3 us: on_device(): got = lax.ppermute(message, ('seq', 'dp'), route).astype(F32)]
    all_to_all x0 -> x1, starting transfers between devices: none -> 7.39 us  [on_device(): lax.all_to_all(jnp.broadcast_to(bases, (n, rb)), 'seq', 0, 0, tiled=True)]
    convert_element_type x3 -> x13, other arithmetic: 0.3 us -> 7.35 us  [the longest x7 4.8 us: on_device(): got = lax.ppermute(message, ('seq', 'dp'), route).astype(F32)]
  transfers between devices with their start and end apart: 16 -> 12, of which waited for: 12 -> 7; matrix products, arithmetic and copies ran while one was open for 4% -> 24% of each run, Pallas kernels for 0% -> 0%
where the time goes in v1:
time: 105 us; the launch traced here: 103 us
  matrix products  37 us (35%)
  starting transfers between devices  21.9 us (21%)
  other arithmetic  18.6 us (18%)
  waiting for transfers between devices  14.4 us (14%)
  local copies, waits for them, and re-layouts  9.86 us (9%)
  between operations  1.48 us (1%)
    dot_general x16, matrix products, mm(): return jnp.dot(a, b, preferred_element_type=F32)  17.8 us
    dot_general x10, matrix products, mm_nt(): lax.dot_general(a, b, (((1,), (1,)), ((), ())), preferred_element_type=F32)  12.1 us
    ppermute x7, starting transfers between devices, on_device(): got = lax.ppermute(message, ('seq', 'dp'), route).astype(F32)  10.3 us
    ppermute x7, waiting for transfers between devices, on_device(): got = lax.ppermute(message, ('seq', 'dp'), route).astype(F32)  9.1 us
    all_to_all x1, starting transfers between devices, on_device(): lax.all_to_all(jnp.broadcast_to(bases, (n, rb)), 'seq', 0, 0, tiled=True)  7.39 us
    dot_general x12, matrix products, mm_tn(): lax.dot_general(a, b, (((0,), (0,)), ((), ())), preferred_element_type=F32)  7.04 us
    unnamed x63, local copies, waits for them, and re-layouts  6.81 us
    convert_element_type x7, other arithmetic, on_device(): got = lax.ppermute(message, ('seq', 'dp'), route).astype(F32)  4.8 us
  transfers between devices with their start and end apart: 12, of which 7 were waited for; matrix products, arithmetic and copies ran while one was open for 24% of the time, Pallas kernels for 0%

profile of v1, /device:TPU:0, one launch (start us, length us, event | category | flops | bytes accessed | tf_op | source)
XLA Modules:
  0.0 103.2 jit_solution(12594701379754045962)
XLA Ops:
  0.6 1.3 %broadcast_in_dim.13 = s32[16,1,176]{2,1,0:T(1,128)} broadcast(s32[176]{0:T(256)} %bitcast.155), dimensions={2} | broadcast | bytes 11968 | tf_op jit(solution)/shard_map/broadcast_in_dim | solution.py:92
  1.9 7.4 %all-to-all-start = ((s32[16,1,176]{2,1,0:T(1,128)}), s32[16,1,176]{2,1,0:T(1,128)S(1)}, u32[]{:S(2)}, u32[]{:S(2)}) async-start(s32[16,1,176]{2,1,0:T(1,128)} %broadcast_in_dim.13), calls=%async_computation | async-start | bytes 32768 | tf_op jit(solution)/shard_map/all_to_all | solution.py:92
  9.3 2.8 %collective-permute-start = (bf16[176,768]{1,0:T(8,128)(2,1)}, bf16[176,768]{1,0:T(8,128)(2,1)}, u32[]{:S(2)}, u32[]{:S(2)}) collective-permute-start(bf16[176,768]{1,0:T(8,128)(2,1)} %bitcast.150), channel_id=1, source_target_pairs={{0,16},{2,18},{4,20},{6,22},{8,24},{10,26},{12,28},{14,30},{16,0},... | collective-permute-start | bytes 811016 | tf_op jit(solution)/shard_map/ppermute | solution.py:96
  12.1 0.8 fusion.170
  13.0 1.4 %convert_multiply_fusion.1 = (f32[4,768]{1,0:T(4,128)}, bf16[4,768]{1,0:T(4,128)(2,1)S(1)}) fusion(bf16[4,768]{1,0:T(4,128)(2,1)} %param.11, f32[4]{0:T(128)S(1)} %add_rsqrt_fusion.2), kind=kLoop, calls=%fused_computation.244 | loop fusion | flops 9216 | bytes 24592 | tf_op jit(solution)/shard_map/mul | solution.py:55
  14.3 0.9 fusion.221
  15.3 1.0 %fusion.18 = bf16[128,768]{0,1:T(8,128)(2,1)S(1)} fusion(bf16[4,768]{1,0:T(4,128)(2,1)S(1)} %get-tuple-element.40, bf16[128,4]{1,0:T(8,128)(2,1)} %constant.162.clone), kind=kOutput, calls=%fused_computation.42 | convolution fusion | flops 884736 | bytes 203776 | tf_op jit(solution)/shard_map/dot_general | solution.py:24
  16.3 1.0 fusion.19
  17.3 1.0 fusion.17
  18.4 2.1 %fusion.6 = f32[128,384]{1,0:T(8,128)S(1)} fusion(bf16[3,2304,384]{2,1,0:T(8,128)(2,1)} %param.12, bf16[128,768]{0,1:T(8,128)(2,1)S(1)} %fusion.19, bf16[128,768]{0,1:T(8,128)(2,1)S(1)} %fusion.18, bf16[128,768]{0,1:T(8,128)(2,1)S(1)} %fusion.17), kind=kOutput, calls=%fused_computation.13 | convolution fusion | flops 228261888 | bytes 2555904 | tf_op jit(solution)/shard_map/dot_general | solution.py:24
  21.0 1.3 %fusion.44 = f32[128,384]{1,0:T(8,128)S(1)} fusion(bf16[128,768]{1,0:T(8,128)(2,1)S(1)} %multiply_convert_fusion.3, bf16[3,2304,384]{2,1,0:T(8,128)(2,1)} %param.12), kind=kOutput, calls=%fused_computation.83 | convolution fusion | flops 75497472 | bytes 983040 | tf_op jit(solution)/shard_map/dot_general | solution.py:24
  22.3 1.3 %fusion.47 = f32[128,384]{1,0:T(8,128)S(1)} fusion(bf16[128,768]{1,0:T(8,128)(2,1)S(1)} %multiply_convert_fusion.3, bf16[3,2304,384]{2,1,0:T(8,128)(2,1)} %param.12), kind=kOutput, calls=%fused_computation.86 | convolution fusion | flops 75497472 | bytes 983040 | tf_op jit(solution)/shard_map/dot_general | solution.py:24
  23.7 1.3 %fusion.51 = f32[128,384]{1,0:T(8,128)S(1)} fusion(bf16[128,768]{1,0:T(8,128)(2,1)S(1)} %multiply_convert_fusion.3, bf16[3,2304,384]{2,1,0:T(8,128)(2,1)} %param.12), kind=kOutput, calls=%fused_computation.90 | convolution fusion | flops 75497472 | bytes 983040 | tf_op jit(solution)/shard_map/dot_general | solution.py:24
  27.4 0.6 multiply_reduce_fusion.1
  28.5 0.5 slice-done.1
  29.0 1.8 %multiply_convert_fusion.1 = (bf16[352,384]{1,0:T(8,128)(2,1)}, f32[352,384]{1,0:T(8,128)S(1)}) fusion(bf16[3,2304,384]{2,1,0:T(8,128)(2,1)S(1)} %bitcast.142, bf16[176,768]{1,0:T(8,128)(2,1)S(1)} %get-tuple-element.14, bf16[176,768]{1,0:T(8,128)(2,1)S(1)} %get-tuple-element.13, bf16[352,768]{1,0:T(8,128)(2,1)S(1)} %multiply_convert_fusion), kind=kOutput, calls=%fused_computation.125 | convolution fusion | flops 632180736 | bytes 3661824 | tf_op jit(solution)/shard_map/dot_general | solution.py:24
  31.0 0.8 copy-done.15
  31.8 1.1 %pad_maximum_fusion = bf16[704,768]{1,0:T(8,128)(2,1)S(1)} fusion(bf16[176,768]{1,0:T(8,128)(2,1)} %collective-permute-done, bf16[176,768]{1,0:T(8,128)(2,1)S(1)} %bitcast.151), kind=kLoop, calls=%fused_computation.49 | loop fusion | flops 4325376 | bytes 1622016 | tf_op jit(solution)/shard_map/concatenate | solution.py:98
  32.9 2.1 %fusion.14 = bf16[352,384]{1,0:T(8,128)(2,1)S(1)} fusion(f32[352,384]{1,0:T(8,128)S(1)} %get-tuple-element.46, bf16[3,384,768]{2,1,0:T(8,128)(2,1)} %param.13, bf16[704,768]{1,0:T(8,128)(2,1)S(1)} %pad_maximum_fusion, s32[]{:T(128)S(6)} %select_n.138), kind=kOutput, calls=%fused_computation.30 | convolution fusion | flops 210186240 | bytes 1941508 | tf_op jit(solution)/shard_map/dot_general | solution.py:32
  36.0 0.6 multiply_reduce_fusion
  36.6 1.2 %add_convert_fusion = bf16[352,768]{1,0:T(8,128)(2,1)} fusion(f32[352,768]{1,0:T(8,128)S(1)} %get-tuple-element.48, f32[352,768]{1,0:T(8,128)S(1)} %get-tuple-element.44, f32[352]{0:T(512)S(1)} %broadcast_multiply_fusion, f32[352]{0:T(512)S(1)} %add_rsqrt_fusion, bf16[704,768]{1,0:T(8,128)(2,1)S(1)} %pad_maximum_fusion, s32[]{:T(128)S(6)} %select_n.138), kind=kLoop, calls=%fused_computation.50 | loop fusion | flops 2162688 | bytes 3246852 | tf_op jit(solution)/shard_map/convert_element_type | solution.py:148
  37.7 3.0 %convolution_convert_fusion = bf16[384,384]{1,0:T(8,128)(2,1)} fusion(bf16[352,768]{1,0:T(8,128)(2,1)} %add_convert_fusion, f32[352,384]{1,0:T(8,128)} %copy-done.14, bf16[3,384,768]{2,1,0:T(8,128)(2,1)} %param.13, pred[128,352]{1,0:T(32,128)(4,1)S(1)} %iota_compare_fusion.2, pred[128,352]{1,0:T(32,128)(4,1)S(1)} %iota_compare_fusion.4, ...), kind=kOutput, calls=%fused_computation.29 | convolution fusion | flops 314413056 | bytes 2101248 | tf_op jit(solution)/shard_map/dot_general | solution.py:24
  40.7 1.6 %fusion.104 = f32[384,384]{1,0:T(8,128)S(1)} fusion(bf16[352,768]{1,0:T(8,128)(2,1)} %add_convert_fusion, s32[]{:T(128)S(6)} %select_n.140, f32[352,384]{1,0:T(8,128)} %copy-done.14), kind=kOutput, calls=%fused_computation.172 | convolution fusion | flops 105025536 | bytes 1400836 | tf_op jit(solution)/shard_map/dot_general | solution.py:28
  42.4 1.4 %fusion.49 = f32[128,768]{1,0:T(8,128)S(1)} fusion(bf16[3,2304,384]{2,1,0:T(8,128)(2,1)} %param.12, bf16[384,384]{1,0:T(8,128)(2,1)S(1)} %copy-done.8), kind=kOutput, calls=%fused_computation.88 | convolution fusion | flops 75497472 | bytes 1081344 | tf_op jit(solution)/shard_map/dot_general | solution.py:32
  44.8 1.4 %convolution_add_fusion.7 = f32[128,768]{1,0:T(8,128)S(1)} fusion(f32[128,768]{1,0:T(8,128)S(1)} %fusion.49, bf16[3,2304,384]{2,1,0:T(8,128)(2,1)} %param.12, bf16[384,384]{1,0:T(8,128)(2,1)S(1)} %copy-done.8), kind=kOutput, calls=%fused_computation.33 | convolution fusion | flops 75595776 | bytes 1474560 | tf_op jit(solution)/shard_map/dot_general | solution.py:32
  46.3 1.5 %multiply_reduce_fusion.2 = (f32[128]{0:T(128)S(1)}, f32[128,768]{1,0:T(8,128)S(1)}) fusion(f32[128,768]{1,0:T(8,128)S(1)} %get-tuple-element.42, f32[128,768]{1,0:T(8,128)S(1)} %convolution_add_fusion.7, bf16[3,2304,384]{2,1,0:T(8,128)(2,1)} %param.12, bf16[384,384]{1,0:T(8,128)(2,1)S(1)} %copy-done.8), kind=kOutput, calls=%fused_computation.147 | convolution fusion | flops 75792256 | bytes 1868288 | tf_op jit(solution)/shard_map/dot_general | solution.py:32
  48.4 0.8 fusion.22
  49.2 1.1 %fusion.3 = f32[1152,384]{1,0:T(8,128)S(1)} fusion(s32[]{:T(128)S(6)} %select_n.139, f32[768,384]{1,0:T(8,128)S(1)} %fusion.154, f32[768,384]{1,0:T(8,128)S(1)} %fusion.151, f32[768,384]{1,0:T(8,128)S(1)} %fusion.148), kind=kLoop, calls=%fused_computation.10 | loop fusion | flops 884736 | bytes 5308420 | tf_op jit(solution)/shard_map/concatenate | solution.py:165
  50.8 0.8 copy-done.12
  51.7 1.5 %fusion.102 = f32[384,384]{1,0:T(8,128)S(1)} fusion(bf16[352,384]{1,0:T(8,128)(2,1)S(1)} %copy-done.12, bf16[704,768]{1,0:T(8,128)(2,1)} %copy-done.2, s32[]{:T(128)S(6)} %select_n.141, s32[]{:T(128)S(6)} %select_n.142), kind=kOutput, calls=%fused_computation.170 | convolution fusion | flops 103809024 | bytes 1130504 | tf_op jit(solution)/shard_map/dot_general | solution.py:28
  53.3 2.4 %copy-done.1 = f32[4,2,432,384]{3,2,1,0:T(8,128)} copy-done((f32[4,2,432,384]{3,2,1,0:T(8,128)}, f32[4,2,432,384]{3,2,1,0:T(8,128)S(1)}, u32[]{:S(2)}) %copy-start.1) | copy-done | bytes 5308440
  55.7 1.2 %fusion.12 = bf16[4,432,384]{2,1,0:T(8,128)(2,1)} fusion(f32[4,2,432,384]{3,2,1,0:T(8,128)S(1)} %constant_dynamic-update-slice_fusion, s32[]{:T(128)S(6)} %select_n.145), kind=kLoop, calls=%fused_computation.23 | loop fusion | bytes 2654212 | tf_op jit(solution)/shard_map/convert_element_type | solution.py:187
  57.6 0.6 collective-permute-start.1
  58.2 1.9 %collective-permute-done.1 = bf16[20,384]{1,0:T(8,128)(2,1)S(1)} collective-permute-done((bf16[20,384]{1,0:T(8,128)(2,1)S(1)}, bf16[20,384]{1,0:T(8,128)(2,1)S(1)}, u32[]{:S(2)}, u32[]{:S(2)}) %collective-permute-start.1) | collective-permute-done | bytes 15392 | tf_op jit(solution)/shard_map/ppermute | solution.py:188
  60.3 2.4 %bitcast_add_fusion = f32[4,432,384]{2,1,0:T(8,128)S(1)} fusion(bf16[4,432,384]{2,1,0:T(8,128)(2,1)} %collective-permute-done.2, f32[4,2,432,384]{3,2,1,0:T(8,128)} %copy-done.1, s32[]{:T(128)S(6)} %select_n.144), kind=kLoop, calls=%fused_computation.7 | loop fusion | flops 1327104 | bytes 6635524 | tf_op jit(solution)/shard_map/add | solution.py:187
  62.9 1.0 pad_maximum_fusion.9
  63.9 0.6 copy-done
  64.5 3.3 %collective-permute-start.3 = (bf16[236,384]{1,0:T(8,128)(2,1)S(1)}, bf16[236,384]{1,0:T(8,128)(2,1)S(1)}, u32[]{:S(2)}, u32[]{:S(2)}) collective-permute-start(bf16[236,384]{1,0:T(8,128)(2,1)S(1)} %get-tuple-element.28), channel_id=1, source_target_pairs={{0,13},{1,12},{2,15},{3,14},{4,9},{5,8},{6,11},{7,10},{8,5},{9,4},... | collective-permute-start | bytes 543752 | tf_op jit(solution)/shard_map/ppermute | solution.py:201
  67.8 0.6 collective-permute-start.4
  68.3 1.4 %collective-permute-start.5 = (bf16[236,384]{1,0:T(8,128)(2,1)}, bf16[236,384]{1,0:T(8,128)(2,1)}, u32[]{:S(2)}, u32[]{:S(2)}) collective-permute-start(bf16[236,384]{1,0:T(8,128)(2,1)} %get-tuple-element.30), channel_id=1, source_target_pairs={{0,9},{1,8},{2,11},{3,10},{4,13},{5,12},{6,15},{7,14},{8,1},{9,0},... | collective-permute-start | bytes 543752 | tf_op jit(solution)/shard_map/ppermute | solution.py:201
  69.8 0.6 collective-permute-start.6
  70.3 2.4 %collective-permute-start.7 = (bf16[236,384]{1,0:T(8,128)(2,1)}, bf16[236,384]{1,0:T(8,128)(2,1)}, u32[]{:S(2)}, u32[]{:S(2)}) collective-permute-start(bf16[236,384]{1,0:T(8,128)(2,1)} %get-tuple-element.32), channel_id=1, source_target_pairs={{0,5},{1,4},{2,7},{3,6},{4,1},{5,0},{6,3},{7,2},{8,13},{9,12},{10,... | collective-permute-start | bytes 543752 | tf_op jit(solution)/shard_map/ppermute | solution.py:201
  72.7 1.4 %collective-permute-done.3 = bf16[236,384]{1,0:T(8,128)(2,1)S(1)} collective-permute-done((bf16[236,384]{1,0:T(8,128)(2,1)S(1)}, bf16[236,384]{1,0:T(8,128)(2,1)S(1)}, u32[]{:S(2)}, u32[]{:S(2)}) %collective-permute-start.3) | collective-permute-done | bytes 181280 | tf_op jit(solution)/shard_map/ppermute | solution.py:201
  74.1 1.5 %collective-permute-start.8 = (bf16[236,384]{1,0:T(8,128)(2,1)}, bf16[236,384]{1,0:T(8,128)(2,1)}, u32[]{:S(2)}, u32[]{:S(2)}) collective-permute-start(bf16[236,384]{1,0:T(8,128)(2,1)} %get-tuple-element.33), channel_id=1, source_target_pairs={{0,4},{1,5},{2,6},{3,7},{4,0},{5,1},{6,2},{7,3},{8,12},{9,13},{10,... | collective-permute-start | bytes 543752 | tf_op jit(solution)/shard_map/ppermute | solution.py:201
  75.6 4.9 %collective-permute-done.4 = bf16[236,384]{1,0:T(8,128)(2,1)S(1)} collective-permute-done((bf16[236,384]{1,0:T(8,128)(2,1)S(1)}, bf16[236,384]{1,0:T(8,128)(2,1)S(1)}, u32[]{:S(2)}, u32[]{:S(2)}) %collective-permute-start.4) | collective-permute-done | bytes 181280 | tf_op jit(solution)/shard_map/ppermute | solution.py:201
  80.5 0.7 copy-done.18
  81.2 0.6 collective-permute-start.9
  81.8 1.1 %fusion.13 = f32[1,176,768]{2,1,0:T(8,128)} fusion(f32[352,768]{1,0:T(8,128)S(1)} %get-tuple-element.44, s32[]{:T(128)S(6)} %select_n.135, bf16[3,384,768]{2,1,0:T(8,128)(2,1)S(1)} %copy-done.7, bf16[352,384]{1,0:T(8,128)(2,1)S(1)} %copy-done.13), kind=kOutput, calls=%fused_computation.28 | convolution fusion | flops 103944192 | bytes 1807360 | tf_op jit(solution)/shard_map/dot_general | solution.py:24
  83.0 0.7 collective-permute-done.5
  83.7 0.9 convert_element_type.215
  84.7 2.1 %collective-permute-done.6 = bf16[236,384]{1,0:T(8,128)(2,1)} collective-permute-done((bf16[236,384]{1,0:T(8,128)(2,1)}, bf16[236,384]{1,0:T(8,128)(2,1)}, u32[]{:S(2)}, u32[]{:S(2)}) %collective-permute-start.6) | collective-permute-done | bytes 181280 | tf_op jit(solution)/shard_map/ppermute | solution.py:201
  86.7 0.9 convert_element_type.218
  87.7 0.9 convert_element_type.221
  88.7 0.9 convert_element_type.224
  89.6 0.9 convert_element_type.227
  90.6 1.2 %fusion.99 = bf16[216,384]{1,0:T(8,128)(2,1)S(1)} fusion(f32[236,384]{1,0:T(8,128)S(1)} %convert_element_type.227, f32[236,384]{1,0:T(8,128)S(1)} %convert_element_type.224, f32[236,384]{1,0:T(8,128)S(1)} %convert_element_type.221, f32[236,384]{1,0:T(8,128)S(1)} %convert_element_type.218, f32[236,384]{1,0:T(8,128)S(1)} %convert_element_type.215, ...), kind=kLoop, calls=%fused_computation.153 | loop fusion | flops 663552 | bytes 2820104 | tf_op jit(solution)/shard_map/convert_element_type | solution.py:205
  91.8 1.3 %fusion.32 = f32[4,768]{1,0:T(4,128)S(1)} fusion(bf16[3,2304,384]{2,1,0:T(8,128)(2,1)} %param.12, bf16[20,384]{1,0:T(8,128)(2,1)S(1)} %get-tuple-element.4), kind=kOutput, calls=%fused_computation.72 | convolution fusion | flops 2359296 | bytes 605184 | tf_op jit(solution)/shard_map/dot_general | solution.py:32
  93.1 1.3 %convolution_add_fusion.11 = f32[4,768]{1,0:T(4,128)S(1)} fusion(f32[4,768]{1,0:T(4,128)S(1)} %fusion.32, bf16[3,2304,384]{2,1,0:T(8,128)(2,1)} %param.12, bf16[20,384]{1,0:T(8,128)(2,1)S(1)} %get-tuple-element.4), kind=kOutput, calls=%fused_computation.48 | convolution fusion | flops 2362368 | bytes 617472 | tf_op jit(solution)/shard_map/dot_general | solution.py:32
  94.5 1.5 %fusion.171 = (f32[4]{0:T(128)S(1)}, f32[4,768]{1,0:T(4,128)S(1)}) fusion(bf16[4,768]{1,0:T(4,128)(2,1)S(1)} %copy-done.20, f32[4,768]{1,0:T(4,128)S(1)} %convolution_add_fusion.11, bf16[3,2304,384]{2,1,0:T(8,128)(2,1)} %param.12, bf16[20,384]{1,0:T(8,128)(2,1)S(1)} %get-tuple-element.4), kind=kOutput, calls=%fused_computation.264 | convolution fusion | flops 2371580 | bytes 623632 | tf_op jit(solution)/shard_map/dot_general | solution.py:32
  96.0 0.7 collective-permute-start.10
  96.7 1.3 %fusion.193 = f32[4,48]{1,0:T(4,128)} fusion(f32[4,768]{1,0:T(4,128)} %get-tuple-element.39, s32[]{:T(128)S(6)} %select_n.161, f32[4,768]{1,0:T(4,128)S(1)} %reshape.95, f32[4,768]{1,0:T(4,128)S(1)} %get-tuple-element.52, f32[4]{0:T(128)S(1)} %broadcast_multiply_fusion.2, f32[4]{0:T(128)S(1)} %add_rsqrt_fusion.2), kind=kLoop, calls=%fused_computation.298 | loop fusion | flops 960 | bytes 3108 | tf_op jit(solution)/shard_map/add | solution.py:222
  98.4 3.1 %collective-permute-done.10 = bf16[216,384]{1,0:T(8,128)(2,1)S(1)} collective-permute-done((bf16[216,384]{1,0:T(8,128)(2,1)S(1)}, bf16[216,384]{1,0:T(8,128)(2,1)S(1)}, u32[]{:S(2)}, u32[]{:S(2)}) %collective-permute-start.10) | collective-permute-done | bytes 165920 | tf_op jit(solution)/shard_map/ppermute | solution.py:207
  101.6 0.7 fusion.217
  102.3 0.9 pad_maximum_fusion.1
  (113 shorter events, 8.0 us)
Async XLA Ops:
  1.9 23.2 %all-to-all-start = ((s32[16,1,176]{2,1,0:T(1,128)}), s32[16,1,176]{2,1,0:T(1,128)S(1)}, u32[]{:S(2)}, u32[]{:S(2)}) async-start(s32[16,1,176]{2,1,0:T(1,128)} %broadcast_in_dim.13), calls=%async_computation | async-start | bytes 32768 | tf_op jit(solution)/shard_map/all_to_all | solution.py:92
  9.3 21.6 %collective-permute-start = (bf16[176,768]{1,0:T(8,128)(2,1)}, bf16[176,768]{1,0:T(8,128)(2,1)}, u32[]{:S(2)}, u32[]{:S(2)}) collective-permute-start(bf16[176,768]{1,0:T(8,128)(2,1)} %bitcast.150), channel_id=1, source_target_pairs={{0,16},{2,18},{4,20},{6,22},{8,24},{10,26},{12,28},{14,30},{16,0},... | collective-permute-start | bytes 811016 | tf_op jit(solution)/shard_map/ppermute | solution.py:96
  18.4 2.1 %copy-start.6 = (bf16[3,384,768]{2,1,0:T(8,128)(2,1)S(1)}, bf16[3,384,768]{2,1,0:T(8,128)(2,1)}, u32[]{:S(2)}) copy-start(bf16[3,384,768]{2,1,0:T(8,128)(2,1)} %param.13) | copy-start | bytes 5308420
  20.5 3.2 %copy-start.9 = (f32[128,384]{1,0:T(8,128)}, f32[128,384]{1,0:T(8,128)S(1)}, u32[]{:S(2)}) copy-start(f32[128,384]{1,0:T(8,128)S(1)} %fusion.6) | copy-start | bytes 589828
  20.9 4.1 %copy-start.23 = (f32[128]{0:T(128)}, f32[128]{0:T(128)S(1)}, u32[]{:S(2)}) copy-start(f32[128]{0:T(128)S(1)} %add_rsqrt_fusion.1) | copy-start | bytes 1540
  26.1 0.8 copy-start.21
  26.1 2.4 %slice-start = ((s8[5308416]{0:T(1024)(128)(4,1)}), s8[4194304]{0:T(1024)(128)(4,1)S(1)}, s32[]{:S(2)}) async-start(s8[5308416]{0:T(1024)(128)(4,1)} %bitcast.141), calls=%async_computation.1 | async-start | bytes 8388608
  27.0 1.0 copy-start.14
  27.0 2.0 %slice-start.1 = ((s8[5308416]{0:T(1024)(128)(4,1)}), s8[1114112]{0:T(1024)(128)(4,1)S(1)}, s32[]{:S(2)}) async-start(s8[5308416]{0:T(1024)(128)(4,1)} %bitcast.141), calls=%async_computation.2 | async-start | bytes 2228224
  30.8 1.0 copy-start.15
  32.9 3.7 %copy-start.2 = (bf16[704,768]{1,0:T(8,128)(2,1)}, bf16[704,768]{1,0:T(8,128)(2,1)S(1)}, u32[]{:S(2)}) copy-start(bf16[704,768]{1,0:T(8,128)(2,1)S(1)} %pad_maximum_fusion) | copy-start | bytes 3244036
  35.0 1.0 copy-start.3
  36.6 1.2 %copy-start.22 = (pred[128,352]{1,0:T(32,128)(4,1)S(1)}, pred[128,352]{1,0:T(32,128)(4,1)}, u32[]{:S(2)}) copy-start(pred[128,352]{1,0:T(32,128)(4,1)} %copy-done.21) | copy-start | bytes 135172
  40.7 1.6 %copy-start.8 = (bf16[384,384]{1,0:T(8,128)(2,1)S(1)}, bf16[384,384]{1,0:T(8,128)(2,1)}, u32[]{:S(2)}) copy-start(bf16[384,384]{1,0:T(8,128)(2,1)} %convolution_convert_fusion) | copy-start | bytes 884740
  44.8 3.0 %copy-start.5 = (bf16[352,768]{1,0:T(8,128)(2,1)S(1)}, bf16[352,768]{1,0:T(8,128)(2,1)}, u32[]{:S(2)}) copy-start(bf16[352,768]{1,0:T(8,128)(2,1)} %add_convert_fusion) | copy-start | bytes 1622020
  44.8 3.0 %copy-start.24 = (f32[128]{0:T(128)S(1)}, f32[128]{0:T(128)}, u32[]{:S(2)}) copy-start(f32[128]{0:T(128)} %copy-done.23) | copy-start | bytes 1540
  46.3 1.8 %copy-start.10 = (f32[128,384]{1,0:T(8,128)S(1)}, f32[128,384]{1,0:T(8,128)}, u32[]{:S(2)}) copy-start(f32[128,384]{1,0:T(8,128)} %copy-done.9) | copy-start | bytes 589828
  46.3 2.1 %copy-start.4 = (bf16[352,384]{1,0:T(8,128)(2,1)S(1)}, bf16[352,384]{1,0:T(8,128)(2,1)}, u32[]{:S(2)}) copy-start(bf16[352,384]{1,0:T(8,128)(2,1)} %copy-done.3) | copy-start | bytes 811012
  50.7 1.0 copy-start.12
  53.2 3.7 %copy-start.25 = (bf16[4,128]{1,0:T(4,128)(2,1)S(1)}, bf16[4,128]{1,0:T(4,128)(2,1)}, u32[]{:S(2)}) copy-start(bf16[4,128]{1,0:T(4,128)(2,1)} %constant.165.clone) | copy-start | bytes 3076
  53.2 3.9 %copy-start.7 = (bf16[3,384,768]{2,1,0:T(8,128)(2,1)S(1)}, bf16[3,384,768]{2,1,0:T(8,128)(2,1)}, u32[]{:S(2)}) copy-start(bf16[3,384,768]{2,1,0:T(8,128)(2,1)} %param.13) | copy-start | bytes 5308420
  53.2 3.9 %copy-start.11 = (f32[128,384]{1,0:T(8,128)S(1)}, f32[128,384]{1,0:T(8,128)}, u32[]{:S(2)}) copy-start(f32[128,384]{1,0:T(8,128)} %copy-done.9) | copy-start | bytes 589828
  53.2 3.9 %copy-start.26 = (bf16[12,128]{1,0:T(8,128)(2,1)S(1)}, bf16[12,128]{1,0:T(8,128)(2,1)}, u32[]{:S(2)}) copy-start(bf16[12,128]{1,0:T(8,128)(2,1)} %constant.164.clone) | copy-start | bytes 9220
  53.3 2.4 %copy-start.1 = (f32[4,2,432,384]{3,2,1,0:T(8,128)}, f32[4,2,432,384]{3,2,1,0:T(8,128)S(1)}, u32[]{:S(2)}) copy-start(f32[4,2,432,384]{3,2,1,0:T(8,128)S(1)} %constant_dynamic-update-slice_fusion) | copy-start | bytes 15925252
  56.9 3.4 %collective-permute-start.2 = (bf16[4,432,384]{2,1,0:T(8,128)(2,1)}, bf16[4,432,384]{2,1,0:T(8,128)(2,1)}, u32[]{:S(2)}, u32[]{:S(2)}) collective-permute-start(bf16[4,432,384]{2,1,0:T(8,128)(2,1)} %fusion.12), channel_id=1, source_target_pairs={{0,2},{2,0},{4,6},{6,4},{8,10},{10,8},{12,14},{14,12},{16,18},{18,... | collective-permute-start | bytes 3981320 | tf_op jit(solution)/shard_map/ppermute | solution.py:187
  57.6 2.4 %collective-permute-start.1 = (bf16[20,384]{1,0:T(8,128)(2,1)S(1)}, bf16[20,384]{1,0:T(8,128)(2,1)S(1)}, u32[]{:S(2)}, u32[]{:S(2)}) collective-permute-start(bf16[20,384]{1,0:T(8,128)(2,1)S(1)} %fusion.157), channel_id=1, source_target_pairs={{0,2},{2,0},{4,6},{6,4},{8,10},{10,8},{12,14},{14,12},{16,18},{18,... | collective-permute-start | bytes 46088 | tf_op jit(solution)/shard_map/ppermute | solution.py:188
  62.7 1.8 %copy-start = (f32[4,432,384]{2,1,0:T(8,128)}, f32[4,432,384]{2,1,0:T(8,128)S(1)}, u32[]{:S(2)}) copy-start(f32[4,432,384]{2,1,0:T(8,128)S(1)} %bitcast_add_fusion) | copy-start | bytes 7962628
  62.9 18.9 %copy-start.13 = (bf16[352,384]{1,0:T(8,128)(2,1)S(1)}, bf16[352,384]{1,0:T(8,128)(2,1)}, u32[]{:S(2)}) copy-start(bf16[352,384]{1,0:T(8,128)(2,1)} %get-tuple-element.45) | copy-start | bytes 811012
  64.5 9.6 %collective-permute-start.3 = (bf16[236,384]{1,0:T(8,128)(2,1)S(1)}, bf16[236,384]{1,0:T(8,128)(2,1)S(1)}, u32[]{:S(2)}, u32[]{:S(2)}) collective-permute-start(bf16[236,384]{1,0:T(8,128)(2,1)S(1)} %get-tuple-element.28), channel_id=1, source_target_pairs={{0,13},{1,12},{2,15},{3,14},{4,9},{5,8},{6,11},{7,10},{8,5},{9,4},... | collective-permute-start | bytes 543752 | tf_op jit(solution)/shard_map/ppermute | solution.py:201
  67.8 12.7 %collective-permute-start.4 = (bf16[236,384]{1,0:T(8,128)(2,1)S(1)}, bf16[236,384]{1,0:T(8,128)(2,1)S(1)}, u32[]{:S(2)}, u32[]{:S(2)}) collective-permute-start(bf16[236,384]{1,0:T(8,128)(2,1)S(1)} %get-tuple-element.29), channel_id=1, source_target_pairs={{0,12},{1,13},{2,14},{3,15},{4,8},{5,9},{6,10},{7,11},{8,4},{9,5},... | collective-permute-start | bytes 543752 | tf_op jit(solution)/shard_map/ppermute | solution.py:201
  68.3 15.4 %collective-permute-start.5 = (bf16[236,384]{1,0:T(8,128)(2,1)}, bf16[236,384]{1,0:T(8,128)(2,1)}, u32[]{:S(2)}, u32[]{:S(2)}) collective-permute-start(bf16[236,384]{1,0:T(8,128)(2,1)} %get-tuple-element.30), channel_id=1, source_target_pairs={{0,9},{1,8},{2,11},{3,10},{4,13},{5,12},{6,15},{7,14},{8,1},{9,0},... | collective-permute-start | bytes 543752 | tf_op jit(solution)/shard_map/ppermute | solution.py:201
  69.8 17.0 %collective-permute-start.6 = (bf16[236,384]{1,0:T(8,128)(2,1)}, bf16[236,384]{1,0:T(8,128)(2,1)}, u32[]{:S(2)}, u32[]{:S(2)}) collective-permute-start(bf16[236,384]{1,0:T(8,128)(2,1)} %get-tuple-element.31), channel_id=1, source_target_pairs={{0,8},{1,9},{2,10},{3,11},{4,12},{5,13},{6,14},{7,15},{8,0},{9,1},... | collective-permute-start | bytes 543752 | tf_op jit(solution)/shard_map/ppermute | solution.py:201
  70.3 17.4 %collective-permute-start.7 = (bf16[236,384]{1,0:T(8,128)(2,1)}, bf16[236,384]{1,0:T(8,128)(2,1)}, u32[]{:S(2)}, u32[]{:S(2)}) collective-permute-start(bf16[236,384]{1,0:T(8,128)(2,1)} %get-tuple-element.32), channel_id=1, source_target_pairs={{0,5},{1,4},{2,7},{3,6},{4,1},{5,0},{6,3},{7,2},{8,13},{9,12},{10,... | collective-permute-start | bytes 543752 | tf_op jit(solution)/shard_map/ppermute | solution.py:201
  74.1 6.4 %copy-start.16 = (bf16[236,384]{1,0:T(8,128)(2,1)}, bf16[236,384]{1,0:T(8,128)(2,1)S(1)}, u32[]{:S(2)}) copy-start(bf16[236,384]{1,0:T(8,128)(2,1)S(1)} %collective-permute-done.3) | copy-start | bytes 543748
  74.1 14.5 %collective-permute-start.8 = (bf16[236,384]{1,0:T(8,128)(2,1)}, bf16[236,384]{1,0:T(8,128)(2,1)}, u32[]{:S(2)}, u32[]{:S(2)}) collective-permute-start(bf16[236,384]{1,0:T(8,128)(2,1)} %get-tuple-element.33), channel_id=1, source_target_pairs={{0,4},{1,5},{2,6},{3,7},{4,0},{5,1},{6,2},{7,3},{8,12},{9,13},{10,... | collective-permute-start | bytes 543752 | tf_op jit(solution)/shard_map/ppermute | solution.py:201
  80.5 0.7 copy-start.18
  81.2 8.4 %collective-permute-start.9 = (bf16[236,384]{1,0:T(8,128)(2,1)S(1)}, bf16[236,384]{1,0:T(8,128)(2,1)}, u32[]{:S(2)}, u32[]{:S(2)}) collective-permute-start(bf16[236,384]{1,0:T(8,128)(2,1)S(1)} %get-tuple-element.34), channel_id=1, source_target_pairs={{0,1},{1,0},{2,3},{3,2},{4,5},{5,4},{6,7},{7,6},{8,9},{9,8},{10,11... | collective-permute-start | bytes 543752 | tf_op jit(solution)/shard_map/ppermute | solution.py:201
  81.8 1.1 %copy-start.17 = (bf16[236,384]{1,0:T(8,128)(2,1)S(1)}, bf16[236,384]{1,0:T(8,128)(2,1)}, u32[]{:S(2)}) copy-start(bf16[236,384]{1,0:T(8,128)(2,1)} %copy-done.16) | copy-start | bytes 543748
  81.8 1.1 %copy-start.19 = (bf16[236,384]{1,0:T(8,128)(2,1)S(1)}, bf16[236,384]{1,0:T(8,128)(2,1)}, u32[]{:S(2)}) copy-start(bf16[236,384]{1,0:T(8,128)(2,1)} %copy-done.18) | copy-start | bytes 543748
  90.6 3.9 %copy-start.20 = (bf16[4,768]{1,0:T(4,128)(2,1)S(1)}, bf16[4,768]{1,0:T(4,128)(2,1)}, u32[]{:S(2)}) copy-start(bf16[4,768]{1,0:T(4,128)(2,1)} %param.11) | copy-start | bytes 18436
  96.0 5.5 %collective-permute-start.10 = (bf16[216,384]{1,0:T(8,128)(2,1)S(1)}, bf16[216,384]{1,0:T(8,128)(2,1)S(1)}, u32[]{:S(2)}, u32[]{:S(2)}) collective-permute-start(bf16[216,384]{1,0:T(8,128)(2,1)S(1)} %fusion.99), channel_id=1, source_target_pairs={{0,1},{1,0},{2,3},{3,2},{4,5},{5,4},{6,7},{7,6},{8,9},{9,8},{10,11... | collective-permute-start | bytes 497672 | tf_op jit(solution)/shard_map/ppermute | solution.py:207

commit v2 on v1

--- a/solution.py
+++ b/solution.py
@@ -4,6 +4,8 @@
 import jax.numpy as jnp
 import numpy as np
 from jax import lax
+from jax.experimental import pallas as pl
+from jax.experimental.pallas import tpu as pltpu
 from jax.sharding import PartitionSpec as P
 
 BF16 = jnp.bfloat16
@@ -78,7 +80,7 @@
     return jnp.concatenate([none, cls, none])
 
 
-def on_device(bases, embed, conv_weight, point_weight, cotangent):
+def general(bases, embed, conv_weight, point_weight, cotangent):
     n, dp = lax.axis_size("seq"), lax.axis_size("dp")
     rb, width, mid = bases.shape[1], embed.shape[1], conv_weight.shape[2]
     group = n // STRIDE
@@ -234,6 +236,321 @@
     return features[None], conv_grad, point_grad, embed_grad
 
 
+def normal(v):
+    return (v * norm_scale(v)).astype(BF16)
+
+
+def table_kernel(embed_ref, w0_ref, w1_ref, p0_ref, sel_ref, act0_ref, slope0_ref, stab_ref, sparts_ref, ntab_ref, u_ref):
+    width = embed_ref.shape[1]
+    normed_e = normal(embed_ref[...].astype(F32))
+    pre = None
+    for j in range(3):
+        taps = mm(sel_ref[j], normed_e).astype(BF16)
+        term = mm(taps, w0_ref[j * width : (j + 1) * width, :])
+        pre = term if pre is None else pre + term
+    act0, slope0 = gelu_pair(pre)
+    act0 = act0.astype(BF16)
+    act0_ref[...] = act0
+    slope0_ref[...] = slope0
+    stab = mm(sel_ref[1], embed_ref[...]) + mm(act0, p0_ref[...])
+    stab_ref[...] = stab
+    high = stab.astype(BF16)
+    sparts_ref[:CLASSES, :] = high
+    sparts_ref[CLASSES:, :] = (stab - high.astype(F32)).astype(BF16)
+    ntab = normal(stab)
+    ntab_ref[...] = ntab
+    for j in range(3):
+        u = mm(ntab, w1_ref[j * width : (j + 1) * width, :])
+        high = u.astype(BF16)
+        u_ref[j * CLASSES : (j + 1) * CLASSES, :] = high
+        u_ref[(3 + j) * CLASSES : (4 + j) * CLASSES, :] = (u - high.astype(F32)).astype(BF16)
+
+
+def main_kernel(
+    crow, prow,
+    rowidx_ref, colidx_ref, cot_ref, w1_ref, w2_ref, p0_ref, p1_ref, p2_ref,
+    act0_ref, slope0_ref, stab_ref, sparts_ref, ntab_ref, u_ref, selt_ref,
+    features_ref, mine_ref, other_ref,
+    stream_ref, normed_ref, act1_ref, act2_ref, slope1_ref, slope2_ref, grad_ref, back_ref,
+    conv_ref, point_ref, bt_ref,
+):
+    rows, width = cot_ref.shape
+    mid = p0_ref.shape[0]
+    rb = rows // 2
+    k = lax.axis_index("seq")
+    zh, core = k // STRIDE, k % 2
+    half = width // 2
+    lanes = lax.broadcasted_iota(jnp.int32, (rows, CLASSES), 1)
+    hot = [(lanes == colidx_ref[:, j : j + 1]).astype(F32).astype(BF16) for j in range(3)]
+    spread = jnp.concatenate(hot + hot, axis=1)
+    act1, slope1 = gelu_pair(mm(spread, u_ref[...]))
+    act1 = act1.astype(BF16)
+    act1_ref[...] = act1
+    slope1_ref[...] = slope1
+    stream = mm(jnp.concatenate([hot[1], hot[1]], axis=1), sparts_ref[...]) + mm(act1, p1_ref[...])
+    stream_ref[...] = stream
+    normed = normal(stream)
+    normed_ref[...] = normed
+    sides = jnp.concatenate(
+        [mm(normed[rb:], w2_ref[2 * width :, :]), mm(normed[:rb], w2_ref[:width, :])]
+    )
+    act2, slope2 = gelu_pair(mm(normed, w2_ref[width : 2 * width, :]) + sides)
+    act2_ref[...] = act2.astype(BF16)
+    place = pl.ds(pl.multiple_of(zh * rb, 16), rb)
+    features_ref[...] = stream_ref[place, :] + mm(act2_ref[place, :], p2_ref[...])
+
+    grad2 = (mm_nt(cot_ref[...], p2_ref[...]) * slope2).astype(BF16)
+    grad_ref[...] = grad2
+    sides = jnp.concatenate(
+        [mm_nt(grad2[rb:], w2_ref[:width, :]), mm_nt(grad2[:rb], w2_ref[2 * width :, :])]
+    )
+    ng = mm_nt(grad2, w2_ref[width : 2 * width, :]) + sides
+    stream = stream_ref[...]
+    scale = norm_scale(stream)
+    inner = jnp.mean(ng * stream, axis=-1, keepdims=True)
+    back = cot_ref[...].astype(F32) + scale * (ng - stream * (scale * scale * inner))
+    back = back.astype(BF16)
+    back_ref[...] = back
+    grad1 = (mm_nt(back, p1_ref[...]) * slope1_ref[...]).astype(BF16)
+
+    ids = lax.broadcasted_iota(jnp.int32, (CLASSES, rows), 0)
+    hott = [(ids == rowidx_ref[j : j + 1, :]).astype(F32).astype(BF16) for j in range(3)]
+    h = [mm(v, grad1).astype(BF16) for v in hott]
+    ng = None
+    for j in range(3):
+        term = mm_nt(h[j], w1_ref[j * width : (j + 1) * width, :])
+        ng = term if ng is None else ng + term
+    stab = stab_ref[...]
+    scale = norm_scale(stab)
+    inner = jnp.mean(ng * stab, axis=-1, keepdims=True)
+    b = mm(hott[1], back) + scale * (ng - stab * (scale * scale * inner))
+    s = (mm_nt(b.astype(BF16), p0_ref[...]) * slope0_ref[...]).astype(BF16)
+    g = mm(selt_ref[...], s)
+    bt_ref[...] = jnp.transpose(b)
+
+    columns = pl.ds(pl.multiple_of(zh * half, 128), half)
+    side_at = pl.ds(pl.multiple_of(zh * half, 16), width)
+    center_at = pl.ds(pl.multiple_of((1 - zh) * width, 16), half)
+    far = pl.ds(pl.multiple_of((1 - zh) * rb, 16), rb)
+    conv_ref[0, side_at, :] = mm_tn(ntab_ref[...], jnp.where(zh == 0, h[0], h[2]))
+    conv_ref[0, center_at, :] = mm_tn(ntab_ref[:, columns], h[1])
+    conv_ref[1, side_at, :] = mm_tn(normed_ref[place, :], grad_ref[far, :])
+    conv_ref[1, center_at, :] = mm_tn(normed_ref[:, columns], grad_ref[...])
+    point_ref[0] = mm_tn(back_ref[:, columns], act1_ref[...])
+    point_ref[1] = mm_tn(cot_ref[:, columns], act2_ref[...])
+    part = crow + prow
+    step = 2 * part + 16
+    for target, side in ((mine_ref, core), (other_ref, 1 - core)):
+        for m in range(STRIDE // 2):
+            tile = 2 * m + side
+            crows = pl.ds(pl.multiple_of(tile * crow, 16), crow)
+            prows = pl.ds(pl.multiple_of(tile * prow, 16), prow)
+            for layer in range(2):
+                at = m * step + layer * part
+                target[at : at + crow, :] = conv_ref[layer, crows, :].astype(target.dtype)
+                target[at + crow : at + part, :] = point_ref[layer, prows, :].astype(target.dtype)
+            at = m * step + 2 * part
+            for q in range(3):
+                place = pl.ds(pl.multiple_of(zh * half + tile * prow + 16 * q, 16), 16)
+                target[at : at + 16, q * CLASSES : (q + 1) * CLASSES] = bt_ref[place, :].astype(target.dtype)
+        at = STRIDE // 2 * step
+        target[at : at + 16, :] = g.astype(target.dtype)
+
+
+def message_kernel(part, mine_ref, other_ref, *out_refs):
+    k, x = lax.axis_index("seq"), lax.axis_index("dp")
+    m = (k % STRIDE) // 2
+    step = 2 * part + 16
+    end = STRIDE // 2 * step
+    small = mine_ref[end : end + 16, :] + other_ref[end : end + 16, :].astype(F32)
+    for mask, out_ref in enumerate(out_refs):
+        target, layer = m ^ (mask // 2), x ^ (mask % 2)
+        at = pl.ds(pl.multiple_of(target * step + layer * part, 16), part)
+        out_ref[:part, :] = (mine_ref[at, :] + other_ref[at, :].astype(F32)).astype(out_ref.dtype)
+        at = pl.ds(pl.multiple_of(target * step + 2 * part, 16), 16)
+        out_ref[part : part + 16, :] = (mine_ref[at, :] + other_ref[at, :].astype(F32)).astype(out_ref.dtype)
+        out_ref[part + 16 :, :] = small.astype(out_ref.dtype)
+
+
+def sum_kernel(own_ref, *refs):
+    got, (total_ref, send_ref, rest_ref) = refs[:-3], refs[-3:]
+    part = total_ref.shape[0]
+    total = own_ref[...]
+    for ref in got:
+        total = total + ref[...].astype(F32)
+    total_ref[...] = total[:part]
+    send_ref[...] = total[:part].astype(BF16)
+    rest_ref[...] = total[part:]
+
+
+def small_kernel(rest_ref, embed_ref, w0_ref, act0_ref, msel_ref, spread_ref, conv0_ref, point0_ref, embed_out_ref, bt_ref):
+    width = embed_ref.shape[1]
+    g = rest_ref[16:, :]
+    bt = jnp.concatenate([rest_ref[:16, q * CLASSES : (q + 1) * CLASSES] for q in range(3)])
+    bt = bt.astype(BF16)
+    stream = embed_ref[...].astype(F32)
+    scale = norm_scale(stream)
+    g16 = g.astype(BF16)
+    ng = None
+    for j in range(3):
+        term = mm_nt(g16, w0_ref[j * width : (j + 1) * width, :])[4 * j : 4 * j + 4]
+        ng = term if ng is None else ng + term
+    inner = jnp.mean(ng * stream, axis=-1, keepdims=True)
+    embed_out_ref[...] = scale * (ng - stream * (scale * scale * inner))
+    bt_ref[...] = mm_nt(msel_ref[...], bt)
+    conv0_ref[...] = mm(spread_ref[...], g16)
+    point0_ref[...] = jnp.transpose(mm(bt, act0_ref[...]))
+
+
+def finish_kernel(total_ref, got_ref, conv0_ref, point0_ref, conv_ref, point_ref):
+    crow = conv_ref.shape[1]
+    x = lax.axis_index("dp")
+    conv_ref[0] = conv0_ref[...]
+    point_ref[0] = point0_ref[...]
+    own = total_ref[...]
+    got = got_ref[...].astype(F32)
+    first = jnp.where(x == 0, own, got)
+    second = jnp.where(x == 0, got, own)
+    conv_ref[1] = first[:crow]
+    conv_ref[2] = second[:crow]
+    point_ref[1] = jnp.transpose(first[crow:])
+    point_ref[2] = jnp.transpose(second[crow:])
+
+
+def call(kernel, outs, *args, scratch=(), limit=32, flops=0, name=None):
+    moved = sum(v.size * v.dtype.itemsize for v in list(args) + list(outs))
+    return pl.pallas_call(
+        kernel,
+        out_shape=outs,
+        in_specs=[pl.BlockSpec(memory_space=pltpu.VMEM)] * len(args),
+        out_specs=[pl.BlockSpec(memory_space=pltpu.VMEM)] * len(outs),
+        scratch_shapes=list(scratch),
+        compiler_params=pltpu.CompilerParams(vmem_limit_bytes=limit * 1024 * 1024),
+        cost_estimate=pl.CostEstimate(flops=flops, bytes_accessed=moved, transcendentals=0),
+        name=name,
+    )(*args)
+
+
+def on_device(bases, embed, conv_weight, point_weight, cotangent):
+    n, dp = lax.axis_size("seq"), lax.axis_size("dp")
+    rb, width, mid = bases.shape[1], embed.shape[1], conv_weight.shape[2]
+    if n != 2 * STRIDE or dp != 2:
+        return general(bases, embed, conv_weight, point_weight, cotangent)
+    k = lax.axis_index("seq")
+    zh, r = k // STRIDE, k % STRIDE
+    rows = 2 * rb
+    crow, prow = 3 * width // n, width // n
+    part = crow + prow
+    w = [conv_weight[i] for i in range(3)]
+    p = [point_weight[i] for i in range(3)]
+    shape = jax.ShapeDtypeStruct
+
+    gathered = lax.all_to_all(jnp.broadcast_to(bases, (n, rb)), "seq", 0, 0, tiled=True)
+    own = cotangent[0]
+    far = lax.ppermute(own, "seq", [(s, (s + STRIDE) % n) for s in range(n)])
+    cot = jnp.where(zh == 0, jnp.concatenate([own, far]), jnp.concatenate([far, own]))
+
+    sel = selectors()
+    act0, slope0, stab, sparts, ntab, u = call(
+        table_kernel,
+        [
+            shape((CLASSES, mid), BF16),
+            shape((CLASSES, mid), F32),
+            shape((CLASSES, width), F32),
+            shape((2 * CLASSES, width), BF16),
+            shape((CLASSES, width), BF16),
+            shape((6 * CLASSES, mid), BF16),
+        ],
+        embed, w[0], w[1], p[0], jnp.asarray(np.stack(sel), BF16),
+        flops=4 * CLASSES * 3 * width * mid,
+        name="tables",
+    )
+
+    cls = classes(gathered, rb // 8)
+    rowidx = jnp.concatenate(
+        [
+            jnp.concatenate(
+                [lax.dynamic_slice(cls, (a * STRIDE + r + 2 * j, 0), (1, rb)) for a in range(2)],
+                axis=1,
+            )
+            for j in range(3)
+        ]
+    )
+    selt = np.concatenate([v.T for v in sel] + [np.zeros((4, CLASSES))])
+    total_rows = STRIDE // 2 * (2 * part + 16) + 16
+    features, mine, other = call(
+        lambda *refs: main_kernel(crow, prow, *refs),
+        [shape((rb, width), F32), shape((total_rows, mid), F32), shape((total_rows, mid), BF16)],
+        rowidx, rowidx.T, cot, w[1], w[2], p[0], p[1], p[2],
+        act0, slope0, stab, sparts, ntab, u, jnp.asarray(selt, BF16),
+        scratch=[
+            pltpu.VMEM((rows, width), F32),
+            pltpu.VMEM((rows, width), BF16),
+            pltpu.VMEM((rows, mid), BF16),
+            pltpu.VMEM((rows, mid), BF16),
+            pltpu.VMEM((rows, mid), F32),
+            pltpu.VMEM((rows, mid), F32),
+            pltpu.VMEM((rows, mid), BF16),
+            pltpu.VMEM((rows, width), BF16),
+            pltpu.VMEM((2, STRIDE * crow, mid), F32),
+            pltpu.VMEM((2, STRIDE * prow, mid), F32),
+            pltpu.VMEM((width, CLASSES), F32),
+        ],
+        flops=8 * rows * 3 * width * mid,
+        name="tower",
+    )
+
+    got = lax.ppermute(other, "seq", [(s, s ^ 1) for s in range(n)])
+    peers = STRIDE // 2 * dp
+    pieces = call(
+        lambda *refs: message_kernel(part, *refs),
+        [shape((part + 32, mid), F32 if i == 0 else BF16) for i in range(peers)],
+        mine, got,
+        name="messages",
+    )
+    arrived = []
+    for mask in range(peers - 1, 0, -1):
+        route = [
+            (s * dp + d, (s ^ (2 * (mask // dp))) * dp + (d ^ (mask % dp)))
+            for s in range(n)
+            for d in range(dp)
+        ]
+        arrived.append(lax.ppermute(pieces[mask], ("seq", "dp"), route))
+    total, send, rest = call(
+        sum_kernel,
+        [shape((part, mid), F32), shape((part, mid), BF16), shape((32, mid), F32)],
+        pieces[0], *arrived,
+        name="sums",
+    )
+    swapped = lax.ppermute(send, "dp", [(d, d ^ 1) for d in range(dp)])
+
+    stream_e = embed.astype(F32)
+    normed_e = (stream_e * norm_scale(stream_e)).astype(BF16)
+    spread = jnp.concatenate(
+        [jnp.pad(normed_e, ((4 * j, 12 - 4 * j), (0, 0))) for j in range(3)], axis=1
+    )
+    spread = lax.dynamic_slice_in_dim(spread, k * crow, crow, axis=1).T
+    conv0, point0, embed_full, bt = call(
+        small_kernel,
+        [
+            shape((crow, mid), F32),
+            shape((mid, prow), F32),
+            shape((4, width), F32),
+            shape((4, prow), F32),
+        ],
+        rest, embed, w[0], act0, jnp.asarray(sel[1].T, BF16), spread,
+        name="layer0",
+    )
+    embed_grad = bt + lax.dynamic_slice_in_dim(embed_full, k * prow, prow, axis=1)
+    conv_grad, point_grad = call(
+        finish_kernel,
+        [shape((3, crow, mid), F32), shape((3, mid, prow), F32)],
+        total, swapped, conv0, point0,
+        name="finish",
+    )
+    return features[None], conv_grad, point_grad, embed_grad
+
+
 def solution(mesh):
     in_specs = (P("dp", "seq"), P(), P(), P(), P("dp", "seq", None))
     out_specs = (P("dp", "seq", None), P(None, "seq", None), P(None, None, "seq"), P(None, "seq"))

time: 105 us -> 81.1 us (0.77)
  matrix products: 37 us -> 0 us
  local copies, waits for them, and re-layouts: 9.86 us -> 25.9 us
  other arithmetic: 18.6 us -> 3.31 us
  Pallas kernels: 0 us -> 12.4 us
    dot_general x38 -> x0, matrix products: 37 us -> none  [the longest x16 17.8 us: mm(): return jnp.dot(a, b, preferred_element_type=F32)]
    pallas_call x0 -> x6, Pallas kernels: none -> 12.4 us  [call(): pl.pallas_call(kernel, out_shape=outs, in_specs=[pl.BlockSpec(memory_spac...]
    unnamed x63 -> x51, local copies, waits for them, and re-layouts: 6.81 us -> 18.1 us
    convert_element_type x13 -> x1, other arithmetic: 7.35 us -> 0.07 us  [on_device(): normed_e = (stream_e * norm_scale(stream_e)).astype(BF16)]
    squeeze x0 -> x2, local copies, waits for them, and re-layouts: none -> 5.45 us  [the longest x1 4.31 us: on_device(): w = [conv_weight[i] for i in range(3)]]
    concatenate x6 -> x2, other arithmetic: 3.43 us -> 0.19 us  [the longest x1 0.11 us: on_device(): jnp.concatenate([jnp.pad(normed_e, ((4 * j, 12 - 4 * j), (0, 0))) for j i...]
    add x3 -> x1, other arithmetic: 3.82 us -> 0.66 us  [on_device(): bt + lax.dynamic_slice_in_dim(embed_full, k * prow, prow, axis=1)]
    select_n x0 -> x1, other arithmetic: none -> 1.45 us  [on_device(): jnp.where(zh == 0, jnp.concatenate([own, far]), jnp.concatenate([far, own]))]
  transfers between devices with their start and end apart: 12 -> 11, of which waited for: 7 -> 7; matrix products, arithmetic and copies ran while one was open for 24% -> 11% of each run, Pallas kernels for 0% -> 3%
where the time goes in v2:
time: 81.1 us; the launch traced here: 80.3 us
  local copies, waits for them, and re-layouts  25.9 us (32%)
  starting transfers between devices  22.5 us (28%)
  waiting for transfers between devices  15.4 us (19%)
  Pallas kernels  12.4 us (15%)
  other arithmetic  3.31 us (4%)
    unnamed x51, local copies, waits for them, and re-layouts  18.1 us
    pallas_call x6, Pallas kernels, call(): pl.pallas_call(kernel, out_shape=outs, in_specs=[pl.BlockSpec(memory_spac...  12.4 us
    ppermute x7, waiting for transfers between devices, on_device(): arrived.append(lax.ppermute(pieces[mask], ('seq', 'dp'), route))  10.7 us
    ppermute x7, starting transfers between devices, on_device(): arrived.append(lax.ppermute(pieces[mask], ('seq', 'dp'), route))  10.4 us
    all_to_all x1, starting transfers between devices, on_device(): lax.all_to_all(jnp.broadcast_to(bases, (n, rb)), 'seq', 0, 0, tiled=True)  7.44 us
    squeeze x1, local copies, waits for them, and re-layouts, on_device(): w = [conv_weight[i] for i in range(3)]  4.31 us
    ppermute x1, starting transfers between devices, on_device(): far = lax.ppermute(own, 'seq', [(s, (s + STRIDE) % n) for s in range(n)])  2.84 us
    ppermute x1, waiting for transfers between devices, on_device(): got = lax.ppermute(other, 'seq', [(s, s ^ 1) for s in range(n)])  2.81 us
  transfers between devices with their start and end apart: 11, of which 7 were waited for; matrix products, arithmetic and copies ran while one was open for 11% of the time, Pallas kernels for 3%

profile of v2, /device:TPU:0, one launch (start us, length us, event | category | flops | bytes accessed | tf_op | source)
XLA Modules:
  0.0 80.3 jit_solution(7183795848811115440)
XLA Ops:
  0.6 1.3 %broadcast_in_dim.13 = s32[16,1,176]{2,1,0:T(1,128)} broadcast(s32[176]{0:T(256)} %bitcast.28), dimensions={2} | broadcast | bytes 11968 | tf_op jit(solution)/shard_map/broadcast_in_dim | solution.py:448
  1.9 7.4 %all-to-all-start = ((s32[16,1,176]{2,1,0:T(1,128)}), s32[16,1,176]{2,1,0:T(1,128)}, u32[]{:S(2)}, u32[]{:S(2)}) async-start(s32[16,1,176]{2,1,0:T(1,128)} %broadcast_in_dim.13), calls=%async_computation | async-start | bytes 32768 | tf_op jit(solution)/shard_map/all_to_all | solution.py:448
  9.4 0.0 copy-start.23
  9.4 2.8 %collective-permute-start = (bf16[176,768]{1,0:T(8,128)(2,1)}, bf16[176,768]{1,0:T(8,128)(2,1)}, u32[]{:S(2)}, u32[]{:S(2)}) collective-permute-start(bf16[176,768]{1,0:T(8,128)(2,1)} %bitcast.24), channel_id=1, source_target_pairs={{0,16},{2,18},{4,20},{6,22},{8,24},{10,26},{12,28},{14,30},{16,0},... | collective-permute-start | bytes 811016 | tf_op jit(solution)/shard_map/ppermute | solution.py:450
  12.2 4.3 %slice_bitcast_fusion = (bf16[2304,384]{1,0:T(8,128)(2,1)S(1)}, bf16[2304,384]{1,0:T(8,128)(2,1)S(1)}, bf16[2304,384]{1,0:T(8,128)(2,1)}) fusion(bf16[3,2304,384]{2,1,0:T(8,128)(2,1)} %param.10), kind=kLoop, calls=%fused_computation | loop fusion | bytes 10616832 | tf_op jit(solution)/shard_map/squeeze | solution.py:444
  16.5 0.0 copy-done.23
  16.5 1.1 %slice_bitcast_fusion.3 = (bf16[384,768]{1,0:T(8,128)(2,1)}, bf16[384,768]{1,0:T(8,128)(2,1)S(1)}, bf16[384,768]{1,0:T(8,128)(2,1)}) fusion(bf16[3,384,768]{2,1,0:T(8,128)(2,1)S(1)} %copy-done.23), kind=kLoop, calls=%fused_computation.3 | loop fusion | bytes 3538944 | tf_op jit(solution)/shard_map/squeeze | solution.py:445
  17.7 1.8 %tables.1 = (bf16[128,384]{1,0:T(8,128)(2,1)S(1)}, f32[128,384]{1,0:T(8,128)S(1)}, f32[128,768]{1,0:T(8,128)S(1)}, bf16[256,768]{1,0:T(8,128)(2,1)S(1)}, bf16[12...) custom-call(bf16[4,768]{1,0:T(4,128)(2,1)S(1)} %copy-done.10, bf16[2304,384]{1,0:T(8,128)(2,1)S(1)} %get-tuple-element.64.w0_ref, ...), custom_call_target="tpu_custom_call" | custom-call | flops 452984832 | bytes 6005760 | tf_op jit(solution)/shard_map/tables/pallas_call | solution.py:422
  19.5 0.6 copy-done.6
  20.1 0.8 %copy-done.12 = bf16[768,384]{1,0:T(8,128)(2,1)} copy-done((bf16[768,384]{1,0:T(8,128)(2,1)}, bf16[768,384]{1,0:T(8,128)(2,1)S(1)}, u32[]{:S(2)}) %copy-start.12) | copy-done | bytes 589848
  21.0 0.7 copy-done.14
  21.7 0.7 copy-done.16
  22.5 0.7 copy-done.18
  23.1 0.7 copy-done.20
  23.8 0.0 all-to-all-done
  23.8 0.7 copy.25
  24.5 0.1 fusion.16
  24.6 0.1 fusion.17
  24.7 0.8 fusion.4
  25.5 0.1 add_add_fusion.refs_0_
  25.6 0.8 %copy.17 = s32[3,352]{0,1:T(8,128)} copy(s32[3,352]{1,0:T(4,128)S(1)} %add_add_fusion.refs_0_) | data formatting | bytes 8448 | tf_op jit(solution)/shard_map/concatenate | solution.py:470
  26.5 0.0 collective-permute-done
  26.5 1.5 %maximum_select_fusion.refs_2_ = bf16[352,768]{1,0:T(8,128)(2,1)S(1)} fusion(bf16[176,768]{1,0:T(8,128)(2,1)} %collective-permute-done, bf16[176,768]{1,0:T(8,128)(2,1)} %bitcast.25, pred[]{:T(512)S(6)} %eq.5), kind=kLoop, calls=%fused_computation.6 | loop fusion | flops 2433024 | bytes 1081345 | tf_op jit(solution)/shard_map/jit(_where)/select_n | solution.py:451
  27.9 1.1 %copy-done.1 = bf16[384,768]{1,0:T(8,128)(2,1)S(1)} copy-done((bf16[384,768]{1,0:T(8,128)(2,1)S(1)}, bf16[384,768]{1,0:T(8,128)(2,1)}, u32[]{:S(2)}) %copy-start.1) | copy-done | bytes 589848
  29.0 1.5 %copy-done.2 = bf16[2304,384]{1,0:T(8,128)(2,1)S(1)} copy-done((bf16[2304,384]{1,0:T(8,128)(2,1)S(1)}, bf16[2304,384]{1,0:T(8,128)(2,1)}, u32[]{:S(2)}) %copy-start.2) | copy-done | bytes 1769496
  30.5 1.1 %copy-done.3 = bf16[384,768]{1,0:T(8,128)(2,1)S(1)} copy-done((bf16[384,768]{1,0:T(8,128)(2,1)S(1)}, bf16[384,768]{1,0:T(8,128)(2,1)}, u32[]{:S(2)}) %copy-start.3) | copy-done | bytes 589848
  31.5 1.1 %copy-done.4 = bf16[384,768]{1,0:T(8,128)(2,1)S(1)} copy-done((bf16[384,768]{1,0:T(8,128)(2,1)S(1)}, bf16[384,768]{1,0:T(8,128)(2,1)}, u32[]{:S(2)}) %copy-start.4) | copy-done | bytes 589848
  32.6 0.9 %copy-done.5 = s32[3,352]{0,1:T(8,128)S(1)} copy-done((s32[3,352]{0,1:T(8,128)S(1)}, s32[3,352]{0,1:T(8,128)}, u32[]{:S(2)}) %copy-start.5) | copy-done | bytes 4248
  33.5 0.9 %copy-done.7 = bf16[128,384]{1,0:T(8,128)(2,1)S(1)} copy-done((bf16[128,384]{1,0:T(8,128)(2,1)S(1)}, bf16[128,384]{1,0:T(8,128)(2,1)}, u32[]{:S(2)}) %copy-start.7) | copy-done | bytes 98328
  34.4 1.1 %copy-done.13 = bf16[768,384]{1,0:T(8,128)(2,1)S(1)} copy-done((bf16[768,384]{1,0:T(8,128)(2,1)S(1)}, bf16[768,384]{1,0:T(8,128)(2,1)}, u32[]{:S(2)}) %copy-start.13) | copy-done | bytes 589848
  35.5 1.0 %copy-done.15 = f32[128,768]{1,0:T(8,128)S(1)} copy-done((f32[128,768]{1,0:T(8,128)S(1)}, f32[128,768]{1,0:T(8,128)}, u32[]{:S(2)}) %copy-start.15) | copy-done | bytes 393240
  36.5 1.0 %copy-done.17 = bf16[256,768]{1,0:T(8,128)(2,1)S(1)} copy-done((bf16[256,768]{1,0:T(8,128)(2,1)S(1)}, bf16[256,768]{1,0:T(8,128)(2,1)}, u32[]{:S(2)}) %copy-start.17) | copy-done | bytes 393240
  37.5 0.9 %copy-done.19 = f32[128,384]{1,0:T(8,128)S(1)} copy-done((f32[128,384]{1,0:T(8,128)S(1)}, f32[128,384]{1,0:T(8,128)}, u32[]{:S(2)}) %copy-start.19) | copy-done | bytes 196632
  38.4 0.9 %copy-done.21 = bf16[128,768]{1,0:T(8,128)(2,1)S(1)} copy-done((bf16[128,768]{1,0:T(8,128)(2,1)S(1)}, bf16[128,768]{1,0:T(8,128)(2,1)}, u32[]{:S(2)}) %copy-start.21) | copy-done | bytes 196632
  39.3 0.7 copy-done.22
  40.0 7.7 %tower.1 = (f32[176,768]{1,0:T(8,128)}, f32[1616,384]{1,0:T(8,128)S(1)}, bf16[1616,384]{1,0:T(8,128)(2,1)S(1)}) custom-call(s32[3,352]{1,0:T(4,128)S(1)} %add_add_fusion.refs_0_, s32[352,3]{1,0:T(8,128)S(1)} %bitcast.22, bf16[352,768]{1,0:T(8,128)(2,1)S(1)} %maximum_select_fusion.refs_2_, bf16[2304,384]{1,0:T(8,128)(2,1)S(1)} %get-tuple-element.65.w1_ref.refs_3_, ...), custom_call_target="tpu_custom_call" | custom-call | flops 2491416576 | bytes 11993344 | tf_op jit(solution)/shard_map/tower/pallas_call | solution.py:422
  47.7 0.0 collective-permute-start.1
  47.7 0.1 fusion.11
  47.8 2.8 %collective-permute-done.1.refs_1_ = bf16[1616,384]{1,0:T(8,128)(2,1)S(1)} collective-permute-done((bf16[1616,384]{1,0:T(8,128)(2,1)S(1)}, bf16[1616,384]{1,0:T(8,128)(2,1)S(1)}, u32[]{:S(2)}, u32[]{:S(2)}) %collective-permute-start.1) | collective-permute-done | bytes 1241120 | tf_op jit(solution)/shard_map/ppermute | solution.py:503
  50.6 1.0 %messages.1 = (f32[224,384]{1,0:T(8,128)S(1)}, bf16[224,384]{1,0:T(8,128)(2,1)}, bf16[224,384]{1,0:T(8,128)(2,1)}, bf16[224,384]{1,0:T(8,128)(2,1)}, bf16[224,38...) custom-call(f32[1616,384]{1,0:T(8,128)S(1)} %get-tuple-element.37.refs_0_, ...), custom_call_target="tpu_custom_call" | custom-call | bytes 5271552 | tf_op jit(solution)/shard_map/messages/pallas_call | solution.py:422
  51.7 3.3 %collective-permute-start.2 = (bf16[224,384]{1,0:T(8,128)(2,1)S(1)}, bf16[224,384]{1,0:T(8,128)(2,1)S(1)}, u32[]{:S(2)}, u32[]{:S(2)}) collective-permute-start(bf16[224,384]{1,0:T(8,128)(2,1)S(1)} %get-tuple-element.40), channel_id=1, source_target_pairs={{0,13},{1,12},{2,15},{3,14},{4,9},{5,8},{6,11},{7,10},{8,5},{9,4},... | collective-permute-start | bytes 516104 | tf_op jit(solution)/shard_map/ppermute | solution.py:518
  54.9 0.6 collective-permute-start.3
  55.5 1.5 %collective-permute-start.4 = (bf16[224,384]{1,0:T(8,128)(2,1)}, bf16[224,384]{1,0:T(8,128)(2,1)S(1)}, u32[]{:S(2)}, u32[]{:S(2)}) collective-permute-start(bf16[224,384]{1,0:T(8,128)(2,1)} %get-tuple-element.42), channel_id=1, source_target_pairs={{0,9},{1,8},{2,11},{3,10},{4,13},{5,12},{6,15},{7,14},{8,1},{9,0},... | collective-permute-start | bytes 516104 | tf_op jit(solution)/shard_map/ppermute | solution.py:518
  56.9 0.6 collective-permute-start.5
  57.5 2.4 %collective-permute-start.6 = (bf16[224,384]{1,0:T(8,128)(2,1)}, bf16[224,384]{1,0:T(8,128)(2,1)S(1)}, u32[]{:S(2)}, u32[]{:S(2)}) collective-permute-start(bf16[224,384]{1,0:T(8,128)(2,1)} %get-tuple-element.44), channel_id=1, source_target_pairs={{0,5},{1,4},{2,7},{3,6},{4,1},{5,0},{6,3},{7,2},{8,13},{9,12},{10,... | collective-permute-start | bytes 516104 | tf_op jit(solution)/shard_map/ppermute | solution.py:518
  59.9 1.0 %collective-permute-done.2.refs_0_ = bf16[224,384]{1,0:T(8,128)(2,1)S(1)} collective-permute-done((bf16[224,384]{1,0:T(8,128)(2,1)S(1)}, bf16[224,384]{1,0:T(8,128)(2,1)S(1)}, u32[]{:S(2)}, u32[]{:S(2)}) %collective-permute-start.2) | collective-permute-done | bytes 172064 | tf_op jit(solution)/shard_map/ppermute | solution.py:518
  60.9 1.5 %collective-permute-start.7 = (bf16[224,384]{1,0:T(8,128)(2,1)}, bf16[224,384]{1,0:T(8,128)(2,1)S(1)}, u32[]{:S(2)}, u32[]{:S(2)}) collective-permute-start(bf16[224,384]{1,0:T(8,128)(2,1)} %get-tuple-element.45), channel_id=1, source_target_pairs={{0,4},{1,5},{2,6},{3,7},{4,0},{5,1},{6,2},{7,3},{8,12},{9,13},{10,... | collective-permute-start | bytes 516104 | tf_op jit(solution)/shard_map/ppermute | solution.py:518
  62.3 4.4 %collective-permute-done.3.refs_1_ = bf16[224,384]{1,0:T(8,128)(2,1)S(1)} collective-permute-done((bf16[224,384]{1,0:T(8,128)(2,1)S(1)}, bf16[224,384]{1,0:T(8,128)(2,1)S(1)}, u32[]{:S(2)}, u32[]{:S(2)}) %collective-permute-start.3) | collective-permute-done | bytes 172064 | tf_op jit(solution)/shard_map/ppermute | solution.py:518
  66.7 0.7 collective-permute-start.8
  67.5 0.1 fusion.12
  67.5 0.1 fusion.14
  67.6 0.1 copy.21
  67.8 1.9 %collective-permute-done.4.refs_2_ = bf16[224,384]{1,0:T(8,128)(2,1)S(1)} collective-permute-done((bf16[224,384]{1,0:T(8,128)(2,1)}, bf16[224,384]{1,0:T(8,128)(2,1)S(1)}, u32[]{:S(2)}, u32[]{:S(2)}) %collective-permute-start.4) | collective-permute-done | bytes 172064 | tf_op jit(solution)/shard_map/ppermute | solution.py:518
  69.7 2.7 %collective-permute-done.5.refs_3_ = bf16[224,384]{1,0:T(8,128)(2,1)S(1)} collective-permute-done((bf16[224,384]{1,0:T(8,128)(2,1)}, bf16[224,384]{1,0:T(8,128)(2,1)S(1)}, u32[]{:S(2)}, u32[]{:S(2)}) %collective-permute-start.5) | collective-permute-done | bytes 172064 | tf_op jit(solution)/shard_map/ppermute | solution.py:518
  72.3 0.0 collective-permute-done.6.refs_4_
  72.3 0.0 collective-permute-done.7.refs_5_
  72.4 0.7 collective-permute-done.8.refs_6_
  73.0 0.2 sums.1
  73.2 1.9 %collective-permute-start.9 = (bf16[192,384]{1,0:T(8,128)(2,1)S(1)}, bf16[192,384]{1,0:T(8,128)(2,1)S(1)}, u32[]{:S(2)}, u32[]{:S(2)}) collective-permute-start(bf16[192,384]{1,0:T(8,128)(2,1)S(1)} %get-tuple-element.48), channel_id=1, source_target_pairs={{0,1},{1,0},{2,3},{3,2},{4,5},{5,4},{6,7},{7,6},{8,9},{9,8},{10,11... | collective-permute-start | bytes 442376 | tf_op jit(solution)/shard_map/ppermute | solution.py:525
  75.1 0.7 layer0.1
  75.8 0.7 fusion.15
  76.5 2.0 %collective-permute-done.9.got_ref = bf16[192,384]{1,0:T(8,128)(2,1)S(1)} collective-permute-done((bf16[192,384]{1,0:T(8,128)(2,1)S(1)}, bf16[192,384]{1,0:T(8,128)(2,1)S(1)}, u32[]{:S(2)}, u32[]{:S(2)}) %collective-permute-start.9) | collective-permute-done | bytes 147488 | tf_op jit(solution)/shard_map/ppermute | solution.py:525
  78.4 1.0 %finish.1 = (f32[3,144,384]{2,1,0:T(8,128)}, f32[3,384,48]{2,1,0:T(8,128)S(1)}) custom-call(f32[192,384]{1,0:T(8,128)S(1)} %get-tuple-element.47.total_ref, bf16[192,384]{1,0:T(8,128)(2,1)S(1)} %collective-permute-done.9.got_ref, f32[144,384]{1,0:T(8,128)S(1)} %get-tuple-element.50.conv0_ref, f32[384,48]{1,0:T(8,128)S(1)} %get-tuple-element.51.point0_ref), custom_call_target="tpu_custom_call" | custom-call | bytes 1622016 | tf_op jit(solution)/shard_map/finish/pallas_call | solution.py:422
  79.4 0.9 %copy.19 = f32[3,384,48]{1,2,0:T(8,128)} copy(f32[3,384,48]{2,1,0:T(8,128)S(1)} %get-tuple-element.62) | data formatting | bytes 442368
  (32 shorter events, 0.1 us)
Async XLA Ops:
  1.9 21.9 %all-to-all-start = ((s32[16,1,176]{2,1,0:T(1,128)}), s32[16,1,176]{2,1,0:T(1,128)}, u32[]{:S(2)}, u32[]{:S(2)}) async-start(s32[16,1,176]{2,1,0:T(1,128)} %broadcast_in_dim.13), calls=%async_computation | async-start | bytes 32768 | tf_op jit(solution)/shard_map/all_to_all | solution.py:448
  9.4 7.2 %copy-start.23 = (bf16[3,384,768]{2,1,0:T(8,128)(2,1)S(1)}, bf16[3,384,768]{2,1,0:T(8,128)(2,1)}, u32[]{:S(2)}) copy-start(bf16[3,384,768]{2,1,0:T(8,128)(2,1)} %param.11) | copy-start | bytes 5308420
  9.4 17.1 %collective-permute-start = (bf16[176,768]{1,0:T(8,128)(2,1)}, bf16[176,768]{1,0:T(8,128)(2,1)}, u32[]{:S(2)}, u32[]{:S(2)}) collective-permute-start(bf16[176,768]{1,0:T(8,128)(2,1)} %bitcast.24), channel_id=1, source_target_pairs={{0,16},{2,18},{4,20},{6,22},{8,24},{10,26},{12,28},{14,30},{16,0},... | collective-permute-start | bytes 811016 | tf_op jit(solution)/shard_map/ppermute | solution.py:450
  16.5 1.1 %copy-start.9 = (bf16[3,128,4]{2,1,0:T(8,128)(2,1)S(1)}, bf16[3,128,4]{2,1,0:T(8,128)(2,1)}, u32[]{:S(2)}) copy-start(bf16[3,128,4]{2,1,0:T(8,128)(2,1)} %constant.81.clone.sel_ref) | copy-start | bytes 9220
  16.5 1.1 %copy-start.10 = (bf16[4,768]{1,0:T(4,128)(2,1)S(1)}, bf16[4,768]{1,0:T(4,128)(2,1)}, u32[]{:S(2)}) copy-start(bf16[4,768]{1,0:T(4,128)(2,1)} %embed_ref.3) | copy-start | bytes 18436
  17.7 1.8 %copy-start = (bf16[384,768]{1,0:T(8,128)(2,1)}, bf16[384,768]{1,0:T(8,128)(2,1)S(1)}, u32[]{:S(2)}) copy-start(bf16[384,768]{1,0:T(8,128)(2,1)S(1)} %get-tuple-element.68.p0_ref.refs_5_) | copy-start | bytes 1769476
  19.5 0.6 copy-start.6
  20.1 0.8 %copy-start.12 = (bf16[768,384]{1,0:T(8,128)(2,1)}, bf16[768,384]{1,0:T(8,128)(2,1)S(1)}, u32[]{:S(2)}) copy-start(bf16[768,384]{1,0:T(8,128)(2,1)S(1)} %get-tuple-element.35.refs_13_) | copy-start | bytes 1769476
  21.0 0.7 copy-start.14
  21.7 0.7 copy-start.16
  22.5 0.7 copy-start.18
  23.1 0.7 copy-start.20
  27.9 1.1 %copy-start.1 = (bf16[384,768]{1,0:T(8,128)(2,1)S(1)}, bf16[384,768]{1,0:T(8,128)(2,1)}, u32[]{:S(2)}) copy-start(bf16[384,768]{1,0:T(8,128)(2,1)} %copy-done) | copy-start | bytes 1769476
  29.0 1.5 %copy-start.2 = (bf16[2304,384]{1,0:T(8,128)(2,1)S(1)}, bf16[2304,384]{1,0:T(8,128)(2,1)}, u32[]{:S(2)}) copy-start(bf16[2304,384]{1,0:T(8,128)(2,1)} %get-tuple-element.66.refs_4_) | copy-start | bytes 5308420
  30.5 1.1 %copy-start.3 = (bf16[384,768]{1,0:T(8,128)(2,1)S(1)}, bf16[384,768]{1,0:T(8,128)(2,1)}, u32[]{:S(2)}) copy-start(bf16[384,768]{1,0:T(8,128)(2,1)} %get-tuple-element.67.refs_7_) | copy-start | bytes 1769476
  31.5 1.1 %copy-start.4 = (bf16[384,768]{1,0:T(8,128)(2,1)S(1)}, bf16[384,768]{1,0:T(8,128)(2,1)}, u32[]{:S(2)}) copy-start(bf16[384,768]{1,0:T(8,128)(2,1)} %get-tuple-element.69.refs_6_) | copy-start | bytes 1769476
  32.6 0.9 %copy-start.5 = (s32[3,352]{0,1:T(8,128)S(1)}, s32[3,352]{0,1:T(8,128)}, u32[]{:S(2)}) copy-start(s32[3,352]{0,1:T(8,128)} %copy.17) | copy-start | bytes 12676
  33.5 0.9 %copy-start.7 = (bf16[128,384]{1,0:T(8,128)(2,1)S(1)}, bf16[128,384]{1,0:T(8,128)(2,1)}, u32[]{:S(2)}) copy-start(bf16[128,384]{1,0:T(8,128)(2,1)} %copy-done.6) | copy-start | bytes 294916
  34.4 1.1 %copy-start.13 = (bf16[768,384]{1,0:T(8,128)(2,1)S(1)}, bf16[768,384]{1,0:T(8,128)(2,1)}, u32[]{:S(2)}) copy-start(bf16[768,384]{1,0:T(8,128)(2,1)} %copy-done.12) | copy-start | bytes 1769476
  35.5 1.0 %copy-start.15 = (f32[128,768]{1,0:T(8,128)S(1)}, f32[128,768]{1,0:T(8,128)}, u32[]{:S(2)}) copy-start(f32[128,768]{1,0:T(8,128)} %copy-done.14) | copy-start | bytes 1179652
  36.5 1.0 %copy-start.17 = (bf16[256,768]{1,0:T(8,128)(2,1)S(1)}, bf16[256,768]{1,0:T(8,128)(2,1)}, u32[]{:S(2)}) copy-start(bf16[256,768]{1,0:T(8,128)(2,1)} %copy-done.16) | copy-start | bytes 1179652
  37.5 0.9 %copy-start.19 = (f32[128,384]{1,0:T(8,128)S(1)}, f32[128,384]{1,0:T(8,128)}, u32[]{:S(2)}) copy-start(f32[128,384]{1,0:T(8,128)} %copy-done.18) | copy-start | bytes 589828
  38.4 0.9 %copy-start.21 = (bf16[128,768]{1,0:T(8,128)(2,1)S(1)}, bf16[128,768]{1,0:T(8,128)(2,1)}, u32[]{:S(2)}) copy-start(bf16[128,768]{1,0:T(8,128)(2,1)} %copy-done.20) | copy-start | bytes 589828
  39.3 0.7 copy-start.22
  47.7 2.9 %collective-permute-start.1 = (bf16[1616,384]{1,0:T(8,128)(2,1)S(1)}, bf16[1616,384]{1,0:T(8,128)(2,1)S(1)}, u32[]{:S(2)}, u32[]{:S(2)}) collective-permute-start(bf16[1616,384]{1,0:T(8,128)(2,1)S(1)} %get-tuple-element.38), channel_id=1, source_target_pairs={{0,2},{2,0},{4,6},{6,4},{8,10},{10,8},{12,14},{14,12},{16,18},{18,... | collective-permute-start | bytes 3723272 | tf_op jit(solution)/shard_map/ppermute | solution.py:503
  50.6 24.5 %copy-start.8 = (bf16[128,384]{1,0:T(8,128)(2,1)S(1)}, bf16[128,384]{1,0:T(8,128)(2,1)}, u32[]{:S(2)}) copy-start(bf16[128,384]{1,0:T(8,128)(2,1)} %copy-done.6) | copy-start | bytes 294916
  50.6 24.5 %copy-start.11 = (bf16[4,128]{1,0:T(4,128)(2,1)S(1)}, bf16[4,128]{1,0:T(4,128)(2,1)}, u32[]{:S(2)}) copy-start(bf16[4,128]{1,0:T(4,128)(2,1)} %constant.83.clone.msel_ref) | copy-start | bytes 3076
  51.7 9.2 %collective-permute-start.2 = (bf16[224,384]{1,0:T(8,128)(2,1)S(1)}, bf16[224,384]{1,0:T(8,128)(2,1)S(1)}, u32[]{:S(2)}, u32[]{:S(2)}) collective-permute-start(bf16[224,384]{1,0:T(8,128)(2,1)S(1)} %get-tuple-element.40), channel_id=1, source_target_pairs={{0,13},{1,12},{2,15},{3,14},{4,9},{5,8},{6,11},{7,10},{8,5},{9,4},... | collective-permute-start | bytes 516104 | tf_op jit(solution)/shard_map/ppermute | solution.py:518
  54.9 11.8 %collective-permute-start.3 = (bf16[224,384]{1,0:T(8,128)(2,1)S(1)}, bf16[224,384]{1,0:T(8,128)(2,1)S(1)}, u32[]{:S(2)}, u32[]{:S(2)}) collective-permute-start(bf16[224,384]{1,0:T(8,128)(2,1)S(1)} %get-tuple-element.41), channel_id=1, source_target_pairs={{0,12},{1,13},{2,14},{3,15},{4,8},{5,9},{6,10},{7,11},{8,4},{9,5},... | collective-permute-start | bytes 516104 | tf_op jit(solution)/shard_map/ppermute | solution.py:518
  55.5 14.2 %collective-permute-start.4 = (bf16[224,384]{1,0:T(8,128)(2,1)}, bf16[224,384]{1,0:T(8,128)(2,1)S(1)}, u32[]{:S(2)}, u32[]{:S(2)}) collective-permute-start(bf16[224,384]{1,0:T(8,128)(2,1)} %get-tuple-element.42), channel_id=1, source_target_pairs={{0,9},{1,8},{2,11},{3,10},{4,13},{5,12},{6,15},{7,14},{8,1},{9,0},... | collective-permute-start | bytes 516104 | tf_op jit(solution)/shard_map/ppermute | solution.py:518
  56.9 15.4 %collective-permute-start.5 = (bf16[224,384]{1,0:T(8,128)(2,1)}, bf16[224,384]{1,0:T(8,128)(2,1)S(1)}, u32[]{:S(2)}, u32[]{:S(2)}) collective-permute-start(bf16[224,384]{1,0:T(8,128)(2,1)} %get-tuple-element.43), channel_id=1, source_target_pairs={{0,8},{1,9},{2,10},{3,11},{4,12},{5,13},{6,14},{7,15},{8,0},{9,1},... | collective-permute-start | bytes 516104 | tf_op jit(solution)/shard_map/ppermute | solution.py:518
  57.5 14.8 %collective-permute-start.6 = (bf16[224,384]{1,0:T(8,128)(2,1)}, bf16[224,384]{1,0:T(8,128)(2,1)S(1)}, u32[]{:S(2)}, u32[]{:S(2)}) collective-permute-start(bf16[224,384]{1,0:T(8,128)(2,1)} %get-tuple-element.44), channel_id=1, source_target_pairs={{0,5},{1,4},{2,7},{3,6},{4,1},{5,0},{6,3},{7,2},{8,13},{9,12},{10,... | collective-permute-start | bytes 516104 | tf_op jit(solution)/shard_map/ppermute | solution.py:518
  60.9 11.5 %collective-permute-start.7 = (bf16[224,384]{1,0:T(8,128)(2,1)}, bf16[224,384]{1,0:T(8,128)(2,1)S(1)}, u32[]{:S(2)}, u32[]{:S(2)}) collective-permute-start(bf16[224,384]{1,0:T(8,128)(2,1)} %get-tuple-element.45), channel_id=1, source_target_pairs={{0,4},{1,5},{2,6},{3,7},{4,0},{5,1},{6,2},{7,3},{8,12},{9,13},{10,... | collective-permute-start | bytes 516104 | tf_op jit(solution)/shard_map/ppermute | solution.py:518
  66.7 6.3 %collective-permute-start.8 = (bf16[224,384]{1,0:T(8,128)(2,1)}, bf16[224,384]{1,0:T(8,128)(2,1)S(1)}, u32[]{:S(2)}, u32[]{:S(2)}) collective-permute-start(bf16[224,384]{1,0:T(8,128)(2,1)} %get-tuple-element.46), channel_id=1, source_target_pairs={{0,1},{1,0},{2,3},{3,2},{4,5},{5,4},{6,7},{7,6},{8,9},{9,8},{10,11... | collective-permute-start | bytes 516104 | tf_op jit(solution)/shard_map/ppermute | solution.py:518
  73.2 5.2 %collective-permute-start.9 = (bf16[192,384]{1,0:T(8,128)(2,1)S(1)}, bf16[192,384]{1,0:T(8,128)(2,1)S(1)}, u32[]{:S(2)}, u32[]{:S(2)}) collective-permute-start(bf16[192,384]{1,0:T(8,128)(2,1)S(1)} %get-tuple-element.48), channel_id=1, source_target_pairs={{0,1},{1,0},{2,3},{3,2},{4,5},{5,4},{6,7},{7,6},{8,9},{9,8},{10,11... | collective-permute-start | bytes 442376 | tf_op jit(solution)/shard_map/ppermute | solution.py:525

commit v3 on v2

--- a/solution.py
+++ b/solution.py
@@ -12,6 +12,7 @@
 F32 = jnp.float32
 CLASSES = 128
 STRIDE = 8
+LIMIT = 52
 
 
 def gelu_pair(v):
@@ -240,66 +241,159 @@
     return (v * norm_scale(v)).astype(BF16)
 
 
-def table_kernel(embed_ref, w0_ref, w1_ref, p0_ref, sel_ref, act0_ref, slope0_ref, stab_ref, sparts_ref, ntab_ref, u_ref):
-    width = embed_ref.shape[1]
+def spread_kernel(bases_ref, out_ref):
+    for i in range(out_ref.shape[0]):
+        out_ref[i] = bases_ref[...]
+
+
+def fetch(source, target, sem):
+    copy = pltpu.make_async_copy(source, target, sem)
+    copy.start()
+    return copy
+
+
+def fetch_taps(w_ref, layer, held_ref, sems, first, order=(0, 1, 2)):
+    width = held_ref.shape[0] // 3
+    copies = {}
+    for j in order:
+        at = pl.ds(j * width, width)
+        copies[j] = fetch(w_ref.at[layer, at, :], held_ref.at[at, :], sems.at[first + j])
+    return copies
+
+
+def digits(shape, axis):
+    c = lax.broadcasted_iota(jnp.int32, shape, axis).astype(F32)
+    left, both = jnp.floor((c + 0.5) / 20.0), jnp.floor((c + 0.5) / 5.0)
+    return c < 100.0, (left, both - 4.0 * left, c - 5.0 * both)
+
+
+def digit_columns():
+    valid, values = digits((CLASSES, 4), 0)
+    base = lax.broadcasted_iota(jnp.int32, (CLASSES, 4), 1).astype(F32)
+    return [jnp.where(valid & (v == base), 1.0, 0.0).astype(BF16) for v in values]
+
+
+def digit_rows():
+    valid, values = digits((16, CLASSES), 1)
+    row = lax.broadcasted_iota(jnp.int32, (16, CLASSES), 0).astype(F32)
+    hit = (values[0] == row) & (row < 4.0)
+    hit |= (values[1] + 4.0 == row) & (row >= 4.0) & (row < 8.0)
+    hit |= (values[2] + 8.0 == row) & (row >= 8.0) & (row < 12.0)
+    return jnp.where(valid & hit, 1.0, 0.0).astype(BF16)
+
+
+def table_kernel(embed_ref, w_ref, p_ref, act0_ref, table_ref, w0_ref, w1_ref, p0_ref, sems):
+    width, mid = embed_ref.shape[1], act0_ref.shape[1]
+    copy_w0 = fetch_taps(w_ref, 0, w0_ref, sems, 0)
+    copy_p0 = fetch(p_ref.at[0], p0_ref, sems.at[6])
+    copy_w1 = fetch_taps(w_ref, 1, w1_ref, sems, 3)
     normed_e = normal(embed_ref[...].astype(F32))
+    sel = digit_columns()
     pre = None
     for j in range(3):
-        taps = mm(sel_ref[j], normed_e).astype(BF16)
+        taps = mm(sel[j], normed_e).astype(BF16)
+        copy_w0[j].wait()
         term = mm(taps, w0_ref[j * width : (j + 1) * width, :])
         pre = term if pre is None else pre + term
     act0, slope0 = gelu_pair(pre)
     act0 = act0.astype(BF16)
     act0_ref[...] = act0
-    slope0_ref[...] = slope0
-    stab = mm(sel_ref[1], embed_ref[...]) + mm(act0, p0_ref[...])
-    stab_ref[...] = stab
-    high = stab.astype(BF16)
-    sparts_ref[:CLASSES, :] = high
-    sparts_ref[CLASSES:, :] = (stab - high.astype(F32)).astype(BF16)
+    copy_p0.wait()
+    stab = mm(sel[1], embed_ref[...]) + mm(act0, p0_ref[...])
+    table_ref[:, :width] = stab
+    table_ref[:, width : width + mid] = slope0
     ntab = normal(stab)
-    ntab_ref[...] = ntab
     for j in range(3):
-        u = mm(ntab, w1_ref[j * width : (j + 1) * width, :])
-        high = u.astype(BF16)
-        u_ref[j * CLASSES : (j + 1) * CLASSES, :] = high
-        u_ref[(3 + j) * CLASSES : (4 + j) * CLASSES, :] = (u - high.astype(F32)).astype(BF16)
+        copy_w1[j].wait()
+        at = width + (j + 1) * mid
+        table_ref[:, at : at + mid] = mm(ntab, w1_ref[j * width : (j + 1) * width, :])
 
 
 def main_kernel(
-    crow, prow,
-    rowidx_ref, colidx_ref, cot_ref, w1_ref, w2_ref, p0_ref, p1_ref, p2_ref,
-    act0_ref, slope0_ref, stab_ref, sparts_ref, ntab_ref, u_ref, selt_ref,
+    crow, prow, bases_ref, own_ref, far_ref, w_ref, p_ref, table_ref,
     features_ref, mine_ref, other_ref,
-    stream_ref, normed_ref, act1_ref, act2_ref, slope1_ref, slope2_ref, grad_ref, back_ref,
-    conv_ref, point_ref, bt_ref,
+    hot_ref, stream_ref, normed_ref, act1_ref, act2_ref, slope1_ref, slope2_ref,
+    cot_ref, grad_ref, back_ref, conv_ref, point_ref, bt_ref, ntab_ref, w1_ref, w2_ref, pt_ref, sems,
 ):
-    rows, width = cot_ref.shape
-    mid = p0_ref.shape[0]
-    rb = rows // 2
+    n, _, rb = bases_ref.shape
+    rows, width = stream_ref.shape
+    mid = act1_ref.shape[1]
+    dil, half = rb // 8, width // 2
     k = lax.axis_index("seq")
-    zh, core = k // STRIDE, k % 2
-    half = width // 2
-    lanes = lax.broadcasted_iota(jnp.int32, (rows, CLASSES), 1)
-    hot = [(lanes == colidx_ref[:, j : j + 1]).astype(F32).astype(BF16) for j in range(3)]
-    spread = jnp.concatenate(hot + hot, axis=1)
-    act1, slope1 = gelu_pair(mm(spread, u_ref[...]))
+    zh, r, core = k // STRIDE, k % STRIDE, k % 2
+    place = pl.ds(pl.multiple_of(zh * rb, 16), rb)
+    far = pl.ds(pl.multiple_of((1 - zh) * rb, 16), rb)
+    copy_p1 = fetch(p_ref.at[1], pt_ref.at[1], sems.at[7])
+    copy_w2 = fetch_taps(w_ref, 2, w2_ref, sems, 3, (2, 0, 1))
+    copy_p2 = fetch(p_ref.at[2], pt_ref.at[2], sems.at[8])
+    copy_w1 = fetch_taps(w_ref, 1, w1_ref, sems, 0)
+    copy_p0 = fetch(p_ref.at[0], pt_ref.at[0], sems.at[6])
+    held = jnp.concatenate([bases_ref[i] for i in range(n)])
+    held = (held - 4).astype(F32)
+    edge = jnp.zeros((1, rb), F32)
+    held = jnp.concatenate(
+        [
+            jnp.concatenate([edge, held[:-1]]).astype(BF16),
+            held.astype(BF16),
+            jnp.concatenate([held[1:], edge]).astype(BF16),
+        ]
+    )
+    ahead = lax.broadcasted_iota(jnp.int32, (rb, rb), 0) - lax.broadcasted_iota(jnp.int32, (rb, rb), 1)
+
+    def weight(gap):
+        value = jnp.where(gap == -dil, 20.0, jnp.where(gap == 0, 5.0, jnp.where(gap == dil, 1.0, 0.0)))
+        return value.astype(BF16)
+
+    cls = (
+        mm(held[:n], weight(ahead - rb)) + mm(held[n : 2 * n], weight(ahead)) + mm(held[2 * n :], weight(ahead + rb))
+        + 105.0
+    ).astype(BF16)
+    block = lax.broadcasted_iota(jnp.int32, (n, CLASSES), 0)
+    slot = lax.broadcasted_iota(jnp.int32, (n, CLASSES), 1)
+    wanted = (slot // 3) * STRIDE + r + 2 * (slot % 3) - 2
+    pick = jnp.where((block == wanted) & (slot < 6), 1.0, 0.0).astype(BF16)
+    column = mm_tn(cls, pick)
+    lanes = (lax.broadcasted_iota(jnp.int32, (rb, CLASSES), 1) + 1).astype(F32)
+    for a in range(2):
+        for j in range(3):
+            i = 3 * a + j
+            hot_ref[a * rb : (a + 1) * rb, j * CLASSES : (j + 1) * CLASSES] = jnp.where(
+                lanes == column[:, i : i + 1], 1.0, 0.0
+            ).astype(BF16)
+
+    hot = hot_ref[...]
+    mid_hot = hot[:, CLASSES : 2 * CLASSES]
+    u = jnp.concatenate(
+        [table_ref[:, width + (j + 1) * mid : width + (j + 2) * mid] for j in range(3)]
+    )
+    u_high = u.astype(BF16)
+    act1, slope1 = gelu_pair(mm(hot, u_high) + mm(hot, (u - u_high.astype(F32)).astype(BF16)))
     act1 = act1.astype(BF16)
     act1_ref[...] = act1
     slope1_ref[...] = slope1
-    stream = mm(jnp.concatenate([hot[1], hot[1]], axis=1), sparts_ref[...]) + mm(act1, p1_ref[...])
+    stab = table_ref[:, :width]
+    s_high = stab.astype(BF16)
+    stream = mm(mid_hot, s_high) + mm(mid_hot, (stab - s_high.astype(F32)).astype(BF16))
+    copy_p1.wait()
+    stream = stream + mm(act1, pt_ref[1])
     stream_ref[...] = stream
     normed = normal(stream)
     normed_ref[...] = normed
+    copy_w2[2].wait()
+    copy_w2[0].wait()
     sides = jnp.concatenate(
         [mm(normed[rb:], w2_ref[2 * width :, :]), mm(normed[:rb], w2_ref[:width, :])]
     )
+    copy_w2[1].wait()
     act2, slope2 = gelu_pair(mm(normed, w2_ref[width : 2 * width, :]) + sides)
     act2_ref[...] = act2.astype(BF16)
-    place = pl.ds(pl.multiple_of(zh * rb, 16), rb)
-    features_ref[...] = stream_ref[place, :] + mm(act2_ref[place, :], p2_ref[...])
-
-    grad2 = (mm_nt(cot_ref[...], p2_ref[...]) * slope2).astype(BF16)
+    slope2_ref[...] = slope2
+    copy_p2.wait()
+    features_ref[...] = stream_ref[place, :] + mm(act2_ref[place, :], pt_ref[2])
+
+    cot_ref[place, :] = own_ref[...]
+    cot_ref[far, :] = far_ref[...]
+    grad2 = (mm_nt(cot_ref[...], pt_ref[2]) * slope2_ref[...]).astype(BF16)
     grad_ref[...] = grad2
     sides = jnp.concatenate(
         [mm_nt(grad2[rb:], w2_ref[:width, :]), mm_nt(grad2[:rb], w2_ref[2 * width :, :])]
@@ -311,27 +405,28 @@
     back = cot_ref[...].astype(F32) + scale * (ng - stream * (scale * scale * inner))
     back = back.astype(BF16)
     back_ref[...] = back
-    grad1 = (mm_nt(back, p1_ref[...]) * slope1_ref[...]).astype(BF16)
-
-    ids = lax.broadcasted_iota(jnp.int32, (CLASSES, rows), 0)
-    hott = [(ids == rowidx_ref[j : j + 1, :]).astype(F32).astype(BF16) for j in range(3)]
-    h = [mm(v, grad1).astype(BF16) for v in hott]
+    grad1 = (mm_nt(back, pt_ref[1]) * slope1_ref[...]).astype(BF16)
+
+    h = mm_tn(hot_ref[...], grad1).astype(BF16)
+    h = [h[j * CLASSES : (j + 1) * CLASSES] for j in range(3)]
     ng = None
     for j in range(3):
+        copy_w1[j].wait()
         term = mm_nt(h[j], w1_ref[j * width : (j + 1) * width, :])
         ng = term if ng is None else ng + term
-    stab = stab_ref[...]
+    stab = table_ref[:, :width]
     scale = norm_scale(stab)
+    ntab_ref[...] = (stab * scale).astype(BF16)
     inner = jnp.mean(ng * stab, axis=-1, keepdims=True)
-    b = mm(hott[1], back) + scale * (ng - stab * (scale * scale * inner))
-    s = (mm_nt(b.astype(BF16), p0_ref[...]) * slope0_ref[...]).astype(BF16)
-    g = mm(selt_ref[...], s)
+    b = mm_tn(hot_ref[:, CLASSES : 2 * CLASSES], back) + scale * (ng - stab * (scale * scale * inner))
+    copy_p0.wait()
+    s = (mm_nt(b.astype(BF16), pt_ref[0]) * table_ref[:, width : width + mid]).astype(BF16)
+    g = mm(digit_rows(), s)
     bt_ref[...] = jnp.transpose(b)
 
     columns = pl.ds(pl.multiple_of(zh * half, 128), half)
     side_at = pl.ds(pl.multiple_of(zh * half, 16), width)
     center_at = pl.ds(pl.multiple_of((1 - zh) * width, 16), half)
-    far = pl.ds(pl.multiple_of((1 - zh) * rb, 16), rb)
     conv_ref[0, side_at, :] = mm_tn(ntab_ref[...], jnp.where(zh == 0, h[0], h[2]))
     conv_ref[0, center_at, :] = mm_tn(ntab_ref[:, columns], h[1])
     conv_ref[1, side_at, :] = mm_tn(normed_ref[place, :], grad_ref[far, :])
@@ -351,8 +446,8 @@
                 target[at + crow : at + part, :] = point_ref[layer, prows, :].astype(target.dtype)
             at = m * step + 2 * part
             for q in range(3):
-                place = pl.ds(pl.multiple_of(zh * half + tile * prow + 16 * q, 16), 16)
-                target[at : at + 16, q * CLASSES : (q + 1) * CLASSES] = bt_ref[place, :].astype(target.dtype)
+                brows = pl.ds(pl.multiple_of(zh * half + tile * prow + 16 * q, 16), 16)
+                target[at : at + 16, q * CLASSES : (q + 1) * CLASSES] = bt_ref[brows, :].astype(target.dtype)
         at = STRIDE // 2 * step
         target[at : at + 16, :] = g.astype(target.dtype)
 
@@ -383,7 +478,8 @@
     rest_ref[...] = total[part:]
 
 
-def small_kernel(rest_ref, embed_ref, w0_ref, act0_ref, msel_ref, spread_ref, conv0_ref, point0_ref, embed_out_ref, bt_ref):
+def small_kernel(rest_ref, embed_ref, w_ref, act0_ref, spread_ref, conv0_ref, point0_ref, embed_out_ref, bt_ref, w0_ref, sems):
+    copy_w0 = fetch_taps(w_ref, 0, w0_ref, sems, 0)
     width = embed_ref.shape[1]
     g = rest_ref[16:, :]
     bt = jnp.concatenate([rest_ref[:16, q * CLASSES : (q + 1) * CLASSES] for q in range(3)])
@@ -393,13 +489,14 @@
     g16 = g.astype(BF16)
     ng = None
     for j in range(3):
+        copy_w0[j].wait()
         term = mm_nt(g16, w0_ref[j * width : (j + 1) * width, :])[4 * j : 4 * j + 4]
         ng = term if ng is None else ng + term
     inner = jnp.mean(ng * stream, axis=-1, keepdims=True)
     embed_out_ref[...] = scale * (ng - stream * (scale * scale * inner))
-    bt_ref[...] = mm_nt(msel_ref[...], bt)
+    bt_ref[...] = mm_nt(digit_rows(), bt)[4:8]
     conv0_ref[...] = mm(spread_ref[...], g16)
-    point0_ref[...] = jnp.transpose(mm(bt, act0_ref[...]))
+    point0_ref[...] = mm(bt, act0_ref[...])
 
 
 def finish_kernel(total_ref, got_ref, conv0_ref, point0_ref, conv_ref, point_ref):
@@ -413,19 +510,21 @@
     second = jnp.where(x == 0, got, own)
     conv_ref[1] = first[:crow]
     conv_ref[2] = second[:crow]
-    point_ref[1] = jnp.transpose(first[crow:])
-    point_ref[2] = jnp.transpose(second[crow:])
-
-
-def call(kernel, outs, *args, scratch=(), limit=32, flops=0, name=None):
+    point_ref[1] = first[crow:]
+    point_ref[2] = second[crow:]
+
+
+def call(kernel, outs, *args, far=(), scratch=(), flops=0, name=None):
     moved = sum(v.size * v.dtype.itemsize for v in list(args) + list(outs))
     return pl.pallas_call(
         kernel,
         out_shape=outs,
-        in_specs=[pl.BlockSpec(memory_space=pltpu.VMEM)] * len(args),
+        in_specs=[
+            pl.BlockSpec(memory_space=pl.ANY if i in far else pltpu.VMEM) for i in range(len(args))
+        ],
         out_specs=[pl.BlockSpec(memory_space=pltpu.VMEM)] * len(outs),
         scratch_shapes=list(scratch),
-        compiler_params=pltpu.CompilerParams(vmem_limit_bytes=limit * 1024 * 1024),
+        compiler_params=pltpu.CompilerParams(vmem_limit_bytes=(LIMIT if far else 24) * 1024 * 1024),
         cost_estimate=pl.CostEstimate(flops=flops, bytes_accessed=moved, transcendentals=0),
         name=name,
     )(*args)
@@ -441,62 +540,50 @@
     rows = 2 * rb
     crow, prow = 3 * width // n, width // n
     part = crow + prow
-    w = [conv_weight[i] for i in range(3)]
-    p = [point_weight[i] for i in range(3)]
     shape = jax.ShapeDtypeStruct
 
-    gathered = lax.all_to_all(jnp.broadcast_to(bases, (n, rb)), "seq", 0, 0, tiled=True)
     own = cotangent[0]
     far = lax.ppermute(own, "seq", [(s, (s + STRIDE) % n) for s in range(n)])
-    cot = jnp.where(zh == 0, jnp.concatenate([own, far]), jnp.concatenate([far, own]))
-
-    sel = selectors()
-    act0, slope0, stab, sparts, ntab, u = call(
+    (copies,) = call(spread_kernel, [shape((n, 1, rb), jnp.int32)], bases, name="spread")
+    gathered = lax.all_to_all(copies, "seq", 0, 0, tiled=True)
+
+    taps = pltpu.VMEM((3 * width, mid), BF16)
+    act0, table = call(
         table_kernel,
-        [
-            shape((CLASSES, mid), BF16),
-            shape((CLASSES, mid), F32),
-            shape((CLASSES, width), F32),
-            shape((2 * CLASSES, width), BF16),
-            shape((CLASSES, width), BF16),
-            shape((6 * CLASSES, mid), BF16),
-        ],
-        embed, w[0], w[1], p[0], jnp.asarray(np.stack(sel), BF16),
+        [shape((CLASSES, mid), BF16), shape((CLASSES, width + 4 * mid), F32)],
+        embed, conv_weight, point_weight,
+        far=(1, 2),
+        scratch=[taps, taps, pltpu.VMEM((mid, width), BF16), pltpu.SemaphoreType.DMA((7,))],
         flops=4 * CLASSES * 3 * width * mid,
         name="tables",
     )
-
-    cls = classes(gathered, rb // 8)
-    rowidx = jnp.concatenate(
-        [
-            jnp.concatenate(
-                [lax.dynamic_slice(cls, (a * STRIDE + r + 2 * j, 0), (1, rb)) for a in range(2)],
-                axis=1,
-            )
-            for j in range(3)
-        ]
-    )
-    selt = np.concatenate([v.T for v in sel] + [np.zeros((4, CLASSES))])
     total_rows = STRIDE // 2 * (2 * part + 16) + 16
     features, mine, other = call(
         lambda *refs: main_kernel(crow, prow, *refs),
         [shape((rb, width), F32), shape((total_rows, mid), F32), shape((total_rows, mid), BF16)],
-        rowidx, rowidx.T, cot, w[1], w[2], p[0], p[1], p[2],
-        act0, slope0, stab, sparts, ntab, u, jnp.asarray(selt, BF16),
+        gathered, own, far, conv_weight, point_weight, table,
+        far=(3, 4),
         scratch=[
+            pltpu.VMEM((rows, 3 * CLASSES), BF16),
             pltpu.VMEM((rows, width), F32),
             pltpu.VMEM((rows, width), BF16),
             pltpu.VMEM((rows, mid), BF16),
             pltpu.VMEM((rows, mid), BF16),
             pltpu.VMEM((rows, mid), F32),
             pltpu.VMEM((rows, mid), F32),
+            pltpu.VMEM((rows, width), BF16),
             pltpu.VMEM((rows, mid), BF16),
             pltpu.VMEM((rows, width), BF16),
             pltpu.VMEM((2, STRIDE * crow, mid), F32),
             pltpu.VMEM((2, STRIDE * prow, mid), F32),
             pltpu.VMEM((width, CLASSES), F32),
+            pltpu.VMEM((CLASSES, width), BF16),
+            taps,
+            taps,
+            pltpu.VMEM((3, mid, width), BF16),
+            pltpu.SemaphoreType.DMA((9,)),
         ],
-        flops=8 * rows * 3 * width * mid,
+        flops=9 * rows * 3 * width * mid,
         name="tower",
     )
 
@@ -534,21 +621,23 @@
         small_kernel,
         [
             shape((crow, mid), F32),
-            shape((mid, prow), F32),
+            shape((prow, mid), F32),
             shape((4, width), F32),
             shape((4, prow), F32),
         ],
-        rest, embed, w[0], act0, jnp.asarray(sel[1].T, BF16), spread,
+        rest, embed, conv_weight, act0, spread,
+        far=(2,),
+        scratch=[taps, pltpu.SemaphoreType.DMA((3,))],
         name="layer0",
     )
     embed_grad = bt + lax.dynamic_slice_in_dim(embed_full, k * prow, prow, axis=1)
     conv_grad, point_grad = call(
         finish_kernel,
-        [shape((3, crow, mid), F32), shape((3, mid, prow), F32)],
+        [shape((3, crow, mid), F32), shape((3, prow, mid), F32)],
         total, swapped, conv0, point0,
         name="finish",
     )
-    return features[None], conv_grad, point_grad, embed_grad
+    return features[None], conv_grad, point_grad.transpose(0, 2, 1), embed_grad
 
 
 def solution(mesh):

time: 81.1 us -> 61.3 us (0.76)
  local copies, waits for them, and re-layouts: 25.9 us -> 3.19 us
  Pallas kernels: 12.4 us -> 17.9 us
  waiting for transfers between devices: 15.4 us -> 19.5 us
  starting transfers between devices: 22.5 us -> 18.8 us
  other arithmetic: 3.31 us -> 0.97 us
    unnamed x51 -> x11, local copies, waits for them, and re-layouts: 18.1 us -> 3.19 us
    pallas_call x6 -> x7, Pallas kernels: 12.4 us -> 17.9 us  [call(): pl.pallas_call(kernel, out_shape=outs, in_specs=[pl.BlockSpec(memory_spac...]
    squeeze x2 -> x0, local copies, waits for them, and re-layouts: 5.45 us -> none  [the longest x1 4.31 us: on_device(): w = [conv_weight[i] for i in range(3)]]
    all_to_all x1, waiting for transfers between devices: 0.01 us -> 4.39 us  [on_device(): gathered = lax.all_to_all(copies, 'seq', 0, 0, tiled=True)]
    all_to_all x1, starting transfers between devices: 7.44 us -> 3.91 us  [on_device(): gathered = lax.all_to_all(copies, 'seq', 0, 0, tiled=True)]
    ppermute x7, starting transfers between devices: 10.4 us -> 8.77 us  [on_device(): arrived.append(lax.ppermute(pieces[mask], ('seq', 'dp'), route))]
    select_n x1 -> x0, other arithmetic: 1.45 us -> none  [on_device(): jnp.where(zh == 0, jnp.concatenate([own, far]), jnp.concatenate([far, own]))]
    ppermute x1, waiting for transfers between devices: 1.95 us -> 0.62 us  [on_device(): swapped = lax.ppermute(send, 'dp', [(d, d ^ 1) for d in range(dp)])]
  transfers between devices with their start and end apart: 11 -> 11, of which waited for: 7 -> 8; matrix products, arithmetic and copies ran while one was open for 11% -> 2% of each run, Pallas kernels for 3% -> 10%
where the time goes in v3:
time: 61.3 us; the launch traced here: 61 us
  waiting for transfers between devices  19.5 us (32%)
  starting transfers between devices  18.8 us (31%)
  Pallas kernels  17.9 us (29%)
  local copies, waits for them, and re-layouts  3.19 us (5%)
  other arithmetic  0.97 us (2%)
  between operations  0.7 us (1%)
    pallas_call x7, Pallas kernels, call(): pl.pallas_call(kernel, out_shape=outs, in_specs=[pl.BlockSpec(memory_spac...  17.9 us
    ppermute x7, waiting for transfers between devices, on_device(): arrived.append(lax.ppermute(pieces[mask], ('seq', 'dp'), route))  11.6 us
    ppermute x7, starting transfers between devices, on_device(): arrived.append(lax.ppermute(pieces[mask], ('seq', 'dp'), route))  8.77 us
    all_to_all x1, waiting for transfers between devices, on_device(): gathered = lax.all_to_all(copies, 'seq', 0, 0, tiled=True)  4.39 us
    ppermute x1, starting transfers between devices, on_device(): far = lax.ppermute(own, 'seq', [(s, (s + STRIDE) % n) for s in range(n)])  4.1 us
    all_to_all x1, starting transfers between devices, on_device(): gathered = lax.all_to_all(copies, 'seq', 0, 0, tiled=True)  3.91 us
    unnamed x11, local copies, waits for them, and re-layouts  3.19 us
    ppermute x1, waiting for transfers between devices, on_device(): got = lax.ppermute(other, 'seq', [(s, s ^ 1) for s in range(n)])  2.91 us
  transfers between devices with their start and end apart: 11, of which 8 were waited for; matrix products, arithmetic and copies ran while one was open for 2% of the time, Pallas kernels for 10%

profile of v3, /device:TPU:0, one launch (start us, length us, event | category | flops | bytes accessed | tf_op | source)
XLA Modules:
  0.0 61.0 jit_solution(9233909680398668131)
XLA Ops:
  0.6 4.1 %collective-permute-start = (bf16[176,768]{1,0:T(8,128)(2,1)}, bf16[176,768]{1,0:T(8,128)(2,1)S(1)}, u32[]{:S(2)}, u32[]{:S(2)}) collective-permute-start(bf16[176,768]{1,0:T(8,128)(2,1)} %bitcast.5), channel_id=1, source_target_pairs={{0,16},{2,18},{4,20},{6,22},{8,24},{10,26},{12,28},{14,30},{16,0},... | collective-permute-start | bytes 811016 | tf_op jit(solution)/shard_map/ppermute | solution.py:546
  4.7 0.0 copy-start.3
  4.7 0.7 %copy-done.3 = s32[1,176]{1,0:T(1,128)S(1)} copy-done((s32[1,176]{1,0:T(1,128)S(1)}, s32[1,176]{1,0:T(1,128)}, u32[]{:S(2)}) %copy-start.3) | copy-done | bytes 728
  5.4 0.6 spread.1
  6.0 3.9 %all-to-all-start = ((s32[16,1,176]{2,1,0:T(1,128)}), s32[16,1,176]{2,1,0:T(1,128)S(1)}, u32[]{:S(2)}, u32[]{:S(2)}) async-start(s32[16,1,176]{2,1,0:T(1,128)} %spread.1), calls=%async_computation | async-start | bytes 32768 | tf_op jit(solution)/shard_map/all_to_all | solution.py:548
  9.9 0.0 copy-start.1
  10.0 0.7 %copy-done.1 = bf16[4,768]{1,0:T(4,128)(2,1)S(1)} copy-done((bf16[4,768]{1,0:T(4,128)(2,1)S(1)}, bf16[4,768]{1,0:T(4,128)(2,1)}, u32[]{:S(2)}) %copy-start.1) | copy-done | bytes 6168
  10.6 0.0 copy-start.4
  10.6 3.5 %tables.1 = (bf16[128,384]{1,0:T(8,128)(2,1)S(1)}, f32[128,2304]{1,0:T(8,128)S(1)}) custom-call(bf16[4,768]{1,0:T(4,128)(2,1)S(1)} %copy-done.1, bf16[3,2304,384]{2,1,0:T(8,128)(2,1)} %w_ref.3, bf16[3,384,768]{2,1,0:T(8,128)(2,1)} %refs_4_.1), custom_call_target="tpu_custom_call" | custom-call | flops 452984832 | bytes 8361984 | tf_op jit(solution)/shard_map/tables/pallas_call | solution.py:519
  14.1 4.4 %all-to-all-done.refs_0_ = s32[16,1,176]{2,1,0:T(1,128)S(1)} async-done(((s32[16,1,176]{2,1,0:T(1,128)}), s32[16,1,176]{2,1,0:T(1,128)S(1)}, u32[]{:S(2)}, u32[]{:S(2)}) %all-to-all-start) | async-done | bytes 11296 | tf_op jit(solution)/shard_map/all_to_all | solution.py:548
  18.5 0.0 collective-permute-done.refs_2_
  18.5 0.0 copy-done.4
  18.5 0.0 copy-start.2
  18.5 10.3 %tower.1 = (f32[176,768]{1,0:T(8,128)}, f32[1616,384]{1,0:T(8,128)}, bf16[1616,384]{1,0:T(8,128)(2,1)}) custom-call(s32[16,1,176]{2,1,0:T(1,128)S(1)} %all-to-all-done.refs_0_, bf16[176,768]{1,0:T(8,128)(2,1)S(1)} %bitcast.6, bf16[176,768]{1,0:T(8,128)(2,1)S(1)} %collective-permute-done.refs_2_, bf16[3,2304,384]{2,1,0:T(8,128)(2,1)} %w_ref.3, ...), custom_call_target="tpu_custom_call" | custom-call | flops 2802843648 | bytes 13073408 | tf_op jit(solution)/shard_map/tower/pallas_call | solution.py:519
  28.8 0.2 collective-permute-start.1
  29.0 0.0 copy-done.2
  29.0 0.1 fusion.8
  29.1 2.9 %collective-permute-done.1.refs_1_ = bf16[1616,384]{1,0:T(8,128)(2,1)S(1)} collective-permute-done((bf16[1616,384]{1,0:T(8,128)(2,1)}, bf16[1616,384]{1,0:T(8,128)(2,1)S(1)}, u32[]{:S(2)}, u32[]{:S(2)}) %collective-permute-start.1) | collective-permute-done | bytes 1241120 | tf_op jit(solution)/shard_map/ppermute | solution.py:590
  32.0 0.0 copy-start
  32.0 1.7 %copy-done = f32[1616,384]{1,0:T(8,128)S(1)} copy-done((f32[1616,384]{1,0:T(8,128)S(1)}, f32[1616,384]{1,0:T(8,128)}, u32[]{:S(2)}) %copy-start) | copy-done | bytes 2482200
  33.7 0.3 messages.1
  34.0 1.7 %collective-permute-start.2 = (bf16[224,384]{1,0:T(8,128)(2,1)S(1)}, bf16[224,384]{1,0:T(8,128)(2,1)S(1)}, u32[]{:S(2)}, u32[]{:S(2)}) collective-permute-start(bf16[224,384]{1,0:T(8,128)(2,1)S(1)} %get-tuple-element.31), channel_id=1, source_target_pairs={{0,13},{1,12},{2,15},{3,14},{4,9},{5,8},{6,11},{7,10},{8,5},{9,4},... | collective-permute-start | bytes 516104 | tf_op jit(solution)/shard_map/ppermute | solution.py:605
  35.7 2.2 %collective-permute-start.3 = (bf16[224,384]{1,0:T(8,128)(2,1)S(1)}, bf16[224,384]{1,0:T(8,128)(2,1)S(1)}, u32[]{:S(2)}, u32[]{:S(2)}) collective-permute-start(bf16[224,384]{1,0:T(8,128)(2,1)S(1)} %get-tuple-element.32), channel_id=1, source_target_pairs={{0,12},{1,13},{2,14},{3,15},{4,8},{5,9},{6,10},{7,11},{8,4},{9,5},... | collective-permute-start | bytes 516104 | tf_op jit(solution)/shard_map/ppermute | solution.py:605
  37.9 0.6 collective-permute-start.4
  38.5 1.4 %collective-permute-start.5 = (bf16[224,384]{1,0:T(8,128)(2,1)S(1)}, bf16[224,384]{1,0:T(8,128)(2,1)S(1)}, u32[]{:S(2)}, u32[]{:S(2)}) collective-permute-start(bf16[224,384]{1,0:T(8,128)(2,1)S(1)} %get-tuple-element.34), channel_id=1, source_target_pairs={{0,8},{1,9},{2,10},{3,11},{4,12},{5,13},{6,14},{7,15},{8,0},{9,1},... | collective-permute-start | bytes 516104 | tf_op jit(solution)/shard_map/ppermute | solution.py:605
  39.9 1.5 %collective-permute-start.6 = (bf16[224,384]{1,0:T(8,128)(2,1)S(1)}, bf16[224,384]{1,0:T(8,128)(2,1)S(1)}, u32[]{:S(2)}, u32[]{:S(2)}) collective-permute-start(bf16[224,384]{1,0:T(8,128)(2,1)S(1)} %get-tuple-element.35), channel_id=1, source_target_pairs={{0,5},{1,4},{2,7},{3,6},{4,1},{5,0},{6,3},{7,2},{8,13},{9,12},{10,... | collective-permute-start | bytes 516104 | tf_op jit(solution)/shard_map/ppermute | solution.py:605
  41.5 1.9 %collective-permute-done.2.refs_0_ = bf16[224,384]{1,0:T(8,128)(2,1)S(1)} collective-permute-done((bf16[224,384]{1,0:T(8,128)(2,1)S(1)}, bf16[224,384]{1,0:T(8,128)(2,1)S(1)}, u32[]{:S(2)}, u32[]{:S(2)}) %collective-permute-start.2) | collective-permute-done | bytes 172064 | tf_op jit(solution)/shard_map/ppermute | solution.py:605
  43.4 0.6 %collective-permute-start.7 = (bf16[224,384]{1,0:T(8,128)(2,1)S(1)}, bf16[224,384]{1,0:T(8,128)(2,1)S(1)}, u32[]{:S(2)}, u32[]{:S(2)}) collective-permute-start(bf16[224,384]{1,0:T(8,128)(2,1)S(1)} %get-tuple-element.36), channel_id=1, source_target_pairs={{0,4},{1,5},{2,6},{3,7},{4,0},{5,1},{6,2},{7,3},{8,12},{9,13},{10,... | collective-permute-start | bytes 516104 | tf_op jit(solution)/shard_map/ppermute | solution.py:605
  44.0 5.2 %collective-permute-done.3.refs_1_ = bf16[224,384]{1,0:T(8,128)(2,1)S(1)} collective-permute-done((bf16[224,384]{1,0:T(8,128)(2,1)S(1)}, bf16[224,384]{1,0:T(8,128)(2,1)S(1)}, u32[]{:S(2)}, u32[]{:S(2)}) %collective-permute-start.3) | collective-permute-done | bytes 172064 | tf_op jit(solution)/shard_map/ppermute | solution.py:605
  49.3 0.7 %collective-permute-start.8 = (bf16[224,384]{1,0:T(8,128)(2,1)S(1)}, bf16[224,384]{1,0:T(8,128)(2,1)S(1)}, u32[]{:S(2)}, u32[]{:S(2)}) collective-permute-start(bf16[224,384]{1,0:T(8,128)(2,1)S(1)} %get-tuple-element.37), channel_id=1, source_target_pairs={{0,1},{1,0},{2,3},{3,2},{4,5},{5,4},{6,7},{7,6},{8,9},{9,8},{10,11... | collective-permute-start | bytes 516104 | tf_op jit(solution)/shard_map/ppermute | solution.py:605
  50.0 0.1 fusion.9
  50.0 0.1 fusion.11
  50.1 0.1 copy.13
  50.3 1.0 %collective-permute-done.4.refs_2_ = bf16[224,384]{1,0:T(8,128)(2,1)S(1)} collective-permute-done((bf16[224,384]{1,0:T(8,128)(2,1)S(1)}, bf16[224,384]{1,0:T(8,128)(2,1)S(1)}, u32[]{:S(2)}, u32[]{:S(2)}) %collective-permute-start.4) | collective-permute-done | bytes 172064 | tf_op jit(solution)/shard_map/ppermute | solution.py:605
  51.3 2.7 %collective-permute-done.5.refs_3_ = bf16[224,384]{1,0:T(8,128)(2,1)S(1)} collective-permute-done((bf16[224,384]{1,0:T(8,128)(2,1)S(1)}, bf16[224,384]{1,0:T(8,128)(2,1)S(1)}, u32[]{:S(2)}, u32[]{:S(2)}) %collective-permute-start.5) | collective-permute-done | bytes 172064 | tf_op jit(solution)/shard_map/ppermute | solution.py:605
  54.0 0.0 collective-permute-done.6.refs_4_
  54.0 0.0 collective-permute-done.7.refs_5_
  54.0 0.6 %collective-permute-done.8.refs_6_ = bf16[224,384]{1,0:T(8,128)(2,1)S(1)} collective-permute-done((bf16[224,384]{1,0:T(8,128)(2,1)S(1)}, bf16[224,384]{1,0:T(8,128)(2,1)S(1)}, u32[]{:S(2)}, u32[]{:S(2)}) %collective-permute-start.8) | collective-permute-done | bytes 172064 | tf_op jit(solution)/shard_map/ppermute | solution.py:605
  54.7 0.2 sums.1
  54.9 1.8 %collective-permute-start.9 = (bf16[192,384]{1,0:T(8,128)(2,1)S(1)}, bf16[192,384]{1,0:T(8,128)(2,1)S(1)}, u32[]{:S(2)}, u32[]{:S(2)}) collective-permute-start(bf16[192,384]{1,0:T(8,128)(2,1)S(1)} %get-tuple-element.39), channel_id=1, source_target_pairs={{0,1},{1,0},{2,3},{3,2},{4,5},{5,4},{6,7},{7,6},{8,9},{9,8},{10,11... | collective-permute-start | bytes 442376 | tf_op jit(solution)/shard_map/ppermute | solution.py:612
  56.7 2.1 %layer0.1 = (f32[144,384]{1,0:T(8,128)S(1)}, f32[48,384]{1,0:T(8,128)S(1)}, f32[4,768]{1,0:T(4,128)S(1)}, f32[4,48]{1,0:T(4,128)S(1)}) custom-call(f32[32,384]{1,0:T(8,128)S(1)} %get-tuple-element.40.rest_ref, bf16[4,768]{1,0:T(4,128)(2,1)S(1)} %copy-done.2, bf16[3,2304,384]{2,1,0:T(8,128)(2,1)} %w_ref.3, bf16[128,384]{1,0:T(8,128)(2,1)S(1)} %get-tuple-element.41.act0_ref, ...), custom_call_target="tpu_custom_call" | custom-call | bytes 5774592 | tf_op jit(solution)/shard_map/layer0/pallas_call | solution.py:519
  58.8 0.7 %dynamic-slice_add_fusion = f32[4,48]{1,0:T(4,128)} fusion(f32[4,48]{1,0:T(4,128)S(1)} %get-tuple-element.46, f32[4,768]{1,0:T(4,128)S(1)} %get-tuple-element.47, s32[]{:T(128)S(6)} %select_n.7), kind=kLoop, calls=%fused_computation.18 | loop fusion | flops 192 | bytes 2308 | tf_op jit(solution)/shard_map/add | solution.py:633
  59.5 0.6 %collective-permute-done.9.got_ref = bf16[192,384]{1,0:T(8,128)(2,1)S(1)} collective-permute-done((bf16[192,384]{1,0:T(8,128)(2,1)S(1)}, bf16[192,384]{1,0:T(8,128)(2,1)S(1)}, u32[]{:S(2)}, u32[]{:S(2)}) %collective-permute-start.9) | collective-permute-done | bytes 147488 | tf_op jit(solution)/shard_map/ppermute | solution.py:612
  60.1 1.0 %finish.1 = (f32[3,144,384]{2,1,0:T(8,128)}, f32[3,48,384]{2,1,0:T(8,128)}) custom-call(f32[192,384]{1,0:T(8,128)S(1)} %get-tuple-element.38.total_ref, bf16[192,384]{1,0:T(8,128)(2,1)S(1)} %collective-permute-done.9.got_ref, f32[144,384]{1,0:T(8,128)S(1)} %get-tuple-element.42.conv0_ref, f32[48,384]{1,0:T(8,128)S(1)} %get-tuple-element.43.point0_ref), custom_call_target="tpu_custom_call" | custom-call | bytes 1622016 | tf_op jit(solution)/shard_map/finish/pallas_call | solution.py:519
  (1 shorter events, 0.0 us)
Async XLA Ops:
  0.6 17.9 %collective-permute-start = (bf16[176,768]{1,0:T(8,128)(2,1)}, bf16[176,768]{1,0:T(8,128)(2,1)S(1)}, u32[]{:S(2)}, u32[]{:S(2)}) collective-permute-start(bf16[176,768]{1,0:T(8,128)(2,1)} %bitcast.5), channel_id=1, source_target_pairs={{0,16},{2,18},{4,20},{6,22},{8,24},{10,26},{12,28},{14,30},{16,0},... | collective-permute-start | bytes 811016 | tf_op jit(solution)/shard_map/ppermute | solution.py:546
  4.7 0.7 %copy-start.3 = (s32[1,176]{1,0:T(1,128)S(1)}, s32[1,176]{1,0:T(1,128)}, u32[]{:S(2)}) copy-start(s32[1,176]{1,0:T(1,128)} %bases_ref.1) | copy-start | bytes 2116
  6.0 12.5 %all-to-all-start = ((s32[16,1,176]{2,1,0:T(1,128)}), s32[16,1,176]{2,1,0:T(1,128)S(1)}, u32[]{:S(2)}, u32[]{:S(2)}) async-start(s32[16,1,176]{2,1,0:T(1,128)} %spread.1), calls=%async_computation | async-start | bytes 32768 | tf_op jit(solution)/shard_map/all_to_all | solution.py:548
  9.9 0.7 %copy-start.1 = (bf16[4,768]{1,0:T(4,128)(2,1)S(1)}, bf16[4,768]{1,0:T(4,128)(2,1)}, u32[]{:S(2)}) copy-start(bf16[4,768]{1,0:T(4,128)(2,1)} %embed_ref.3) | copy-start | bytes 18436
  10.6 7.9 %copy-start.4 = (bf16[1,176,768]{2,1,0:T(8,128)(2,1)S(1)}, bf16[1,176,768]{2,1,0:T(8,128)(2,1)}, u32[]{:S(2)}) copy-start(bf16[1,176,768]{2,1,0:T(8,128)(2,1)} %param.9) | copy-start | bytes 811012
  18.5 10.5 %copy-start.2 = (bf16[4,768]{1,0:T(4,128)(2,1)S(1)}, bf16[4,768]{1,0:T(4,128)(2,1)}, u32[]{:S(2)}) copy-start(bf16[4,768]{1,0:T(4,128)(2,1)} %embed_ref.3) | copy-start | bytes 18436
  28.8 3.2 %collective-permute-start.1 = (bf16[1616,384]{1,0:T(8,128)(2,1)}, bf16[1616,384]{1,0:T(8,128)(2,1)S(1)}, u32[]{:S(2)}, u32[]{:S(2)}) collective-permute-start(bf16[1616,384]{1,0:T(8,128)(2,1)} %get-tuple-element.29), channel_id=1, source_target_pairs={{0,2},{2,0},{4,6},{6,4},{8,10},{10,8},{12,14},{14,12},{16,18},{18,... | collective-permute-start | bytes 3723272 | tf_op jit(solution)/shard_map/ppermute | solution.py:590
  32.0 1.7 %copy-start = (f32[1616,384]{1,0:T(8,128)S(1)}, f32[1616,384]{1,0:T(8,128)}, u32[]{:S(2)}) copy-start(f32[1616,384]{1,0:T(8,128)} %get-tuple-element.28.refs_0_) | copy-start | bytes 7446532
  34.0 9.4 %collective-permute-start.2 = (bf16[224,384]{1,0:T(8,128)(2,1)S(1)}, bf16[224,384]{1,0:T(8,128)(2,1)S(1)}, u32[]{:S(2)}, u32[]{:S(2)}) collective-permute-start(bf16[224,384]{1,0:T(8,128)(2,1)S(1)} %get-tuple-element.31), channel_id=1, source_target_pairs={{0,13},{1,12},{2,15},{3,14},{4,9},{5,8},{6,11},{7,10},{8,5},{9,4},... | collective-permute-start | bytes 516104 | tf_op jit(solution)/shard_map/ppermute | solution.py:605
  35.7 13.5 %collective-permute-start.3 = (bf16[224,384]{1,0:T(8,128)(2,1)S(1)}, bf16[224,384]{1,0:T(8,128)(2,1)S(1)}, u32[]{:S(2)}, u32[]{:S(2)}) collective-permute-start(bf16[224,384]{1,0:T(8,128)(2,1)S(1)} %get-tuple-element.32), channel_id=1, source_target_pairs={{0,12},{1,13},{2,14},{3,15},{4,8},{5,9},{6,10},{7,11},{8,4},{9,5},... | collective-permute-start | bytes 516104 | tf_op jit(solution)/shard_map/ppermute | solution.py:605
  37.9 13.4 %collective-permute-start.4 = (bf16[224,384]{1,0:T(8,128)(2,1)S(1)}, bf16[224,384]{1,0:T(8,128)(2,1)S(1)}, u32[]{:S(2)}, u32[]{:S(2)}) collective-permute-start(bf16[224,384]{1,0:T(8,128)(2,1)S(1)} %get-tuple-element.33), channel_id=1, source_target_pairs={{0,9},{1,8},{2,11},{3,10},{4,13},{5,12},{6,15},{7,14},{8,1},{9,0},... | collective-permute-start | bytes 516104 | tf_op jit(solution)/shard_map/ppermute | solution.py:605
  38.5 15.5 %collective-permute-start.5 = (bf16[224,384]{1,0:T(8,128)(2,1)S(1)}, bf16[224,384]{1,0:T(8,128)(2,1)S(1)}, u32[]{:S(2)}, u32[]{:S(2)}) collective-permute-start(bf16[224,384]{1,0:T(8,128)(2,1)S(1)} %get-tuple-element.34), channel_id=1, source_target_pairs={{0,8},{1,9},{2,10},{3,11},{4,12},{5,13},{6,14},{7,15},{8,0},{9,1},... | collective-permute-start | bytes 516104 | tf_op jit(solution)/shard_map/ppermute | solution.py:605
  39.9 14.1 %collective-permute-start.6 = (bf16[224,384]{1,0:T(8,128)(2,1)S(1)}, bf16[224,384]{1,0:T(8,128)(2,1)S(1)}, u32[]{:S(2)}, u32[]{:S(2)}) collective-permute-start(bf16[224,384]{1,0:T(8,128)(2,1)S(1)} %get-tuple-element.35), channel_id=1, source_target_pairs={{0,5},{1,4},{2,7},{3,6},{4,1},{5,0},{6,3},{7,2},{8,13},{9,12},{10,... | collective-permute-start | bytes 516104 | tf_op jit(solution)/shard_map/ppermute | solution.py:605
  43.4 10.6 %collective-permute-start.7 = (bf16[224,384]{1,0:T(8,128)(2,1)S(1)}, bf16[224,384]{1,0:T(8,128)(2,1)S(1)}, u32[]{:S(2)}, u32[]{:S(2)}) collective-permute-start(bf16[224,384]{1,0:T(8,128)(2,1)S(1)} %get-tuple-element.36), channel_id=1, source_target_pairs={{0,4},{1,5},{2,6},{3,7},{4,0},{5,1},{6,2},{7,3},{8,12},{9,13},{10,... | collective-permute-start | bytes 516104 | tf_op jit(solution)/shard_map/ppermute | solution.py:605
  49.3 5.4 %collective-permute-start.8 = (bf16[224,384]{1,0:T(8,128)(2,1)S(1)}, bf16[224,384]{1,0:T(8,128)(2,1)S(1)}, u32[]{:S(2)}, u32[]{:S(2)}) collective-permute-start(bf16[224,384]{1,0:T(8,128)(2,1)S(1)} %get-tuple-element.37), channel_id=1, source_target_pairs={{0,1},{1,0},{2,3},{3,2},{4,5},{5,4},{6,7},{7,6},{8,9},{9,8},{10,11... | collective-permute-start | bytes 516104 | tf_op jit(solution)/shard_map/ppermute | solution.py:605
  54.9 5.2 %collective-permute-start.9 = (bf16[192,384]{1,0:T(8,128)(2,1)S(1)}, bf16[192,384]{1,0:T(8,128)(2,1)S(1)}, u32[]{:S(2)}, u32[]{:S(2)}) collective-permute-start(bf16[192,384]{1,0:T(8,128)(2,1)S(1)} %get-tuple-element.39), channel_id=1, source_target_pairs={{0,1},{1,0},{2,3},{3,2},{4,5},{5,4},{6,7},{7,6},{8,9},{9,8},{10,11... | collective-permute-start | bytes 442376 | tf_op jit(solution)/shard_map/ppermute | solution.py:612

commit v4 on v3

--- a/solution.py
+++ b/solution.py
@@ -12,7 +12,6 @@
 F32 = jnp.float32
 CLASSES = 128
 STRIDE = 8
-LIMIT = 52
 
 
 def gelu_pair(v):
@@ -313,7 +312,7 @@
     crow, prow, bases_ref, own_ref, far_ref, w_ref, p_ref, table_ref,
     features_ref, mine_ref, other_ref,
     hot_ref, stream_ref, normed_ref, act1_ref, act2_ref, slope1_ref, slope2_ref,
-    cot_ref, grad_ref, back_ref, conv_ref, point_ref, bt_ref, ntab_ref, w1_ref, w2_ref, pt_ref, sems,
+    cot_ref, grad_ref, back_ref, conv_ref, point_ref, bt_ref, ntab_ref, w1_ref, w2_ref, pt_ref, sent_ref, sems,
 ):
     n, _, rb = bases_ref.shape
     rows, width = stream_ref.shape
@@ -389,7 +388,8 @@
     act2_ref[...] = act2.astype(BF16)
     slope2_ref[...] = slope2
     copy_p2.wait()
-    features_ref[...] = stream_ref[place, :] + mm(act2_ref[place, :], pt_ref[2])
+    sent_ref[...] = stream_ref[place, :] + mm(act2_ref[place, :], pt_ref[2])
+    copy_features = fetch(sent_ref, features_ref, sems.at[9])
 
     cot_ref[place, :] = own_ref[...]
     cot_ref[far, :] = far_ref[...]
@@ -450,6 +450,7 @@
                 target[at : at + 16, q * CLASSES : (q + 1) * CLASSES] = bt_ref[brows, :].astype(target.dtype)
         at = STRIDE // 2 * step
         target[at : at + 16, :] = g.astype(target.dtype)
+    copy_features.wait()
 
 
 def message_kernel(part, mine_ref, other_ref, *out_refs):
@@ -514,7 +515,7 @@
     point_ref[2] = second[crow:]
 
 
-def call(kernel, outs, *args, far=(), scratch=(), flops=0, name=None):
+def call(kernel, outs, *args, far=(), away=(), scratch=(), limit=24, flops=0, name=None):
     moved = sum(v.size * v.dtype.itemsize for v in list(args) + list(outs))
     return pl.pallas_call(
         kernel,
@@ -522,9 +523,11 @@
         in_specs=[
             pl.BlockSpec(memory_space=pl.ANY if i in far else pltpu.VMEM) for i in range(len(args))
         ],
-        out_specs=[pl.BlockSpec(memory_space=pltpu.VMEM)] * len(outs),
+        out_specs=[
+            pl.BlockSpec(memory_space=pl.ANY if i in away else pltpu.VMEM) for i in range(len(outs))
+        ],
         scratch_shapes=list(scratch),
-        compiler_params=pltpu.CompilerParams(vmem_limit_bytes=(LIMIT if far else 24) * 1024 * 1024),
+        compiler_params=pltpu.CompilerParams(vmem_limit_bytes=limit * 1024 * 1024),
         cost_estimate=pl.CostEstimate(flops=flops, bytes_accessed=moved, transcendentals=0),
         name=name,
     )(*args)
@@ -554,6 +557,7 @@
         embed, conv_weight, point_weight,
         far=(1, 2),
         scratch=[taps, taps, pltpu.VMEM((mid, width), BF16), pltpu.SemaphoreType.DMA((7,))],
+        limit=52,
         flops=4 * CLASSES * 3 * width * mid,
         name="tables",
     )
@@ -581,8 +585,11 @@
             taps,
             taps,
             pltpu.VMEM((3, mid, width), BF16),
-            pltpu.SemaphoreType.DMA((9,)),
+            pltpu.VMEM((rb, width), F32),
+            pltpu.SemaphoreType.DMA((10,)),
         ],
+        away=(0,),
+        limit=46,
         flops=9 * rows * 3 * width * mid,
         name="tower",
     )
@@ -628,6 +635,7 @@
         rest, embed, conv_weight, act0, spread,
         far=(2,),
         scratch=[taps, pltpu.SemaphoreType.DMA((3,))],
+        limit=52,
         name="layer0",
     )
     embed_grad = bt + lax.dynamic_slice_in_dim(embed_full, k * prow, prow, axis=1)

time: 61.3 us -> 58.9 us (0.961)
  local copies, waits for them, and re-layouts: 3.19 us -> 1.5 us
    unnamed x11, local copies, waits for them, and re-layouts: 3.19 us -> 1.5 us
  transfers between devices with their start and end apart: 11 -> 11, of which waited for: 8 -> 8; matrix products, arithmetic and copies ran while one was open for 2% -> 2% of each run, Pallas kernels for 10% -> 11%
where the time goes in v4:
time: 58.9 us; the launch traced here: 58.6 us
  starting transfers between devices  19 us (32%)
  waiting for transfers between devices  19 us (32%)
  Pallas kernels  17.5 us (30%)
  local copies, waits for them, and re-layouts  1.5 us (3%)
  other arithmetic  0.97 us (2%)
  between operations  0.71 us (1%)
    pallas_call x7, Pallas kernels, call(): pl.pallas_call(kernel, out_shape=outs, in_specs=[pl.BlockSpec(memory_spac...  17.5 us
    ppermute x7, waiting for transfers between devices, on_device(): arrived.append(lax.ppermute(pieces[mask], ('seq', 'dp'), route))  11.5 us
    ppermute x7, starting transfers between devices, on_device(): arrived.append(lax.ppermute(pieces[mask], ('seq', 'dp'), route))  8.88 us
    all_to_all x1, waiting for transfers between devices, on_device(): gathered = lax.all_to_all(copies, 'seq', 0, 0, tiled=True)  4.29 us
    ppermute x1, starting transfers between devices, on_device(): far = lax.ppermute(own, 'seq', [(s, (s + STRIDE) % n) for s in range(n)])  4.1 us
    all_to_all x1, starting transfers between devices, on_device(): gathered = lax.all_to_all(copies, 'seq', 0, 0, tiled=True)  3.91 us
    ppermute x1, waiting for transfers between devices, on_device(): got = lax.ppermute(other, 'seq', [(s, s ^ 1) for s in range(n)])  2.7 us
    ppermute x1, starting transfers between devices, on_device(): swapped = lax.ppermute(send, 'dp', [(d, d ^ 1) for d in range(dp)])  1.88 us
  transfers between devices with their start and end apart: 11, of which 8 were waited for; matrix products, arithmetic and copies ran while one was open for 2% of the time, Pallas kernels for 11%

profile of v4, /device:TPU:0, one launch (start us, length us, event | category | flops | bytes accessed | tf_op | source)
XLA Modules:
  0.0 58.6 jit_solution(4060169646412257843)
XLA Ops:
  0.6 4.1 %collective-permute-start = (bf16[176,768]{1,0:T(8,128)(2,1)}, bf16[176,768]{1,0:T(8,128)(2,1)}, u32[]{:S(2)}, u32[]{:S(2)}) collective-permute-start(bf16[176,768]{1,0:T(8,128)(2,1)} %bitcast.5), channel_id=1, source_target_pairs={{0,16},{2,18},{4,20},{6,22},{8,24},{10,26},{12,28},{14,30},{16,0},... | collective-permute-start | bytes 811016 | tf_op jit(solution)/shard_map/ppermute | solution.py:549
  4.7 0.0 copy-start.3
  4.7 0.7 %copy-done.3 = s32[1,176]{1,0:T(1,128)S(1)} copy-done((s32[1,176]{1,0:T(1,128)S(1)}, s32[1,176]{1,0:T(1,128)}, u32[]{:S(2)}) %copy-start.3) | copy-done | bytes 728
  5.4 0.6 %spread.1 = s32[16,1,176]{2,1,0:T(1,128)} custom-call(s32[1,176]{1,0:T(1,128)S(1)} %copy-done.3), custom_call_target="tpu_custom_call" | custom-call | bytes 11968 | tf_op jit(solution)/shard_map/spread/pallas_call | solution.py:520
  6.0 3.9 %all-to-all-start = ((s32[16,1,176]{2,1,0:T(1,128)}), s32[16,1,176]{2,1,0:T(1,128)S(1)}, u32[]{:S(2)}, u32[]{:S(2)}) async-start(s32[16,1,176]{2,1,0:T(1,128)} %spread.1), calls=%async_computation | async-start | bytes 32768 | tf_op jit(solution)/shard_map/all_to_all | solution.py:551
  9.9 0.0 copy-start.1
  10.0 0.7 %copy-done.1 = bf16[4,768]{1,0:T(4,128)(2,1)S(1)} copy-done((bf16[4,768]{1,0:T(4,128)(2,1)S(1)}, bf16[4,768]{1,0:T(4,128)(2,1)}, u32[]{:S(2)}) %copy-start.1) | copy-done | bytes 6168
  10.6 0.0 copy-start
  10.6 0.0 copy-start.4
  10.6 3.6 %tables.1 = (bf16[128,384]{1,0:T(8,128)(2,1)S(1)}, f32[128,2304]{1,0:T(8,128)S(1)}) custom-call(bf16[4,768]{1,0:T(4,128)(2,1)S(1)} %copy-done.1, bf16[3,2304,384]{2,1,0:T(8,128)(2,1)} %w_ref.3, bf16[3,384,768]{2,1,0:T(8,128)(2,1)} %refs_4_.1), custom_call_target="tpu_custom_call" | custom-call | flops 452984832 | bytes 8361984 | tf_op jit(solution)/shard_map/tables/pallas_call | solution.py:520
  14.2 4.3 %all-to-all-done.refs_0_ = s32[16,1,176]{2,1,0:T(1,128)S(1)} async-done(((s32[16,1,176]{2,1,0:T(1,128)}), s32[16,1,176]{2,1,0:T(1,128)S(1)}, u32[]{:S(2)}, u32[]{:S(2)}) %all-to-all-start) | async-done | bytes 11296 | tf_op jit(solution)/shard_map/all_to_all | solution.py:551
  18.5 0.0 collective-permute-done.refs_2_
  18.5 0.0 copy-done
  18.5 0.0 copy-done.4
  18.5 0.0 copy-start.2
  18.5 9.7 %tower.1 = (f32[176,768]{1,0:T(8,128)}, f32[1616,384]{1,0:T(8,128)S(1)}, bf16[1616,384]{1,0:T(8,128)(2,1)S(1)}) custom-call(s32[16,1,176]{2,1,0:T(1,128)S(1)} %all-to-all-done.refs_0_, bf16[176,768]{1,0:T(8,128)(2,1)S(1)} %bitcast.6, bf16[176,768]{1,0:T(8,128)(2,1)} %collective-permute-done.refs_2_, bf16[3,2304,384]{2,1,0:T(8,128)(2,1)} %w_ref.3, ...), custom_call_target="tpu_custom_call" | custom-call | flops 2802843648 | bytes 13073408 | tf_op jit(solution)/shard_map/tower/pallas_call | solution.py:520
  28.3 0.2 collective-permute-start.1
  28.5 0.0 copy-done.2
  28.5 0.1 fusion.8
  28.6 2.7 %collective-permute-done.1.refs_1_ = bf16[1616,384]{1,0:T(8,128)(2,1)S(1)} collective-permute-done((bf16[1616,384]{1,0:T(8,128)(2,1)S(1)}, bf16[1616,384]{1,0:T(8,128)(2,1)S(1)}, u32[]{:S(2)}, u32[]{:S(2)}) %collective-permute-start.1) | collective-permute-done | bytes 1241120 | tf_op jit(solution)/shard_map/ppermute | solution.py:597
  31.3 0.3 messages.1
  31.6 1.7 %collective-permute-start.2 = (bf16[224,384]{1,0:T(8,128)(2,1)S(1)}, bf16[224,384]{1,0:T(8,128)(2,1)S(1)}, u32[]{:S(2)}, u32[]{:S(2)}) collective-permute-start(bf16[224,384]{1,0:T(8,128)(2,1)S(1)} %get-tuple-element.31), channel_id=1, source_target_pairs={{0,13},{1,12},{2,15},{3,14},{4,9},{5,8},{6,11},{7,10},{8,5},{9,4},... | collective-permute-start | bytes 516104 | tf_op jit(solution)/shard_map/ppermute | solution.py:612
  33.3 2.2 %collective-permute-start.3 = (bf16[224,384]{1,0:T(8,128)(2,1)S(1)}, bf16[224,384]{1,0:T(8,128)(2,1)S(1)}, u32[]{:S(2)}, u32[]{:S(2)}) collective-permute-start(bf16[224,384]{1,0:T(8,128)(2,1)S(1)} %get-tuple-element.32), channel_id=1, source_target_pairs={{0,12},{1,13},{2,14},{3,15},{4,8},{5,9},{6,10},{7,11},{8,4},{9,5},... | collective-permute-start | bytes 516104 | tf_op jit(solution)/shard_map/ppermute | solution.py:612
  35.5 0.6 collective-permute-start.4
  36.1 1.4 %collective-permute-start.5 = (bf16[224,384]{1,0:T(8,128)(2,1)S(1)}, bf16[224,384]{1,0:T(8,128)(2,1)S(1)}, u32[]{:S(2)}, u32[]{:S(2)}) collective-permute-start(bf16[224,384]{1,0:T(8,128)(2,1)S(1)} %get-tuple-element.34), channel_id=1, source_target_pairs={{0,8},{1,9},{2,10},{3,11},{4,12},{5,13},{6,14},{7,15},{8,0},{9,1},... | collective-permute-start | bytes 516104 | tf_op jit(solution)/shard_map/ppermute | solution.py:612
  37.5 1.6 %collective-permute-start.6 = (bf16[224,384]{1,0:T(8,128)(2,1)S(1)}, bf16[224,384]{1,0:T(8,128)(2,1)S(1)}, u32[]{:S(2)}, u32[]{:S(2)}) collective-permute-start(bf16[224,384]{1,0:T(8,128)(2,1)S(1)} %get-tuple-element.35), channel_id=1, source_target_pairs={{0,5},{1,4},{2,7},{3,6},{4,1},{5,0},{6,3},{7,2},{8,13},{9,12},{10,... | collective-permute-start | bytes 516104 | tf_op jit(solution)/shard_map/ppermute | solution.py:612
  39.1 1.9 %collective-permute-done.2.refs_0_ = bf16[224,384]{1,0:T(8,128)(2,1)S(1)} collective-permute-done((bf16[224,384]{1,0:T(8,128)(2,1)S(1)}, bf16[224,384]{1,0:T(8,128)(2,1)S(1)}, u32[]{:S(2)}, u32[]{:S(2)}) %collective-permute-start.2) | collective-permute-done | bytes 172064 | tf_op jit(solution)/shard_map/ppermute | solution.py:612
  41.0 0.7 %collective-permute-start.7 = (bf16[224,384]{1,0:T(8,128)(2,1)S(1)}, bf16[224,384]{1,0:T(8,128)(2,1)S(1)}, u32[]{:S(2)}, u32[]{:S(2)}) collective-permute-start(bf16[224,384]{1,0:T(8,128)(2,1)S(1)} %get-tuple-element.36), channel_id=1, source_target_pairs={{0,4},{1,5},{2,6},{3,7},{4,0},{5,1},{6,2},{7,3},{8,12},{9,13},{10,... | collective-permute-start | bytes 516104 | tf_op jit(solution)/shard_map/ppermute | solution.py:612
  41.7 5.2 %collective-permute-done.3.refs_1_ = bf16[224,384]{1,0:T(8,128)(2,1)S(1)} collective-permute-done((bf16[224,384]{1,0:T(8,128)(2,1)S(1)}, bf16[224,384]{1,0:T(8,128)(2,1)S(1)}, u32[]{:S(2)}, u32[]{:S(2)}) %collective-permute-start.3) | collective-permute-done | bytes 172064 | tf_op jit(solution)/shard_map/ppermute | solution.py:612
  46.8 0.7 %collective-permute-start.8 = (bf16[224,384]{1,0:T(8,128)(2,1)S(1)}, bf16[224,384]{1,0:T(8,128)(2,1)S(1)}, u32[]{:S(2)}, u32[]{:S(2)}) collective-permute-start(bf16[224,384]{1,0:T(8,128)(2,1)S(1)} %get-tuple-element.37), channel_id=1, source_target_pairs={{0,1},{1,0},{2,3},{3,2},{4,5},{5,4},{6,7},{7,6},{8,9},{9,8},{10,11... | collective-permute-start | bytes 516104 | tf_op jit(solution)/shard_map/ppermute | solution.py:612
  47.5 0.1 fusion.9
  47.6 0.1 fusion.11
  47.7 0.1 copy.13
  47.8 1.1 %collective-permute-done.4.refs_2_ = bf16[224,384]{1,0:T(8,128)(2,1)S(1)} collective-permute-done((bf16[224,384]{1,0:T(8,128)(2,1)S(1)}, bf16[224,384]{1,0:T(8,128)(2,1)S(1)}, u32[]{:S(2)}, u32[]{:S(2)}) %collective-permute-start.4) | collective-permute-done | bytes 172064 | tf_op jit(solution)/shard_map/ppermute | solution.py:612
  48.9 2.7 %collective-permute-done.5.refs_3_ = bf16[224,384]{1,0:T(8,128)(2,1)S(1)} collective-permute-done((bf16[224,384]{1,0:T(8,128)(2,1)S(1)}, bf16[224,384]{1,0:T(8,128)(2,1)S(1)}, u32[]{:S(2)}, u32[]{:S(2)}) %collective-permute-start.5) | collective-permute-done | bytes 172064 | tf_op jit(solution)/shard_map/ppermute | solution.py:612
  51.7 0.0 collective-permute-done.6.refs_4_
  51.7 0.0 collective-permute-done.7.refs_5_
  51.7 0.6 collective-permute-done.8.refs_6_
  52.2 0.2 sums.1
  52.4 1.9 %collective-permute-start.9 = (bf16[192,384]{1,0:T(8,128)(2,1)S(1)}, bf16[192,384]{1,0:T(8,128)(2,1)S(1)}, u32[]{:S(2)}, u32[]{:S(2)}) collective-permute-start(bf16[192,384]{1,0:T(8,128)(2,1)S(1)} %get-tuple-element.39), channel_id=1, source_target_pairs={{0,1},{1,0},{2,3},{3,2},{4,5},{5,4},{6,7},{7,6},{8,9},{9,8},{10,11... | collective-permute-start | bytes 442376 | tf_op jit(solution)/shard_map/ppermute | solution.py:619
  54.3 2.1 %layer0.1 = (f32[144,384]{1,0:T(8,128)S(1)}, f32[48,384]{1,0:T(8,128)S(1)}, f32[4,768]{1,0:T(4,128)S(1)}, f32[4,48]{1,0:T(4,128)S(1)}) custom-call(f32[32,384]{1,0:T(8,128)S(1)} %get-tuple-element.40.rest_ref, bf16[4,768]{1,0:T(4,128)(2,1)S(1)} %copy-done.2, bf16[3,2304,384]{2,1,0:T(8,128)(2,1)} %w_ref.3, bf16[128,384]{1,0:T(8,128)(2,1)S(1)} %get-tuple-element.41.act0_ref, ...), custom_call_target="tpu_custom_call" | custom-call | bytes 5774592 | tf_op jit(solution)/shard_map/layer0/pallas_call | solution.py:520
  56.4 0.7 %dynamic-slice_add_fusion = f32[4,48]{1,0:T(4,128)} fusion(f32[4,48]{1,0:T(4,128)S(1)} %get-tuple-element.46, f32[4,768]{1,0:T(4,128)S(1)} %get-tuple-element.47, s32[]{:T(128)S(6)} %select_n.7), kind=kLoop, calls=%fused_computation.18 | loop fusion | flops 192 | bytes 2308 | tf_op jit(solution)/shard_map/add | solution.py:641
  57.1 0.6 collective-permute-done.9.got_ref
  57.6 1.0 %finish.1 = (f32[3,144,384]{2,1,0:T(8,128)}, f32[3,48,384]{2,1,0:T(8,128)}) custom-call(f32[192,384]{1,0:T(8,128)S(1)} %get-tuple-element.38.total_ref, bf16[192,384]{1,0:T(8,128)(2,1)S(1)} %collective-permute-done.9.got_ref, f32[144,384]{1,0:T(8,128)S(1)} %get-tuple-element.42.conv0_ref, f32[48,384]{1,0:T(8,128)S(1)} %get-tuple-element.43.point0_ref), custom_call_target="tpu_custom_call" | custom-call | bytes 1622016 | tf_op jit(solution)/shard_map/finish/pallas_call | solution.py:520
  (1 shorter events, 0.0 us)
Async XLA Ops:
  0.6 17.9 %collective-permute-start = (bf16[176,768]{1,0:T(8,128)(2,1)}, bf16[176,768]{1,0:T(8,128)(2,1)}, u32[]{:S(2)}, u32[]{:S(2)}) collective-permute-start(bf16[176,768]{1,0:T(8,128)(2,1)} %bitcast.5), channel_id=1, source_target_pairs={{0,16},{2,18},{4,20},{6,22},{8,24},{10,26},{12,28},{14,30},{16,0},... | collective-permute-start | bytes 811016 | tf_op jit(solution)/shard_map/ppermute | solution.py:549
  4.7 0.7 %copy-start.3 = (s32[1,176]{1,0:T(1,128)S(1)}, s32[1,176]{1,0:T(1,128)}, u32[]{:S(2)}) copy-start(s32[1,176]{1,0:T(1,128)} %bases_ref.1) | copy-start | bytes 2116
  6.0 12.5 %all-to-all-start = ((s32[16,1,176]{2,1,0:T(1,128)}), s32[16,1,176]{2,1,0:T(1,128)S(1)}, u32[]{:S(2)}, u32[]{:S(2)}) async-start(s32[16,1,176]{2,1,0:T(1,128)} %spread.1), calls=%async_computation | async-start | bytes 32768 | tf_op jit(solution)/shard_map/all_to_all | solution.py:551
  9.9 0.7 %copy-start.1 = (bf16[4,768]{1,0:T(4,128)(2,1)S(1)}, bf16[4,768]{1,0:T(4,128)(2,1)}, u32[]{:S(2)}) copy-start(bf16[4,768]{1,0:T(4,128)(2,1)} %embed_ref.3) | copy-start | bytes 18436
  10.6 7.9 %copy-start = (bf16[3,384,768]{2,1,0:T(8,128)(2,1)S(1)}, bf16[3,384,768]{2,1,0:T(8,128)(2,1)}, u32[]{:S(2)}) copy-start(bf16[3,384,768]{2,1,0:T(8,128)(2,1)} %refs_4_.1) | copy-start | bytes 5308420
  10.6 7.9 %copy-start.4 = (bf16[1,176,768]{2,1,0:T(8,128)(2,1)S(1)}, bf16[1,176,768]{2,1,0:T(8,128)(2,1)}, u32[]{:S(2)}) copy-start(bf16[1,176,768]{2,1,0:T(8,128)(2,1)} %param.9) | copy-start | bytes 811012
  18.5 9.9 %copy-start.2 = (bf16[4,768]{1,0:T(4,128)(2,1)S(1)}, bf16[4,768]{1,0:T(4,128)(2,1)}, u32[]{:S(2)}) copy-start(bf16[4,768]{1,0:T(4,128)(2,1)} %embed_ref.3) | copy-start | bytes 18436
  28.3 3.0 %collective-permute-start.1 = (bf16[1616,384]{1,0:T(8,128)(2,1)S(1)}, bf16[1616,384]{1,0:T(8,128)(2,1)S(1)}, u32[]{:S(2)}, u32[]{:S(2)}) collective-permute-start(bf16[1616,384]{1,0:T(8,128)(2,1)S(1)} %get-tuple-element.29), channel_id=1, source_target_pairs={{0,2},{2,0},{4,6},{6,4},{8,10},{10,8},{12,14},{14,12},{16,18},{18,... | collective-permute-start | bytes 3723272 | tf_op jit(solution)/shard_map/ppermute | solution.py:597
  31.6 9.4 %collective-permute-start.2 = (bf16[224,384]{1,0:T(8,128)(2,1)S(1)}, bf16[224,384]{1,0:T(8,128)(2,1)S(1)}, u32[]{:S(2)}, u32[]{:S(2)}) collective-permute-start(bf16[224,384]{1,0:T(8,128)(2,1)S(1)} %get-tuple-element.31), channel_id=1, source_target_pairs={{0,13},{1,12},{2,15},{3,14},{4,9},{5,8},{6,11},{7,10},{8,5},{9,4},... | collective-permute-start | bytes 516104 | tf_op jit(solution)/shard_map/ppermute | solution.py:612
  33.3 13.5 %collective-permute-start.3 = (bf16[224,384]{1,0:T(8,128)(2,1)S(1)}, bf16[224,384]{1,0:T(8,128)(2,1)S(1)}, u32[]{:S(2)}, u32[]{:S(2)}) collective-permute-start(bf16[224,384]{1,0:T(8,128)(2,1)S(1)} %get-tuple-element.32), channel_id=1, source_target_pairs={{0,12},{1,13},{2,14},{3,15},{4,8},{5,9},{6,10},{7,11},{8,4},{9,5},... | collective-permute-start | bytes 516104 | tf_op jit(solution)/shard_map/ppermute | solution.py:612
  35.5 13.4 %collective-permute-start.4 = (bf16[224,384]{1,0:T(8,128)(2,1)S(1)}, bf16[224,384]{1,0:T(8,128)(2,1)S(1)}, u32[]{:S(2)}, u32[]{:S(2)}) collective-permute-start(bf16[224,384]{1,0:T(8,128)(2,1)S(1)} %get-tuple-element.33), channel_id=1, source_target_pairs={{0,9},{1,8},{2,11},{3,10},{4,13},{5,12},{6,15},{7,14},{8,1},{9,0},... | collective-permute-start | bytes 516104 | tf_op jit(solution)/shard_map/ppermute | solution.py:612
  36.1 15.6 %collective-permute-start.5 = (bf16[224,384]{1,0:T(8,128)(2,1)S(1)}, bf16[224,384]{1,0:T(8,128)(2,1)S(1)}, u32[]{:S(2)}, u32[]{:S(2)}) collective-permute-start(bf16[224,384]{1,0:T(8,128)(2,1)S(1)} %get-tuple-element.34), channel_id=1, source_target_pairs={{0,8},{1,9},{2,10},{3,11},{4,12},{5,13},{6,14},{7,15},{8,0},{9,1},... | collective-permute-start | bytes 516104 | tf_op jit(solution)/shard_map/ppermute | solution.py:612
  37.5 14.2 %collective-permute-start.6 = (bf16[224,384]{1,0:T(8,128)(2,1)S(1)}, bf16[224,384]{1,0:T(8,128)(2,1)S(1)}, u32[]{:S(2)}, u32[]{:S(2)}) collective-permute-start(bf16[224,384]{1,0:T(8,128)(2,1)S(1)} %get-tuple-element.35), channel_id=1, source_target_pairs={{0,5},{1,4},{2,7},{3,6},{4,1},{5,0},{6,3},{7,2},{8,13},{9,12},{10,... | collective-permute-start | bytes 516104 | tf_op jit(solution)/shard_map/ppermute | solution.py:612
  41.0 10.7 %collective-permute-start.7 = (bf16[224,384]{1,0:T(8,128)(2,1)S(1)}, bf16[224,384]{1,0:T(8,128)(2,1)S(1)}, u32[]{:S(2)}, u32[]{:S(2)}) collective-permute-start(bf16[224,384]{1,0:T(8,128)(2,1)S(1)} %get-tuple-element.36), channel_id=1, source_target_pairs={{0,4},{1,5},{2,6},{3,7},{4,0},{5,1},{6,2},{7,3},{8,12},{9,13},{10,... | collective-permute-start | bytes 516104 | tf_op jit(solution)/shard_map/ppermute | solution.py:612
  46.8 5.4 %collective-permute-start.8 = (bf16[224,384]{1,0:T(8,128)(2,1)S(1)}, bf16[224,384]{1,0:T(8,128)(2,1)S(1)}, u32[]{:S(2)}, u32[]{:S(2)}) collective-permute-start(bf16[224,384]{1,0:T(8,128)(2,1)S(1)} %get-tuple-element.37), channel_id=1, source_target_pairs={{0,1},{1,0},{2,3},{3,2},{4,5},{5,4},{6,7},{7,6},{8,9},{9,8},{10,11... | collective-permute-start | bytes 516104 | tf_op jit(solution)/shard_map/ppermute | solution.py:612
  52.4 5.2 %collective-permute-start.9 = (bf16[192,384]{1,0:T(8,128)(2,1)S(1)}, bf16[192,384]{1,0:T(8,128)(2,1)S(1)}, u32[]{:S(2)}, u32[]{:S(2)}) collective-permute-start(bf16[192,384]{1,0:T(8,128)(2,1)S(1)} %get-tuple-element.39), channel_id=1, source_target_pairs={{0,1},{1,0},{2,3},{3,2},{4,5},{5,4},{6,7},{7,6},{8,9},{9,8},{10,11... | collective-permute-start | bytes 442376 | tf_op jit(solution)/shard_map/ppermute | solution.py:619

commit v5 on v4

--- a/solution.py
+++ b/solution.py
@@ -12,6 +12,7 @@
 F32 = jnp.float32
 CLASSES = 128
 STRIDE = 8
+ORDER = (7, 6, 1, 5, 2, 3, 4)
 
 
 def gelu_pair(v):
@@ -281,11 +282,12 @@
     return jnp.where(valid & hit, 1.0, 0.0).astype(BF16)
 
 
-def table_kernel(embed_ref, w_ref, p_ref, act0_ref, table_ref, w0_ref, w1_ref, p0_ref, sems):
+def table_kernel(embed_ref, w_ref, p_ref, act0_ref, table_ref, w2_ref, w0_ref, w1_ref, p0_ref, sems):
     width, mid = embed_ref.shape[1], act0_ref.shape[1]
     copy_w0 = fetch_taps(w_ref, 0, w0_ref, sems, 0)
     copy_p0 = fetch(p_ref.at[0], p0_ref, sems.at[6])
     copy_w1 = fetch_taps(w_ref, 1, w1_ref, sems, 3)
+    copy_w2 = fetch(w_ref.at[2], w2_ref, sems.at[7])
     normed_e = normal(embed_ref[...].astype(F32))
     sel = digit_columns()
     pre = None
@@ -306,13 +308,14 @@
         copy_w1[j].wait()
         at = width + (j + 1) * mid
         table_ref[:, at : at + mid] = mm(ntab, w1_ref[j * width : (j + 1) * width, :])
+    copy_w2.wait()
 
 
 def main_kernel(
-    crow, prow, bases_ref, own_ref, far_ref, w_ref, p_ref, table_ref,
+    crow, prow, bases_ref, own_ref, far_ref, w_ref, p_ref, w2_ref, table_ref,
     features_ref, mine_ref, other_ref,
     hot_ref, stream_ref, normed_ref, act1_ref, act2_ref, slope1_ref, slope2_ref,
-    cot_ref, grad_ref, back_ref, conv_ref, point_ref, bt_ref, ntab_ref, w1_ref, w2_ref, pt_ref, sent_ref, sems,
+    cot_ref, grad_ref, back_ref, conv_ref, point_ref, bt_ref, ntab_ref, w1_ref, pt_ref, sent_ref, sems,
 ):
     n, _, rb = bases_ref.shape
     rows, width = stream_ref.shape
@@ -323,7 +326,6 @@
     place = pl.ds(pl.multiple_of(zh * rb, 16), rb)
     far = pl.ds(pl.multiple_of((1 - zh) * rb, 16), rb)
     copy_p1 = fetch(p_ref.at[1], pt_ref.at[1], sems.at[7])
-    copy_w2 = fetch_taps(w_ref, 2, w2_ref, sems, 3, (2, 0, 1))
     copy_p2 = fetch(p_ref.at[2], pt_ref.at[2], sems.at[8])
     copy_w1 = fetch_taps(w_ref, 1, w1_ref, sems, 0)
     copy_p0 = fetch(p_ref.at[0], pt_ref.at[0], sems.at[6])
@@ -378,12 +380,9 @@
     stream_ref[...] = stream
     normed = normal(stream)
     normed_ref[...] = normed
-    copy_w2[2].wait()
-    copy_w2[0].wait()
     sides = jnp.concatenate(
         [mm(normed[rb:], w2_ref[2 * width :, :]), mm(normed[:rb], w2_ref[:width, :])]
     )
-    copy_w2[1].wait()
     act2, slope2 = gelu_pair(mm(normed, w2_ref[width : 2 * width, :]) + sides)
     act2_ref[...] = act2.astype(BF16)
     slope2_ref[...] = slope2
@@ -515,13 +514,15 @@
     point_ref[2] = second[crow:]
 
 
-def call(kernel, outs, *args, far=(), away=(), scratch=(), limit=24, flops=0, name=None):
-    moved = sum(v.size * v.dtype.itemsize for v in list(args) + list(outs))
+def call(kernel, outs, *args, far=(), whole=(), away=(), scratch=(), limit=24, flops=0, name=None):
+    args = [pltpu.with_memory_space_constraint(v, pltpu.HBM) if i in far else v for i, v in enumerate(args)]
+    moved = sum(math.prod(v.shape) * jnp.dtype(v.dtype).itemsize for v in list(args) + list(outs))
     return pl.pallas_call(
         kernel,
         out_shape=outs,
         in_specs=[
-            pl.BlockSpec(memory_space=pl.ANY if i in far else pltpu.VMEM) for i in range(len(args))
+            pl.BlockSpec(memory_space=pl.ANY if i in far and i not in whole else pltpu.VMEM)
+            for i in range(len(args))
         ],
         out_specs=[
             pl.BlockSpec(memory_space=pl.ANY if i in away else pltpu.VMEM) for i in range(len(outs))
@@ -547,17 +548,22 @@
 
     own = cotangent[0]
     far = lax.ppermute(own, "seq", [(s, (s + STRIDE) % n) for s in range(n)])
-    (copies,) = call(spread_kernel, [shape((n, 1, rb), jnp.int32)], bases, name="spread")
+    (copies,) = call(spread_kernel, [shape((n, 1, rb), jnp.int32)], bases, far=(0,), whole=(0,), name="spread")
     gathered = lax.all_to_all(copies, "seq", 0, 0, tiled=True)
 
     taps = pltpu.VMEM((3 * width, mid), BF16)
-    act0, table = call(
+    act0, table, w2 = call(
         table_kernel,
-        [shape((CLASSES, mid), BF16), shape((CLASSES, width + 4 * mid), F32)],
+        [
+            shape((CLASSES, mid), BF16),
+            pltpu.VMEM((CLASSES, width + 4 * mid), F32),
+            pltpu.VMEM((3 * width, mid), BF16),
+        ],
         embed, conv_weight, point_weight,
-        far=(1, 2),
-        scratch=[taps, taps, pltpu.VMEM((mid, width), BF16), pltpu.SemaphoreType.DMA((7,))],
-        limit=52,
+        far=(0, 1, 2),
+        whole=(0,),
+        scratch=[taps, taps, pltpu.VMEM((mid, width), BF16), pltpu.SemaphoreType.DMA((8,))],
+        limit=20,
         flops=4 * CLASSES * 3 * width * mid,
         name="tables",
     )
@@ -565,7 +571,7 @@
     features, mine, other = call(
         lambda *refs: main_kernel(crow, prow, *refs),
         [shape((rb, width), F32), shape((total_rows, mid), F32), shape((total_rows, mid), BF16)],
-        gathered, own, far, conv_weight, point_weight, table,
+        gathered, own, far, conv_weight, point_weight, w2, table,
         far=(3, 4),
         scratch=[
             pltpu.VMEM((rows, 3 * CLASSES), BF16),
@@ -583,13 +589,12 @@
             pltpu.VMEM((width, CLASSES), F32),
             pltpu.VMEM((CLASSES, width), BF16),
             taps,
-            taps,
             pltpu.VMEM((3, mid, width), BF16),
             pltpu.VMEM((rb, width), F32),
             pltpu.SemaphoreType.DMA((10,)),
         ],
         away=(0,),
-        limit=46,
+        limit=24,
         flops=9 * rows * 3 * width * mid,
         name="tower",
     )
@@ -603,7 +608,7 @@
         name="messages",
     )
     arrived = []
-    for mask in range(peers - 1, 0, -1):
+    for mask in ORDER:
         route = [
             (s * dp + d, (s ^ (2 * (mask // dp))) * dp + (d ^ (mask % dp)))
             for s in range(n)
@@ -635,7 +640,7 @@
         rest, embed, conv_weight, act0, spread,
         far=(2,),
         scratch=[taps, pltpu.SemaphoreType.DMA((3,))],
-        limit=52,
+        limit=24,
         name="layer0",
     )
     embed_grad = bt + lax.dynamic_slice_in_dim(embed_full, k * prow, prow, axis=1)

time: 58.9 us -> 56.2 us (0.954)
  waiting for transfers between devices: 19 us -> 17.1 us
  local copies, waits for them, and re-layouts: 1.5 us -> 0.77 us
    ppermute x7, waiting for transfers between devices: 11.5 us -> 9.62 us  [on_device(): arrived.append(lax.ppermute(pieces[mask], ('seq', 'dp'), route))]
    unnamed x11 -> x9, local copies, waits for them, and re-layouts: 1.5 us -> 0.77 us
    ppermute x7, starting transfers between devices: 8.88 us -> 9.5 us  [on_device(): arrived.append(lax.ppermute(pieces[mask], ('seq', 'dp'), route))]
  transfers between devices with their start and end apart: 11 -> 11, of which waited for: 8 -> 8; matrix products, arithmetic and copies ran while one was open for 2% -> 2% of each run, Pallas kernels for 11% -> 14%
where the time goes in v5:
time: 56.2 us; the launch traced here: 55.9 us
  starting transfers between devices  19.3 us (34%)
  Pallas kernels  17.1 us (30%)
  waiting for transfers between devices  17.1 us (30%)
  other arithmetic  0.97 us (2%)
  local copies, waits for them, and re-layouts  0.77 us (1%)
  between operations  0.71 us (1%)
    pallas_call x7, Pallas kernels, call(): pl.pallas_call(kernel, out_shape=outs, in_specs=[pl.BlockSpec(memory_spac...  17.1 us
    ppermute x7, waiting for transfers between devices, on_device(): arrived.append(lax.ppermute(pieces[mask], ('seq', 'dp'), route))  9.62 us
    ppermute x7, starting transfers between devices, on_device(): arrived.append(lax.ppermute(pieces[mask], ('seq', 'dp'), route))  9.5 us
    ppermute x1, starting transfers between devices, on_device(): far = lax.ppermute(own, 'seq', [(s, (s + STRIDE) % n) for s in range(n)])  4.1 us
    all_to_all x1, starting transfers between devices, on_device(): gathered = lax.all_to_all(copies, 'seq', 0, 0, tiled=True)  3.91 us
    all_to_all x1, waiting for transfers between devices, on_device(): gathered = lax.all_to_all(copies, 'seq', 0, 0, tiled=True)  3.72 us
    ppermute x1, waiting for transfers between devices, on_device(): got = lax.ppermute(other, 'seq', [(s, s ^ 1) for s in range(n)])  2.68 us
    ppermute x1, starting transfers between devices, on_device(): swapped = lax.ppermute(send, 'dp', [(d, d ^ 1) for d in range(dp)])  1.58 us
  transfers between devices with their start and end apart: 11, of which 8 were waited for; matrix products, arithmetic and copies ran while one was open for 2% of the time, Pallas kernels for 14%

profile of v5, /device:TPU:0, one launch (start us, length us, event | category | flops | bytes accessed | tf_op | source)
XLA Modules:
  0.0 55.9 jit_solution(15958936423405500011)
XLA Ops:
  0.6 4.1 %collective-permute-start = (bf16[176,768]{1,0:T(8,128)(2,1)}, bf16[176,768]{1,0:T(8,128)(2,1)S(1)}, u32[]{:S(2)}, u32[]{:S(2)}) collective-permute-start(bf16[176,768]{1,0:T(8,128)(2,1)} %bitcast.4), channel_id=1, source_target_pairs={{0,16},{2,18},{4,20},{6,22},{8,24},{10,26},{12,28},{14,30},{16,0},... | collective-permute-start | bytes 811016 | tf_op jit(solution)/shard_map/ppermute | solution.py:550
  4.7 1.3 %spread.1 = s32[16,1,176]{2,1,0:T(1,128)} custom-call(s32[1,176]{1,0:T(1,128)} %bases_ref.1), custom_call_target="tpu_custom_call" | custom-call | bytes 11968 | tf_op jit(solution)/shard_map/spread/pallas_call | solution.py:520
  6.0 3.9 %all-to-all-start = ((s32[16,1,176]{2,1,0:T(1,128)}), s32[16,1,176]{2,1,0:T(1,128)S(1)}, u32[]{:S(2)}, u32[]{:S(2)}) async-start(s32[16,1,176]{2,1,0:T(1,128)} %spread.1), calls=%async_computation | async-start | bytes 32768 | tf_op jit(solution)/shard_map/all_to_all | solution.py:552
  9.9 0.0 copy-start
  10.0 4.2 %tables.1 = (bf16[128,384]{1,0:T(8,128)(2,1)S(1)}, f32[128,2304]{1,0:T(8,128)S(1)}, bf16[2304,384]{1,0:T(8,128)(2,1)S(1)}) custom-call(bf16[4,768]{1,0:T(4,128)(2,1)} %embed_ref.3, bf16[3,2304,384]{2,1,0:T(8,128)(2,1)} %w_ref.3, bf16[3,384,768]{2,1,0:T(8,128)(2,1)} %refs_4_.1), custom_call_target="tpu_custom_call" | custom-call | flops 452984832 | bytes 10131456 | tf_op jit(solution)/shard_map/tables/pallas_call | solution.py:520
  14.2 0.0 copy-start.2
  14.2 0.6 %copy-done.2 = bf16[128,384]{1,0:T(8,128)(2,1)} copy-done((bf16[128,384]{1,0:T(8,128)(2,1)}, bf16[128,384]{1,0:T(8,128)(2,1)S(1)}, u32[]{:S(2)}) %copy-start.2) | copy-done | bytes 98328
  14.8 3.7 %all-to-all-done.refs_0_ = s32[16,1,176]{2,1,0:T(1,128)S(1)} async-done(((s32[16,1,176]{2,1,0:T(1,128)}), s32[16,1,176]{2,1,0:T(1,128)S(1)}, u32[]{:S(2)}, u32[]{:S(2)}) %all-to-all-start) | async-done | bytes 11296 | tf_op jit(solution)/shard_map/all_to_all | solution.py:552
  18.5 0.0 collective-permute-done.refs_2_
  18.5 0.0 copy-done
  18.5 0.0 copy-start.1
  18.5 8.1 %tower.1 = (f32[176,768]{1,0:T(8,128)}, f32[1616,384]{1,0:T(8,128)S(1)}, bf16[1616,384]{1,0:T(8,128)(2,1)S(1)}) custom-call(s32[16,1,176]{2,1,0:T(1,128)S(1)} %all-to-all-done.refs_0_, bf16[176,768]{1,0:T(8,128)(2,1)S(1)} %bitcast.5, bf16[176,768]{1,0:T(8,128)(2,1)S(1)} %collective-permute-done.refs_2_, bf16[3,2304,384]{2,1,0:T(8,128)(2,1)} %w_ref.3, ...), custom_call_target="tpu_custom_call" | custom-call | flops 2802843648 | bytes 14842880 | tf_op jit(solution)/shard_map/tower/pallas_call | solution.py:520
  26.6 0.2 collective-permute-start.1
  26.8 0.0 copy-done.1
  26.9 0.1 fusion.8
  27.0 2.7 %collective-permute-done.1.refs_1_ = bf16[1616,384]{1,0:T(8,128)(2,1)S(1)} collective-permute-done((bf16[1616,384]{1,0:T(8,128)(2,1)S(1)}, bf16[1616,384]{1,0:T(8,128)(2,1)S(1)}, u32[]{:S(2)}, u32[]{:S(2)}) %collective-permute-start.1) | collective-permute-done | bytes 1241120 | tf_op jit(solution)/shard_map/ppermute | solution.py:602
  29.6 0.0 copy-start.3
  29.7 0.3 messages.1
  29.9 1.7 %collective-permute-start.2 = (bf16[224,384]{1,0:T(8,128)(2,1)S(1)}, bf16[224,384]{1,0:T(8,128)(2,1)S(1)}, u32[]{:S(2)}, u32[]{:S(2)}) collective-permute-start(bf16[224,384]{1,0:T(8,128)(2,1)S(1)} %get-tuple-element.33), channel_id=1, source_target_pairs={{0,13},{1,12},{2,15},{3,14},{4,9},{5,8},{6,11},{7,10},{8,5},{9,4},... | collective-permute-start | bytes 516104 | tf_op jit(solution)/shard_map/ppermute | solution.py:617
  31.7 2.2 %collective-permute-start.3 = (bf16[224,384]{1,0:T(8,128)(2,1)S(1)}, bf16[224,384]{1,0:T(8,128)(2,1)S(1)}, u32[]{:S(2)}, u32[]{:S(2)}) collective-permute-start(bf16[224,384]{1,0:T(8,128)(2,1)S(1)} %get-tuple-element.34), channel_id=1, source_target_pairs={{0,12},{1,13},{2,14},{3,15},{4,8},{5,9},{6,10},{7,11},{8,4},{9,5},... | collective-permute-start | bytes 516104 | tf_op jit(solution)/shard_map/ppermute | solution.py:617
  33.9 0.5 collective-permute-start.4
  34.4 1.5 %collective-permute-start.5 = (bf16[224,384]{1,0:T(8,128)(2,1)S(1)}, bf16[224,384]{1,0:T(8,128)(2,1)S(1)}, u32[]{:S(2)}, u32[]{:S(2)}) collective-permute-start(bf16[224,384]{1,0:T(8,128)(2,1)S(1)} %get-tuple-element.36), channel_id=1, source_target_pairs={{0,9},{1,8},{2,11},{3,10},{4,13},{5,12},{6,15},{7,14},{8,1},{9,0},... | collective-permute-start | bytes 516104 | tf_op jit(solution)/shard_map/ppermute | solution.py:617
  35.9 0.7 %collective-permute-start.6 = (bf16[224,384]{1,0:T(8,128)(2,1)S(1)}, bf16[224,384]{1,0:T(8,128)(2,1)S(1)}, u32[]{:S(2)}, u32[]{:S(2)}) collective-permute-start(bf16[224,384]{1,0:T(8,128)(2,1)S(1)} %get-tuple-element.37), channel_id=1, source_target_pairs={{0,4},{1,5},{2,6},{3,7},{4,0},{5,1},{6,2},{7,3},{8,12},{9,13},{10,... | collective-permute-start | bytes 516104 | tf_op jit(solution)/shard_map/ppermute | solution.py:617
  36.6 2.5 %collective-permute-done.2.refs_0_ = bf16[224,384]{1,0:T(8,128)(2,1)S(1)} collective-permute-done((bf16[224,384]{1,0:T(8,128)(2,1)S(1)}, bf16[224,384]{1,0:T(8,128)(2,1)S(1)}, u32[]{:S(2)}, u32[]{:S(2)}) %collective-permute-start.2) | collective-permute-done | bytes 172064 | tf_op jit(solution)/shard_map/ppermute | solution.py:617
  39.2 2.2 %collective-permute-start.7 = (bf16[224,384]{1,0:T(8,128)(2,1)S(1)}, bf16[224,384]{1,0:T(8,128)(2,1)S(1)}, u32[]{:S(2)}, u32[]{:S(2)}) collective-permute-start(bf16[224,384]{1,0:T(8,128)(2,1)S(1)} %get-tuple-element.38), channel_id=1, source_target_pairs={{0,5},{1,4},{2,7},{3,6},{4,1},{5,0},{6,3},{7,2},{8,13},{9,12},{10,... | collective-permute-start | bytes 516104 | tf_op jit(solution)/shard_map/ppermute | solution.py:617
  41.4 1.6 %collective-permute-done.3.refs_1_ = bf16[224,384]{1,0:T(8,128)(2,1)S(1)} collective-permute-done((bf16[224,384]{1,0:T(8,128)(2,1)S(1)}, bf16[224,384]{1,0:T(8,128)(2,1)S(1)}, u32[]{:S(2)}, u32[]{:S(2)}) %collective-permute-start.3) | collective-permute-done | bytes 172064 | tf_op jit(solution)/shard_map/ppermute | solution.py:617
  43.0 0.6 %collective-permute-start.8 = (bf16[224,384]{1,0:T(8,128)(2,1)S(1)}, bf16[224,384]{1,0:T(8,128)(2,1)S(1)}, u32[]{:S(2)}, u32[]{:S(2)}) collective-permute-start(bf16[224,384]{1,0:T(8,128)(2,1)S(1)} %get-tuple-element.39), channel_id=1, source_target_pairs={{0,8},{1,9},{2,10},{3,11},{4,12},{5,13},{6,14},{7,15},{8,0},{9,1},... | collective-permute-start | bytes 516104 | tf_op jit(solution)/shard_map/ppermute | solution.py:617
  43.5 0.1 fusion.9
  43.6 0.1 fusion.11
  43.7 0.1 copy.13
  43.9 0.0 collective-permute-done.4.refs_2_
  43.9 2.8 %collective-permute-done.5.refs_3_ = bf16[224,384]{1,0:T(8,128)(2,1)S(1)} collective-permute-done((bf16[224,384]{1,0:T(8,128)(2,1)S(1)}, bf16[224,384]{1,0:T(8,128)(2,1)S(1)}, u32[]{:S(2)}, u32[]{:S(2)}) %collective-permute-start.5) | collective-permute-done | bytes 172064 | tf_op jit(solution)/shard_map/ppermute | solution.py:617
  46.6 1.0 %collective-permute-done.6.refs_4_ = bf16[224,384]{1,0:T(8,128)(2,1)S(1)} collective-permute-done((bf16[224,384]{1,0:T(8,128)(2,1)S(1)}, bf16[224,384]{1,0:T(8,128)(2,1)S(1)}, u32[]{:S(2)}, u32[]{:S(2)}) %collective-permute-start.6) | collective-permute-done | bytes 172064 | tf_op jit(solution)/shard_map/ppermute | solution.py:617
  47.6 1.7 %collective-permute-done.7.refs_5_ = bf16[224,384]{1,0:T(8,128)(2,1)S(1)} collective-permute-done((bf16[224,384]{1,0:T(8,128)(2,1)S(1)}, bf16[224,384]{1,0:T(8,128)(2,1)S(1)}, u32[]{:S(2)}, u32[]{:S(2)}) %collective-permute-start.7) | collective-permute-done | bytes 172064 | tf_op jit(solution)/shard_map/ppermute | solution.py:617
  49.4 0.0 collective-permute-done.8.refs_6_
  49.4 0.2 sums.1
  49.6 1.6 %collective-permute-start.9 = (bf16[192,384]{1,0:T(8,128)(2,1)S(1)}, bf16[192,384]{1,0:T(8,128)(2,1)S(1)}, u32[]{:S(2)}, u32[]{:S(2)}) collective-permute-start(bf16[192,384]{1,0:T(8,128)(2,1)S(1)} %get-tuple-element.41), channel_id=1, source_target_pairs={{0,1},{1,0},{2,3},{3,2},{4,5},{5,4},{6,7},{7,6},{8,9},{9,8},{10,11... | collective-permute-start | bytes 442376 | tf_op jit(solution)/shard_map/ppermute | solution.py:624
  51.2 0.0 copy-done.3
  51.2 2.1 %layer0.1 = (f32[144,384]{1,0:T(8,128)S(1)}, f32[48,384]{1,0:T(8,128)S(1)}, f32[4,768]{1,0:T(4,128)S(1)}, f32[4,48]{1,0:T(4,128)S(1)}) custom-call(f32[32,384]{1,0:T(8,128)S(1)} %get-tuple-element.42.rest_ref, bf16[4,768]{1,0:T(4,128)(2,1)S(1)} %copy-done.1, bf16[3,2304,384]{2,1,0:T(8,128)(2,1)} %w_ref.3, bf16[128,384]{1,0:T(8,128)(2,1)S(1)} %copy-done.3, ...), custom_call_target="tpu_custom_call" | custom-call | bytes 5774592 | tf_op jit(solution)/shard_map/layer0/pallas_call | solution.py:520
  53.3 0.7 %dynamic-slice_add_fusion = f32[4,48]{1,0:T(4,128)} fusion(f32[4,48]{1,0:T(4,128)S(1)} %get-tuple-element.48, f32[4,768]{1,0:T(4,128)S(1)} %get-tuple-element.49, s32[]{:T(128)S(6)} %select_n.7), kind=kLoop, calls=%fused_computation.18 | loop fusion | flops 192 | bytes 2308 | tf_op jit(solution)/shard_map/add | solution.py:646
  53.9 1.0 %collective-permute-done.9.got_ref = bf16[192,384]{1,0:T(8,128)(2,1)S(1)} collective-permute-done((bf16[192,384]{1,0:T(8,128)(2,1)S(1)}, bf16[192,384]{1,0:T(8,128)(2,1)S(1)}, u32[]{:S(2)}, u32[]{:S(2)}) %collective-permute-start.9) | collective-permute-done | bytes 147488 | tf_op jit(solution)/shard_map/ppermute | solution.py:624
  55.0 1.0 %finish.1 = (f32[3,144,384]{2,1,0:T(8,128)}, f32[3,48,384]{2,1,0:T(8,128)}) custom-call(f32[192,384]{1,0:T(8,128)S(1)} %get-tuple-element.40.total_ref, bf16[192,384]{1,0:T(8,128)(2,1)S(1)} %collective-permute-done.9.got_ref, f32[144,384]{1,0:T(8,128)S(1)} %get-tuple-element.44.conv0_ref, f32[48,384]{1,0:T(8,128)S(1)} %get-tuple-element.45.point0_ref), custom_call_target="tpu_custom_call" | custom-call | bytes 1622016 | tf_op jit(solution)/shard_map/finish/pallas_call | solution.py:520
  (1 shorter events, 0.0 us)
Async XLA Ops:
  0.6 17.9 %collective-permute-start = (bf16[176,768]{1,0:T(8,128)(2,1)}, bf16[176,768]{1,0:T(8,128)(2,1)S(1)}, u32[]{:S(2)}, u32[]{:S(2)}) collective-permute-start(bf16[176,768]{1,0:T(8,128)(2,1)} %bitcast.4), channel_id=1, source_target_pairs={{0,16},{2,18},{4,20},{6,22},{8,24},{10,26},{12,28},{14,30},{16,0},... | collective-permute-start | bytes 811016 | tf_op jit(solution)/shard_map/ppermute | solution.py:550
  6.0 12.5 %all-to-all-start = ((s32[16,1,176]{2,1,0:T(1,128)}), s32[16,1,176]{2,1,0:T(1,128)S(1)}, u32[]{:S(2)}, u32[]{:S(2)}) async-start(s32[16,1,176]{2,1,0:T(1,128)} %spread.1), calls=%async_computation | async-start | bytes 32768 | tf_op jit(solution)/shard_map/all_to_all | solution.py:552
  9.9 8.6 %copy-start = (bf16[1,176,768]{2,1,0:T(8,128)(2,1)S(1)}, bf16[1,176,768]{2,1,0:T(8,128)(2,1)}, u32[]{:S(2)}) copy-start(bf16[1,176,768]{2,1,0:T(8,128)(2,1)} %param.9) | copy-start | bytes 811012
  14.2 0.6 %copy-start.2 = (bf16[128,384]{1,0:T(8,128)(2,1)}, bf16[128,384]{1,0:T(8,128)(2,1)S(1)}, u32[]{:S(2)}) copy-start(bf16[128,384]{1,0:T(8,128)(2,1)S(1)} %get-tuple-element.43.act0_ref) | copy-start | bytes 294916
  18.5 8.3 %copy-start.1 = (bf16[4,768]{1,0:T(4,128)(2,1)S(1)}, bf16[4,768]{1,0:T(4,128)(2,1)}, u32[]{:S(2)}) copy-start(bf16[4,768]{1,0:T(4,128)(2,1)} %embed_ref.3) | copy-start | bytes 18436
  26.6 3.0 %collective-permute-start.1 = (bf16[1616,384]{1,0:T(8,128)(2,1)S(1)}, bf16[1616,384]{1,0:T(8,128)(2,1)S(1)}, u32[]{:S(2)}, u32[]{:S(2)}) collective-permute-start(bf16[1616,384]{1,0:T(8,128)(2,1)S(1)} %get-tuple-element.31), channel_id=1, source_target_pairs={{0,2},{2,0},{4,6},{6,4},{8,10},{10,8},{12,14},{14,12},{16,18},{18,... | collective-permute-start | bytes 3723272 | tf_op jit(solution)/shard_map/ppermute | solution.py:602
  29.6 21.5 %copy-start.3 = (bf16[128,384]{1,0:T(8,128)(2,1)S(1)}, bf16[128,384]{1,0:T(8,128)(2,1)}, u32[]{:S(2)}) copy-start(bf16[128,384]{1,0:T(8,128)(2,1)} %copy-done.2) | copy-start | bytes 294916
  29.9 9.2 %collective-permute-start.2 = (bf16[224,384]{1,0:T(8,128)(2,1)S(1)}, bf16[224,384]{1,0:T(8,128)(2,1)S(1)}, u32[]{:S(2)}, u32[]{:S(2)}) collective-permute-start(bf16[224,384]{1,0:T(8,128)(2,1)S(1)} %get-tuple-element.33), channel_id=1, source_target_pairs={{0,13},{1,12},{2,15},{3,14},{4,9},{5,8},{6,11},{7,10},{8,5},{9,4},... | collective-permute-start | bytes 516104 | tf_op jit(solution)/shard_map/ppermute | solution.py:617
  31.7 11.3 %collective-permute-start.3 = (bf16[224,384]{1,0:T(8,128)(2,1)S(1)}, bf16[224,384]{1,0:T(8,128)(2,1)S(1)}, u32[]{:S(2)}, u32[]{:S(2)}) collective-permute-start(bf16[224,384]{1,0:T(8,128)(2,1)S(1)} %get-tuple-element.34), channel_id=1, source_target_pairs={{0,12},{1,13},{2,14},{3,15},{4,8},{5,9},{6,10},{7,11},{8,4},{9,5},... | collective-permute-start | bytes 516104 | tf_op jit(solution)/shard_map/ppermute | solution.py:617
  33.9 10.0 %collective-permute-start.4 = (bf16[224,384]{1,0:T(8,128)(2,1)S(1)}, bf16[224,384]{1,0:T(8,128)(2,1)S(1)}, u32[]{:S(2)}, u32[]{:S(2)}) collective-permute-start(bf16[224,384]{1,0:T(8,128)(2,1)S(1)} %get-tuple-element.35), channel_id=1, source_target_pairs={{0,1},{1,0},{2,3},{3,2},{4,5},{5,4},{6,7},{7,6},{8,9},{9,8},{10,11... | collective-permute-start | bytes 516104 | tf_op jit(solution)/shard_map/ppermute | solution.py:617
  34.4 12.2 %collective-permute-start.5 = (bf16[224,384]{1,0:T(8,128)(2,1)S(1)}, bf16[224,384]{1,0:T(8,128)(2,1)S(1)}, u32[]{:S(2)}, u32[]{:S(2)}) collective-permute-start(bf16[224,384]{1,0:T(8,128)(2,1)S(1)} %get-tuple-element.36), channel_id=1, source_target_pairs={{0,9},{1,8},{2,11},{3,10},{4,13},{5,12},{6,15},{7,14},{8,1},{9,0},... | collective-permute-start | bytes 516104 | tf_op jit(solution)/shard_map/ppermute | solution.py:617
  35.9 11.7 %collective-permute-start.6 = (bf16[224,384]{1,0:T(8,128)(2,1)S(1)}, bf16[224,384]{1,0:T(8,128)(2,1)S(1)}, u32[]{:S(2)}, u32[]{:S(2)}) collective-permute-start(bf16[224,384]{1,0:T(8,128)(2,1)S(1)} %get-tuple-element.37), channel_id=1, source_target_pairs={{0,4},{1,5},{2,6},{3,7},{4,0},{5,1},{6,2},{7,3},{8,12},{9,13},{10,... | collective-permute-start | bytes 516104 | tf_op jit(solution)/shard_map/ppermute | solution.py:617
  39.2 10.2 %collective-permute-start.7 = (bf16[224,384]{1,0:T(8,128)(2,1)S(1)}, bf16[224,384]{1,0:T(8,128)(2,1)S(1)}, u32[]{:S(2)}, u32[]{:S(2)}) collective-permute-start(bf16[224,384]{1,0:T(8,128)(2,1)S(1)} %get-tuple-element.38), channel_id=1, source_target_pairs={{0,5},{1,4},{2,7},{3,6},{4,1},{5,0},{6,3},{7,2},{8,13},{9,12},{10,... | collective-permute-start | bytes 516104 | tf_op jit(solution)/shard_map/ppermute | solution.py:617
  43.0 6.4 %collective-permute-start.8 = (bf16[224,384]{1,0:T(8,128)(2,1)S(1)}, bf16[224,384]{1,0:T(8,128)(2,1)S(1)}, u32[]{:S(2)}, u32[]{:S(2)}) collective-permute-start(bf16[224,384]{1,0:T(8,128)(2,1)S(1)} %get-tuple-element.39), channel_id=1, source_target_pairs={{0,8},{1,9},{2,10},{3,11},{4,12},{5,13},{6,14},{7,15},{8,0},{9,1},... | collective-permute-start | bytes 516104 | tf_op jit(solution)/shard_map/ppermute | solution.py:617
  49.6 5.4 %collective-permute-start.9 = (bf16[192,384]{1,0:T(8,128)(2,1)S(1)}, bf16[192,384]{1,0:T(8,128)(2,1)S(1)}, u32[]{:S(2)}, u32[]{:S(2)}) collective-permute-start(bf16[192,384]{1,0:T(8,128)(2,1)S(1)} %get-tuple-element.41), channel_id=1, source_target_pairs={{0,1},{1,0},{2,3},{3,2},{4,5},{5,4},{6,7},{7,6},{8,9},{9,8},{10,11... | collective-permute-start | bytes 442376 | tf_op jit(solution)/shard_map/ppermute | solution.py:624

commit v6 on v5

--- a/solution.py
+++ b/solution.py
@@ -313,9 +313,9 @@
 
 def main_kernel(
     crow, prow, bases_ref, own_ref, far_ref, w_ref, p_ref, w2_ref, table_ref,
-    features_ref, mine_ref, other_ref,
+    features_ref, mine_ref, other_ref, h_ref, c_ref, w1_ref, p0_ref,
     hot_ref, stream_ref, normed_ref, act1_ref, act2_ref, slope1_ref, slope2_ref,
-    cot_ref, grad_ref, back_ref, conv_ref, point_ref, bt_ref, ntab_ref, w1_ref, pt_ref, sent_ref, sems,
+    cot_ref, grad_ref, back_ref, conv_ref, point_ref, ntab_ref, pt_ref, sent_ref, sems,
 ):
     n, _, rb = bases_ref.shape
     rows, width = stream_ref.shape
@@ -325,10 +325,10 @@
     zh, r, core = k // STRIDE, k % STRIDE, k % 2
     place = pl.ds(pl.multiple_of(zh * rb, 16), rb)
     far = pl.ds(pl.multiple_of((1 - zh) * rb, 16), rb)
-    copy_p1 = fetch(p_ref.at[1], pt_ref.at[1], sems.at[7])
-    copy_p2 = fetch(p_ref.at[2], pt_ref.at[2], sems.at[8])
-    copy_w1 = fetch_taps(w_ref, 1, w1_ref, sems, 0)
-    copy_p0 = fetch(p_ref.at[0], pt_ref.at[0], sems.at[6])
+    copy_p1 = fetch(p_ref.at[1], pt_ref.at[0], sems.at[0])
+    copy_p2 = fetch(p_ref.at[2], pt_ref.at[1], sems.at[1])
+    copy_w1 = fetch(w_ref.at[1], w1_ref, sems.at[2])
+    copy_p0 = fetch(p_ref.at[0], p0_ref, sems.at[3])
     held = jnp.concatenate([bases_ref[i] for i in range(n)])
     held = (held - 4).astype(F32)
     edge = jnp.zeros((1, rb), F32)
@@ -376,7 +376,7 @@
     s_high = stab.astype(BF16)
     stream = mm(mid_hot, s_high) + mm(mid_hot, (stab - s_high.astype(F32)).astype(BF16))
     copy_p1.wait()
-    stream = stream + mm(act1, pt_ref[1])
+    stream = stream + mm(act1, pt_ref[0])
     stream_ref[...] = stream
     normed = normal(stream)
     normed_ref[...] = normed
@@ -387,12 +387,12 @@
     act2_ref[...] = act2.astype(BF16)
     slope2_ref[...] = slope2
     copy_p2.wait()
-    sent_ref[...] = stream_ref[place, :] + mm(act2_ref[place, :], pt_ref[2])
-    copy_features = fetch(sent_ref, features_ref, sems.at[9])
+    sent_ref[...] = stream_ref[place, :] + mm(act2_ref[place, :], pt_ref[1])
+    copy_features = fetch(sent_ref, features_ref, sems.at[4])
 
     cot_ref[place, :] = own_ref[...]
     cot_ref[far, :] = far_ref[...]
-    grad2 = (mm_nt(cot_ref[...], pt_ref[2]) * slope2_ref[...]).astype(BF16)
+    grad2 = (mm_nt(cot_ref[...], pt_ref[1]) * slope2_ref[...]).astype(BF16)
     grad_ref[...] = grad2
     sides = jnp.concatenate(
         [mm_nt(grad2[rb:], w2_ref[:width, :]), mm_nt(grad2[:rb], w2_ref[2 * width :, :])]
@@ -404,24 +404,13 @@
     back = cot_ref[...].astype(F32) + scale * (ng - stream * (scale * scale * inner))
     back = back.astype(BF16)
     back_ref[...] = back
-    grad1 = (mm_nt(back, pt_ref[1]) * slope1_ref[...]).astype(BF16)
+    grad1 = (mm_nt(back, pt_ref[0]) * slope1_ref[...]).astype(BF16)
 
     h = mm_tn(hot_ref[...], grad1).astype(BF16)
+    h_ref[...] = h
     h = [h[j * CLASSES : (j + 1) * CLASSES] for j in range(3)]
-    ng = None
-    for j in range(3):
-        copy_w1[j].wait()
-        term = mm_nt(h[j], w1_ref[j * width : (j + 1) * width, :])
-        ng = term if ng is None else ng + term
-    stab = table_ref[:, :width]
-    scale = norm_scale(stab)
-    ntab_ref[...] = (stab * scale).astype(BF16)
-    inner = jnp.mean(ng * stab, axis=-1, keepdims=True)
-    b = mm_tn(hot_ref[:, CLASSES : 2 * CLASSES], back) + scale * (ng - stab * (scale * scale * inner))
-    copy_p0.wait()
-    s = (mm_nt(b.astype(BF16), pt_ref[0]) * table_ref[:, width : width + mid]).astype(BF16)
-    g = mm(digit_rows(), s)
-    bt_ref[...] = jnp.transpose(b)
+    c_ref[...] = mm_tn(hot_ref[:, CLASSES : 2 * CLASSES], back)
+    ntab_ref[...] = normal(table_ref[:, :width])
 
     columns = pl.ds(pl.multiple_of(zh * half, 128), half)
     side_at = pl.ds(pl.multiple_of(zh * half, 16), width)
@@ -433,38 +422,60 @@
     point_ref[0] = mm_tn(back_ref[:, columns], act1_ref[...])
     point_ref[1] = mm_tn(cot_ref[:, columns], act2_ref[...])
     part = crow + prow
-    step = 2 * part + 16
     for target, side in ((mine_ref, core), (other_ref, 1 - core)):
         for m in range(STRIDE // 2):
             tile = 2 * m + side
             crows = pl.ds(pl.multiple_of(tile * crow, 16), crow)
             prows = pl.ds(pl.multiple_of(tile * prow, 16), prow)
             for layer in range(2):
-                at = m * step + layer * part
+                at = (2 * m + layer) * part
                 target[at : at + crow, :] = conv_ref[layer, crows, :].astype(target.dtype)
                 target[at + crow : at + part, :] = point_ref[layer, prows, :].astype(target.dtype)
-            at = m * step + 2 * part
+    for copy in (copy_features, copy_w1, copy_p0):
+        copy.wait()
+
+
+def class_kernel(prow, h_ref, c_ref, table_ref, w1_ref, p0_ref, mine_ref, other_ref, bt_ref):
+    width, mid = c_ref.shape[1], h_ref.shape[1]
+    half = width // 2
+    k = lax.axis_index("seq")
+    zh, core = k // STRIDE, k % 2
+    ng = None
+    for j in range(3):
+        term = mm_nt(
+            h_ref[j * CLASSES : (j + 1) * CLASSES, :], w1_ref[j * width : (j + 1) * width, :]
+        )
+        ng = term if ng is None else ng + term
+    stab = table_ref[:, :width]
+    scale = norm_scale(stab)
+    inner = jnp.mean(ng * stab, axis=-1, keepdims=True)
+    b = c_ref[...] + scale * (ng - stab * (scale * scale * inner))
+    s = (mm_nt(b.astype(BF16), p0_ref[...]) * table_ref[:, width : width + mid]).astype(BF16)
+    g = mm(digit_rows(), s)
+    bt_ref[...] = jnp.transpose(b)
+    for target, side in ((mine_ref, core), (other_ref, 1 - core)):
+        for m in range(STRIDE // 2):
             for q in range(3):
-                brows = pl.ds(pl.multiple_of(zh * half + tile * prow + 16 * q, 16), 16)
-                target[at : at + 16, q * CLASSES : (q + 1) * CLASSES] = bt_ref[brows, :].astype(target.dtype)
-        at = STRIDE // 2 * step
-        target[at : at + 16, :] = g.astype(target.dtype)
-    copy_features.wait()
-
-
-def message_kernel(part, mine_ref, other_ref, *out_refs):
+                at = pl.ds(pl.multiple_of(zh * half + (2 * m + side) * prow + 16 * q, 16), 16)
+                target[16 * m : 16 * m + 16, q * CLASSES : (q + 1) * CLASSES] = bt_ref[at, :].astype(
+                    target.dtype
+                )
+        target[8 * STRIDE : 8 * STRIDE + 16, :] = g.astype(target.dtype)
+
+
+def message_kernel(part, mine_ref, other_ref, mine_small_ref, other_small_ref, *out_refs):
     k, x = lax.axis_index("seq"), lax.axis_index("dp")
     m = (k % STRIDE) // 2
-    step = 2 * part + 16
-    end = STRIDE // 2 * step
-    small = mine_ref[end : end + 16, :] + other_ref[end : end + 16, :].astype(F32)
+    end = 8 * STRIDE
+    g = mine_small_ref[end:, :] + other_small_ref[end:, :].astype(F32)
     for mask, out_ref in enumerate(out_refs):
         target, layer = m ^ (mask // 2), x ^ (mask % 2)
-        at = pl.ds(pl.multiple_of(target * step + layer * part, 16), part)
+        at = pl.ds(pl.multiple_of((2 * target + layer) * part, 16), part)
         out_ref[:part, :] = (mine_ref[at, :] + other_ref[at, :].astype(F32)).astype(out_ref.dtype)
-        at = pl.ds(pl.multiple_of(target * step + 2 * part, 16), 16)
-        out_ref[part : part + 16, :] = (mine_ref[at, :] + other_ref[at, :].astype(F32)).astype(out_ref.dtype)
-        out_ref[part + 16 :, :] = small.astype(out_ref.dtype)
+        at = pl.ds(pl.multiple_of(target * 16, 16), 16)
+        small = mine_small_ref[at, :] + other_small_ref[at, :].astype(F32)
+        out_ref[part : part + 16, :] = small.astype(out_ref.dtype)
+        out_ref[part + 16 :, :] = g.astype(out_ref.dtype)
 
 
 def sum_kernel(own_ref, *refs):
@@ -478,15 +489,29 @@
     rest_ref[...] = total[part:]
 
 
-def small_kernel(rest_ref, embed_ref, w_ref, act0_ref, spread_ref, conv0_ref, point0_ref, embed_out_ref, bt_ref, w0_ref, sems):
+def small_kernel(
+    rest_ref, total_ref, embed_ref, w_ref, act0_ref, spread_ref,
+    conv_ref, point_ref, embed_out_ref, bt_ref, w0_ref, conv0_ref, point0_ref, sems,
+):
     copy_w0 = fetch_taps(w_ref, 0, w0_ref, sems, 0)
     width = embed_ref.shape[1]
+    crow = conv_ref.shape[1]
+    own = lax.axis_index("dp") + 1
+    copies = [
+        fetch(total_ref.at[pl.ds(0, crow), :], conv_ref.at[own], sems.at[3]),
+        fetch(total_ref.at[pl.ds(crow, point_ref.shape[1]), :], point_ref.at[own], sems.at[4]),
+    ]
     g = rest_ref[16:, :]
     bt = jnp.concatenate([rest_ref[:16, q * CLASSES : (q + 1) * CLASSES] for q in range(3)])
     bt = bt.astype(BF16)
+    g16 = g.astype(BF16)
+    conv0_ref[...] = mm(spread_ref[...], g16)
+    copies.append(fetch(conv0_ref, conv_ref.at[0], sems.at[5]))
+    point0_ref[...] = mm(bt, act0_ref[...])
+    copies.append(fetch(point0_ref, point_ref.at[0], sems.at[6]))
+    bt_ref[...] = mm_nt(digit_rows(), bt)[4:8]
     stream = embed_ref[...].astype(F32)
     scale = norm_scale(stream)
-    g16 = g.astype(BF16)
     ng = None
     for j in range(3):
         copy_w0[j].wait()
@@ -494,40 +519,37 @@
         ng = term if ng is None else ng + term
     inner = jnp.mean(ng * stream, axis=-1, keepdims=True)
     embed_out_ref[...] = scale * (ng - stream * (scale * scale * inner))
-    bt_ref[...] = mm_nt(digit_rows(), bt)[4:8]
-    conv0_ref[...] = mm(spread_ref[...], g16)
-    point0_ref[...] = mm(bt, act0_ref[...])
-
-
-def finish_kernel(total_ref, got_ref, conv0_ref, point0_ref, conv_ref, point_ref):
+    for copy in copies:
+        copy.wait()
+
+
+def finish_kernel(got_ref, _, __, conv_ref, point_ref, held_ref, sems):
     crow = conv_ref.shape[1]
-    x = lax.axis_index("dp")
-    conv_ref[0] = conv0_ref[...]
-    point_ref[0] = point0_ref[...]
-    own = total_ref[...]
-    got = got_ref[...].astype(F32)
-    first = jnp.where(x == 0, own, got)
-    second = jnp.where(x == 0, got, own)
-    conv_ref[1] = first[:crow]
-    conv_ref[2] = second[:crow]
-    point_ref[1] = first[crow:]
-    point_ref[2] = second[crow:]
-
-
-def call(kernel, outs, *args, far=(), whole=(), away=(), scratch=(), limit=24, flops=0, name=None):
+    other = 2 - lax.axis_index("dp")
+    held_ref[...] = got_ref[...].astype(F32)
+    copies = [
+        fetch(held_ref.at[pl.ds(0, crow), :], conv_ref.at[other], sems.at[0]),
+        fetch(held_ref.at[pl.ds(crow, point_ref.shape[1]), :], point_ref.at[other], sems.at[1]),
+    ]
+    for copy in copies:
+        copy.wait()
+
+
+def call(kernel, outs, *args, far=(), whole=(), away=(), scratch=(), limit=24, aliases=None, flops=0, name=None):
     args = [pltpu.with_memory_space_constraint(v, pltpu.HBM) if i in far else v for i, v in enumerate(args)]
     moved = sum(math.prod(v.shape) * jnp.dtype(v.dtype).itemsize for v in list(args) + list(outs))
     return pl.pallas_call(
         kernel,
         out_shape=outs,
         in_specs=[
-            pl.BlockSpec(memory_space=pl.ANY if i in far and i not in whole else pltpu.VMEM)
+            pl.BlockSpec(memory_space=pltpu.HBM if i in far and i not in whole else pltpu.VMEM)
             for i in range(len(args))
         ],
         out_specs=[
-            pl.BlockSpec(memory_space=pl.ANY if i in away else pltpu.VMEM) for i in range(len(outs))
+            pl.BlockSpec(memory_space=pltpu.HBM if i in away else pltpu.VMEM) for i in range(len(outs))
         ],
         scratch_shapes=list(scratch),
+        input_output_aliases=aliases or {},
         compiler_params=pltpu.CompilerParams(vmem_limit_bytes=limit * 1024 * 1024),
         cost_estimate=pl.CostEstimate(flops=flops, bytes_accessed=moved, transcendentals=0),
         name=name,
@@ -544,11 +566,11 @@
     rows = 2 * rb
     crow, prow = 3 * width // n, width // n
     part = crow + prow
-    shape = jax.ShapeDtypeStruct
+    shape, near = jax.ShapeDtypeStruct, pltpu.VMEM
 
     own = cotangent[0]
     far = lax.ppermute(own, "seq", [(s, (s + STRIDE) % n) for s in range(n)])
-    (copies,) = call(spread_kernel, [shape((n, 1, rb), jnp.int32)], bases, far=(0,), whole=(0,), name="spread")
+    (copies,) = call(spread_kernel, [near((n, 1, rb), jnp.int32)], bases, far=(0,), whole=(0,), name="spread")
     gathered = lax.all_to_all(copies, "seq", 0, 0, tiled=True)
 
     taps = pltpu.VMEM((3 * width, mid), BF16)
@@ -567,10 +589,17 @@
         flops=4 * CLASSES * 3 * width * mid,
         name="tables",
     )
-    total_rows = STRIDE // 2 * (2 * part + 16) + 16
-    features, mine, other = call(
+    features, mine, other, h, c, w1, p0 = call(
         lambda *refs: main_kernel(crow, prow, *refs),
-        [shape((rb, width), F32), shape((total_rows, mid), F32), shape((total_rows, mid), BF16)],
+        [
+            shape((rb, width), F32),
+            near((STRIDE * part, mid), F32),
+            near((STRIDE * part, mid), BF16),
+            near((3 * CLASSES, mid), BF16),
+            near((CLASSES, width), F32),
+            near((3 * width, mid), BF16),
+            near((mid, width), BF16),
+        ],
         gathered, own, far, conv_weight, point_weight, w2, table,
         far=(3, 4),
         scratch=[
@@ -586,25 +615,33 @@
             pltpu.VMEM((rows, width), BF16),
             pltpu.VMEM((2, STRIDE * crow, mid), F32),
             pltpu.VMEM((2, STRIDE * prow, mid), F32),
-            pltpu.VMEM((width, CLASSES), F32),
             pltpu.VMEM((CLASSES, width), BF16),
-            taps,
-            pltpu.VMEM((3, mid, width), BF16),
+            pltpu.VMEM((2, mid, width), BF16),
             pltpu.VMEM((rb, width), F32),
-            pltpu.SemaphoreType.DMA((10,)),
+            pltpu.SemaphoreType.DMA((5,)),
         ],
         away=(0,),
-        limit=24,
         flops=9 * rows * 3 * width * mid,
         name="tower",
     )
 
-    got = lax.ppermute(other, "seq", [(s, s ^ 1) for s in range(n)])
+    swap = [(s, s ^ 1) for s in range(n)]
+    got = lax.ppermute(other, "seq", swap)
+    small_rows = 8 * STRIDE + 16
+    mine_small, other_small = call(
+        lambda *refs: class_kernel(prow, *refs),
+        [near((small_rows, mid), F32), near((small_rows, mid), BF16)],
+        h, c, table, w1, p0,
+        scratch=[pltpu.VMEM((width, CLASSES), F32)],
+        flops=4 * CLASSES * 3 * width * mid,
+        name="classes",
+    )
+    got_small = lax.ppermute(other_small, "seq", swap)
     peers = STRIDE // 2 * dp
     pieces = call(
         lambda *refs: message_kernel(part, *refs),
         [shape((part + 32, mid), F32 if i == 0 else BF16) for i in range(peers)],
-        mine, got,
+        mine, got, mine_small, got_small,
         name="messages",
     )
     arrived = []
@@ -629,25 +666,34 @@
         [jnp.pad(normed_e, ((4 * j, 12 - 4 * j), (0, 0))) for j in range(3)], axis=1
     )
     spread = lax.dynamic_slice_in_dim(spread, k * crow, crow, axis=1).T
-    conv0, point0, embed_full, bt = call(
+    conv_grad, point_grad, embed_full, bt = call(
         small_kernel,
         [
-            shape((crow, mid), F32),
-            shape((prow, mid), F32),
+            shape((3, crow, mid), F32),
+            shape((3, prow, mid), F32),
             shape((4, width), F32),
             shape((4, prow), F32),
         ],
-        rest, embed, conv_weight, act0, spread,
-        far=(2,),
-        scratch=[taps, pltpu.SemaphoreType.DMA((3,))],
-        limit=24,
+        rest, total, embed, conv_weight, act0, spread,
+        far=(3,),
+        away=(0, 1),
+        scratch=[
+            pltpu.VMEM((3 * width, mid), BF16),
+            pltpu.VMEM((crow, mid), F32),
+            pltpu.VMEM((prow, mid), F32),
+            pltpu.SemaphoreType.DMA((7,)),
+        ],
         name="layer0",
     )
     embed_grad = bt + lax.dynamic_slice_in_dim(embed_full, k * prow, prow, axis=1)
     conv_grad, point_grad = call(
         finish_kernel,
         [shape((3, crow, mid), F32), shape((3, prow, mid), F32)],
-        total, swapped, conv0, point0,
+        swapped, conv_grad, point_grad,
+        far=(1, 2),
+        away=(0, 1),
+        aliases={1: 0, 2: 1},
+        scratch=[pltpu.VMEM((part, mid), F32), pltpu.SemaphoreType.DMA((2,))],
         name="finish",
     )
     return features[None], conv_grad, point_grad.transpose(0, 2, 1), embed_grad

time: 56.2 us -> 54.8 us (0.975)
  waiting for transfers between devices: 17.1 us -> 15.1 us
    ppermute x1 -> x2, waiting for transfers between devices: 2.68 us -> 0.92 us  [the longest x1 0.92 us: on_device(): got_small = lax.ppermute(other_small, 'seq', swap)]
    pallas_call x7 -> x8, Pallas kernels: 17.1 us -> 17.3 us  [call(): pl.pallas_call(kernel, out_shape=outs, in_specs=[pl.BlockSpec(memory_spac...]
  transfers between devices with their start and end apart: 11 -> 12, of which waited for: 8 -> 8; matrix products, arithmetic and copies ran while one was open for 2% -> 2% of each run, Pallas kernels for 14% -> 17%
where the time goes in v6:
time: 54.8 us; the launch traced here: 54.5 us
  starting transfers between devices  19.7 us (36%)
  Pallas kernels  17.3 us (32%)
  waiting for transfers between devices  15.1 us (28%)
  other arithmetic  0.97 us (2%)
  local copies, waits for them, and re-layouts  0.77 us (1%)
  between operations  0.71 us (1%)
    pallas_call x8, Pallas kernels, call(): pl.pallas_call(kernel, out_shape=outs, in_specs=[pl.BlockSpec(memory_spac...  17.3 us
    ppermute x7, waiting for transfers between devices, on_device(): arrived.append(lax.ppermute(pieces[mask], ('seq', 'dp'), route))  9.63 us
    ppermute x7, starting transfers between devices, on_device(): arrived.append(lax.ppermute(pieces[mask], ('seq', 'dp'), route))  9.55 us
    ppermute x1, starting transfers between devices, on_device(): far = lax.ppermute(own, 'seq', [(s, (s + STRIDE) % n) for s in range(n)])  4.1 us
    all_to_all x1, starting transfers between devices, on_device(): gathered = lax.all_to_all(copies, 'seq', 0, 0, tiled=True)  3.91 us
    all_to_all x1, waiting for transfers between devices, on_device(): gathered = lax.all_to_all(copies, 'seq', 0, 0, tiled=True)  3.72 us
    ppermute x1, starting transfers between devices, on_device(): swapped = lax.ppermute(send, 'dp', [(d, d ^ 1) for d in range(dp)])  1.58 us
  transfers between devices with their start and end apart: 12, of which 8 were waited for; matrix products, arithmetic and copies ran while one was open for 2% of the time, Pallas kernels for 17%

profile of v6, /device:TPU:0, one launch (start us, length us, event | category | flops | bytes accessed | tf_op | source)
XLA Modules:
  0.0 54.5 jit_solution(3300168631629259823)
XLA Ops:
  0.6 4.1 %collective-permute-start = (bf16[176,768]{1,0:T(8,128)(2,1)}, bf16[176,768]{1,0:T(8,128)(2,1)S(1)}, u32[]{:S(2)}, u32[]{:S(2)}) collective-permute-start(bf16[176,768]{1,0:T(8,128)(2,1)} %bitcast.4), channel_id=1, source_target_pairs={{0,16},{2,18},{4,20},{6,22},{8,24},{10,26},{12,28},{14,30},{16,0},... | collective-permute-start | bytes 811016 | tf_op jit(solution)/shard_map/ppermute | solution.py:572
  4.7 1.3 %spread.1 = s32[16,1,176]{2,1,0:T(1,128)} custom-call(s32[1,176]{1,0:T(1,128)} %bases_ref.1), custom_call_target="tpu_custom_call" | custom-call | bytes 11968 | tf_op jit(solution)/shard_map/spread/pallas_call | solution.py:541
  6.0 3.9 %all-to-all-start = ((s32[16,1,176]{2,1,0:T(1,128)}), s32[16,1,176]{2,1,0:T(1,128)S(1)}, u32[]{:S(2)}, u32[]{:S(2)}) async-start(s32[16,1,176]{2,1,0:T(1,128)} %spread.1), calls=%async_computation | async-start | bytes 32768 | tf_op jit(solution)/shard_map/all_to_all | solution.py:574
  9.9 0.0 copy-start
  10.0 4.2 %tables.1 = (bf16[128,384]{1,0:T(8,128)(2,1)S(1)}, f32[128,2304]{1,0:T(8,128)S(1)}, bf16[2304,384]{1,0:T(8,128)(2,1)S(1)}) custom-call(bf16[4,768]{1,0:T(4,128)(2,1)} %embed_ref.3, bf16[3,2304,384]{2,1,0:T(8,128)(2,1)} %w_ref.3, bf16[3,384,768]{2,1,0:T(8,128)(2,1)} %refs_4_.1), custom_call_target="tpu_custom_call" | custom-call | flops 452984832 | bytes 10131456 | tf_op jit(solution)/shard_map/tables/pallas_call | solution.py:541
  14.2 0.0 copy-start.1
  14.2 0.6 %copy-done.1 = bf16[128,384]{1,0:T(8,128)(2,1)} copy-done((bf16[128,384]{1,0:T(8,128)(2,1)}, bf16[128,384]{1,0:T(8,128)(2,1)S(1)}, u32[]{:S(2)}) %copy-start.1) | copy-done | bytes 98328
  14.8 3.7 %all-to-all-done.refs_0_ = s32[16,1,176]{2,1,0:T(1,128)S(1)} async-done(((s32[16,1,176]{2,1,0:T(1,128)}), s32[16,1,176]{2,1,0:T(1,128)S(1)}, u32[]{:S(2)}, u32[]{:S(2)}) %all-to-all-start) | async-done | bytes 11296 | tf_op jit(solution)/shard_map/all_to_all | solution.py:574
  18.5 0.0 collective-permute-done.refs_2_
  18.5 0.0 copy-done
  18.5 6.9 %tower.1 = (f32[176,768]{1,0:T(8,128)}, f32[1536,384]{1,0:T(8,128)S(1)}, bf16[1536,384]{1,0:T(8,128)(2,1)S(1)}, bf16[384,384]{1,0:T(8,128)(2,1)S(1)}, f32[128,76...) custom-call(s32[16,1,176]{2,1,0:T(1,128)S(1)} %all-to-all-done.refs_0_, ...), custom_call_target="tpu_custom_call" | custom-call | flops 2802843648 | bytes 17705984 | tf_op jit(solution)/shard_map/tower/pallas_call | solution.py:541
  25.4 0.2 collective-permute-start.1
  25.6 0.0 copy-start.3
  25.6 1.4 %classes.1 = (f32[80,384]{1,0:T(8,128)S(1)}, bf16[80,384]{1,0:T(8,128)(2,1)S(1)}) custom-call(bf16[384,384]{1,0:T(8,128)(2,1)S(1)} %get-tuple-element.38.refs_0_, f32[128,768]{1,0:T(8,128)S(1)} %get-tuple-element.39.refs_1_, f32[128,2304]{1,0:T(8,128)S(1)} %get-tuple-element.34.refs_6_.refs_2_, bf16[2304,384]{1,0:T(8,128)(2,1)S(1)} %get-tuple-element.40.refs_3_, ...), custom_call_target="tpu_custom_call" | custom-call | flops 452984832 | bytes 4411392 | tf_op jit(solution)/shard_map/classes/pallas_call | solution.py:541
  27.0 0.4 collective-permute-start.2
  27.4 0.0 copy-done.3
  27.4 0.1 fusion.8
  27.5 0.9 %collective-permute-done.2.refs_3_ = bf16[80,384]{1,0:T(8,128)(2,1)S(1)} collective-permute-done((bf16[80,384]{1,0:T(8,128)(2,1)S(1)}, bf16[80,384]{1,0:T(8,128)(2,1)S(1)}, u32[]{:S(2)}, u32[]{:S(2)}) %collective-permute-start.2) | collective-permute-done | bytes 61472 | tf_op jit(solution)/shard_map/ppermute | solution.py:639
  28.4 0.0 collective-permute-done.1.refs_1_
  28.4 0.0 copy-start.2
  28.4 0.2 messages.1
  28.7 1.7 %collective-permute-start.3 = (bf16[224,384]{1,0:T(8,128)(2,1)S(1)}, bf16[224,384]{1,0:T(8,128)(2,1)S(1)}, u32[]{:S(2)}, u32[]{:S(2)}) collective-permute-start(bf16[224,384]{1,0:T(8,128)(2,1)S(1)} %get-tuple-element.45), channel_id=1, source_target_pairs={{0,13},{1,12},{2,15},{3,14},{4,9},{5,8},{6,11},{7,10},{8,5},{9,4},... | collective-permute-start | bytes 516104 | tf_op jit(solution)/shard_map/ppermute | solution.py:654
  30.4 2.2 %collective-permute-start.4 = (bf16[224,384]{1,0:T(8,128)(2,1)S(1)}, bf16[224,384]{1,0:T(8,128)(2,1)S(1)}, u32[]{:S(2)}, u32[]{:S(2)}) collective-permute-start(bf16[224,384]{1,0:T(8,128)(2,1)S(1)} %get-tuple-element.46), channel_id=1, source_target_pairs={{0,12},{1,13},{2,14},{3,15},{4,8},{5,9},{6,10},{7,11},{8,4},{9,5},... | collective-permute-start | bytes 516104 | tf_op jit(solution)/shard_map/ppermute | solution.py:654
  32.6 0.5 collective-permute-start.5
  33.1 1.5 %collective-permute-start.6 = (bf16[224,384]{1,0:T(8,128)(2,1)S(1)}, bf16[224,384]{1,0:T(8,128)(2,1)S(1)}, u32[]{:S(2)}, u32[]{:S(2)}) collective-permute-start(bf16[224,384]{1,0:T(8,128)(2,1)S(1)} %get-tuple-element.48), channel_id=1, source_target_pairs={{0,9},{1,8},{2,11},{3,10},{4,13},{5,12},{6,15},{7,14},{8,1},{9,0},... | collective-permute-start | bytes 516104 | tf_op jit(solution)/shard_map/ppermute | solution.py:654
  34.6 0.7 %collective-permute-start.7 = (bf16[224,384]{1,0:T(8,128)(2,1)S(1)}, bf16[224,384]{1,0:T(8,128)(2,1)S(1)}, u32[]{:S(2)}, u32[]{:S(2)}) collective-permute-start(bf16[224,384]{1,0:T(8,128)(2,1)S(1)} %get-tuple-element.49), channel_id=1, source_target_pairs={{0,4},{1,5},{2,6},{3,7},{4,0},{5,1},{6,2},{7,3},{8,12},{9,13},{10,... | collective-permute-start | bytes 516104 | tf_op jit(solution)/shard_map/ppermute | solution.py:654
  35.4 2.5 %collective-permute-done.3.refs_0_ = bf16[224,384]{1,0:T(8,128)(2,1)S(1)} collective-permute-done((bf16[224,384]{1,0:T(8,128)(2,1)S(1)}, bf16[224,384]{1,0:T(8,128)(2,1)S(1)}, u32[]{:S(2)}, u32[]{:S(2)}) %collective-permute-start.3) | collective-permute-done | bytes 172064 | tf_op jit(solution)/shard_map/ppermute | solution.py:654
  37.9 2.3 %collective-permute-start.8 = (bf16[224,384]{1,0:T(8,128)(2,1)S(1)}, bf16[224,384]{1,0:T(8,128)(2,1)S(1)}, u32[]{:S(2)}, u32[]{:S(2)}) collective-permute-start(bf16[224,384]{1,0:T(8,128)(2,1)S(1)} %get-tuple-element.50), channel_id=1, source_target_pairs={{0,5},{1,4},{2,7},{3,6},{4,1},{5,0},{6,3},{7,2},{8,13},{9,12},{10,... | collective-permute-start | bytes 516104 | tf_op jit(solution)/shard_map/ppermute | solution.py:654
  40.2 1.6 %collective-permute-done.4.refs_1_ = bf16[224,384]{1,0:T(8,128)(2,1)S(1)} collective-permute-done((bf16[224,384]{1,0:T(8,128)(2,1)S(1)}, bf16[224,384]{1,0:T(8,128)(2,1)S(1)}, u32[]{:S(2)}, u32[]{:S(2)}) %collective-permute-start.4) | collective-permute-done | bytes 172064 | tf_op jit(solution)/shard_map/ppermute | solution.py:654
  41.7 0.6 %collective-permute-start.9 = (bf16[224,384]{1,0:T(8,128)(2,1)S(1)}, bf16[224,384]{1,0:T(8,128)(2,1)S(1)}, u32[]{:S(2)}, u32[]{:S(2)}) collective-permute-start(bf16[224,384]{1,0:T(8,128)(2,1)S(1)} %get-tuple-element.51), channel_id=1, source_target_pairs={{0,8},{1,9},{2,10},{3,11},{4,12},{5,13},{6,14},{7,15},{8,0},{9,1},... | collective-permute-start | bytes 516104 | tf_op jit(solution)/shard_map/ppermute | solution.py:654
  42.3 0.1 fusion.9
  42.4 0.1 fusion.11
  42.5 0.1 copy.15
  42.6 0.0 collective-permute-done.5.refs_2_
  42.6 2.7 %collective-permute-done.6.refs_3_ = bf16[224,384]{1,0:T(8,128)(2,1)S(1)} collective-permute-done((bf16[224,384]{1,0:T(8,128)(2,1)S(1)}, bf16[224,384]{1,0:T(8,128)(2,1)S(1)}, u32[]{:S(2)}, u32[]{:S(2)}) %collective-permute-start.6) | collective-permute-done | bytes 172064 | tf_op jit(solution)/shard_map/ppermute | solution.py:654
  45.4 1.0 %collective-permute-done.7.refs_4_ = bf16[224,384]{1,0:T(8,128)(2,1)S(1)} collective-permute-done((bf16[224,384]{1,0:T(8,128)(2,1)S(1)}, bf16[224,384]{1,0:T(8,128)(2,1)S(1)}, u32[]{:S(2)}, u32[]{:S(2)}) %collective-permute-start.7) | collective-permute-done | bytes 172064 | tf_op jit(solution)/shard_map/ppermute | solution.py:654
  46.4 1.8 %collective-permute-done.8.refs_5_ = bf16[224,384]{1,0:T(8,128)(2,1)S(1)} collective-permute-done((bf16[224,384]{1,0:T(8,128)(2,1)S(1)}, bf16[224,384]{1,0:T(8,128)(2,1)S(1)}, u32[]{:S(2)}, u32[]{:S(2)}) %collective-permute-start.8) | collective-permute-done | bytes 172064 | tf_op jit(solution)/shard_map/ppermute | solution.py:654
  48.2 0.0 collective-permute-done.9.refs_6_
  48.2 0.2 sums.1
  48.4 1.6 %collective-permute-start.10 = (bf16[192,384]{1,0:T(8,128)(2,1)S(1)}, bf16[192,384]{1,0:T(8,128)(2,1)S(1)}, u32[]{:S(2)}, u32[]{:S(2)}) collective-permute-start(bf16[192,384]{1,0:T(8,128)(2,1)S(1)} %get-tuple-element.52), channel_id=1, source_target_pairs={{0,1},{1,0},{2,3},{3,2},{4,5},{5,4},{6,7},{7,6},{8,9},{9,8},{10,11... | collective-permute-start | bytes 442376 | tf_op jit(solution)/shard_map/ppermute | solution.py:661
  50.0 0.0 copy-done.2
  50.0 2.4 %layer0.1 = (f32[3,144,384]{2,1,0:T(8,128)}, f32[3,48,384]{2,1,0:T(8,128)}, f32[4,768]{1,0:T(4,128)S(1)}, f32[4,48]{1,0:T(4,128)S(1)}) custom-call(f32[32,384]{1,0:T(8,128)S(1)} %get-tuple-element.53.rest_ref, f32[192,384]{1,0:T(8,128)S(1)} %get-tuple-element.54.total_ref, bf16[4,768]{1,0:T(4,128)(2,1)S(1)} %copy-done.3, bf16[3,2304,384]{2,1,0:T(8,128)(2,1)} %w_ref.3, ...), custom_call_target="tpu_custom_call" | custom-call | bytes 6659328 | tf_op jit(solution)/shard_map/layer0/pallas_call | solution.py:541
  52.3 0.7 %dynamic-slice_add_fusion = f32[4,48]{1,0:T(4,128)} fusion(f32[4,48]{1,0:T(4,128)S(1)} %get-tuple-element.60, f32[4,768]{1,0:T(4,128)S(1)} %get-tuple-element.61, s32[]{:T(128)S(6)} %select_n.7), kind=kLoop, calls=%fused_computation.18 | loop fusion | flops 192 | bytes 2308 | tf_op jit(solution)/shard_map/add | solution.py:688
  53.0 0.8 %collective-permute-done.10.got_ref = bf16[192,384]{1,0:T(8,128)(2,1)S(1)} collective-permute-done((bf16[192,384]{1,0:T(8,128)(2,1)S(1)}, bf16[192,384]{1,0:T(8,128)(2,1)S(1)}, u32[]{:S(2)}, u32[]{:S(2)}) %collective-permute-start.10) | collective-permute-done | bytes 147488 | tf_op jit(solution)/shard_map/ppermute | solution.py:661
  53.8 0.7 %finish.1 = (f32[3,144,384]{2,1,0:T(8,128)}, f32[3,48,384]{2,1,0:T(8,128)}) custom-call(bf16[192,384]{1,0:T(8,128)(2,1)S(1)} %collective-permute-done.10.got_ref, f32[3,144,384]{2,1,0:T(8,128)} %get-tuple-element.56._, f32[3,48,384]{2,1,0:T(8,128)} %get-tuple-element.57.__), custom_call_target="tpu_custom_call", output_to_operand_aliasing={{0}: (1, {}), {1}: (2, {})} | custom-call | bytes 1916928 | tf_op jit(solution)/shard_map/finish/pallas_call | solution.py:541
  (1 shorter events, 0.0 us)
Async XLA Ops:
  0.6 17.9 %collective-permute-start = (bf16[176,768]{1,0:T(8,128)(2,1)}, bf16[176,768]{1,0:T(8,128)(2,1)S(1)}, u32[]{:S(2)}, u32[]{:S(2)}) collective-permute-start(bf16[176,768]{1,0:T(8,128)(2,1)} %bitcast.4), channel_id=1, source_target_pairs={{0,16},{2,18},{4,20},{6,22},{8,24},{10,26},{12,28},{14,30},{16,0},... | collective-permute-start | bytes 811016 | tf_op jit(solution)/shard_map/ppermute | solution.py:572
  6.0 12.5 %all-to-all-start = ((s32[16,1,176]{2,1,0:T(1,128)}), s32[16,1,176]{2,1,0:T(1,128)S(1)}, u32[]{:S(2)}, u32[]{:S(2)}) async-start(s32[16,1,176]{2,1,0:T(1,128)} %spread.1), calls=%async_computation | async-start | bytes 32768 | tf_op jit(solution)/shard_map/all_to_all | solution.py:574
  9.9 8.6 %copy-start = (bf16[1,176,768]{2,1,0:T(8,128)(2,1)S(1)}, bf16[1,176,768]{2,1,0:T(8,128)(2,1)}, u32[]{:S(2)}) copy-start(bf16[1,176,768]{2,1,0:T(8,128)(2,1)} %param.9) | copy-start | bytes 811012
  14.2 0.6 %copy-start.1 = (bf16[128,384]{1,0:T(8,128)(2,1)}, bf16[128,384]{1,0:T(8,128)(2,1)S(1)}, u32[]{:S(2)}) copy-start(bf16[128,384]{1,0:T(8,128)(2,1)S(1)} %get-tuple-element.55.act0_ref) | copy-start | bytes 294916
  25.4 3.0 %collective-permute-start.1 = (bf16[1536,384]{1,0:T(8,128)(2,1)S(1)}, bf16[1536,384]{1,0:T(8,128)(2,1)S(1)}, u32[]{:S(2)}, u32[]{:S(2)}) collective-permute-start(bf16[1536,384]{1,0:T(8,128)(2,1)S(1)} %get-tuple-element.37), channel_id=1, source_target_pairs={{0,2},{2,0},{4,6},{6,4},{8,10},{10,8},{12,14},{14,12},{16,18},{18,... | collective-permute-start | bytes 3538952 | tf_op jit(solution)/shard_map/ppermute | solution.py:629
  25.6 1.8 %copy-start.3 = (bf16[4,768]{1,0:T(4,128)(2,1)S(1)}, bf16[4,768]{1,0:T(4,128)(2,1)}, u32[]{:S(2)}) copy-start(bf16[4,768]{1,0:T(4,128)(2,1)} %embed_ref.3) | copy-start | bytes 18436
  27.0 1.5 %collective-permute-start.2 = (bf16[80,384]{1,0:T(8,128)(2,1)S(1)}, bf16[80,384]{1,0:T(8,128)(2,1)S(1)}, u32[]{:S(2)}, u32[]{:S(2)}) collective-permute-start(bf16[80,384]{1,0:T(8,128)(2,1)S(1)} %get-tuple-element.43), channel_id=1, source_target_pairs={{0,2},{2,0},{4,6},{6,4},{8,10},{10,8},{12,14},{14,12},{16,18},{18,... | collective-permute-start | bytes 184328 | tf_op jit(solution)/shard_map/ppermute | solution.py:639
  28.4 21.5 %copy-start.2 = (bf16[128,384]{1,0:T(8,128)(2,1)S(1)}, bf16[128,384]{1,0:T(8,128)(2,1)}, u32[]{:S(2)}) copy-start(bf16[128,384]{1,0:T(8,128)(2,1)} %copy-done.1) | copy-start | bytes 294916
  28.7 9.2 %collective-permute-start.3 = (bf16[224,384]{1,0:T(8,128)(2,1)S(1)}, bf16[224,384]{1,0:T(8,128)(2,1)S(1)}, u32[]{:S(2)}, u32[]{:S(2)}) collective-permute-start(bf16[224,384]{1,0:T(8,128)(2,1)S(1)} %get-tuple-element.45), channel_id=1, source_target_pairs={{0,13},{1,12},{2,15},{3,14},{4,9},{5,8},{6,11},{7,10},{8,5},{9,4},... | collective-permute-start | bytes 516104 | tf_op jit(solution)/shard_map/ppermute | solution.py:654
  30.4 11.3 %collective-permute-start.4 = (bf16[224,384]{1,0:T(8,128)(2,1)S(1)}, bf16[224,384]{1,0:T(8,128)(2,1)S(1)}, u32[]{:S(2)}, u32[]{:S(2)}) collective-permute-start(bf16[224,384]{1,0:T(8,128)(2,1)S(1)} %get-tuple-element.46), channel_id=1, source_target_pairs={{0,12},{1,13},{2,14},{3,15},{4,8},{5,9},{6,10},{7,11},{8,4},{9,5},... | collective-permute-start | bytes 516104 | tf_op jit(solution)/shard_map/ppermute | solution.py:654
  32.6 10.0 %collective-permute-start.5 = (bf16[224,384]{1,0:T(8,128)(2,1)S(1)}, bf16[224,384]{1,0:T(8,128)(2,1)S(1)}, u32[]{:S(2)}, u32[]{:S(2)}) collective-permute-start(bf16[224,384]{1,0:T(8,128)(2,1)S(1)} %get-tuple-element.47), channel_id=1, source_target_pairs={{0,1},{1,0},{2,3},{3,2},{4,5},{5,4},{6,7},{7,6},{8,9},{9,8},{10,11... | collective-permute-start | bytes 516104 | tf_op jit(solution)/shard_map/ppermute | solution.py:654
  33.1 12.2 %collective-permute-start.6 = (bf16[224,384]{1,0:T(8,128)(2,1)S(1)}, bf16[224,384]{1,0:T(8,128)(2,1)S(1)}, u32[]{:S(2)}, u32[]{:S(2)}) collective-permute-start(bf16[224,384]{1,0:T(8,128)(2,1)S(1)} %get-tuple-element.48), channel_id=1, source_target_pairs={{0,9},{1,8},{2,11},{3,10},{4,13},{5,12},{6,15},{7,14},{8,1},{9,0},... | collective-permute-start | bytes 516104 | tf_op jit(solution)/shard_map/ppermute | solution.py:654
  34.6 11.7 %collective-permute-start.7 = (bf16[224,384]{1,0:T(8,128)(2,1)S(1)}, bf16[224,384]{1,0:T(8,128)(2,1)S(1)}, u32[]{:S(2)}, u32[]{:S(2)}) collective-permute-start(bf16[224,384]{1,0:T(8,128)(2,1)S(1)} %get-tuple-element.49), channel_id=1, source_target_pairs={{0,4},{1,5},{2,6},{3,7},{4,0},{5,1},{6,2},{7,3},{8,12},{9,13},{10,... | collective-permute-start | bytes 516104 | tf_op jit(solution)/shard_map/ppermute | solution.py:654
  37.9 10.3 %collective-permute-start.8 = (bf16[224,384]{1,0:T(8,128)(2,1)S(1)}, bf16[224,384]{1,0:T(8,128)(2,1)S(1)}, u32[]{:S(2)}, u32[]{:S(2)}) collective-permute-start(bf16[224,384]{1,0:T(8,128)(2,1)S(1)} %get-tuple-element.50), channel_id=1, source_target_pairs={{0,5},{1,4},{2,7},{3,6},{4,1},{5,0},{6,3},{7,2},{8,13},{9,12},{10,... | collective-permute-start | bytes 516104 | tf_op jit(solution)/shard_map/ppermute | solution.py:654
  41.7 6.5 %collective-permute-start.9 = (bf16[224,384]{1,0:T(8,128)(2,1)S(1)}, bf16[224,384]{1,0:T(8,128)(2,1)S(1)}, u32[]{:S(2)}, u32[]{:S(2)}) collective-permute-start(bf16[224,384]{1,0:T(8,128)(2,1)S(1)} %get-tuple-element.51), channel_id=1, source_target_pairs={{0,8},{1,9},{2,10},{3,11},{4,12},{5,13},{6,14},{7,15},{8,0},{9,1},... | collective-permute-start | bytes 516104 | tf_op jit(solution)/shard_map/ppermute | solution.py:654
  48.4 5.4 %collective-permute-start.10 = (bf16[192,384]{1,0:T(8,128)(2,1)S(1)}, bf16[192,384]{1,0:T(8,128)(2,1)S(1)}, u32[]{:S(2)}, u32[]{:S(2)}) collective-permute-start(bf16[192,384]{1,0:T(8,128)(2,1)S(1)} %get-tuple-element.52), channel_id=1, source_target_pairs={{0,1},{1,0},{2,3},{3,2},{4,5},{5,4},{6,7},{7,6},{8,9},{9,8},{10,11... | collective-permute-start | bytes 442376 | tf_op jit(solution)/shard_map/ppermute | solution.py:661

commit v7 on v6

--- a/solution.py
+++ b/solution.py
@@ -241,9 +241,10 @@
     return (v * norm_scale(v)).astype(BF16)
 
 
-def spread_kernel(bases_ref, out_ref):
-    for i in range(out_ref.shape[0]):
-        out_ref[i] = bases_ref[...]
+def spread_kernel(bases_ref, out_ref, sems):
+    copies = [fetch(bases_ref, out_ref.at[i], sems.at[i]) for i in range(out_ref.shape[0])]
+    for copy in copies:
+        copy.wait()
 
 
 def fetch(source, target, sem):
@@ -313,9 +314,9 @@
 
 def main_kernel(
     crow, prow, bases_ref, own_ref, far_ref, w_ref, p_ref, w2_ref, table_ref,
-    features_ref, mine_ref, other_ref, h_ref, c_ref, w1_ref, p0_ref,
+    features_ref, conv_ref, point_ref, other_ref, h_ref, c_ref, w1_ref, p0_ref,
     hot_ref, stream_ref, normed_ref, act1_ref, act2_ref, slope1_ref, slope2_ref,
-    cot_ref, grad_ref, back_ref, conv_ref, point_ref, ntab_ref, pt_ref, sent_ref, sems,
+    cot_ref, grad_ref, back_ref, ntab_ref, pt_ref, sent_ref, sems,
 ):
     n, _, rb = bases_ref.shape
     rows, width = stream_ref.shape
@@ -422,15 +423,14 @@
     point_ref[0] = mm_tn(back_ref[:, columns], act1_ref[...])
     point_ref[1] = mm_tn(cot_ref[:, columns], act2_ref[...])
     part = crow + prow
-    for target, side in ((mine_ref, core), (other_ref, 1 - core)):
-        for m in range(STRIDE // 2):
-            tile = 2 * m + side
-            crows = pl.ds(pl.multiple_of(tile * crow, 16), crow)
-            prows = pl.ds(pl.multiple_of(tile * prow, 16), prow)
-            for layer in range(2):
-                at = (2 * m + layer) * part
-                target[at : at + crow, :] = conv_ref[layer, crows, :].astype(target.dtype)
-                target[at + crow : at + part, :] = point_ref[layer, prows, :].astype(target.dtype)
+    for m in range(STRIDE // 2):
+        tile = 2 * m + 1 - core
+        crows = pl.ds(pl.multiple_of(tile * crow, 16), crow)
+        prows = pl.ds(pl.multiple_of(tile * prow, 16), prow)
+        for layer in range(2):
+            at = (2 * m + layer) * part
+            other_ref[at : at + crow, :] = conv_ref[layer, crows, :].astype(BF16)
+            other_ref[at + crow : at + part, :] = point_ref[layer, prows, :].astype(BF16)
     for copy in (copy_features, copy_w1, copy_p0):
         copy.wait()
 
@@ -463,15 +463,23 @@
         target[8 * STRIDE : 8 * STRIDE + 16, :] = g.astype(target.dtype)
 
 
-def message_kernel(part, mine_ref, other_ref, mine_small_ref, other_small_ref, *out_refs):
+def message_kernel(
+    crow, prow, conv_ref, point_ref, other_ref, mine_small_ref, other_small_ref, *out_refs
+):
     k, x = lax.axis_index("seq"), lax.axis_index("dp")
-    m = (k % STRIDE) // 2
-    end = 8 * STRIDE
+    m, core = (k % STRIDE) // 2, k % 2
+    part, end = crow + prow, 8 * STRIDE
     g = mine_small_ref[end:, :] + other_small_ref[end:, :].astype(F32)
     for mask, out_ref in enumerate(out_refs):
         target, layer = m ^ (mask // 2), x ^ (mask % 2)
-        at = pl.ds(pl.multiple_of((2 * target + layer) * part, 16), part)
-        out_ref[:part, :] = (mine_ref[at, :] + other_ref[at, :].astype(F32)).astype(out_ref.dtype)
+        tile = 2 * target + core
+        at = (2 * target + layer) * part
+        mine = conv_ref[layer, pl.ds(pl.multiple_of(tile * crow, 16), crow), :]
+        got = other_ref[pl.ds(pl.multiple_of(at, 16), crow), :].astype(F32)
+        out_ref[:crow, :] = (mine + got).astype(out_ref.dtype)
+        mine = point_ref[layer, pl.ds(pl.multiple_of(tile * prow, 16), prow), :]
+        got = other_ref[pl.ds(pl.multiple_of(at + crow, 16), prow), :].astype(F32)
+        out_ref[crow:part, :] = (mine + got).astype(out_ref.dtype)
         at = pl.ds(pl.multiple_of(target * 16, 16), 16)
         small = mine_small_ref[at, :] + other_small_ref[at, :].astype(F32)
         out_ref[part : part + 16, :] = small.astype(out_ref.dtype)
@@ -570,7 +578,15 @@
 
     own = cotangent[0]
     far = lax.ppermute(own, "seq", [(s, (s + STRIDE) % n) for s in range(n)])
-    (copies,) = call(spread_kernel, [near((n, 1, rb), jnp.int32)], bases, far=(0,), whole=(0,), name="spread")
+    (copies,) = call(
+        spread_kernel,
+        [shape((n, 1, rb), jnp.int32)],
+        bases,
+        far=(0,),
+        away=(0,),
+        scratch=[pltpu.SemaphoreType.DMA((n,))],
+        name="spread",
+    )
     gathered = lax.all_to_all(copies, "seq", 0, 0, tiled=True)
 
     taps = pltpu.VMEM((3 * width, mid), BF16)
@@ -589,11 +605,12 @@
         flops=4 * CLASSES * 3 * width * mid,
         name="tables",
     )
-    features, mine, other, h, c, w1, p0 = call(
+    features, conv, points, other, h, c, w1, p0 = call(
         lambda *refs: main_kernel(crow, prow, *refs),
         [
             shape((rb, width), F32),
-            near((STRIDE * part, mid), F32),
+            near((2, STRIDE * crow, mid), F32),
+            near((2, STRIDE * prow, mid), F32),
             near((STRIDE * part, mid), BF16),
             near((3 * CLASSES, mid), BF16),
             near((CLASSES, width), F32),
@@ -613,8 +630,6 @@
             pltpu.VMEM((rows, width), BF16),
             pltpu.VMEM((rows, mid), BF16),
             pltpu.VMEM((rows, width), BF16),
-            pltpu.VMEM((2, STRIDE * crow, mid), F32),
-            pltpu.VMEM((2, STRIDE * prow, mid), F32),
             pltpu.VMEM((CLASSES, width), BF16),
             pltpu.VMEM((2, mid, width), BF16),
             pltpu.VMEM((rb, width), F32),
@@ -639,9 +654,9 @@
     got_small = lax.ppermute(other_small, "seq", swap)
     peers = STRIDE // 2 * dp
     pieces = call(
-        lambda *refs: message_kernel(part, *refs),
+        lambda *refs: message_kernel(crow, prow, *refs),
         [shape((part + 32, mid), F32 if i == 0 else BF16) for i in range(peers)],
-        mine, got, mine_small, got_small,
+        conv, points, got, mine_small, got_small,
         name="messages",
     )
     arrived = []

time: 54.8 us -> 54.9 us (level)
  Pallas kernels: 17.3 us -> 17.9 us
    pallas_call x8, Pallas kernels: 17.3 us -> 17.9 us  [call(): pl.pallas_call(kernel, out_shape=outs, in_specs=[pl.BlockSpec(memory_spac...]
  transfers between devices with their start and end apart: 12 -> 12, of which waited for: 8 -> 8; matrix products, arithmetic and copies ran while one was open for 2% -> 2% of each run, Pallas kernels for 17% -> 18%
where the time goes in v7:
time: 54.9 us; the launch traced here: 54.7 us
  starting transfers between devices  19.7 us (36%)
  Pallas kernels  17.9 us (33%)
  waiting for transfers between devices  14.6 us (27%)
  other arithmetic  0.97 us (2%)
  local copies, waits for them, and re-layouts  0.77 us (1%)
  between operations  0.72 us (1%)
    pallas_call x8, Pallas kernels, call(): pl.pallas_call(kernel, out_shape=outs, in_specs=[pl.BlockSpec(memory_spac...  17.9 us
    ppermute x7, waiting for transfers between devices, on_device(): arrived.append(lax.ppermute(pieces[mask], ('seq', 'dp'), route))  9.72 us
    ppermute x7, starting transfers between devices, on_device(): arrived.append(lax.ppermute(pieces[mask], ('seq', 'dp'), route))  9.54 us
    ppermute x1, starting transfers between devices, on_device(): far = lax.ppermute(own, 'seq', [(s, (s + STRIDE) % n) for s in range(n)])  4.1 us
    all_to_all x1, starting transfers between devices, on_device(): gathered = lax.all_to_all(copies, 'seq', 0, 0, tiled=True)  3.92 us
    all_to_all x1, waiting for transfers between devices, on_device(): gathered = lax.all_to_all(copies, 'seq', 0, 0, tiled=True)  3.19 us
    ppermute x1, starting transfers between devices, on_device(): swapped = lax.ppermute(send, 'dp', [(d, d ^ 1) for d in range(dp)])  1.57 us
  transfers between devices with their start and end apart: 12, of which 8 were waited for; matrix products, arithmetic and copies ran while one was open for 2% of the time, Pallas kernels for 18%

profile of v7, /device:TPU:0, one launch (start us, length us, event | category | flops | bytes accessed | tf_op | source)
XLA Modules:
  0.0 54.7 jit_solution(1818672489128210339)
XLA Ops:
  0.6 4.1 %collective-permute-start = (bf16[176,768]{1,0:T(8,128)(2,1)}, bf16[176,768]{1,0:T(8,128)(2,1)S(1)}, u32[]{:S(2)}, u32[]{:S(2)}) collective-permute-start(bf16[176,768]{1,0:T(8,128)(2,1)} %bitcast.4), channel_id=1, source_target_pairs={{0,16},{2,18},{4,20},{6,22},{8,24},{10,26},{12,28},{14,30},{16,0},... | collective-permute-start | bytes 811016 | tf_op jit(solution)/shard_map/ppermute | solution.py:580
  4.7 1.8 %spread.1 = s32[16,1,176]{2,1,0:T(1,128)} custom-call(s32[1,176]{1,0:T(1,128)} %bases_ref.1), custom_call_target="tpu_custom_call" | custom-call | bytes 11968 | tf_op jit(solution)/shard_map/spread/pallas_call | solution.py:549
  6.5 3.9 %all-to-all-start = ((s32[16,1,176]{2,1,0:T(1,128)}), s32[16,1,176]{2,1,0:T(1,128)S(1)}, u32[]{:S(2)}, u32[]{:S(2)}) async-start(s32[16,1,176]{2,1,0:T(1,128)} %spread.1), calls=%async_computation | async-start | bytes 32768 | tf_op jit(solution)/shard_map/all_to_all | solution.py:590
  10.5 0.0 copy-start
  10.5 4.2 %tables.1 = (bf16[128,384]{1,0:T(8,128)(2,1)S(1)}, f32[128,2304]{1,0:T(8,128)S(1)}, bf16[2304,384]{1,0:T(8,128)(2,1)S(1)}) custom-call(bf16[4,768]{1,0:T(4,128)(2,1)} %embed_ref.3, bf16[3,2304,384]{2,1,0:T(8,128)(2,1)} %w_ref.3, bf16[3,384,768]{2,1,0:T(8,128)(2,1)} %refs_4_.1), custom_call_target="tpu_custom_call" | custom-call | flops 452984832 | bytes 10131456 | tf_op jit(solution)/shard_map/tables/pallas_call | solution.py:549
  14.7 0.0 copy-start.1
  14.7 0.6 %copy-done.1 = bf16[128,384]{1,0:T(8,128)(2,1)} copy-done((bf16[128,384]{1,0:T(8,128)(2,1)}, bf16[128,384]{1,0:T(8,128)(2,1)S(1)}, u32[]{:S(2)}) %copy-start.1) | copy-done | bytes 98328
  15.3 3.2 %all-to-all-done.refs_0_ = s32[16,1,176]{2,1,0:T(1,128)S(1)} async-done(((s32[16,1,176]{2,1,0:T(1,128)}), s32[16,1,176]{2,1,0:T(1,128)S(1)}, u32[]{:S(2)}, u32[]{:S(2)}) %all-to-all-start) | async-done | bytes 11296 | tf_op jit(solution)/shard_map/all_to_all | solution.py:590
  18.5 0.0 collective-permute-done.refs_2_
  18.5 0.0 copy-done
  18.5 7.0 %tower.1 = (f32[176,768]{1,0:T(8,128)}, f32[2,1152,384]{2,1,0:T(8,128)S(1)}, f32[2,384,384]{2,1,0:T(8,128)S(1)}, bf16[1536,384]{1,0:T(8,128)(2,1)S(1)}, bf16[384...) custom-call(s32[16,1,176]{2,1,0:T(1,128)S(1)} %all-to-all-done.refs_, ...), custom_call_target="tpu_custom_call" | custom-call | flops 2802843648 | bytes 20065280 | tf_op jit(solution)/shard_map/tower/pallas_call | solution.py:549
  25.5 0.2 collective-permute-start.1
  25.7 0.0 copy-start.3
  25.7 1.4 %classes.1 = (f32[80,384]{1,0:T(8,128)S(1)}, bf16[80,384]{1,0:T(8,128)(2,1)S(1)}) custom-call(bf16[384,384]{1,0:T(8,128)(2,1)S(1)} %get-tuple-element.40.refs_0_, f32[128,768]{1,0:T(8,128)S(1)} %get-tuple-element.41.refs_1_, f32[128,2304]{1,0:T(8,128)S(1)} %get-tuple-element.35.refs_6_.refs_2_, bf16[2304,384]{1,0:T(8,128)(2,1)S(1)} %get-tuple-element.42.refs_3_, ...), custom_call_target="tpu_custom_call" | custom-call | flops 452984832 | bytes 4411392 | tf_op jit(solution)/shard_map/classes/pallas_call | solution.py:549
  27.1 0.4 collective-permute-start.2
  27.5 0.0 copy-done.3
  27.5 0.1 fusion.8
  27.6 0.9 %collective-permute-done.2.refs_4_ = bf16[80,384]{1,0:T(8,128)(2,1)S(1)} collective-permute-done((bf16[80,384]{1,0:T(8,128)(2,1)S(1)}, bf16[80,384]{1,0:T(8,128)(2,1)S(1)}, u32[]{:S(2)}, u32[]{:S(2)}) %collective-permute-start.2) | collective-permute-done | bytes 61472 | tf_op jit(solution)/shard_map/ppermute | solution.py:654
  28.5 0.0 collective-permute-done.1.refs_2_
  28.5 0.0 copy-start.2
  28.5 0.3 messages.1
  28.8 1.7 %collective-permute-start.3 = (bf16[224,384]{1,0:T(8,128)(2,1)S(1)}, bf16[224,384]{1,0:T(8,128)(2,1)S(1)}, u32[]{:S(2)}, u32[]{:S(2)}) collective-permute-start(bf16[224,384]{1,0:T(8,128)(2,1)S(1)} %get-tuple-element.47), channel_id=1, source_target_pairs={{0,13},{1,12},{2,15},{3,14},{4,9},{5,8},{6,11},{7,10},{8,5},{9,4},... | collective-permute-start | bytes 516104 | tf_op jit(solution)/shard_map/ppermute | solution.py:669
  30.5 2.2 %collective-permute-start.4 = (bf16[224,384]{1,0:T(8,128)(2,1)S(1)}, bf16[224,384]{1,0:T(8,128)(2,1)S(1)}, u32[]{:S(2)}, u32[]{:S(2)}) collective-permute-start(bf16[224,384]{1,0:T(8,128)(2,1)S(1)} %get-tuple-element.48), channel_id=1, source_target_pairs={{0,12},{1,13},{2,14},{3,15},{4,8},{5,9},{6,10},{7,11},{8,4},{9,5},... | collective-permute-start | bytes 516104 | tf_op jit(solution)/shard_map/ppermute | solution.py:669
  32.7 0.5 collective-permute-start.5
  33.2 1.5 %collective-permute-start.6 = (bf16[224,384]{1,0:T(8,128)(2,1)S(1)}, bf16[224,384]{1,0:T(8,128)(2,1)S(1)}, u32[]{:S(2)}, u32[]{:S(2)}) collective-permute-start(bf16[224,384]{1,0:T(8,128)(2,1)S(1)} %get-tuple-element.50), channel_id=1, source_target_pairs={{0,9},{1,8},{2,11},{3,10},{4,13},{5,12},{6,15},{7,14},{8,1},{9,0},... | collective-permute-start | bytes 516104 | tf_op jit(solution)/shard_map/ppermute | solution.py:669
  34.8 0.7 %collective-permute-start.7 = (bf16[224,384]{1,0:T(8,128)(2,1)S(1)}, bf16[224,384]{1,0:T(8,128)(2,1)S(1)}, u32[]{:S(2)}, u32[]{:S(2)}) collective-permute-start(bf16[224,384]{1,0:T(8,128)(2,1)S(1)} %get-tuple-element.51), channel_id=1, source_target_pairs={{0,4},{1,5},{2,6},{3,7},{4,0},{5,1},{6,2},{7,3},{8,12},{9,13},{10,... | collective-permute-start | bytes 516104 | tf_op jit(solution)/shard_map/ppermute | solution.py:669
  35.5 2.5 %collective-permute-done.3.refs_0_ = bf16[224,384]{1,0:T(8,128)(2,1)S(1)} collective-permute-done((bf16[224,384]{1,0:T(8,128)(2,1)S(1)}, bf16[224,384]{1,0:T(8,128)(2,1)S(1)}, u32[]{:S(2)}, u32[]{:S(2)}) %collective-permute-start.3) | collective-permute-done | bytes 172064 | tf_op jit(solution)/shard_map/ppermute | solution.py:669
  38.0 2.3 %collective-permute-start.8 = (bf16[224,384]{1,0:T(8,128)(2,1)S(1)}, bf16[224,384]{1,0:T(8,128)(2,1)S(1)}, u32[]{:S(2)}, u32[]{:S(2)}) collective-permute-start(bf16[224,384]{1,0:T(8,128)(2,1)S(1)} %get-tuple-element.52), channel_id=1, source_target_pairs={{0,5},{1,4},{2,7},{3,6},{4,1},{5,0},{6,3},{7,2},{8,13},{9,12},{10,... | collective-permute-start | bytes 516104 | tf_op jit(solution)/shard_map/ppermute | solution.py:669
  40.3 1.6 %collective-permute-done.4.refs_1_ = bf16[224,384]{1,0:T(8,128)(2,1)S(1)} collective-permute-done((bf16[224,384]{1,0:T(8,128)(2,1)S(1)}, bf16[224,384]{1,0:T(8,128)(2,1)S(1)}, u32[]{:S(2)}, u32[]{:S(2)}) %collective-permute-start.4) | collective-permute-done | bytes 172064 | tf_op jit(solution)/shard_map/ppermute | solution.py:669
  41.9 0.6 %collective-permute-start.9 = (bf16[224,384]{1,0:T(8,128)(2,1)S(1)}, bf16[224,384]{1,0:T(8,128)(2,1)S(1)}, u32[]{:S(2)}, u32[]{:S(2)}) collective-permute-start(bf16[224,384]{1,0:T(8,128)(2,1)S(1)} %get-tuple-element.53), channel_id=1, source_target_pairs={{0,8},{1,9},{2,10},{3,11},{4,12},{5,13},{6,14},{7,15},{8,0},{9,1},... | collective-permute-start | bytes 516104 | tf_op jit(solution)/shard_map/ppermute | solution.py:669
  42.5 0.1 fusion.9
  42.5 0.1 fusion.11
  42.6 0.1 copy.15
  42.8 0.0 collective-permute-done.5.refs_2_
  42.8 2.7 %collective-permute-done.6.refs_3_ = bf16[224,384]{1,0:T(8,128)(2,1)S(1)} collective-permute-done((bf16[224,384]{1,0:T(8,128)(2,1)S(1)}, bf16[224,384]{1,0:T(8,128)(2,1)S(1)}, u32[]{:S(2)}, u32[]{:S(2)}) %collective-permute-start.6) | collective-permute-done | bytes 172064 | tf_op jit(solution)/shard_map/ppermute | solution.py:669
  45.5 1.0 %collective-permute-done.7.refs_4_ = bf16[224,384]{1,0:T(8,128)(2,1)S(1)} collective-permute-done((bf16[224,384]{1,0:T(8,128)(2,1)S(1)}, bf16[224,384]{1,0:T(8,128)(2,1)S(1)}, u32[]{:S(2)}, u32[]{:S(2)}) %collective-permute-start.7) | collective-permute-done | bytes 172064 | tf_op jit(solution)/shard_map/ppermute | solution.py:669
  46.5 1.9 %collective-permute-done.8.refs_5_ = bf16[224,384]{1,0:T(8,128)(2,1)S(1)} collective-permute-done((bf16[224,384]{1,0:T(8,128)(2,1)S(1)}, bf16[224,384]{1,0:T(8,128)(2,1)S(1)}, u32[]{:S(2)}, u32[]{:S(2)}) %collective-permute-start.8) | collective-permute-done | bytes 172064 | tf_op jit(solution)/shard_map/ppermute | solution.py:669
  48.4 0.0 collective-permute-done.9.refs_6_
  48.4 0.2 sums.1
  48.6 1.6 %collective-permute-start.10 = (bf16[192,384]{1,0:T(8,128)(2,1)S(1)}, bf16[192,384]{1,0:T(8,128)(2,1)S(1)}, u32[]{:S(2)}, u32[]{:S(2)}) collective-permute-start(bf16[192,384]{1,0:T(8,128)(2,1)S(1)} %get-tuple-element.54), channel_id=1, source_target_pairs={{0,1},{1,0},{2,3},{3,2},{4,5},{5,4},{6,7},{7,6},{8,9},{9,8},{10,11... | collective-permute-start | bytes 442376 | tf_op jit(solution)/shard_map/ppermute | solution.py:676
  50.1 0.0 copy-done.2
  50.1 2.4 %layer0.1 = (f32[3,144,384]{2,1,0:T(8,128)}, f32[3,48,384]{2,1,0:T(8,128)}, f32[4,768]{1,0:T(4,128)S(1)}, f32[4,48]{1,0:T(4,128)S(1)}) custom-call(f32[32,384]{1,0:T(8,128)S(1)} %get-tuple-element.55.rest_ref, f32[192,384]{1,0:T(8,128)S(1)} %get-tuple-element.56.total_ref, bf16[4,768]{1,0:T(4,128)(2,1)S(1)} %copy-done.3, bf16[3,2304,384]{2,1,0:T(8,128)(2,1)} %w_ref.3, ...), custom_call_target="tpu_custom_call" | custom-call | bytes 6659328 | tf_op jit(solution)/shard_map/layer0/pallas_call | solution.py:549
  52.5 0.7 %dynamic-slice_add_fusion = f32[4,48]{1,0:T(4,128)} fusion(f32[4,48]{1,0:T(4,128)S(1)} %get-tuple-element.62, f32[4,768]{1,0:T(4,128)S(1)} %get-tuple-element.63, s32[]{:T(128)S(6)} %select_n.7), kind=kLoop, calls=%fused_computation.18 | loop fusion | flops 192 | bytes 2308 | tf_op jit(solution)/shard_map/add | solution.py:703
  53.2 0.8 %collective-permute-done.10.got_ref = bf16[192,384]{1,0:T(8,128)(2,1)S(1)} collective-permute-done((bf16[192,384]{1,0:T(8,128)(2,1)S(1)}, bf16[192,384]{1,0:T(8,128)(2,1)S(1)}, u32[]{:S(2)}, u32[]{:S(2)}) %collective-permute-start.10) | collective-permute-done | bytes 147488 | tf_op jit(solution)/shard_map/ppermute | solution.py:676
  53.9 0.7 %finish.1 = (f32[3,144,384]{2,1,0:T(8,128)}, f32[3,48,384]{2,1,0:T(8,128)}) custom-call(bf16[192,384]{1,0:T(8,128)(2,1)S(1)} %collective-permute-done.10.got_ref, f32[3,144,384]{2,1,0:T(8,128)} %get-tuple-element.58._, f32[3,48,384]{2,1,0:T(8,128)} %get-tuple-element.59.__), custom_call_target="tpu_custom_call", output_to_operand_aliasing={{0}: (1, {}), {1}: (2, {})} | custom-call | bytes 1916928 | tf_op jit(solution)/shard_map/finish/pallas_call | solution.py:549
  (1 shorter events, 0.0 us)
Async XLA Ops:
  0.6 17.9 %collective-permute-start = (bf16[176,768]{1,0:T(8,128)(2,1)}, bf16[176,768]{1,0:T(8,128)(2,1)S(1)}, u32[]{:S(2)}, u32[]{:S(2)}) collective-permute-start(bf16[176,768]{1,0:T(8,128)(2,1)} %bitcast.4), channel_id=1, source_target_pairs={{0,16},{2,18},{4,20},{6,22},{8,24},{10,26},{12,28},{14,30},{16,0},... | collective-permute-start | bytes 811016 | tf_op jit(solution)/shard_map/ppermute | solution.py:580
  6.5 12.0 %all-to-all-start = ((s32[16,1,176]{2,1,0:T(1,128)}), s32[16,1,176]{2,1,0:T(1,128)S(1)}, u32[]{:S(2)}, u32[]{:S(2)}) async-start(s32[16,1,176]{2,1,0:T(1,128)} %spread.1), calls=%async_computation | async-start | bytes 32768 | tf_op jit(solution)/shard_map/all_to_all | solution.py:590
  10.5 8.0 %copy-start = (bf16[1,176,768]{2,1,0:T(8,128)(2,1)S(1)}, bf16[1,176,768]{2,1,0:T(8,128)(2,1)}, u32[]{:S(2)}) copy-start(bf16[1,176,768]{2,1,0:T(8,128)(2,1)} %param.9) | copy-start | bytes 811012
  14.7 0.6 %copy-start.1 = (bf16[128,384]{1,0:T(8,128)(2,1)}, bf16[128,384]{1,0:T(8,128)(2,1)S(1)}, u32[]{:S(2)}) copy-start(bf16[128,384]{1,0:T(8,128)(2,1)S(1)} %get-tuple-element.57.act0_ref) | copy-start | bytes 294916
  25.5 3.0 %collective-permute-start.1 = (bf16[1536,384]{1,0:T(8,128)(2,1)S(1)}, bf16[1536,384]{1,0:T(8,128)(2,1)S(1)}, u32[]{:S(2)}, u32[]{:S(2)}) collective-permute-start(bf16[1536,384]{1,0:T(8,128)(2,1)S(1)} %get-tuple-element.39), channel_id=1, source_target_pairs={{0,2},{2,0},{4,6},{6,4},{8,10},{10,8},{12,14},{14,12},{16,18},{18,... | collective-permute-start | bytes 3538952 | tf_op jit(solution)/shard_map/ppermute | solution.py:644
  25.7 1.8 %copy-start.3 = (bf16[4,768]{1,0:T(4,128)(2,1)S(1)}, bf16[4,768]{1,0:T(4,128)(2,1)}, u32[]{:S(2)}) copy-start(bf16[4,768]{1,0:T(4,128)(2,1)} %embed_ref.3) | copy-start | bytes 18436
  27.1 1.4 %collective-permute-start.2 = (bf16[80,384]{1,0:T(8,128)(2,1)S(1)}, bf16[80,384]{1,0:T(8,128)(2,1)S(1)}, u32[]{:S(2)}, u32[]{:S(2)}) collective-permute-start(bf16[80,384]{1,0:T(8,128)(2,1)S(1)} %get-tuple-element.45), channel_id=1, source_target_pairs={{0,2},{2,0},{4,6},{6,4},{8,10},{10,8},{12,14},{14,12},{16,18},{18,... | collective-permute-start | bytes 184328 | tf_op jit(solution)/shard_map/ppermute | solution.py:654
  28.5 21.6 %copy-start.2 = (bf16[128,384]{1,0:T(8,128)(2,1)S(1)}, bf16[128,384]{1,0:T(8,128)(2,1)}, u32[]{:S(2)}) copy-start(bf16[128,384]{1,0:T(8,128)(2,1)} %copy-done.1) | copy-start | bytes 294916
  28.8 9.2 %collective-permute-start.3 = (bf16[224,384]{1,0:T(8,128)(2,1)S(1)}, bf16[224,384]{1,0:T(8,128)(2,1)S(1)}, u32[]{:S(2)}, u32[]{:S(2)}) collective-permute-start(bf16[224,384]{1,0:T(8,128)(2,1)S(1)} %get-tuple-element.47), channel_id=1, source_target_pairs={{0,13},{1,12},{2,15},{3,14},{4,9},{5,8},{6,11},{7,10},{8,5},{9,4},... | collective-permute-start | bytes 516104 | tf_op jit(solution)/shard_map/ppermute | solution.py:669
  30.5 11.4 %collective-permute-start.4 = (bf16[224,384]{1,0:T(8,128)(2,1)S(1)}, bf16[224,384]{1,0:T(8,128)(2,1)S(1)}, u32[]{:S(2)}, u32[]{:S(2)}) collective-permute-start(bf16[224,384]{1,0:T(8,128)(2,1)S(1)} %get-tuple-element.48), channel_id=1, source_target_pairs={{0,12},{1,13},{2,14},{3,15},{4,8},{5,9},{6,10},{7,11},{8,4},{9,5},... | collective-permute-start | bytes 516104 | tf_op jit(solution)/shard_map/ppermute | solution.py:669
  32.7 10.0 %collective-permute-start.5 = (bf16[224,384]{1,0:T(8,128)(2,1)S(1)}, bf16[224,384]{1,0:T(8,128)(2,1)S(1)}, u32[]{:S(2)}, u32[]{:S(2)}) collective-permute-start(bf16[224,384]{1,0:T(8,128)(2,1)S(1)} %get-tuple-element.49), channel_id=1, source_target_pairs={{0,1},{1,0},{2,3},{3,2},{4,5},{5,4},{6,7},{7,6},{8,9},{9,8},{10,11... | collective-permute-start | bytes 516104 | tf_op jit(solution)/shard_map/ppermute | solution.py:669
  33.2 12.2 %collective-permute-start.6 = (bf16[224,384]{1,0:T(8,128)(2,1)S(1)}, bf16[224,384]{1,0:T(8,128)(2,1)S(1)}, u32[]{:S(2)}, u32[]{:S(2)}) collective-permute-start(bf16[224,384]{1,0:T(8,128)(2,1)S(1)} %get-tuple-element.50), channel_id=1, source_target_pairs={{0,9},{1,8},{2,11},{3,10},{4,13},{5,12},{6,15},{7,14},{8,1},{9,0},... | collective-permute-start | bytes 516104 | tf_op jit(solution)/shard_map/ppermute | solution.py:669
  34.8 11.7 %collective-permute-start.7 = (bf16[224,384]{1,0:T(8,128)(2,1)S(1)}, bf16[224,384]{1,0:T(8,128)(2,1)S(1)}, u32[]{:S(2)}, u32[]{:S(2)}) collective-permute-start(bf16[224,384]{1,0:T(8,128)(2,1)S(1)} %get-tuple-element.51), channel_id=1, source_target_pairs={{0,4},{1,5},{2,6},{3,7},{4,0},{5,1},{6,2},{7,3},{8,12},{9,13},{10,... | collective-permute-start | bytes 516104 | tf_op jit(solution)/shard_map/ppermute | solution.py:669
  38.0 10.4 %collective-permute-start.8 = (bf16[224,384]{1,0:T(8,128)(2,1)S(1)}, bf16[224,384]{1,0:T(8,128)(2,1)S(1)}, u32[]{:S(2)}, u32[]{:S(2)}) collective-permute-start(bf16[224,384]{1,0:T(8,128)(2,1)S(1)} %get-tuple-element.52), channel_id=1, source_target_pairs={{0,5},{1,4},{2,7},{3,6},{4,1},{5,0},{6,3},{7,2},{8,13},{9,12},{10,... | collective-permute-start | bytes 516104 | tf_op jit(solution)/shard_map/ppermute | solution.py:669
  41.9 6.5 %collective-permute-start.9 = (bf16[224,384]{1,0:T(8,128)(2,1)S(1)}, bf16[224,384]{1,0:T(8,128)(2,1)S(1)}, u32[]{:S(2)}, u32[]{:S(2)}) collective-permute-start(bf16[224,384]{1,0:T(8,128)(2,1)S(1)} %get-tuple-element.53), channel_id=1, source_target_pairs={{0,8},{1,9},{2,10},{3,11},{4,12},{5,13},{6,14},{7,15},{8,0},{9,1},... | collective-permute-start | bytes 516104 | tf_op jit(solution)/shard_map/ppermute | solution.py:669
  48.6 5.4 %collective-permute-start.10 = (bf16[192,384]{1,0:T(8,128)(2,1)S(1)}, bf16[192,384]{1,0:T(8,128)(2,1)S(1)}, u32[]{:S(2)}, u32[]{:S(2)}) collective-permute-start(bf16[192,384]{1,0:T(8,128)(2,1)S(1)} %get-tuple-element.54), channel_id=1, source_target_pairs={{0,1},{1,0},{2,3},{3,2},{4,5},{5,4},{6,7},{7,6},{8,9},{9,8},{10,11... | collective-permute-start | bytes 442376 | tf_op jit(solution)/shard_map/ppermute | solution.py:676

commit v8 on v6

--- a/solution.py
+++ b/solution.py
@@ -12,7 +12,7 @@
 F32 = jnp.float32
 CLASSES = 128
 STRIDE = 8
-ORDER = (7, 6, 1, 5, 2, 3, 4)
+ORDER = (3, 4, 5, 2, 1, 6, 7)
 
 
 def gelu_pair(v):

time: 54.8 us -> 54.9 us (level)
  no operation moved by 1% of the time
where the time goes in v8:
time: 54.9 us; the launch traced here: 54.6 us
  starting transfers between devices  20.2 us (37%)
  Pallas kernels  17.3 us (32%)
  waiting for transfers between devices  14.7 us (27%)
  other arithmetic  0.97 us (2%)
  local copies, waits for them, and re-layouts  0.77 us (1%)
  between operations  0.72 us (1%)
    pallas_call x8, Pallas kernels, call(): pl.pallas_call(kernel, out_shape=outs, in_specs=[pl.BlockSpec(memory_spac...  17.3 us
    ppermute x7, starting transfers between devices, on_device(): arrived.append(lax.ppermute(pieces[mask], ('seq', 'dp'), route))  10.1 us
    ppermute x7, waiting for transfers between devices, on_device(): arrived.append(lax.ppermute(pieces[mask], ('seq', 'dp'), route))  9.37 us
    ppermute x1, starting transfers between devices, on_device(): far = lax.ppermute(own, 'seq', [(s, (s + STRIDE) % n) for s in range(n)])  4.1 us
    all_to_all x1, starting transfers between devices, on_device(): gathered = lax.all_to_all(copies, 'seq', 0, 0, tiled=True)  3.91 us
    all_to_all x1, waiting for transfers between devices, on_device(): gathered = lax.all_to_all(copies, 'seq', 0, 0, tiled=True)  3.72 us
    ppermute x1, starting transfers between devices, on_device(): swapped = lax.ppermute(send, 'dp', [(d, d ^ 1) for d in range(dp)])  1.53 us
  transfers between devices with their start and end apart: 12, of which 8 were waited for; matrix products, arithmetic and copies ran while one was open for 2% of the time, Pallas kernels for 17%

profile of v8, /device:TPU:0, one launch (start us, length us, event | category | flops | bytes accessed | tf_op | source)
XLA Modules:
  0.0 54.6 jit_solution(17065532582746924137)
XLA Ops:
  0.6 4.1 %collective-permute-start = (bf16[176,768]{1,0:T(8,128)(2,1)}, bf16[176,768]{1,0:T(8,128)(2,1)S(1)}, u32[]{:S(2)}, u32[]{:S(2)}) collective-permute-start(bf16[176,768]{1,0:T(8,128)(2,1)} %bitcast.4), channel_id=1, source_target_pairs={{0,16},{2,18},{4,20},{6,22},{8,24},{10,26},{12,28},{14,30},{16,0},... | collective-permute-start | bytes 811016 | tf_op jit(solution)/shard_map/ppermute | solution.py:572
  4.7 1.3 %spread.1 = s32[16,1,176]{2,1,0:T(1,128)} custom-call(s32[1,176]{1,0:T(1,128)} %bases_ref.1), custom_call_target="tpu_custom_call" | custom-call | bytes 11968 | tf_op jit(solution)/shard_map/spread/pallas_call | solution.py:541
  6.0 3.9 %all-to-all-start = ((s32[16,1,176]{2,1,0:T(1,128)}), s32[16,1,176]{2,1,0:T(1,128)S(1)}, u32[]{:S(2)}, u32[]{:S(2)}) async-start(s32[16,1,176]{2,1,0:T(1,128)} %spread.1), calls=%async_computation | async-start | bytes 32768 | tf_op jit(solution)/shard_map/all_to_all | solution.py:574
  9.9 0.0 copy-start
  10.0 4.2 %tables.1 = (bf16[128,384]{1,0:T(8,128)(2,1)S(1)}, f32[128,2304]{1,0:T(8,128)S(1)}, bf16[2304,384]{1,0:T(8,128)(2,1)S(1)}) custom-call(bf16[4,768]{1,0:T(4,128)(2,1)} %embed_ref.3, bf16[3,2304,384]{2,1,0:T(8,128)(2,1)} %w_ref.3, bf16[3,384,768]{2,1,0:T(8,128)(2,1)} %refs_4_.1), custom_call_target="tpu_custom_call" | custom-call | flops 452984832 | bytes 10131456 | tf_op jit(solution)/shard_map/tables/pallas_call | solution.py:541
  14.2 0.0 copy-start.1
  14.2 0.6 %copy-done.1 = bf16[128,384]{1,0:T(8,128)(2,1)} copy-done((bf16[128,384]{1,0:T(8,128)(2,1)}, bf16[128,384]{1,0:T(8,128)(2,1)S(1)}, u32[]{:S(2)}) %copy-start.1) | copy-done | bytes 98328
  14.8 3.7 %all-to-all-done.refs_0_ = s32[16,1,176]{2,1,0:T(1,128)S(1)} async-done(((s32[16,1,176]{2,1,0:T(1,128)}), s32[16,1,176]{2,1,0:T(1,128)S(1)}, u32[]{:S(2)}, u32[]{:S(2)}) %all-to-all-start) | async-done | bytes 11296 | tf_op jit(solution)/shard_map/all_to_all | solution.py:574
  18.5 0.0 collective-permute-done.refs_2_
  18.5 0.0 copy-done
  18.5 6.9 %tower.1 = (f32[176,768]{1,0:T(8,128)}, f32[1536,384]{1,0:T(8,128)S(1)}, bf16[1536,384]{1,0:T(8,128)(2,1)S(1)}, bf16[384,384]{1,0:T(8,128)(2,1)S(1)}, f32[128,76...) custom-call(s32[16,1,176]{2,1,0:T(1,128)S(1)} %all-to-all-done.refs_0_, ...), custom_call_target="tpu_custom_call" | custom-call | flops 2802843648 | bytes 17705984 | tf_op jit(solution)/shard_map/tower/pallas_call | solution.py:541
  25.4 0.2 collective-permute-start.1
  25.6 0.0 copy-start.3
  25.6 1.4 %classes.1 = (f32[80,384]{1,0:T(8,128)S(1)}, bf16[80,384]{1,0:T(8,128)(2,1)S(1)}) custom-call(bf16[384,384]{1,0:T(8,128)(2,1)S(1)} %get-tuple-element.38.refs_0_, f32[128,768]{1,0:T(8,128)S(1)} %get-tuple-element.39.refs_1_, f32[128,2304]{1,0:T(8,128)S(1)} %get-tuple-element.34.refs_6_.refs_2_, bf16[2304,384]{1,0:T(8,128)(2,1)S(1)} %get-tuple-element.40.refs_3_, ...), custom_call_target="tpu_custom_call" | custom-call | flops 452984832 | bytes 4411392 | tf_op jit(solution)/shard_map/classes/pallas_call | solution.py:541
  27.0 0.4 collective-permute-start.2
  27.4 0.0 copy-done.3
  27.4 0.1 fusion.8
  27.5 0.9 %collective-permute-done.2.refs_3_ = bf16[80,384]{1,0:T(8,128)(2,1)S(1)} collective-permute-done((bf16[80,384]{1,0:T(8,128)(2,1)S(1)}, bf16[80,384]{1,0:T(8,128)(2,1)S(1)}, u32[]{:S(2)}, u32[]{:S(2)}) %collective-permute-start.2) | collective-permute-done | bytes 61472 | tf_op jit(solution)/shard_map/ppermute | solution.py:639
  28.4 0.0 collective-permute-done.1.refs_1_
  28.4 0.0 copy-start.2
  28.4 0.2 messages.1
  28.7 1.6 %collective-permute-start.3 = (bf16[224,384]{1,0:T(8,128)(2,1)S(1)}, bf16[224,384]{1,0:T(8,128)(2,1)S(1)}, u32[]{:S(2)}, u32[]{:S(2)}) collective-permute-start(bf16[224,384]{1,0:T(8,128)(2,1)S(1)} %get-tuple-element.45), channel_id=1, source_target_pairs={{0,5},{1,4},{2,7},{3,6},{4,1},{5,0},{6,3},{7,2},{8,13},{9,12},{10,... | collective-permute-start | bytes 516104 | tf_op jit(solution)/shard_map/ppermute | solution.py:654
  30.3 0.7 %collective-permute-start.4 = (bf16[224,384]{1,0:T(8,128)(2,1)S(1)}, bf16[224,384]{1,0:T(8,128)(2,1)S(1)}, u32[]{:S(2)}, u32[]{:S(2)}) collective-permute-start(bf16[224,384]{1,0:T(8,128)(2,1)S(1)} %get-tuple-element.46), channel_id=1, source_target_pairs={{0,8},{1,9},{2,10},{3,11},{4,12},{5,13},{6,14},{7,15},{8,0},{9,1},... | collective-permute-start | bytes 516104 | tf_op jit(solution)/shard_map/ppermute | solution.py:654
  31.0 1.3 %collective-permute-start.5 = (bf16[224,384]{1,0:T(8,128)(2,1)S(1)}, bf16[224,384]{1,0:T(8,128)(2,1)S(1)}, u32[]{:S(2)}, u32[]{:S(2)}) collective-permute-start(bf16[224,384]{1,0:T(8,128)(2,1)S(1)} %get-tuple-element.47), channel_id=1, source_target_pairs={{0,9},{1,8},{2,11},{3,10},{4,13},{5,12},{6,15},{7,14},{8,1},{9,0},... | collective-permute-start | bytes 516104 | tf_op jit(solution)/shard_map/ppermute | solution.py:654
  32.3 1.4 %collective-permute-start.6 = (bf16[224,384]{1,0:T(8,128)(2,1)S(1)}, bf16[224,384]{1,0:T(8,128)(2,1)S(1)}, u32[]{:S(2)}, u32[]{:S(2)}) collective-permute-start(bf16[224,384]{1,0:T(8,128)(2,1)S(1)} %get-tuple-element.48), channel_id=1, source_target_pairs={{0,4},{1,5},{2,6},{3,7},{4,0},{5,1},{6,2},{7,3},{8,12},{9,13},{10,... | collective-permute-start | bytes 516104 | tf_op jit(solution)/shard_map/ppermute | solution.py:654
  33.7 1.5 %collective-permute-start.7 = (bf16[224,384]{1,0:T(8,128)(2,1)S(1)}, bf16[224,384]{1,0:T(8,128)(2,1)S(1)}, u32[]{:S(2)}, u32[]{:S(2)}) collective-permute-start(bf16[224,384]{1,0:T(8,128)(2,1)S(1)} %get-tuple-element.49), channel_id=1, source_target_pairs={{0,1},{1,0},{2,3},{3,2},{4,5},{5,4},{6,7},{7,6},{8,9},{9,8},{10,11... | collective-permute-start | bytes 516104 | tf_op jit(solution)/shard_map/ppermute | solution.py:654
  35.2 2.0 %collective-permute-done.3.refs_0_ = bf16[224,384]{1,0:T(8,128)(2,1)S(1)} collective-permute-done((bf16[224,384]{1,0:T(8,128)(2,1)S(1)}, bf16[224,384]{1,0:T(8,128)(2,1)S(1)}, u32[]{:S(2)}, u32[]{:S(2)}) %collective-permute-start.3) | collective-permute-done | bytes 172064 | tf_op jit(solution)/shard_map/ppermute | solution.py:654
  37.2 0.0 collective-permute-start.8
  37.2 0.4 collective-permute-done.4.refs_1_
  37.6 3.6 %collective-permute-start.9 = (bf16[224,384]{1,0:T(8,128)(2,1)S(1)}, bf16[224,384]{1,0:T(8,128)(2,1)S(1)}, u32[]{:S(2)}, u32[]{:S(2)}) collective-permute-start(bf16[224,384]{1,0:T(8,128)(2,1)S(1)} %get-tuple-element.51), channel_id=1, source_target_pairs={{0,13},{1,12},{2,15},{3,14},{4,9},{5,8},{6,11},{7,10},{8,5},{9,4},... | collective-permute-start | bytes 516104 | tf_op jit(solution)/shard_map/ppermute | solution.py:654
  41.1 0.1 fusion.9
  41.2 0.1 fusion.11
  41.3 0.1 copy.15
  41.4 0.0 collective-permute-done.5.refs_2_
  41.4 0.0 collective-permute-done.6.refs_3_
  41.4 1.3 %collective-permute-done.7.refs_4_ = bf16[224,384]{1,0:T(8,128)(2,1)S(1)} collective-permute-done((bf16[224,384]{1,0:T(8,128)(2,1)S(1)}, bf16[224,384]{1,0:T(8,128)(2,1)S(1)}, u32[]{:S(2)}, u32[]{:S(2)}) %collective-permute-start.7) | collective-permute-done | bytes 172064 | tf_op jit(solution)/shard_map/ppermute | solution.py:654
  42.8 3.4 %collective-permute-done.8.refs_5_ = bf16[224,384]{1,0:T(8,128)(2,1)S(1)} collective-permute-done((bf16[224,384]{1,0:T(8,128)(2,1)S(1)}, bf16[224,384]{1,0:T(8,128)(2,1)S(1)}, u32[]{:S(2)}, u32[]{:S(2)}) %collective-permute-start.8) | collective-permute-done | bytes 172064 | tf_op jit(solution)/shard_map/ppermute | solution.py:654
  46.2 2.3 %collective-permute-done.9.refs_6_ = bf16[224,384]{1,0:T(8,128)(2,1)S(1)} collective-permute-done((bf16[224,384]{1,0:T(8,128)(2,1)S(1)}, bf16[224,384]{1,0:T(8,128)(2,1)S(1)}, u32[]{:S(2)}, u32[]{:S(2)}) %collective-permute-start.9) | collective-permute-done | bytes 172064 | tf_op jit(solution)/shard_map/ppermute | solution.py:654
  48.5 0.2 sums.1
  48.7 1.5 %collective-permute-start.10 = (bf16[192,384]{1,0:T(8,128)(2,1)S(1)}, bf16[192,384]{1,0:T(8,128)(2,1)S(1)}, u32[]{:S(2)}, u32[]{:S(2)}) collective-permute-start(bf16[192,384]{1,0:T(8,128)(2,1)S(1)} %get-tuple-element.52), channel_id=1, source_target_pairs={{0,1},{1,0},{2,3},{3,2},{4,5},{5,4},{6,7},{7,6},{8,9},{9,8},{10,11... | collective-permute-start | bytes 442376 | tf_op jit(solution)/shard_map/ppermute | solution.py:661
  50.2 0.0 copy-done.2
  50.2 2.4 %layer0.1 = (f32[3,144,384]{2,1,0:T(8,128)}, f32[3,48,384]{2,1,0:T(8,128)}, f32[4,768]{1,0:T(4,128)S(1)}, f32[4,48]{1,0:T(4,128)S(1)}) custom-call(f32[32,384]{1,0:T(8,128)S(1)} %get-tuple-element.53.rest_ref, f32[192,384]{1,0:T(8,128)S(1)} %get-tuple-element.54.total_ref, bf16[4,768]{1,0:T(4,128)(2,1)S(1)} %copy-done.3, bf16[3,2304,384]{2,1,0:T(8,128)(2,1)} %w_ref.3, ...), custom_call_target="tpu_custom_call" | custom-call | bytes 6659328 | tf_op jit(solution)/shard_map/layer0/pallas_call | solution.py:541
  52.6 0.7 %dynamic-slice_add_fusion = f32[4,48]{1,0:T(4,128)} fusion(f32[4,48]{1,0:T(4,128)S(1)} %get-tuple-element.60, f32[4,768]{1,0:T(4,128)S(1)} %get-tuple-element.61, s32[]{:T(128)S(6)} %select_n.7), kind=kLoop, calls=%fused_computation.18 | loop fusion | flops 192 | bytes 2308 | tf_op jit(solution)/shard_map/add | solution.py:688
  53.2 0.7 %collective-permute-done.10.got_ref = bf16[192,384]{1,0:T(8,128)(2,1)S(1)} collective-permute-done((bf16[192,384]{1,0:T(8,128)(2,1)S(1)}, bf16[192,384]{1,0:T(8,128)(2,1)S(1)}, u32[]{:S(2)}, u32[]{:S(2)}) %collective-permute-start.10) | collective-permute-done | bytes 147488 | tf_op jit(solution)/shard_map/ppermute | solution.py:661
  53.9 0.7 %finish.1 = (f32[3,144,384]{2,1,0:T(8,128)}, f32[3,48,384]{2,1,0:T(8,128)}) custom-call(bf16[192,384]{1,0:T(8,128)(2,1)S(1)} %collective-permute-done.10.got_ref, f32[3,144,384]{2,1,0:T(8,128)} %get-tuple-element.56._, f32[3,48,384]{2,1,0:T(8,128)} %get-tuple-element.57.__), custom_call_target="tpu_custom_call", output_to_operand_aliasing={{0}: (1, {}), {1}: (2, {})} | custom-call | bytes 1916928 | tf_op jit(solution)/shard_map/finish/pallas_call | solution.py:541
  (1 shorter events, 0.0 us)
Async XLA Ops:
  0.6 17.9 %collective-permute-start = (bf16[176,768]{1,0:T(8,128)(2,1)}, bf16[176,768]{1,0:T(8,128)(2,1)S(1)}, u32[]{:S(2)}, u32[]{:S(2)}) collective-permute-start(bf16[176,768]{1,0:T(8,128)(2,1)} %bitcast.4), channel_id=1, source_target_pairs={{0,16},{2,18},{4,20},{6,22},{8,24},{10,26},{12,28},{14,30},{16,0},... | collective-permute-start | bytes 811016 | tf_op jit(solution)/shard_map/ppermute | solution.py:572
  6.0 12.5 %all-to-all-start = ((s32[16,1,176]{2,1,0:T(1,128)}), s32[16,1,176]{2,1,0:T(1,128)S(1)}, u32[]{:S(2)}, u32[]{:S(2)}) async-start(s32[16,1,176]{2,1,0:T(1,128)} %spread.1), calls=%async_computation | async-start | bytes 32768 | tf_op jit(solution)/shard_map/all_to_all | solution.py:574
  9.9 8.6 %copy-start = (bf16[1,176,768]{2,1,0:T(8,128)(2,1)S(1)}, bf16[1,176,768]{2,1,0:T(8,128)(2,1)}, u32[]{:S(2)}) copy-start(bf16[1,176,768]{2,1,0:T(8,128)(2,1)} %param.9) | copy-start | bytes 811012
  14.2 0.6 %copy-start.1 = (bf16[128,384]{1,0:T(8,128)(2,1)}, bf16[128,384]{1,0:T(8,128)(2,1)S(1)}, u32[]{:S(2)}) copy-start(bf16[128,384]{1,0:T(8,128)(2,1)S(1)} %get-tuple-element.55.act0_ref) | copy-start | bytes 294916
  25.4 3.0 %collective-permute-start.1 = (bf16[1536,384]{1,0:T(8,128)(2,1)S(1)}, bf16[1536,384]{1,0:T(8,128)(2,1)S(1)}, u32[]{:S(2)}, u32[]{:S(2)}) collective-permute-start(bf16[1536,384]{1,0:T(8,128)(2,1)S(1)} %get-tuple-element.37), channel_id=1, source_target_pairs={{0,2},{2,0},{4,6},{6,4},{8,10},{10,8},{12,14},{14,12},{16,18},{18,... | collective-permute-start | bytes 3538952 | tf_op jit(solution)/shard_map/ppermute | solution.py:629
  25.6 1.8 %copy-start.3 = (bf16[4,768]{1,0:T(4,128)(2,1)S(1)}, bf16[4,768]{1,0:T(4,128)(2,1)}, u32[]{:S(2)}) copy-start(bf16[4,768]{1,0:T(4,128)(2,1)} %embed_ref.3) | copy-start | bytes 18436
  27.0 1.5 %collective-permute-start.2 = (bf16[80,384]{1,0:T(8,128)(2,1)S(1)}, bf16[80,384]{1,0:T(8,128)(2,1)S(1)}, u32[]{:S(2)}, u32[]{:S(2)}) collective-permute-start(bf16[80,384]{1,0:T(8,128)(2,1)S(1)} %get-tuple-element.43), channel_id=1, source_target_pairs={{0,2},{2,0},{4,6},{6,4},{8,10},{10,8},{12,14},{14,12},{16,18},{18,... | collective-permute-start | bytes 184328 | tf_op jit(solution)/shard_map/ppermute | solution.py:639
  28.4 21.8 %copy-start.2 = (bf16[128,384]{1,0:T(8,128)(2,1)S(1)}, bf16[128,384]{1,0:T(8,128)(2,1)}, u32[]{:S(2)}) copy-start(bf16[128,384]{1,0:T(8,128)(2,1)} %copy-done.1) | copy-start | bytes 294916
  28.7 8.5 %collective-permute-start.3 = (bf16[224,384]{1,0:T(8,128)(2,1)S(1)}, bf16[224,384]{1,0:T(8,128)(2,1)S(1)}, u32[]{:S(2)}, u32[]{:S(2)}) collective-permute-start(bf16[224,384]{1,0:T(8,128)(2,1)S(1)} %get-tuple-element.45), channel_id=1, source_target_pairs={{0,5},{1,4},{2,7},{3,6},{4,1},{5,0},{6,3},{7,2},{8,13},{9,12},{10,... | collective-permute-start | bytes 516104 | tf_op jit(solution)/shard_map/ppermute | solution.py:654
  30.3 7.3 %collective-permute-start.4 = (bf16[224,384]{1,0:T(8,128)(2,1)S(1)}, bf16[224,384]{1,0:T(8,128)(2,1)S(1)}, u32[]{:S(2)}, u32[]{:S(2)}) collective-permute-start(bf16[224,384]{1,0:T(8,128)(2,1)S(1)} %get-tuple-element.46), channel_id=1, source_target_pairs={{0,8},{1,9},{2,10},{3,11},{4,12},{5,13},{6,14},{7,15},{8,0},{9,1},... | collective-permute-start | bytes 516104 | tf_op jit(solution)/shard_map/ppermute | solution.py:654
  31.0 10.5 %collective-permute-start.5 = (bf16[224,384]{1,0:T(8,128)(2,1)S(1)}, bf16[224,384]{1,0:T(8,128)(2,1)S(1)}, u32[]{:S(2)}, u32[]{:S(2)}) collective-permute-start(bf16[224,384]{1,0:T(8,128)(2,1)S(1)} %get-tuple-element.47), channel_id=1, source_target_pairs={{0,9},{1,8},{2,11},{3,10},{4,13},{5,12},{6,15},{7,14},{8,1},{9,0},... | collective-permute-start | bytes 516104 | tf_op jit(solution)/shard_map/ppermute | solution.py:654
  32.3 9.1 %collective-permute-start.6 = (bf16[224,384]{1,0:T(8,128)(2,1)S(1)}, bf16[224,384]{1,0:T(8,128)(2,1)S(1)}, u32[]{:S(2)}, u32[]{:S(2)}) collective-permute-start(bf16[224,384]{1,0:T(8,128)(2,1)S(1)} %get-tuple-element.48), channel_id=1, source_target_pairs={{0,4},{1,5},{2,6},{3,7},{4,0},{5,1},{6,2},{7,3},{8,12},{9,13},{10,... | collective-permute-start | bytes 516104 | tf_op jit(solution)/shard_map/ppermute | solution.py:654
  33.7 9.1 %collective-permute-start.7 = (bf16[224,384]{1,0:T(8,128)(2,1)S(1)}, bf16[224,384]{1,0:T(8,128)(2,1)S(1)}, u32[]{:S(2)}, u32[]{:S(2)}) collective-permute-start(bf16[224,384]{1,0:T(8,128)(2,1)S(1)} %get-tuple-element.49), channel_id=1, source_target_pairs={{0,1},{1,0},{2,3},{3,2},{4,5},{5,4},{6,7},{7,6},{8,9},{9,8},{10,11... | collective-permute-start | bytes 516104 | tf_op jit(solution)/shard_map/ppermute | solution.py:654
  37.2 9.0 %collective-permute-start.8 = (bf16[224,384]{1,0:T(8,128)(2,1)S(1)}, bf16[224,384]{1,0:T(8,128)(2,1)S(1)}, u32[]{:S(2)}, u32[]{:S(2)}) collective-permute-start(bf16[224,384]{1,0:T(8,128)(2,1)S(1)} %get-tuple-element.50), channel_id=1, source_target_pairs={{0,12},{1,13},{2,14},{3,15},{4,8},{5,9},{6,10},{7,11},{8,4},{9,5},... | collective-permute-start | bytes 516104 | tf_op jit(solution)/shard_map/ppermute | solution.py:654
  37.6 10.9 %collective-permute-start.9 = (bf16[224,384]{1,0:T(8,128)(2,1)S(1)}, bf16[224,384]{1,0:T(8,128)(2,1)S(1)}, u32[]{:S(2)}, u32[]{:S(2)}) collective-permute-start(bf16[224,384]{1,0:T(8,128)(2,1)S(1)} %get-tuple-element.51), channel_id=1, source_target_pairs={{0,13},{1,12},{2,15},{3,14},{4,9},{5,8},{6,11},{7,10},{8,5},{9,4},... | collective-permute-start | bytes 516104 | tf_op jit(solution)/shard_map/ppermute | solution.py:654
  48.7 5.2 %collective-permute-start.10 = (bf16[192,384]{1,0:T(8,128)(2,1)S(1)}, bf16[192,384]{1,0:T(8,128)(2,1)S(1)}, u32[]{:S(2)}, u32[]{:S(2)}) collective-permute-start(bf16[192,384]{1,0:T(8,128)(2,1)S(1)} %get-tuple-element.52), channel_id=1, source_target_pairs={{0,1},{1,0},{2,3},{3,2},{4,5},{5,4},{6,7},{7,6},{8,9},{9,8},{10,11... | collective-permute-start | bytes 442376 | tf_op jit(solution)/shard_map/ppermute | solution.py:661

commit v9 on v8

--- a/solution.py
+++ b/solution.py
@@ -12,7 +12,7 @@
 F32 = jnp.float32
 CLASSES = 128
 STRIDE = 8
-ORDER = (3, 4, 5, 2, 1, 6, 7)
+ORDER = ((0, 6, 5, 3, 7, 1, 2, 4), (0, 1, 2, 4, 7, 6, 5, 3))
 
 
 def gelu_pair(v):
@@ -468,7 +468,8 @@
     m = (k % STRIDE) // 2
     end = 8 * STRIDE
     g = mine_small_ref[end:, :] + other_small_ref[end:, :].astype(F32)
-    for mask, out_ref in enumerate(out_refs):
+    for i, out_ref in enumerate(out_refs):
+        mask = jnp.where(k % 2 == 0, ORDER[0][i], ORDER[1][i])
         target, layer = m ^ (mask // 2), x ^ (mask % 2)
         at = pl.ds(pl.multiple_of((2 * target + layer) * part, 16), part)
         out_ref[:part, :] = (mine_ref[at, :] + other_ref[at, :].astype(F32)).astype(out_ref.dtype)
@@ -645,13 +646,14 @@
         name="messages",
     )
     arrived = []
-    for mask in ORDER:
-        route = [
-            (s * dp + d, (s ^ (2 * (mask // dp))) * dp + (d ^ (mask % dp)))
-            for s in range(n)
-            for d in range(dp)
-        ]
-        arrived.append(lax.ppermute(pieces[mask], ("seq", "dp"), route))
+    for i in range(1, peers):
+        route = []
+        for s in range(n):
+            mask = ORDER[s % 2][i]
+            route += [
+                (s * dp + d, (s ^ (2 * (mask // dp))) * dp + (d ^ (mask % dp))) for d in range(dp)
+            ]
+        arrived.append(lax.ppermute(pieces[i], ("seq", "dp"), route))
     total, send, rest = call(
         sum_kernel,
         [shape((part, mid), F32), shape((part, mid), BF16), shape((32, mid), F32)],

time: 54.9 us -> 56.4 us (1.027)
  waiting for transfers between devices: 14.7 us -> 18.9 us
  starting transfers between devices: 20.2 us -> 17.6 us
    ppermute x7, waiting for transfers between devices: 9.37 us -> 13.1 us  [on_device(): arrived.append(lax.ppermute(pieces[i], ('seq', 'dp'), route))]
    ppermute x7, starting transfers between devices: 10.1 us -> 7.96 us  [on_device(): arrived.append(lax.ppermute(pieces[i], ('seq', 'dp'), route))]
  transfers between devices with their start and end apart: 12 -> 12, of which waited for: 8 -> 8; matrix products, arithmetic and copies ran while one was open for 2% -> 2% of each run, Pallas kernels for 17% -> 16%
where the time goes in v9:
time: 56.4 us; the launch traced here: 56.2 us
  waiting for transfers between devices  18.9 us (34%)
  starting transfers between devices  17.6 us (31%)
  Pallas kernels  17.3 us (31%)
  other arithmetic  0.97 us (2%)
  local copies, waits for them, and re-layouts  0.77 us (1%)
  between operations  0.71 us (1%)
    pallas_call x8, Pallas kernels, call(): pl.pallas_call(kernel, out_shape=outs, in_specs=[pl.BlockSpec(memory_spac...  17.3 us
    ppermute x7, waiting for transfers between devices, on_device(): arrived.append(lax.ppermute(pieces[i], ('seq', 'dp'), route))  13.1 us
    ppermute x7, starting transfers between devices, on_device(): arrived.append(lax.ppermute(pieces[i], ('seq', 'dp'), route))  7.96 us
    ppermute x1, starting transfers between devices, on_device(): far = lax.ppermute(own, 'seq', [(s, (s + STRIDE) % n) for s in range(n)])  4.1 us
    all_to_all x1, starting transfers between devices, on_device(): gathered = lax.all_to_all(copies, 'seq', 0, 0, tiled=True)  3.91 us
    all_to_all x1, waiting for transfers between devices, on_device(): gathered = lax.all_to_all(copies, 'seq', 0, 0, tiled=True)  3.72 us
    ppermute x1, waiting for transfers between devices, on_device(): swapped = lax.ppermute(send, 'dp', [(d, d ^ 1) for d in range(dp)])  1.17 us
  transfers between devices with their start and end apart: 12, of which 8 were waited for; matrix products, arithmetic and copies ran while one was open for 2% of the time, Pallas kernels for 16%

profile of v9, /device:TPU:0, one launch (start us, length us, event | category | flops | bytes accessed | tf_op | source)
XLA Modules:
  0.0 56.2 jit_solution(7229790600840666690)
XLA Ops:
  0.6 4.1 %collective-permute-start = (bf16[176,768]{1,0:T(8,128)(2,1)}, bf16[176,768]{1,0:T(8,128)(2,1)S(1)}, u32[]{:S(2)}, u32[]{:S(2)}) collective-permute-start(bf16[176,768]{1,0:T(8,128)(2,1)} %bitcast.4), channel_id=1, source_target_pairs={{0,16},{2,18},{4,20},{6,22},{8,24},{10,26},{12,28},{14,30},{16,0},... | collective-permute-start | bytes 811016 | tf_op jit(solution)/shard_map/ppermute | solution.py:573
  4.7 1.3 %spread.1 = s32[16,1,176]{2,1,0:T(1,128)} custom-call(s32[1,176]{1,0:T(1,128)} %bases_ref.1), custom_call_target="tpu_custom_call" | custom-call | bytes 11968 | tf_op jit(solution)/shard_map/spread/pallas_call | solution.py:542
  6.0 3.9 %all-to-all-start = ((s32[16,1,176]{2,1,0:T(1,128)}), s32[16,1,176]{2,1,0:T(1,128)S(1)}, u32[]{:S(2)}, u32[]{:S(2)}) async-start(s32[16,1,176]{2,1,0:T(1,128)} %spread.1), calls=%async_computation | async-start | bytes 32768 | tf_op jit(solution)/shard_map/all_to_all | solution.py:575
  9.9 0.0 copy-start
  10.0 4.2 %tables.1 = (bf16[128,384]{1,0:T(8,128)(2,1)S(1)}, f32[128,2304]{1,0:T(8,128)S(1)}, bf16[2304,384]{1,0:T(8,128)(2,1)S(1)}) custom-call(bf16[4,768]{1,0:T(4,128)(2,1)} %embed_ref.3, bf16[3,2304,384]{2,1,0:T(8,128)(2,1)} %w_ref.3, bf16[3,384,768]{2,1,0:T(8,128)(2,1)} %refs_4_.1), custom_call_target="tpu_custom_call" | custom-call | flops 452984832 | bytes 10131456 | tf_op jit(solution)/shard_map/tables/pallas_call | solution.py:542
  14.2 0.0 copy-start.1
  14.2 0.6 %copy-done.1 = bf16[128,384]{1,0:T(8,128)(2,1)} copy-done((bf16[128,384]{1,0:T(8,128)(2,1)}, bf16[128,384]{1,0:T(8,128)(2,1)S(1)}, u32[]{:S(2)}) %copy-start.1) | copy-done | bytes 98328
  14.8 3.7 %all-to-all-done.refs_0_ = s32[16,1,176]{2,1,0:T(1,128)S(1)} async-done(((s32[16,1,176]{2,1,0:T(1,128)}), s32[16,1,176]{2,1,0:T(1,128)S(1)}, u32[]{:S(2)}, u32[]{:S(2)}) %all-to-all-start) | async-done | bytes 11296 | tf_op jit(solution)/shard_map/all_to_all | solution.py:575
  18.5 0.0 collective-permute-done.refs_2_
  18.5 0.0 copy-done
  18.5 6.9 %tower.1 = (f32[176,768]{1,0:T(8,128)}, f32[1536,384]{1,0:T(8,128)S(1)}, bf16[1536,384]{1,0:T(8,128)(2,1)S(1)}, bf16[384,384]{1,0:T(8,128)(2,1)S(1)}, f32[128,76...) custom-call(s32[16,1,176]{2,1,0:T(1,128)S(1)} %all-to-all-done.refs_0_, ...), custom_call_target="tpu_custom_call" | custom-call | flops 2802843648 | bytes 17705984 | tf_op jit(solution)/shard_map/tower/pallas_call | solution.py:542
  25.4 0.2 collective-permute-start.1
  25.6 0.0 copy-start.3
  25.6 1.4 %classes.1 = (f32[80,384]{1,0:T(8,128)S(1)}, bf16[80,384]{1,0:T(8,128)(2,1)S(1)}) custom-call(bf16[384,384]{1,0:T(8,128)(2,1)S(1)} %get-tuple-element.38.refs_0_, f32[128,768]{1,0:T(8,128)S(1)} %get-tuple-element.39.refs_1_, f32[128,2304]{1,0:T(8,128)S(1)} %get-tuple-element.34.refs_6_.refs_2_, bf16[2304,384]{1,0:T(8,128)(2,1)S(1)} %get-tuple-element.40.refs_3_, ...), custom_call_target="tpu_custom_call" | custom-call | flops 452984832 | bytes 4411392 | tf_op jit(solution)/shard_map/classes/pallas_call | solution.py:542
  27.0 0.4 collective-permute-start.2
  27.4 0.0 copy-done.3
  27.4 0.1 fusion.8
  27.5 0.9 %collective-permute-done.2.refs_3_ = bf16[80,384]{1,0:T(8,128)(2,1)S(1)} collective-permute-done((bf16[80,384]{1,0:T(8,128)(2,1)S(1)}, bf16[80,384]{1,0:T(8,128)(2,1)S(1)}, u32[]{:S(2)}, u32[]{:S(2)}) %collective-permute-start.2) | collective-permute-done | bytes 61472 | tf_op jit(solution)/shard_map/ppermute | solution.py:640
  28.4 0.0 collective-permute-done.1.refs_1_
  28.4 0.0 copy-start.2
  28.4 0.3 messages.1
  28.7 0.8 %collective-permute-start.3 = (bf16[224,384]{1,0:T(8,128)(2,1)S(1)}, bf16[224,384]{1,0:T(8,128)(2,1)S(1)}, u32[]{:S(2)}, u32[]{:S(2)}) collective-permute-start(bf16[224,384]{1,0:T(8,128)(2,1)S(1)} %get-tuple-element.45), channel_id=1, source_target_pairs={{0,12},{1,13},{2,3},{3,2},{4,8},{5,9},{6,7},{7,6},{8,4},{9,5},{10,... | collective-permute-start | bytes 516104 | tf_op jit(solution)/shard_map/ppermute | solution.py:656
  29.5 2.3 %collective-permute-start.4 = (bf16[224,384]{1,0:T(8,128)(2,1)S(1)}, bf16[224,384]{1,0:T(8,128)(2,1)S(1)}, u32[]{:S(2)}, u32[]{:S(2)}) collective-permute-start(bf16[224,384]{1,0:T(8,128)(2,1)S(1)} %get-tuple-element.46), channel_id=1, source_target_pairs={{0,9},{1,8},{2,6},{3,7},{4,13},{5,12},{6,2},{7,3},{8,1},{9,0},{10,... | collective-permute-start | bytes 516104 | tf_op jit(solution)/shard_map/ppermute | solution.py:656
  31.8 1.4 %collective-permute-start.5 = (bf16[224,384]{1,0:T(8,128)(2,1)S(1)}, bf16[224,384]{1,0:T(8,128)(2,1)S(1)}, u32[]{:S(2)}, u32[]{:S(2)}) collective-permute-start(bf16[224,384]{1,0:T(8,128)(2,1)S(1)} %get-tuple-element.47), channel_id=1, source_target_pairs={{0,5},{1,4},{2,10},{3,11},{4,1},{5,0},{6,14},{7,15},{8,13},{9,12},... | collective-permute-start | bytes 516104 | tf_op jit(solution)/shard_map/ppermute | solution.py:656
  33.2 1.7 %collective-permute-start.6 = (bf16[224,384]{1,0:T(8,128)(2,1)S(1)}, bf16[224,384]{1,0:T(8,128)(2,1)S(1)}, u32[]{:S(2)}, u32[]{:S(2)}) collective-permute-start(bf16[224,384]{1,0:T(8,128)(2,1)S(1)} %get-tuple-element.48), channel_id=1, source_target_pairs={{0,13},{1,12},{2,15},{3,14},{4,9},{5,8},{6,11},{7,10},{8,5},{9,4},... | collective-permute-start | bytes 516104 | tf_op jit(solution)/shard_map/ppermute | solution.py:656
  34.8 0.5 collective-permute-start.7
  35.3 0.8 %collective-permute-done.3.refs_0_ = bf16[224,384]{1,0:T(8,128)(2,1)S(1)} collective-permute-done((bf16[224,384]{1,0:T(8,128)(2,1)S(1)}, bf16[224,384]{1,0:T(8,128)(2,1)S(1)}, u32[]{:S(2)}, u32[]{:S(2)}) %collective-permute-start.3) | collective-permute-done | bytes 172064 | tf_op jit(solution)/shard_map/ppermute | solution.py:656
  36.2 0.6 %collective-permute-start.8 = (bf16[224,384]{1,0:T(8,128)(2,1)S(1)}, bf16[224,384]{1,0:T(8,128)(2,1)S(1)}, u32[]{:S(2)}, u32[]{:S(2)}) collective-permute-start(bf16[224,384]{1,0:T(8,128)(2,1)S(1)} %get-tuple-element.50), channel_id=1, source_target_pairs={{0,4},{1,5},{2,11},{3,10},{4,0},{5,1},{6,15},{7,14},{8,12},{9,13},... | collective-permute-start | bytes 516104 | tf_op jit(solution)/shard_map/ppermute | solution.py:656
  36.8 3.9 %collective-permute-done.4.refs_1_ = bf16[224,384]{1,0:T(8,128)(2,1)S(1)} collective-permute-done((bf16[224,384]{1,0:T(8,128)(2,1)S(1)}, bf16[224,384]{1,0:T(8,128)(2,1)S(1)}, u32[]{:S(2)}, u32[]{:S(2)}) %collective-permute-start.4) | collective-permute-done | bytes 172064 | tf_op jit(solution)/shard_map/ppermute | solution.py:656
  40.7 0.7 %collective-permute-start.9 = (bf16[224,384]{1,0:T(8,128)(2,1)S(1)}, bf16[224,384]{1,0:T(8,128)(2,1)S(1)}, u32[]{:S(2)}, u32[]{:S(2)}) collective-permute-start(bf16[224,384]{1,0:T(8,128)(2,1)S(1)} %get-tuple-element.51), channel_id=1, source_target_pairs={{0,8},{1,9},{2,7},{3,6},{4,12},{5,13},{6,3},{7,2},{8,0},{9,1},{10,... | collective-permute-start | bytes 516104 | tf_op jit(solution)/shard_map/ppermute | solution.py:656
  41.4 0.1 fusion.9
  41.5 0.1 fusion.11
  41.6 0.1 copy.15
  41.7 3.2 %collective-permute-done.5.refs_2_ = bf16[224,384]{1,0:T(8,128)(2,1)S(1)} collective-permute-done((bf16[224,384]{1,0:T(8,128)(2,1)S(1)}, bf16[224,384]{1,0:T(8,128)(2,1)S(1)}, u32[]{:S(2)}, u32[]{:S(2)}) %collective-permute-start.5) | collective-permute-done | bytes 172064 | tf_op jit(solution)/shard_map/ppermute | solution.py:656
  44.9 1.0 %collective-permute-done.6.refs_3_ = bf16[224,384]{1,0:T(8,128)(2,1)S(1)} collective-permute-done((bf16[224,384]{1,0:T(8,128)(2,1)S(1)}, bf16[224,384]{1,0:T(8,128)(2,1)S(1)}, u32[]{:S(2)}, u32[]{:S(2)}) %collective-permute-start.6) | collective-permute-done | bytes 172064 | tf_op jit(solution)/shard_map/ppermute | solution.py:656
  45.9 4.1 %collective-permute-done.7.refs_4_ = bf16[224,384]{1,0:T(8,128)(2,1)S(1)} collective-permute-done((bf16[224,384]{1,0:T(8,128)(2,1)S(1)}, bf16[224,384]{1,0:T(8,128)(2,1)S(1)}, u32[]{:S(2)}, u32[]{:S(2)}) %collective-permute-start.7) | collective-permute-done | bytes 172064 | tf_op jit(solution)/shard_map/ppermute | solution.py:656
  50.1 0.0 collective-permute-done.8.refs_5_
  50.1 0.0 collective-permute-done.9.refs_6_
  50.1 0.2 sums.1
  50.3 1.0 %collective-permute-start.10 = (bf16[192,384]{1,0:T(8,128)(2,1)S(1)}, bf16[192,384]{1,0:T(8,128)(2,1)S(1)}, u32[]{:S(2)}, u32[]{:S(2)}) collective-permute-start(bf16[192,384]{1,0:T(8,128)(2,1)S(1)} %get-tuple-element.52), channel_id=1, source_target_pairs={{0,1},{1,0},{2,3},{3,2},{4,5},{5,4},{6,7},{7,6},{8,9},{9,8},{10,11... | collective-permute-start | bytes 442376 | tf_op jit(solution)/shard_map/ppermute | solution.py:663
  51.3 0.0 copy-done.2
  51.3 2.4 %layer0.1 = (f32[3,144,384]{2,1,0:T(8,128)}, f32[3,48,384]{2,1,0:T(8,128)}, f32[4,768]{1,0:T(4,128)S(1)}, f32[4,48]{1,0:T(4,128)S(1)}) custom-call(f32[32,384]{1,0:T(8,128)S(1)} %get-tuple-element.53.rest_ref, f32[192,384]{1,0:T(8,128)S(1)} %get-tuple-element.54.total_ref, bf16[4,768]{1,0:T(4,128)(2,1)S(1)} %copy-done.3, bf16[3,2304,384]{2,1,0:T(8,128)(2,1)} %w_ref.3, ...), custom_call_target="tpu_custom_call" | custom-call | bytes 6659328 | tf_op jit(solution)/shard_map/layer0/pallas_call | solution.py:542
  53.6 0.7 %dynamic-slice_add_fusion = f32[4,48]{1,0:T(4,128)} fusion(f32[4,48]{1,0:T(4,128)S(1)} %get-tuple-element.60, f32[4,768]{1,0:T(4,128)S(1)} %get-tuple-element.61, s32[]{:T(128)S(6)} %select_n.7), kind=kLoop, calls=%fused_computation.18 | loop fusion | flops 192 | bytes 2308 | tf_op jit(solution)/shard_map/add | solution.py:690
  54.3 1.2 %collective-permute-done.10.got_ref = bf16[192,384]{1,0:T(8,128)(2,1)S(1)} collective-permute-done((bf16[192,384]{1,0:T(8,128)(2,1)S(1)}, bf16[192,384]{1,0:T(8,128)(2,1)S(1)}, u32[]{:S(2)}, u32[]{:S(2)}) %collective-permute-start.10) | collective-permute-done | bytes 147488 | tf_op jit(solution)/shard_map/ppermute | solution.py:663
  55.5 0.7 %finish.1 = (f32[3,144,384]{2,1,0:T(8,128)}, f32[3,48,384]{2,1,0:T(8,128)}) custom-call(bf16[192,384]{1,0:T(8,128)(2,1)S(1)} %collective-permute-done.10.got_ref, f32[3,144,384]{2,1,0:T(8,128)} %get-tuple-element.56._, f32[3,48,384]{2,1,0:T(8,128)} %get-tuple-element.57.__), custom_call_target="tpu_custom_call", output_to_operand_aliasing={{0}: (1, {}), {1}: (2, {})} | custom-call | bytes 1916928 | tf_op jit(solution)/shard_map/finish/pallas_call | solution.py:542
  (1 shorter events, 0.0 us)
Async XLA Ops:
  0.6 17.9 %collective-permute-start = (bf16[176,768]{1,0:T(8,128)(2,1)}, bf16[176,768]{1,0:T(8,128)(2,1)S(1)}, u32[]{:S(2)}, u32[]{:S(2)}) collective-permute-start(bf16[176,768]{1,0:T(8,128)(2,1)} %bitcast.4), channel_id=1, source_target_pairs={{0,16},{2,18},{4,20},{6,22},{8,24},{10,26},{12,28},{14,30},{16,0},... | collective-permute-start | bytes 811016 | tf_op jit(solution)/shard_map/ppermute | solution.py:573
  6.0 12.5 %all-to-all-start = ((s32[16,1,176]{2,1,0:T(1,128)}), s32[16,1,176]{2,1,0:T(1,128)S(1)}, u32[]{:S(2)}, u32[]{:S(2)}) async-start(s32[16,1,176]{2,1,0:T(1,128)} %spread.1), calls=%async_computation | async-start | bytes 32768 | tf_op jit(solution)/shard_map/all_to_all | solution.py:575
  9.9 8.6 %copy-start = (bf16[1,176,768]{2,1,0:T(8,128)(2,1)S(1)}, bf16[1,176,768]{2,1,0:T(8,128)(2,1)}, u32[]{:S(2)}) copy-start(bf16[1,176,768]{2,1,0:T(8,128)(2,1)} %param.9) | copy-start | bytes 811012
  14.2 0.6 %copy-start.1 = (bf16[128,384]{1,0:T(8,128)(2,1)}, bf16[128,384]{1,0:T(8,128)(2,1)S(1)}, u32[]{:S(2)}) copy-start(bf16[128,384]{1,0:T(8,128)(2,1)S(1)} %get-tuple-element.55.act0_ref) | copy-start | bytes 294916
  25.4 3.0 %collective-permute-start.1 = (bf16[1536,384]{1,0:T(8,128)(2,1)S(1)}, bf16[1536,384]{1,0:T(8,128)(2,1)S(1)}, u32[]{:S(2)}, u32[]{:S(2)}) collective-permute-start(bf16[1536,384]{1,0:T(8,128)(2,1)S(1)} %get-tuple-element.37), channel_id=1, source_target_pairs={{0,2},{2,0},{4,6},{6,4},{8,10},{10,8},{12,14},{14,12},{16,18},{18,... | collective-permute-start | bytes 3538952 | tf_op jit(solution)/shard_map/ppermute | solution.py:630
  25.6 1.8 %copy-start.3 = (bf16[4,768]{1,0:T(4,128)(2,1)S(1)}, bf16[4,768]{1,0:T(4,128)(2,1)}, u32[]{:S(2)}) copy-start(bf16[4,768]{1,0:T(4,128)(2,1)} %embed_ref.3) | copy-start | bytes 18436
  27.0 1.5 %collective-permute-start.2 = (bf16[80,384]{1,0:T(8,128)(2,1)S(1)}, bf16[80,384]{1,0:T(8,128)(2,1)S(1)}, u32[]{:S(2)}, u32[]{:S(2)}) collective-permute-start(bf16[80,384]{1,0:T(8,128)(2,1)S(1)} %get-tuple-element.43), channel_id=1, source_target_pairs={{0,2},{2,0},{4,6},{6,4},{8,10},{10,8},{12,14},{14,12},{16,18},{18,... | collective-permute-start | bytes 184328 | tf_op jit(solution)/shard_map/ppermute | solution.py:640
  28.4 22.8 %copy-start.2 = (bf16[128,384]{1,0:T(8,128)(2,1)S(1)}, bf16[128,384]{1,0:T(8,128)(2,1)}, u32[]{:S(2)}) copy-start(bf16[128,384]{1,0:T(8,128)(2,1)} %copy-done.1) | copy-start | bytes 294916
  28.7 7.5 %collective-permute-start.3 = (bf16[224,384]{1,0:T(8,128)(2,1)S(1)}, bf16[224,384]{1,0:T(8,128)(2,1)S(1)}, u32[]{:S(2)}, u32[]{:S(2)}) collective-permute-start(bf16[224,384]{1,0:T(8,128)(2,1)S(1)} %get-tuple-element.45), channel_id=1, source_target_pairs={{0,12},{1,13},{2,3},{3,2},{4,8},{5,9},{6,7},{7,6},{8,4},{9,5},{10,... | collective-permute-start | bytes 516104 | tf_op jit(solution)/shard_map/ppermute | solution.py:656
  29.5 11.2 %collective-permute-start.4 = (bf16[224,384]{1,0:T(8,128)(2,1)S(1)}, bf16[224,384]{1,0:T(8,128)(2,1)S(1)}, u32[]{:S(2)}, u32[]{:S(2)}) collective-permute-start(bf16[224,384]{1,0:T(8,128)(2,1)S(1)} %get-tuple-element.46), channel_id=1, source_target_pairs={{0,9},{1,8},{2,6},{3,7},{4,13},{5,12},{6,2},{7,3},{8,1},{9,0},{10,... | collective-permute-start | bytes 516104 | tf_op jit(solution)/shard_map/ppermute | solution.py:656
  31.8 13.2 %collective-permute-start.5 = (bf16[224,384]{1,0:T(8,128)(2,1)S(1)}, bf16[224,384]{1,0:T(8,128)(2,1)S(1)}, u32[]{:S(2)}, u32[]{:S(2)}) collective-permute-start(bf16[224,384]{1,0:T(8,128)(2,1)S(1)} %get-tuple-element.47), channel_id=1, source_target_pairs={{0,5},{1,4},{2,10},{3,11},{4,1},{5,0},{6,14},{7,15},{8,13},{9,12},... | collective-permute-start | bytes 516104 | tf_op jit(solution)/shard_map/ppermute | solution.py:656
  33.2 12.8 %collective-permute-start.6 = (bf16[224,384]{1,0:T(8,128)(2,1)S(1)}, bf16[224,384]{1,0:T(8,128)(2,1)S(1)}, u32[]{:S(2)}, u32[]{:S(2)}) collective-permute-start(bf16[224,384]{1,0:T(8,128)(2,1)S(1)} %get-tuple-element.48), channel_id=1, source_target_pairs={{0,13},{1,12},{2,15},{3,14},{4,9},{5,8},{6,11},{7,10},{8,5},{9,4},... | collective-permute-start | bytes 516104 | tf_op jit(solution)/shard_map/ppermute | solution.py:656
  34.8 15.2 %collective-permute-start.7 = (bf16[224,384]{1,0:T(8,128)(2,1)S(1)}, bf16[224,384]{1,0:T(8,128)(2,1)S(1)}, u32[]{:S(2)}, u32[]{:S(2)}) collective-permute-start(bf16[224,384]{1,0:T(8,128)(2,1)S(1)} %get-tuple-element.49), channel_id=1, source_target_pairs={{0,1},{1,0},{2,14},{3,15},{4,5},{5,4},{6,10},{7,11},{8,9},{9,8},{1... | collective-permute-start | bytes 516104 | tf_op jit(solution)/shard_map/ppermute | solution.py:656
  36.2 13.9 %collective-permute-start.8 = (bf16[224,384]{1,0:T(8,128)(2,1)S(1)}, bf16[224,384]{1,0:T(8,128)(2,1)S(1)}, u32[]{:S(2)}, u32[]{:S(2)}) collective-permute-start(bf16[224,384]{1,0:T(8,128)(2,1)S(1)} %get-tuple-element.50), channel_id=1, source_target_pairs={{0,4},{1,5},{2,11},{3,10},{4,0},{5,1},{6,15},{7,14},{8,12},{9,13},... | collective-permute-start | bytes 516104 | tf_op jit(solution)/shard_map/ppermute | solution.py:656
  40.7 9.3 %collective-permute-start.9 = (bf16[224,384]{1,0:T(8,128)(2,1)S(1)}, bf16[224,384]{1,0:T(8,128)(2,1)S(1)}, u32[]{:S(2)}, u32[]{:S(2)}) collective-permute-start(bf16[224,384]{1,0:T(8,128)(2,1)S(1)} %get-tuple-element.51), channel_id=1, source_target_pairs={{0,8},{1,9},{2,7},{3,6},{4,12},{5,13},{6,3},{7,2},{8,0},{9,1},{10,... | collective-permute-start | bytes 516104 | tf_op jit(solution)/shard_map/ppermute | solution.py:656
  50.3 5.2 %collective-permute-start.10 = (bf16[192,384]{1,0:T(8,128)(2,1)S(1)}, bf16[192,384]{1,0:T(8,128)(2,1)S(1)}, u32[]{:S(2)}, u32[]{:S(2)}) collective-permute-start(bf16[192,384]{1,0:T(8,128)(2,1)S(1)} %get-tuple-element.52), channel_id=1, source_target_pairs={{0,1},{1,0},{2,3},{3,2},{4,5},{5,4},{6,7},{7,6},{8,9},{9,8},{10,11... | collective-permute-start | bytes 442376 | tf_op jit(solution)/shard_map/ppermute | solution.py:663

commit v10 on v6

--- a/solution.py
+++ b/solution.py
@@ -471,7 +471,7 @@
     for mask, out_ref in enumerate(out_refs):
         target, layer = m ^ (mask // 2), x ^ (mask % 2)
         at = pl.ds(pl.multiple_of((2 * target + layer) * part, 16), part)
-        out_ref[:part, :] = (mine_ref[at, :] + other_ref[at, :].astype(F32)).astype(out_ref.dtype)
+        out_ref[:part, :] = (mine_ref[at, :].astype(F32) + other_ref[at, :].astype(F32)).astype(out_ref.dtype)
         at = pl.ds(pl.multiple_of(target * 16, 16), 16)
         small = mine_small_ref[at, :] + other_small_ref[at, :].astype(F32)
         out_ref[part : part + 16, :] = small.astype(out_ref.dtype)
@@ -593,7 +593,7 @@
         lambda *refs: main_kernel(crow, prow, *refs),
         [
             shape((rb, width), F32),
-            near((STRIDE * part, mid), F32),
+            near((STRIDE * part, mid), BF16),
             near((STRIDE * part, mid), BF16),
             near((3 * CLASSES, mid), BF16),
             near((CLASSES, width), F32),

time: 54.8 us -> 54.9 us (level)
  no operation moved by 1% of the time
where the time goes in v10:
time: 54.9 us; the launch traced here: 54.7 us
  starting transfers between devices  19.7 us (36%)
  Pallas kernels  17.5 us (32%)
  waiting for transfers between devices  15.1 us (28%)
  other arithmetic  0.97 us (2%)
  local copies, waits for them, and re-layouts  0.77 us (1%)
  between operations  0.71 us (1%)
    pallas_call x8, Pallas kernels, call(): pl.pallas_call(kernel, out_shape=outs, in_specs=[pl.BlockSpec(memory_spac...  17.5 us
    ppermute x7, waiting for transfers between devices, on_device(): arrived.append(lax.ppermute(pieces[mask], ('seq', 'dp'), route))  9.67 us
    ppermute x7, starting transfers between devices, on_device(): arrived.append(lax.ppermute(pieces[mask], ('seq', 'dp'), route))  9.52 us
    ppermute x1, starting transfers between devices, on_device(): far = lax.ppermute(own, 'seq', [(s, (s + STRIDE) % n) for s in range(n)])  4.1 us
    all_to_all x1, starting transfers between devices, on_device(): gathered = lax.all_to_all(copies, 'seq', 0, 0, tiled=True)  3.91 us
    all_to_all x1, waiting for transfers between devices, on_device(): gathered = lax.all_to_all(copies, 'seq', 0, 0, tiled=True)  3.72 us
    ppermute x1, starting transfers between devices, on_device(): swapped = lax.ppermute(send, 'dp', [(d, d ^ 1) for d in range(dp)])  1.57 us
  transfers between devices with their start and end apart: 12, of which 8 were waited for; matrix products, arithmetic and copies ran while one was open for 2% of the time, Pallas kernels for 17%

profile of v10, /device:TPU:0, one launch (start us, length us, event | category | flops | bytes accessed | tf_op | source)
XLA Modules:
  0.0 54.7 jit_solution(3782342897657599207)
XLA Ops:
  0.6 4.1 %collective-permute-start = (bf16[176,768]{1,0:T(8,128)(2,1)}, bf16[176,768]{1,0:T(8,128)(2,1)S(1)}, u32[]{:S(2)}, u32[]{:S(2)}) collective-permute-start(bf16[176,768]{1,0:T(8,128)(2,1)} %bitcast.4), channel_id=1, source_target_pairs={{0,16},{2,18},{4,20},{6,22},{8,24},{10,26},{12,28},{14,30},{16,0},... | collective-permute-start | bytes 811016 | tf_op jit(solution)/shard_map/ppermute | solution.py:572
  4.7 1.3 %spread.1 = s32[16,1,176]{2,1,0:T(1,128)} custom-call(s32[1,176]{1,0:T(1,128)} %bases_ref.1), custom_call_target="tpu_custom_call" | custom-call | bytes 11968 | tf_op jit(solution)/shard_map/spread/pallas_call | solution.py:541
  6.0 3.9 %all-to-all-start = ((s32[16,1,176]{2,1,0:T(1,128)}), s32[16,1,176]{2,1,0:T(1,128)S(1)}, u32[]{:S(2)}, u32[]{:S(2)}) async-start(s32[16,1,176]{2,1,0:T(1,128)} %spread.1), calls=%async_computation | async-start | bytes 32768 | tf_op jit(solution)/shard_map/all_to_all | solution.py:574
  9.9 0.0 copy-start
  10.0 4.2 %tables.1 = (bf16[128,384]{1,0:T(8,128)(2,1)S(1)}, f32[128,2304]{1,0:T(8,128)S(1)}, bf16[2304,384]{1,0:T(8,128)(2,1)S(1)}) custom-call(bf16[4,768]{1,0:T(4,128)(2,1)} %embed_ref.3, bf16[3,2304,384]{2,1,0:T(8,128)(2,1)} %w_ref.3, bf16[3,384,768]{2,1,0:T(8,128)(2,1)} %refs_4_.1), custom_call_target="tpu_custom_call" | custom-call | flops 452984832 | bytes 10131456 | tf_op jit(solution)/shard_map/tables/pallas_call | solution.py:541
  14.2 0.0 copy-start.1
  14.2 0.6 %copy-done.1 = bf16[128,384]{1,0:T(8,128)(2,1)} copy-done((bf16[128,384]{1,0:T(8,128)(2,1)}, bf16[128,384]{1,0:T(8,128)(2,1)S(1)}, u32[]{:S(2)}) %copy-start.1) | copy-done | bytes 98328
  14.8 3.7 %all-to-all-done.refs_0_ = s32[16,1,176]{2,1,0:T(1,128)S(1)} async-done(((s32[16,1,176]{2,1,0:T(1,128)}), s32[16,1,176]{2,1,0:T(1,128)S(1)}, u32[]{:S(2)}, u32[]{:S(2)}) %all-to-all-start) | async-done | bytes 11296 | tf_op jit(solution)/shard_map/all_to_all | solution.py:574
  18.5 0.0 collective-permute-done.refs_2_
  18.5 0.0 copy-done
  18.5 7.0 %tower.1 = (f32[176,768]{1,0:T(8,128)}, bf16[1536,384]{1,0:T(8,128)(2,1)S(1)}, bf16[1536,384]{1,0:T(8,128)(2,1)S(1)}, bf16[384,384]{1,0:T(8,128)(2,1)S(1)}, f32[...) custom-call(s32[16,1,176]{2,1,0:T(1,128)S(1)} %all-to-all-done.refs_0_, ...), custom_call_target="tpu_custom_call" | custom-call | flops 2802843648 | bytes 16526336 | tf_op jit(solution)/shard_map/tower/pallas_call | solution.py:541
  25.5 0.2 collective-permute-start.1
  25.7 0.0 copy-start.3
  25.7 1.4 %classes.1 = (f32[80,384]{1,0:T(8,128)S(1)}, bf16[80,384]{1,0:T(8,128)(2,1)S(1)}) custom-call(bf16[384,384]{1,0:T(8,128)(2,1)S(1)} %get-tuple-element.38.refs_0_, f32[128,768]{1,0:T(8,128)S(1)} %get-tuple-element.39.refs_1_, f32[128,2304]{1,0:T(8,128)S(1)} %get-tuple-element.34.refs_6_.refs_2_, bf16[2304,384]{1,0:T(8,128)(2,1)S(1)} %get-tuple-element.40.refs_3_, ...), custom_call_target="tpu_custom_call" | custom-call | flops 452984832 | bytes 4411392 | tf_op jit(solution)/shard_map/classes/pallas_call | solution.py:541
  27.1 0.4 collective-permute-start.2
  27.5 0.0 copy-done.3
  27.5 0.1 fusion.8
  27.6 0.9 %collective-permute-done.2.refs_3_ = bf16[80,384]{1,0:T(8,128)(2,1)S(1)} collective-permute-done((bf16[80,384]{1,0:T(8,128)(2,1)S(1)}, bf16[80,384]{1,0:T(8,128)(2,1)S(1)}, u32[]{:S(2)}, u32[]{:S(2)}) %collective-permute-start.2) | collective-permute-done | bytes 61472 | tf_op jit(solution)/shard_map/ppermute | solution.py:639
  28.5 0.0 collective-permute-done.1.refs_1_
  28.5 0.0 copy-start.2
  28.5 0.3 messages.1
  28.9 1.7 %collective-permute-start.3 = (bf16[224,384]{1,0:T(8,128)(2,1)S(1)}, bf16[224,384]{1,0:T(8,128)(2,1)S(1)}, u32[]{:S(2)}, u32[]{:S(2)}) collective-permute-start(bf16[224,384]{1,0:T(8,128)(2,1)S(1)} %get-tuple-element.45), channel_id=1, source_target_pairs={{0,13},{1,12},{2,15},{3,14},{4,9},{5,8},{6,11},{7,10},{8,5},{9,4},... | collective-permute-start | bytes 516104 | tf_op jit(solution)/shard_map/ppermute | solution.py:654
  30.6 2.2 %collective-permute-start.4 = (bf16[224,384]{1,0:T(8,128)(2,1)S(1)}, bf16[224,384]{1,0:T(8,128)(2,1)S(1)}, u32[]{:S(2)}, u32[]{:S(2)}) collective-permute-start(bf16[224,384]{1,0:T(8,128)(2,1)S(1)} %get-tuple-element.46), channel_id=1, source_target_pairs={{0,12},{1,13},{2,14},{3,15},{4,8},{5,9},{6,10},{7,11},{8,4},{9,5},... | collective-permute-start | bytes 516104 | tf_op jit(solution)/shard_map/ppermute | solution.py:654
  32.8 0.5 collective-permute-start.5
  33.3 1.5 %collective-permute-start.6 = (bf16[224,384]{1,0:T(8,128)(2,1)S(1)}, bf16[224,384]{1,0:T(8,128)(2,1)S(1)}, u32[]{:S(2)}, u32[]{:S(2)}) collective-permute-start(bf16[224,384]{1,0:T(8,128)(2,1)S(1)} %get-tuple-element.48), channel_id=1, source_target_pairs={{0,9},{1,8},{2,11},{3,10},{4,13},{5,12},{6,15},{7,14},{8,1},{9,0},... | collective-permute-start | bytes 516104 | tf_op jit(solution)/shard_map/ppermute | solution.py:654
  34.8 0.7 %collective-permute-start.7 = (bf16[224,384]{1,0:T(8,128)(2,1)S(1)}, bf16[224,384]{1,0:T(8,128)(2,1)S(1)}, u32[]{:S(2)}, u32[]{:S(2)}) collective-permute-start(bf16[224,384]{1,0:T(8,128)(2,1)S(1)} %get-tuple-element.49), channel_id=1, source_target_pairs={{0,4},{1,5},{2,6},{3,7},{4,0},{5,1},{6,2},{7,3},{8,12},{9,13},{10,... | collective-permute-start | bytes 516104 | tf_op jit(solution)/shard_map/ppermute | solution.py:654
  35.5 2.5 %collective-permute-done.3.refs_0_ = bf16[224,384]{1,0:T(8,128)(2,1)S(1)} collective-permute-done((bf16[224,384]{1,0:T(8,128)(2,1)S(1)}, bf16[224,384]{1,0:T(8,128)(2,1)S(1)}, u32[]{:S(2)}, u32[]{:S(2)}) %collective-permute-start.3) | collective-permute-done | bytes 172064 | tf_op jit(solution)/shard_map/ppermute | solution.py:654
  38.1 2.3 %collective-permute-start.8 = (bf16[224,384]{1,0:T(8,128)(2,1)S(1)}, bf16[224,384]{1,0:T(8,128)(2,1)S(1)}, u32[]{:S(2)}, u32[]{:S(2)}) collective-permute-start(bf16[224,384]{1,0:T(8,128)(2,1)S(1)} %get-tuple-element.50), channel_id=1, source_target_pairs={{0,5},{1,4},{2,7},{3,6},{4,1},{5,0},{6,3},{7,2},{8,13},{9,12},{10,... | collective-permute-start | bytes 516104 | tf_op jit(solution)/shard_map/ppermute | solution.py:654
  40.3 1.6 %collective-permute-done.4.refs_1_ = bf16[224,384]{1,0:T(8,128)(2,1)S(1)} collective-permute-done((bf16[224,384]{1,0:T(8,128)(2,1)S(1)}, bf16[224,384]{1,0:T(8,128)(2,1)S(1)}, u32[]{:S(2)}, u32[]{:S(2)}) %collective-permute-start.4) | collective-permute-done | bytes 172064 | tf_op jit(solution)/shard_map/ppermute | solution.py:654
  41.9 0.6 %collective-permute-start.9 = (bf16[224,384]{1,0:T(8,128)(2,1)S(1)}, bf16[224,384]{1,0:T(8,128)(2,1)S(1)}, u32[]{:S(2)}, u32[]{:S(2)}) collective-permute-start(bf16[224,384]{1,0:T(8,128)(2,1)S(1)} %get-tuple-element.51), channel_id=1, source_target_pairs={{0,8},{1,9},{2,10},{3,11},{4,12},{5,13},{6,14},{7,15},{8,0},{9,1},... | collective-permute-start | bytes 516104 | tf_op jit(solution)/shard_map/ppermute | solution.py:654
  42.5 0.1 fusion.9
  42.6 0.1 fusion.11
  42.7 0.1 copy.15
  42.8 0.0 collective-permute-done.5.refs_2_
  42.8 2.7 %collective-permute-done.6.refs_3_ = bf16[224,384]{1,0:T(8,128)(2,1)S(1)} collective-permute-done((bf16[224,384]{1,0:T(8,128)(2,1)S(1)}, bf16[224,384]{1,0:T(8,128)(2,1)S(1)}, u32[]{:S(2)}, u32[]{:S(2)}) %collective-permute-start.6) | collective-permute-done | bytes 172064 | tf_op jit(solution)/shard_map/ppermute | solution.py:654
  45.6 1.0 %collective-permute-done.7.refs_4_ = bf16[224,384]{1,0:T(8,128)(2,1)S(1)} collective-permute-done((bf16[224,384]{1,0:T(8,128)(2,1)S(1)}, bf16[224,384]{1,0:T(8,128)(2,1)S(1)}, u32[]{:S(2)}, u32[]{:S(2)}) %collective-permute-start.7) | collective-permute-done | bytes 172064 | tf_op jit(solution)/shard_map/ppermute | solution.py:654
  46.5 1.8 %collective-permute-done.8.refs_5_ = bf16[224,384]{1,0:T(8,128)(2,1)S(1)} collective-permute-done((bf16[224,384]{1,0:T(8,128)(2,1)S(1)}, bf16[224,384]{1,0:T(8,128)(2,1)S(1)}, u32[]{:S(2)}, u32[]{:S(2)}) %collective-permute-start.8) | collective-permute-done | bytes 172064 | tf_op jit(solution)/shard_map/ppermute | solution.py:654
  48.4 0.0 collective-permute-done.9.refs_6_
  48.4 0.2 sums.1
  48.6 1.6 %collective-permute-start.10 = (bf16[192,384]{1,0:T(8,128)(2,1)S(1)}, bf16[192,384]{1,0:T(8,128)(2,1)S(1)}, u32[]{:S(2)}, u32[]{:S(2)}) collective-permute-start(bf16[192,384]{1,0:T(8,128)(2,1)S(1)} %get-tuple-element.52), channel_id=1, source_target_pairs={{0,1},{1,0},{2,3},{3,2},{4,5},{5,4},{6,7},{7,6},{8,9},{9,8},{10,11... | collective-permute-start | bytes 442376 | tf_op jit(solution)/shard_map/ppermute | solution.py:661
  50.1 0.0 copy-done.2
  50.1 2.4 %layer0.1 = (f32[3,144,384]{2,1,0:T(8,128)}, f32[3,48,384]{2,1,0:T(8,128)}, f32[4,768]{1,0:T(4,128)S(1)}, f32[4,48]{1,0:T(4,128)S(1)}) custom-call(f32[32,384]{1,0:T(8,128)S(1)} %get-tuple-element.53.rest_ref, f32[192,384]{1,0:T(8,128)S(1)} %get-tuple-element.54.total_ref, bf16[4,768]{1,0:T(4,128)(2,1)S(1)} %copy-done.3, bf16[3,2304,384]{2,1,0:T(8,128)(2,1)} %w_ref.3, ...), custom_call_target="tpu_custom_call" | custom-call | bytes 6659328 | tf_op jit(solution)/shard_map/layer0/pallas_call | solution.py:541
  52.5 0.7 %dynamic-slice_add_fusion = f32[4,48]{1,0:T(4,128)} fusion(f32[4,48]{1,0:T(4,128)S(1)} %get-tuple-element.60, f32[4,768]{1,0:T(4,128)S(1)} %get-tuple-element.61, s32[]{:T(128)S(6)} %select_n.7), kind=kLoop, calls=%fused_computation.18 | loop fusion | flops 192 | bytes 2308 | tf_op jit(solution)/shard_map/add | solution.py:688
  53.2 0.8 %collective-permute-done.10.got_ref = bf16[192,384]{1,0:T(8,128)(2,1)S(1)} collective-permute-done((bf16[192,384]{1,0:T(8,128)(2,1)S(1)}, bf16[192,384]{1,0:T(8,128)(2,1)S(1)}, u32[]{:S(2)}, u32[]{:S(2)}) %collective-permute-start.10) | collective-permute-done | bytes 147488 | tf_op jit(solution)/shard_map/ppermute | solution.py:661
  54.0 0.7 %finish.1 = (f32[3,144,384]{2,1,0:T(8,128)}, f32[3,48,384]{2,1,0:T(8,128)}) custom-call(bf16[192,384]{1,0:T(8,128)(2,1)S(1)} %collective-permute-done.10.got_ref, f32[3,144,384]{2,1,0:T(8,128)} %get-tuple-element.56._, f32[3,48,384]{2,1,0:T(8,128)} %get-tuple-element.57.__), custom_call_target="tpu_custom_call", output_to_operand_aliasing={{0}: (1, {}), {1}: (2, {})} | custom-call | bytes 1916928 | tf_op jit(solution)/shard_map/finish/pallas_call | solution.py:541
  (1 shorter events, 0.0 us)
Async XLA Ops:
  0.6 17.9 %collective-permute-start = (bf16[176,768]{1,0:T(8,128)(2,1)}, bf16[176,768]{1,0:T(8,128)(2,1)S(1)}, u32[]{:S(2)}, u32[]{:S(2)}) collective-permute-start(bf16[176,768]{1,0:T(8,128)(2,1)} %bitcast.4), channel_id=1, source_target_pairs={{0,16},{2,18},{4,20},{6,22},{8,24},{10,26},{12,28},{14,30},{16,0},... | collective-permute-start | bytes 811016 | tf_op jit(solution)/shard_map/ppermute | solution.py:572
  6.0 12.5 %all-to-all-start = ((s32[16,1,176]{2,1,0:T(1,128)}), s32[16,1,176]{2,1,0:T(1,128)S(1)}, u32[]{:S(2)}, u32[]{:S(2)}) async-start(s32[16,1,176]{2,1,0:T(1,128)} %spread.1), calls=%async_computation | async-start | bytes 32768 | tf_op jit(solution)/shard_map/all_to_all | solution.py:574
  9.9 8.6 %copy-start = (bf16[1,176,768]{2,1,0:T(8,128)(2,1)S(1)}, bf16[1,176,768]{2,1,0:T(8,128)(2,1)}, u32[]{:S(2)}) copy-start(bf16[1,176,768]{2,1,0:T(8,128)(2,1)} %param.9) | copy-start | bytes 811012
  14.2 0.6 %copy-start.1 = (bf16[128,384]{1,0:T(8,128)(2,1)}, bf16[128,384]{1,0:T(8,128)(2,1)S(1)}, u32[]{:S(2)}) copy-start(bf16[128,384]{1,0:T(8,128)(2,1)S(1)} %get-tuple-element.55.act0_ref) | copy-start | bytes 294916
  25.5 3.0 %collective-permute-start.1 = (bf16[1536,384]{1,0:T(8,128)(2,1)S(1)}, bf16[1536,384]{1,0:T(8,128)(2,1)S(1)}, u32[]{:S(2)}, u32[]{:S(2)}) collective-permute-start(bf16[1536,384]{1,0:T(8,128)(2,1)S(1)} %get-tuple-element.37), channel_id=1, source_target_pairs={{0,2},{2,0},{4,6},{6,4},{8,10},{10,8},{12,14},{14,12},{16,18},{18,... | collective-permute-start | bytes 3538952 | tf_op jit(solution)/shard_map/ppermute | solution.py:629
  25.7 1.8 %copy-start.3 = (bf16[4,768]{1,0:T(4,128)(2,1)S(1)}, bf16[4,768]{1,0:T(4,128)(2,1)}, u32[]{:S(2)}) copy-start(bf16[4,768]{1,0:T(4,128)(2,1)} %embed_ref.3) | copy-start | bytes 18436
  27.1 1.4 %collective-permute-start.2 = (bf16[80,384]{1,0:T(8,128)(2,1)S(1)}, bf16[80,384]{1,0:T(8,128)(2,1)S(1)}, u32[]{:S(2)}, u32[]{:S(2)}) collective-permute-start(bf16[80,384]{1,0:T(8,128)(2,1)S(1)} %get-tuple-element.43), channel_id=1, source_target_pairs={{0,2},{2,0},{4,6},{6,4},{8,10},{10,8},{12,14},{14,12},{16,18},{18,... | collective-permute-start | bytes 184328 | tf_op jit(solution)/shard_map/ppermute | solution.py:639
  28.5 21.6 %copy-start.2 = (bf16[128,384]{1,0:T(8,128)(2,1)S(1)}, bf16[128,384]{1,0:T(8,128)(2,1)}, u32[]{:S(2)}) copy-start(bf16[128,384]{1,0:T(8,128)(2,1)} %copy-done.1) | copy-start | bytes 294916
  28.9 9.2 %collective-permute-start.3 = (bf16[224,384]{1,0:T(8,128)(2,1)S(1)}, bf16[224,384]{1,0:T(8,128)(2,1)S(1)}, u32[]{:S(2)}, u32[]{:S(2)}) collective-permute-start(bf16[224,384]{1,0:T(8,128)(2,1)S(1)} %get-tuple-element.45), channel_id=1, source_target_pairs={{0,13},{1,12},{2,15},{3,14},{4,9},{5,8},{6,11},{7,10},{8,5},{9,4},... | collective-permute-start | bytes 516104 | tf_op jit(solution)/shard_map/ppermute | solution.py:654
  30.6 11.3 %collective-permute-start.4 = (bf16[224,384]{1,0:T(8,128)(2,1)S(1)}, bf16[224,384]{1,0:T(8,128)(2,1)S(1)}, u32[]{:S(2)}, u32[]{:S(2)}) collective-permute-start(bf16[224,384]{1,0:T(8,128)(2,1)S(1)} %get-tuple-element.46), channel_id=1, source_target_pairs={{0,12},{1,13},{2,14},{3,15},{4,8},{5,9},{6,10},{7,11},{8,4},{9,5},... | collective-permute-start | bytes 516104 | tf_op jit(solution)/shard_map/ppermute | solution.py:654
  32.8 10.0 %collective-permute-start.5 = (bf16[224,384]{1,0:T(8,128)(2,1)S(1)}, bf16[224,384]{1,0:T(8,128)(2,1)S(1)}, u32[]{:S(2)}, u32[]{:S(2)}) collective-permute-start(bf16[224,384]{1,0:T(8,128)(2,1)S(1)} %get-tuple-element.47), channel_id=1, source_target_pairs={{0,1},{1,0},{2,3},{3,2},{4,5},{5,4},{6,7},{7,6},{8,9},{9,8},{10,11... | collective-permute-start | bytes 516104 | tf_op jit(solution)/shard_map/ppermute | solution.py:654
  33.3 12.2 %collective-permute-start.6 = (bf16[224,384]{1,0:T(8,128)(2,1)S(1)}, bf16[224,384]{1,0:T(8,128)(2,1)S(1)}, u32[]{:S(2)}, u32[]{:S(2)}) collective-permute-start(bf16[224,384]{1,0:T(8,128)(2,1)S(1)} %get-tuple-element.48), channel_id=1, source_target_pairs={{0,9},{1,8},{2,11},{3,10},{4,13},{5,12},{6,15},{7,14},{8,1},{9,0},... | collective-permute-start | bytes 516104 | tf_op jit(solution)/shard_map/ppermute | solution.py:654
  34.8 11.7 %collective-permute-start.7 = (bf16[224,384]{1,0:T(8,128)(2,1)S(1)}, bf16[224,384]{1,0:T(8,128)(2,1)S(1)}, u32[]{:S(2)}, u32[]{:S(2)}) collective-permute-start(bf16[224,384]{1,0:T(8,128)(2,1)S(1)} %get-tuple-element.49), channel_id=1, source_target_pairs={{0,4},{1,5},{2,6},{3,7},{4,0},{5,1},{6,2},{7,3},{8,12},{9,13},{10,... | collective-permute-start | bytes 516104 | tf_op jit(solution)/shard_map/ppermute | solution.py:654
  38.1 10.3 %collective-permute-start.8 = (bf16[224,384]{1,0:T(8,128)(2,1)S(1)}, bf16[224,384]{1,0:T(8,128)(2,1)S(1)}, u32[]{:S(2)}, u32[]{:S(2)}) collective-permute-start(bf16[224,384]{1,0:T(8,128)(2,1)S(1)} %get-tuple-element.50), channel_id=1, source_target_pairs={{0,5},{1,4},{2,7},{3,6},{4,1},{5,0},{6,3},{7,2},{8,13},{9,12},{10,... | collective-permute-start | bytes 516104 | tf_op jit(solution)/shard_map/ppermute | solution.py:654
  41.9 6.5 %collective-permute-start.9 = (bf16[224,384]{1,0:T(8,128)(2,1)S(1)}, bf16[224,384]{1,0:T(8,128)(2,1)S(1)}, u32[]{:S(2)}, u32[]{:S(2)}) collective-permute-start(bf16[224,384]{1,0:T(8,128)(2,1)S(1)} %get-tuple-element.51), channel_id=1, source_target_pairs={{0,8},{1,9},{2,10},{3,11},{4,12},{5,13},{6,14},{7,15},{8,0},{9,1},... | collective-permute-start | bytes 516104 | tf_op jit(solution)/shard_map/ppermute | solution.py:654
  48.6 5.4 %collective-permute-start.10 = (bf16[192,384]{1,0:T(8,128)(2,1)S(1)}, bf16[192,384]{1,0:T(8,128)(2,1)S(1)}, u32[]{:S(2)}, u32[]{:S(2)}) collective-permute-start(bf16[192,384]{1,0:T(8,128)(2,1)S(1)} %get-tuple-element.52), channel_id=1, source_target_pairs={{0,1},{1,0},{2,3},{3,2},{4,5},{5,4},{6,7},{7,6},{8,9},{9,8},{10,11... | collective-permute-start | bytes 442376 | tf_op jit(solution)/shard_map/ppermute | solution.py:661

commit v11 on v6

--- a/solution.py
+++ b/solution.py
@@ -435,7 +435,7 @@
         copy.wait()
 
 
-def class_kernel(prow, h_ref, c_ref, table_ref, w1_ref, p0_ref, mine_ref, other_ref, bt_ref):
+def class_kernel(prow, h_ref, c_ref, table_ref, w1_ref, p0_ref, mine_ref, other_ref, b_ref, bt_ref):
     width, mid = c_ref.shape[1], h_ref.shape[1]
     half = width // 2
     k = lax.axis_index("seq")
@@ -452,11 +452,12 @@
     b = c_ref[...] + scale * (ng - stab * (scale * scale * inner))
     s = (mm_nt(b.astype(BF16), p0_ref[...]) * table_ref[:, width : width + mid]).astype(BF16)
     g = mm(digit_rows(), s)
-    bt_ref[...] = jnp.transpose(b)
+    b_ref[...] = b
+    bt_ref[...] = jnp.transpose(b_ref[:, pl.ds(pl.multiple_of(zh * half, 128), half)])
     for target, side in ((mine_ref, core), (other_ref, 1 - core)):
         for m in range(STRIDE // 2):
             for q in range(3):
-                at = pl.ds(pl.multiple_of(zh * half + (2 * m + side) * prow + 16 * q, 16), 16)
+                at = pl.ds(pl.multiple_of((2 * m + side) * prow + 16 * q, 16), 16)
                 target[16 * m : 16 * m + 16, q * CLASSES : (q + 1) * CLASSES] = bt_ref[at, :].astype(
                     target.dtype
                 )
@@ -632,7 +633,7 @@
         lambda *refs: class_kernel(prow, *refs),
         [near((small_rows, mid), F32), near((small_rows, mid), BF16)],
         h, c, table, w1, p0,
-        scratch=[pltpu.VMEM((width, CLASSES), F32)],
+        scratch=[pltpu.VMEM((CLASSES, width), F32), pltpu.VMEM((width // 2, CLASSES), F32)],
         flops=4 * CLASSES * 3 * width * mid,
         name="classes",
     )

time: 54.8 us -> 54.8 us (level)
  no operation moved by 1% of the time
where the time goes in v11:
time: 54.8 us; the launch traced here: 54.5 us
  starting transfers between devices  19.7 us (36%)
  Pallas kernels  17.3 us (32%)
  waiting for transfers between devices  15.1 us (28%)
  other arithmetic  0.97 us (2%)
  local copies, waits for them, and re-layouts  0.77 us (1%)
  between operations  0.71 us (1%)
    pallas_call x8, Pallas kernels, call(): pl.pallas_call(kernel, out_shape=outs, in_specs=[pl.BlockSpec(memory_spac...  17.3 us
    ppermute x7, waiting for transfers between devices, on_device(): arrived.append(lax.ppermute(pieces[mask], ('seq', 'dp'), route))  9.64 us
    ppermute x7, starting transfers between devices, on_device(): arrived.append(lax.ppermute(pieces[mask], ('seq', 'dp'), route))  9.54 us
    ppermute x1, starting transfers between devices, on_device(): far = lax.ppermute(own, 'seq', [(s, (s + STRIDE) % n) for s in range(n)])  4.1 us
    all_to_all x1, starting transfers between devices, on_device(): gathered = lax.all_to_all(copies, 'seq', 0, 0, tiled=True)  3.91 us
    all_to_all x1, waiting for transfers between devices, on_device(): gathered = lax.all_to_all(copies, 'seq', 0, 0, tiled=True)  3.72 us
    ppermute x1, starting transfers between devices, on_device(): swapped = lax.ppermute(send, 'dp', [(d, d ^ 1) for d in range(dp)])  1.58 us
  transfers between devices with their start and end apart: 12, of which 8 were waited for; matrix products, arithmetic and copies ran while one was open for 2% of the time, Pallas kernels for 17%

profile of v11, /device:TPU:0, one launch (start us, length us, event | category | flops | bytes accessed | tf_op | source)
XLA Modules:
  0.0 54.5 jit_solution(8692144361918663000)
XLA Ops:
  0.6 4.1 %collective-permute-start = (bf16[176,768]{1,0:T(8,128)(2,1)}, bf16[176,768]{1,0:T(8,128)(2,1)S(1)}, u32[]{:S(2)}, u32[]{:S(2)}) collective-permute-start(bf16[176,768]{1,0:T(8,128)(2,1)} %bitcast.4), channel_id=1, source_target_pairs={{0,16},{2,18},{4,20},{6,22},{8,24},{10,26},{12,28},{14,30},{16,0},... | collective-permute-start | bytes 811016 | tf_op jit(solution)/shard_map/ppermute | solution.py:573
  4.7 1.3 %spread.1 = s32[16,1,176]{2,1,0:T(1,128)} custom-call(s32[1,176]{1,0:T(1,128)} %bases_ref.1), custom_call_target="tpu_custom_call" | custom-call | bytes 11968 | tf_op jit(solution)/shard_map/spread/pallas_call | solution.py:542
  6.0 3.9 %all-to-all-start = ((s32[16,1,176]{2,1,0:T(1,128)}), s32[16,1,176]{2,1,0:T(1,128)S(1)}, u32[]{:S(2)}, u32[]{:S(2)}) async-start(s32[16,1,176]{2,1,0:T(1,128)} %spread.1), calls=%async_computation | async-start | bytes 32768 | tf_op jit(solution)/shard_map/all_to_all | solution.py:575
  9.9 0.0 copy-start
  10.0 4.2 %tables.1 = (bf16[128,384]{1,0:T(8,128)(2,1)S(1)}, f32[128,2304]{1,0:T(8,128)S(1)}, bf16[2304,384]{1,0:T(8,128)(2,1)S(1)}) custom-call(bf16[4,768]{1,0:T(4,128)(2,1)} %embed_ref.3, bf16[3,2304,384]{2,1,0:T(8,128)(2,1)} %w_ref.3, bf16[3,384,768]{2,1,0:T(8,128)(2,1)} %refs_4_.1), custom_call_target="tpu_custom_call" | custom-call | flops 452984832 | bytes 10131456 | tf_op jit(solution)/shard_map/tables/pallas_call | solution.py:542
  14.2 0.0 copy-start.1
  14.2 0.6 %copy-done.1 = bf16[128,384]{1,0:T(8,128)(2,1)} copy-done((bf16[128,384]{1,0:T(8,128)(2,1)}, bf16[128,384]{1,0:T(8,128)(2,1)S(1)}, u32[]{:S(2)}) %copy-start.1) | copy-done | bytes 98328
  14.8 3.7 %all-to-all-done.refs_0_ = s32[16,1,176]{2,1,0:T(1,128)S(1)} async-done(((s32[16,1,176]{2,1,0:T(1,128)}), s32[16,1,176]{2,1,0:T(1,128)S(1)}, u32[]{:S(2)}, u32[]{:S(2)}) %all-to-all-start) | async-done | bytes 11296 | tf_op jit(solution)/shard_map/all_to_all | solution.py:575
  18.5 0.0 collective-permute-done.refs_2_
  18.5 0.0 copy-done
  18.5 6.9 %tower.1 = (f32[176,768]{1,0:T(8,128)}, f32[1536,384]{1,0:T(8,128)S(1)}, bf16[1536,384]{1,0:T(8,128)(2,1)S(1)}, bf16[384,384]{1,0:T(8,128)(2,1)S(1)}, f32[128,76...) custom-call(s32[16,1,176]{2,1,0:T(1,128)S(1)} %all-to-all-done.refs_0_, ...), custom_call_target="tpu_custom_call" | custom-call | flops 2802843648 | bytes 17705984 | tf_op jit(solution)/shard_map/tower/pallas_call | solution.py:542
  25.4 0.2 collective-permute-start.1
  25.6 0.0 copy-start.3
  25.6 1.4 %classes.1 = (f32[80,384]{1,0:T(8,128)S(1)}, bf16[80,384]{1,0:T(8,128)(2,1)S(1)}) custom-call(bf16[384,384]{1,0:T(8,128)(2,1)S(1)} %get-tuple-element.38.refs_0_, f32[128,768]{1,0:T(8,128)S(1)} %get-tuple-element.39.refs_1_, f32[128,2304]{1,0:T(8,128)S(1)} %get-tuple-element.34.refs_6_.refs_2_, bf16[2304,384]{1,0:T(8,128)(2,1)S(1)} %get-tuple-element.40.refs_3_, ...), custom_call_target="tpu_custom_call" | custom-call | flops 452984832 | bytes 4411392 | tf_op jit(solution)/shard_map/classes/pallas_call | solution.py:542
  27.0 0.4 collective-permute-start.2
  27.4 0.0 copy-done.3
  27.4 0.1 fusion.8
  27.5 0.9 %collective-permute-done.2.refs_3_ = bf16[80,384]{1,0:T(8,128)(2,1)S(1)} collective-permute-done((bf16[80,384]{1,0:T(8,128)(2,1)S(1)}, bf16[80,384]{1,0:T(8,128)(2,1)S(1)}, u32[]{:S(2)}, u32[]{:S(2)}) %collective-permute-start.2) | collective-permute-done | bytes 61472 | tf_op jit(solution)/shard_map/ppermute | solution.py:640
  28.4 0.0 collective-permute-done.1.refs_1_
  28.4 0.0 copy-start.2
  28.4 0.2 messages.1
  28.7 1.7 %collective-permute-start.3 = (bf16[224,384]{1,0:T(8,128)(2,1)S(1)}, bf16[224,384]{1,0:T(8,128)(2,1)S(1)}, u32[]{:S(2)}, u32[]{:S(2)}) collective-permute-start(bf16[224,384]{1,0:T(8,128)(2,1)S(1)} %get-tuple-element.45), channel_id=1, source_target_pairs={{0,13},{1,12},{2,15},{3,14},{4,9},{5,8},{6,11},{7,10},{8,5},{9,4},... | collective-permute-start | bytes 516104 | tf_op jit(solution)/shard_map/ppermute | solution.py:655
  30.4 2.2 %collective-permute-start.4 = (bf16[224,384]{1,0:T(8,128)(2,1)S(1)}, bf16[224,384]{1,0:T(8,128)(2,1)S(1)}, u32[]{:S(2)}, u32[]{:S(2)}) collective-permute-start(bf16[224,384]{1,0:T(8,128)(2,1)S(1)} %get-tuple-element.46), channel_id=1, source_target_pairs={{0,12},{1,13},{2,14},{3,15},{4,8},{5,9},{6,10},{7,11},{8,4},{9,5},... | collective-permute-start | bytes 516104 | tf_op jit(solution)/shard_map/ppermute | solution.py:655
  32.6 0.5 collective-permute-start.5
  33.1 1.5 %collective-permute-start.6 = (bf16[224,384]{1,0:T(8,128)(2,1)S(1)}, bf16[224,384]{1,0:T(8,128)(2,1)S(1)}, u32[]{:S(2)}, u32[]{:S(2)}) collective-permute-start(bf16[224,384]{1,0:T(8,128)(2,1)S(1)} %get-tuple-element.48), channel_id=1, source_target_pairs={{0,9},{1,8},{2,11},{3,10},{4,13},{5,12},{6,15},{7,14},{8,1},{9,0},... | collective-permute-start | bytes 516104 | tf_op jit(solution)/shard_map/ppermute | solution.py:655
  34.6 0.7 %collective-permute-start.7 = (bf16[224,384]{1,0:T(8,128)(2,1)S(1)}, bf16[224,384]{1,0:T(8,128)(2,1)S(1)}, u32[]{:S(2)}, u32[]{:S(2)}) collective-permute-start(bf16[224,384]{1,0:T(8,128)(2,1)S(1)} %get-tuple-element.49), channel_id=1, source_target_pairs={{0,4},{1,5},{2,6},{3,7},{4,0},{5,1},{6,2},{7,3},{8,12},{9,13},{10,... | collective-permute-start | bytes 516104 | tf_op jit(solution)/shard_map/ppermute | solution.py:655
  35.4 2.5 %collective-permute-done.3.refs_0_ = bf16[224,384]{1,0:T(8,128)(2,1)S(1)} collective-permute-done((bf16[224,384]{1,0:T(8,128)(2,1)S(1)}, bf16[224,384]{1,0:T(8,128)(2,1)S(1)}, u32[]{:S(2)}, u32[]{:S(2)}) %collective-permute-start.3) | collective-permute-done | bytes 172064 | tf_op jit(solution)/shard_map/ppermute | solution.py:655
  37.9 2.3 %collective-permute-start.8 = (bf16[224,384]{1,0:T(8,128)(2,1)S(1)}, bf16[224,384]{1,0:T(8,128)(2,1)S(1)}, u32[]{:S(2)}, u32[]{:S(2)}) collective-permute-start(bf16[224,384]{1,0:T(8,128)(2,1)S(1)} %get-tuple-element.50), channel_id=1, source_target_pairs={{0,5},{1,4},{2,7},{3,6},{4,1},{5,0},{6,3},{7,2},{8,13},{9,12},{10,... | collective-permute-start | bytes 516104 | tf_op jit(solution)/shard_map/ppermute | solution.py:655
  40.2 1.6 %collective-permute-done.4.refs_1_ = bf16[224,384]{1,0:T(8,128)(2,1)S(1)} collective-permute-done((bf16[224,384]{1,0:T(8,128)(2,1)S(1)}, bf16[224,384]{1,0:T(8,128)(2,1)S(1)}, u32[]{:S(2)}, u32[]{:S(2)}) %collective-permute-start.4) | collective-permute-done | bytes 172064 | tf_op jit(solution)/shard_map/ppermute | solution.py:655
  41.7 0.6 %collective-permute-start.9 = (bf16[224,384]{1,0:T(8,128)(2,1)S(1)}, bf16[224,384]{1,0:T(8,128)(2,1)S(1)}, u32[]{:S(2)}, u32[]{:S(2)}) collective-permute-start(bf16[224,384]{1,0:T(8,128)(2,1)S(1)} %get-tuple-element.51), channel_id=1, source_target_pairs={{0,8},{1,9},{2,10},{3,11},{4,12},{5,13},{6,14},{7,15},{8,0},{9,1},... | collective-permute-start | bytes 516104 | tf_op jit(solution)/shard_map/ppermute | solution.py:655
  42.3 0.1 fusion.9
  42.4 0.1 fusion.11
  42.5 0.1 copy.15
  42.6 0.0 collective-permute-done.5.refs_2_
  42.6 2.7 %collective-permute-done.6.refs_3_ = bf16[224,384]{1,0:T(8,128)(2,1)S(1)} collective-permute-done((bf16[224,384]{1,0:T(8,128)(2,1)S(1)}, bf16[224,384]{1,0:T(8,128)(2,1)S(1)}, u32[]{:S(2)}, u32[]{:S(2)}) %collective-permute-start.6) | collective-permute-done | bytes 172064 | tf_op jit(solution)/shard_map/ppermute | solution.py:655
  45.4 1.0 %collective-permute-done.7.refs_4_ = bf16[224,384]{1,0:T(8,128)(2,1)S(1)} collective-permute-done((bf16[224,384]{1,0:T(8,128)(2,1)S(1)}, bf16[224,384]{1,0:T(8,128)(2,1)S(1)}, u32[]{:S(2)}, u32[]{:S(2)}) %collective-permute-start.7) | collective-permute-done | bytes 172064 | tf_op jit(solution)/shard_map/ppermute | solution.py:655
  46.4 1.8 %collective-permute-done.8.refs_5_ = bf16[224,384]{1,0:T(8,128)(2,1)S(1)} collective-permute-done((bf16[224,384]{1,0:T(8,128)(2,1)S(1)}, bf16[224,384]{1,0:T(8,128)(2,1)S(1)}, u32[]{:S(2)}, u32[]{:S(2)}) %collective-permute-start.8) | collective-permute-done | bytes 172064 | tf_op jit(solution)/shard_map/ppermute | solution.py:655
  48.2 0.0 collective-permute-done.9.refs_6_
  48.2 0.2 sums.1
  48.4 1.6 %collective-permute-start.10 = (bf16[192,384]{1,0:T(8,128)(2,1)S(1)}, bf16[192,384]{1,0:T(8,128)(2,1)S(1)}, u32[]{:S(2)}, u32[]{:S(2)}) collective-permute-start(bf16[192,384]{1,0:T(8,128)(2,1)S(1)} %get-tuple-element.52), channel_id=1, source_target_pairs={{0,1},{1,0},{2,3},{3,2},{4,5},{5,4},{6,7},{7,6},{8,9},{9,8},{10,11... | collective-permute-start | bytes 442376 | tf_op jit(solution)/shard_map/ppermute | solution.py:662
  50.0 0.0 copy-done.2
  50.0 2.4 %layer0.1 = (f32[3,144,384]{2,1,0:T(8,128)}, f32[3,48,384]{2,1,0:T(8,128)}, f32[4,768]{1,0:T(4,128)S(1)}, f32[4,48]{1,0:T(4,128)S(1)}) custom-call(f32[32,384]{1,0:T(8,128)S(1)} %get-tuple-element.53.rest_ref, f32[192,384]{1,0:T(8,128)S(1)} %get-tuple-element.54.total_ref, bf16[4,768]{1,0:T(4,128)(2,1)S(1)} %copy-done.3, bf16[3,2304,384]{2,1,0:T(8,128)(2,1)} %w_ref.3, ...), custom_call_target="tpu_custom_call" | custom-call | bytes 6659328 | tf_op jit(solution)/shard_map/layer0/pallas_call | solution.py:542
  52.3 0.7 %dynamic-slice_add_fusion = f32[4,48]{1,0:T(4,128)} fusion(f32[4,48]{1,0:T(4,128)S(1)} %get-tuple-element.60, f32[4,768]{1,0:T(4,128)S(1)} %get-tuple-element.61, s32[]{:T(128)S(6)} %select_n.7), kind=kLoop, calls=%fused_computation.18 | loop fusion | flops 192 | bytes 2308 | tf_op jit(solution)/shard_map/add | solution.py:689
  53.0 0.8 %collective-permute-done.10.got_ref = bf16[192,384]{1,0:T(8,128)(2,1)S(1)} collective-permute-done((bf16[192,384]{1,0:T(8,128)(2,1)S(1)}, bf16[192,384]{1,0:T(8,128)(2,1)S(1)}, u32[]{:S(2)}, u32[]{:S(2)}) %collective-permute-start.10) | collective-permute-done | bytes 147488 | tf_op jit(solution)/shard_map/ppermute | solution.py:662
  53.8 0.7 %finish.1 = (f32[3,144,384]{2,1,0:T(8,128)}, f32[3,48,384]{2,1,0:T(8,128)}) custom-call(bf16[192,384]{1,0:T(8,128)(2,1)S(1)} %collective-permute-done.10.got_ref, f32[3,144,384]{2,1,0:T(8,128)} %get-tuple-element.56._, f32[3,48,384]{2,1,0:T(8,128)} %get-tuple-element.57.__), custom_call_target="tpu_custom_call", output_to_operand_aliasing={{0}: (1, {}), {1}: (2, {})} | custom-call | bytes 1916928 | tf_op jit(solution)/shard_map/finish/pallas_call | solution.py:542
  (1 shorter events, 0.0 us)
Async XLA Ops:
  0.6 17.9 %collective-permute-start = (bf16[176,768]{1,0:T(8,128)(2,1)}, bf16[176,768]{1,0:T(8,128)(2,1)S(1)}, u32[]{:S(2)}, u32[]{:S(2)}) collective-permute-start(bf16[176,768]{1,0:T(8,128)(2,1)} %bitcast.4), channel_id=1, source_target_pairs={{0,16},{2,18},{4,20},{6,22},{8,24},{10,26},{12,28},{14,30},{16,0},... | collective-permute-start | bytes 811016 | tf_op jit(solution)/shard_map/ppermute | solution.py:573
  6.0 12.5 %all-to-all-start = ((s32[16,1,176]{2,1,0:T(1,128)}), s32[16,1,176]{2,1,0:T(1,128)S(1)}, u32[]{:S(2)}, u32[]{:S(2)}) async-start(s32[16,1,176]{2,1,0:T(1,128)} %spread.1), calls=%async_computation | async-start | bytes 32768 | tf_op jit(solution)/shard_map/all_to_all | solution.py:575
  9.9 8.6 %copy-start = (bf16[1,176,768]{2,1,0:T(8,128)(2,1)S(1)}, bf16[1,176,768]{2,1,0:T(8,128)(2,1)}, u32[]{:S(2)}) copy-start(bf16[1,176,768]{2,1,0:T(8,128)(2,1)} %param.9) | copy-start | bytes 811012
  14.2 0.6 %copy-start.1 = (bf16[128,384]{1,0:T(8,128)(2,1)}, bf16[128,384]{1,0:T(8,128)(2,1)S(1)}, u32[]{:S(2)}) copy-start(bf16[128,384]{1,0:T(8,128)(2,1)S(1)} %get-tuple-element.55.act0_ref) | copy-start | bytes 294916
  25.4 3.0 %collective-permute-start.1 = (bf16[1536,384]{1,0:T(8,128)(2,1)S(1)}, bf16[1536,384]{1,0:T(8,128)(2,1)S(1)}, u32[]{:S(2)}, u32[]{:S(2)}) collective-permute-start(bf16[1536,384]{1,0:T(8,128)(2,1)S(1)} %get-tuple-element.37), channel_id=1, source_target_pairs={{0,2},{2,0},{4,6},{6,4},{8,10},{10,8},{12,14},{14,12},{16,18},{18,... | collective-permute-start | bytes 3538952 | tf_op jit(solution)/shard_map/ppermute | solution.py:630
  25.6 1.8 %copy-start.3 = (bf16[4,768]{1,0:T(4,128)(2,1)S(1)}, bf16[4,768]{1,0:T(4,128)(2,1)}, u32[]{:S(2)}) copy-start(bf16[4,768]{1,0:T(4,128)(2,1)} %embed_ref.3) | copy-start | bytes 18436
  27.0 1.5 %collective-permute-start.2 = (bf16[80,384]{1,0:T(8,128)(2,1)S(1)}, bf16[80,384]{1,0:T(8,128)(2,1)S(1)}, u32[]{:S(2)}, u32[]{:S(2)}) collective-permute-start(bf16[80,384]{1,0:T(8,128)(2,1)S(1)} %get-tuple-element.43), channel_id=1, source_target_pairs={{0,2},{2,0},{4,6},{6,4},{8,10},{10,8},{12,14},{14,12},{16,18},{18,... | collective-permute-start | bytes 184328 | tf_op jit(solution)/shard_map/ppermute | solution.py:640
  28.4 21.5 %copy-start.2 = (bf16[128,384]{1,0:T(8,128)(2,1)S(1)}, bf16[128,384]{1,0:T(8,128)(2,1)}, u32[]{:S(2)}) copy-start(bf16[128,384]{1,0:T(8,128)(2,1)} %copy-done.1) | copy-start | bytes 294916
  28.7 9.2 %collective-permute-start.3 = (bf16[224,384]{1,0:T(8,128)(2,1)S(1)}, bf16[224,384]{1,0:T(8,128)(2,1)S(1)}, u32[]{:S(2)}, u32[]{:S(2)}) collective-permute-start(bf16[224,384]{1,0:T(8,128)(2,1)S(1)} %get-tuple-element.45), channel_id=1, source_target_pairs={{0,13},{1,12},{2,15},{3,14},{4,9},{5,8},{6,11},{7,10},{8,5},{9,4},... | collective-permute-start | bytes 516104 | tf_op jit(solution)/shard_map/ppermute | solution.py:655
  30.4 11.3 %collective-permute-start.4 = (bf16[224,384]{1,0:T(8,128)(2,1)S(1)}, bf16[224,384]{1,0:T(8,128)(2,1)S(1)}, u32[]{:S(2)}, u32[]{:S(2)}) collective-permute-start(bf16[224,384]{1,0:T(8,128)(2,1)S(1)} %get-tuple-element.46), channel_id=1, source_target_pairs={{0,12},{1,13},{2,14},{3,15},{4,8},{5,9},{6,10},{7,11},{8,4},{9,5},... | collective-permute-start | bytes 516104 | tf_op jit(solution)/shard_map/ppermute | solution.py:655
  32.6 10.0 %collective-permute-start.5 = (bf16[224,384]{1,0:T(8,128)(2,1)S(1)}, bf16[224,384]{1,0:T(8,128)(2,1)S(1)}, u32[]{:S(2)}, u32[]{:S(2)}) collective-permute-start(bf16[224,384]{1,0:T(8,128)(2,1)S(1)} %get-tuple-element.47), channel_id=1, source_target_pairs={{0,1},{1,0},{2,3},{3,2},{4,5},{5,4},{6,7},{7,6},{8,9},{9,8},{10,11... | collective-permute-start | bytes 516104 | tf_op jit(solution)/shard_map/ppermute | solution.py:655
  33.1 12.2 %collective-permute-start.6 = (bf16[224,384]{1,0:T(8,128)(2,1)S(1)}, bf16[224,384]{1,0:T(8,128)(2,1)S(1)}, u32[]{:S(2)}, u32[]{:S(2)}) collective-permute-start(bf16[224,384]{1,0:T(8,128)(2,1)S(1)} %get-tuple-element.48), channel_id=1, source_target_pairs={{0,9},{1,8},{2,11},{3,10},{4,13},{5,12},{6,15},{7,14},{8,1},{9,0},... | collective-permute-start | bytes 516104 | tf_op jit(solution)/shard_map/ppermute | solution.py:655
  34.6 11.7 %collective-permute-start.7 = (bf16[224,384]{1,0:T(8,128)(2,1)S(1)}, bf16[224,384]{1,0:T(8,128)(2,1)S(1)}, u32[]{:S(2)}, u32[]{:S(2)}) collective-permute-start(bf16[224,384]{1,0:T(8,128)(2,1)S(1)} %get-tuple-element.49), channel_id=1, source_target_pairs={{0,4},{1,5},{2,6},{3,7},{4,0},{5,1},{6,2},{7,3},{8,12},{9,13},{10,... | collective-permute-start | bytes 516104 | tf_op jit(solution)/shard_map/ppermute | solution.py:655
  37.9 10.3 %collective-permute-start.8 = (bf16[224,384]{1,0:T(8,128)(2,1)S(1)}, bf16[224,384]{1,0:T(8,128)(2,1)S(1)}, u32[]{:S(2)}, u32[]{:S(2)}) collective-permute-start(bf16[224,384]{1,0:T(8,128)(2,1)S(1)} %get-tuple-element.50), channel_id=1, source_target_pairs={{0,5},{1,4},{2,7},{3,6},{4,1},{5,0},{6,3},{7,2},{8,13},{9,12},{10,... | collective-permute-start | bytes 516104 | tf_op jit(solution)/shard_map/ppermute | solution.py:655
  41.7 6.5 %collective-permute-start.9 = (bf16[224,384]{1,0:T(8,128)(2,1)S(1)}, bf16[224,384]{1,0:T(8,128)(2,1)S(1)}, u32[]{:S(2)}, u32[]{:S(2)}) collective-permute-start(bf16[224,384]{1,0:T(8,128)(2,1)S(1)} %get-tuple-element.51), channel_id=1, source_target_pairs={{0,8},{1,9},{2,10},{3,11},{4,12},{5,13},{6,14},{7,15},{8,0},{9,1},... | collective-permute-start | bytes 516104 | tf_op jit(solution)/shard_map/ppermute | solution.py:655
  48.4 5.4 %collective-permute-start.10 = (bf16[192,384]{1,0:T(8,128)(2,1)S(1)}, bf16[192,384]{1,0:T(8,128)(2,1)S(1)}, u32[]{:S(2)}, u32[]{:S(2)}) collective-permute-start(bf16[192,384]{1,0:T(8,128)(2,1)S(1)} %get-tuple-element.52), channel_id=1, source_target_pairs={{0,1},{1,0},{2,3},{3,2},{4,5},{5,4},{6,7},{7,6},{8,9},{9,8},{10,11... | collective-permute-start | bytes 442376 | tf_op jit(solution)/shard_map/ppermute | solution.py:662
